TPU v7x, 256 devices: a whole 4x4x8 slice. The times are simulated.
256 devices in a mesh: ka: 8 (over z_lo, core), ga: 32 (over x, y, z_hi).
Axes of the slice: x: 4, y: 4, z: 8 (z_hi: 2, z_lo: 4; z = z_hi * 4 + z_lo), core: 2. Of those that a mesh axis runs over, the one named last changes fastest.
Arguments:
- wavefunctions: bfloat16 [64, 2, 16, 32, 256], P('ka', None, None, 'ga'), may hold values from -6 to 6
- partner: int32 [64], replicated, may hold values from 0 to 63, each once
- gmap: int32 [8192], replicated, may hold values from 0 to 8191, as said below
- screened: bfloat16 [8192, 8192], P('ga'), may hold values from -0.0007324219 to 0.0007324219
Outputs:
- kernel_rows: float32 [64, 2, 4096], P('ka')
- kernel_mirror: float32 [64, 2, 4096], P('ka')
Inputs may be any that keep to these rules, and one draw needn't show every extreme that they name: `partner`: each k-point appears exactly once. Entries j and gmap[j] lie in the same aligned block of 32; within each block every index appears once.
All inputs are finite; a program needn't handle non-finite values.
Results may differ from a plain program's by a relative error of at most 0.0042.
Values may be sent and summed in bfloat16 or wider, within the bound.
No kernel may reach another device: no remote copies, remote signals or barrier semaphores. Data moves between devices by JAX's collectives and lax.ppermute only.
A program may use at most 256 MiB of HBM per device.

v0:
```python
import math

import jax
import jax.numpy as jnp
import numpy as np
from jax import lax
from jax.experimental import pallas as pl
from jax.experimental.pallas import tpu as pltpu
from jax.sharding import PartitionSpec as P

NX = 16
NY = 16
NZ = 32
NG = 8192
PLANE = NX * NY
HALF = NZ // 2 + 1
LINE_BLOCKS = 4
NORM = 1.0 / math.sqrt(NG)
EXACT = lax.Precision.HIGHEST
BF = jnp.bfloat16
F32 = jnp.float32
MIB = 1 << 20

SHAPE = (4, 4, 2)
XS = ((1, 0, 0), (3, 0, 0), (2, 0, 0))
YS = ((0, 1, 0), (0, 3, 0), (0, 2, 0))
ZS = ((0, 0, 1),)
SLOT = (0, 1, 3, 2)
LEVELS = [[place * 2 + z for place in range(16)] for z in range(2)]


def split_table(table):
    high = table.astype(np.float32).astype(BF)
    low = (table - high.astype(np.float64)).astype(np.float32).astype(BF)
    return high, low


def plane_angles():
    index = np.arange(PLANE)
    x, y = index // NY, index % NY
    turns = (np.outer(x, x) % NX) / NX + (np.outer(y, y) % NY) / NY
    return 2.0 * np.pi * turns


def line_angles():
    index = np.arange(NZ)
    return 2.0 * np.pi * (np.outer(index, index) % NZ) / NZ


def shifted(value, offset):
    pairs = []
    for source in range(32):
        place = (source // 8, source // 2 % 4, source % 2)
        x, y, z = ((a + b) % n for a, b, n in zip(place, offset, SHAPE))
        pairs.append((source, x * 8 + y * 2 + z))
    return lax.ppermute(value, "ga", pairs)


def spread(value, offsets):
    return jnp.stack([value] + [shifted(value, offset) for offset in offsets])


def around_ka(value):
    return [value] + [
        lax.ppermute(value, "ka", [(i, (i + d) % 8) for i in range(8)]) for d in range(1, 8)
    ]


def gather_planes(value):
    for offsets in (ZS, XS, YS):
        value = spread(value, offsets)
    return value.reshape((32,) + value.shape[3:])


def copies_to_all(value, count, axis, groups=None):
    copies = jnp.broadcast_to(value[None], (count,) + value.shape)
    return lax.all_to_all(
        copies, axis, split_axis=0, concat_axis=0, axis_index_groups=groups, tiled=True
    )


def gather_early(value):
    both = spread(value, ZS)
    full = lax.all_gather(both, "ga", axis_index_groups=LEVELS)
    return full.reshape((32,) + value.shape)


def plane_slots(place):
    z = jnp.arange(32, dtype=jnp.int32)
    slot = jnp.array(SLOT, dtype=jnp.int32)
    sx = slot[(place // 8 - z // 8) % 4]
    sy = slot[(place // 2 - z // 2) % 4]
    sz = (place - z) % 2
    return z // 2 * 2 + sz, (sy * 4 + sx) * 2 + sz


def dot(a, b, contract=((1,), (0,)), precision=None):
    return lax.dot_general(
        a, b, (contract, ((), ())), precision=precision, preferred_element_type=F32
    )


def line_kernel(gmap_ref, high_ref, low_ref, w_ref, y_ref):
    rows = 2 * HALF * 8
    keep = (lax.broadcasted_iota(jnp.int32, (rows, 256), 0) & 7) == (
        lax.broadcasted_iota(jnp.int32, (rows, 256), 1) >> 5
    )
    for b in range(LINE_BLOCKS):
        level = gmap_ref[b] & (NZ - 1)
        hot = (lax.broadcasted_iota(jnp.int32, (NZ, 256), 0) == level).astype(F32).astype(BF)
        block = w_ref[:, b * 256 : (b + 1) * 256]
        total = None
        for table in (high_ref, low_ref):
            picked = jnp.where(keep, dot(table[...], hot), 0.0).astype(BF)
            part = dot(picked, block, ((1,), (1,)))
            total = part if total is None else total + part
        y_ref[:, :, b * 8 : (b + 1) * 8, :] = total.reshape(2, HALF, 8, 256)


def line_transform(screened, gmap):
    angles = line_angles()[:HALF]
    table = np.stack([np.cos(angles), -np.sin(angles)])
    table = np.repeat(table.reshape(2 * HALF, NZ), 8, axis=0)
    high, low = split_table(table)
    rows = 2 * HALF * 8
    n = LINE_BLOCKS
    return pl.pallas_call(
        line_kernel,
        grid=(32 // n,),
        in_specs=[
            pl.BlockSpec((n, 1, 256), lambda b: (b, 0, 0)),
            pl.BlockSpec((rows, NZ), lambda b: (0, 0)),
            pl.BlockSpec((rows, NZ), lambda b: (0, 0)),
            pl.BlockSpec((256, n * 256), lambda b: (0, b)),
        ],
        out_specs=pl.BlockSpec((2, HALF, n * 8, 256), lambda b: (0, 0, b, 0)),
        out_shape=jax.ShapeDtypeStruct((2, HALF, PLANE, 256), F32),
        compiler_params=pltpu.CompilerParams(vmem_limit_bytes=32 * MIB),
        cost_estimate=pl.CostEstimate(
            flops=4 * rows * 256 * 8192, bytes_accessed=14 * MIB, transcendentals=0
        ),
        name="screened_line",
    )(gmap.reshape(32, 1, 256), jnp.asarray(high), jnp.asarray(low), screened)


def plane_kernel(high_ref, low_ref, y_ref, w_ref):
    real, imag = y_ref[0, 0], y_ref[1, 0]
    for odd in range(2):
        if odd:
            both = [real[:128] - real[128:], imag[:128] - imag[128:]]
        else:
            both = [real[:128] + real[128:], imag[:128] + imag[128:]]
        both = jnp.concatenate(both, axis=0)
        top = both.astype(BF)
        rest = (both - top.astype(F32)).astype(BF)
        high, low = high_ref[odd], low_ref[odd]
        prod = (dot(high, top) + (dot(high, rest) + dot(low, top))).astype(BF)
        for half in range(8):
            at = (2 * half + odd) * NY
            w_ref[0, at : at + NY] = prod[half * NY : (half + 1) * NY]
            w_ref[0, 256 + at : 256 + at + NY] = prod[128 + half * NY : 128 + (half + 1) * NY]


def plane_transform(lines):
    angles = plane_angles().reshape(NX, NY, PLANE)[:, :, :128]
    tables = []
    for odd in range(2):
        part = angles[odd::2].reshape(128, 128)
        cosine, sine = np.cos(part), np.sin(part)
        tables.append(np.block([[cosine, sine], [sine, -cosine]]))
    high, low = split_table(np.stack(tables))
    return pl.pallas_call(
        plane_kernel,
        grid=(HALF,),
        in_specs=[
            pl.BlockSpec((2, 256, 256), lambda z: (0, 0, 0)),
            pl.BlockSpec((2, 256, 256), lambda z: (0, 0, 0)),
            pl.BlockSpec((2, 1, 256, 256), lambda z: (0, z, 0, 0)),
        ],
        out_specs=pl.BlockSpec((1, 512, 256), lambda z: (z, 0, 0)),
        out_shape=jax.ShapeDtypeStruct((HALF, 512, 256), BF),
        compiler_params=pltpu.CompilerParams(vmem_limit_bytes=24 * MIB),
        cost_estimate=pl.CostEstimate(
            flops=12 * 256 * 256 * 256 * HALF, bytes_accessed=14 * MIB, transcendentals=0
        ),
        name="screened_plane",
    )(jnp.asarray(high), jnp.asarray(low), lines)


def choose_kernel(slot_ref, flip_ref, *refs):
    slots, (val_ref, cond_ref) = refs[:8], refs[8:]
    for m in range(8):
        wanted = slot_ref[m]
        for d in range(8):

            @pl.when(wanted // 8 == d)
            def _(m=m, d=d):
                row = slots[d][wanted % 8]
                val_ref[m] = dot(row[:16], flip_ref[...]).astype(BF)
                cond_ref[m] = row[16:]


def choose(slots, wanted, flip):
    shape = jax.ShapeDtypeStruct((8, 16, 256), BF)
    return pl.pallas_call(
        choose_kernel,
        in_specs=[pl.BlockSpec(memory_space=pltpu.SMEM)]
        + [pl.BlockSpec(memory_space=pltpu.VMEM)] * 9,
        out_specs=[pl.BlockSpec(memory_space=pltpu.VMEM)] * 2,
        out_shape=[shape, shape],
        compiler_params=pltpu.CompilerParams(vmem_limit_bytes=16 * MIB),
        name="partner_choice",
    )(wanted, flip, *slots)


def cond_kernel(table_ref, home_ref, away_ref, x_ref, rows_ref):
    for k in range(8):
        home, away = home_ref[k].astype(F32), away_ref[k].astype(F32)
        hr, hi = home[:8], home[8:]
        for place, band in enumerate((0, 2, 4, 6, 1, 3, 5, 7)):
            ar, ai = away[band : band + 1], away[8 + band : 9 + band]
            real = hr * ar + hi * ai
            imag = hr * ai - hi * ar
            at = k * 128 + place * 8
            rows_ref[at : at + 8, :256] = real
            rows_ref[at : at + 8, 256:] = imag
            rows_ref[at + 64 : at + 72, :256] = imag
            rows_ref[at + 64 : at + 72, 256:] = -real
    for k in range(8):
        x_ref[:, k * 128 : (k + 1) * 128] = dot(
            table_ref[...], rows_ref[k * 128 : (k + 1) * 128], ((1,), (1,)), EXACT
        )


def cond_planes(home, away):
    angles = plane_angles()
    table = np.concatenate([np.cos(angles), np.sin(angles)], axis=1).astype(np.float32)
    return pl.pallas_call(
        cond_kernel,
        out_shape=jax.ShapeDtypeStruct((256, 1024), F32),
        in_specs=[pl.BlockSpec(memory_space=pltpu.VMEM)] * 3,
        out_specs=pl.BlockSpec(memory_space=pltpu.VMEM),
        scratch_shapes=[pltpu.VMEM((1024, 512), F32)],
        compiler_params=pltpu.CompilerParams(vmem_limit_bytes=24 * MIB),
        cost_estimate=pl.CostEstimate(
            flops=12 * 256 * 512 * 1024, bytes_accessed=2 * MIB, transcendentals=0
        ),
        name="cond_planes",
    )(jnp.asarray(table), home, away)


def response_kernel(ih_ref, ia_ref, *refs):
    (home_ref, away_ref, home_back_ref, away_back_ref), (w_ref, out_ref, rows_ref) = refs[:4], refs[4:]
    z = pl.program_id(0)
    mirrored = jnp.where(lax.rem(z, 16) == 0, 0.0, 1.0)

    @pl.when(z == 0)
    def _():
        out_ref[...] = jnp.zeros_like(out_ref)

    def density(home, away, v):
        hr, hi = home[v : v + 1], home[8 + v : 9 + v]
        ar, ai = away[:8], away[8:]
        return hr * ar + hi * ai, hr * ai - hi * ar

    def one(k, carry):
        home, away = home_ref[0, k].astype(F32), away_ref[0, k].astype(F32)
        home_back = home_back_ref[0, k].astype(F32) * mirrored
        away_back = away_back_ref[0, k].astype(F32)
        at = k * 128
        for pair in range(4):
            pieces = []
            for v in (2 * pair, 2 * pair + 1):
                real, imag = density(home, away, v)
                real_back, imag_back = density(home_back, away_back, v)
                pieces.append(
                    (real + real_back, imag - imag_back, imag + imag_back, real_back - real)
                )
            even_re, odd_im, even_im, odd_re = (
                jnp.concatenate(p, axis=0).astype(BF) for p in zip(*pieces)
            )
            here = pl.ds(pl.multiple_of(at + pair * 16, 16), 16)
            there = pl.ds(pl.multiple_of(at + 64 + pair * 16, 16), 16)
            rows_ref[here, :256] = even_re
            rows_ref[here, 256:] = odd_im
            rows_ref[there, :256] = even_im
            rows_ref[there, 256:] = odd_re
        return carry

    lax.fori_loop(0, 8, one, 0)
    out_ref[...] += dot(rows_ref[...], w_ref[0])


def response(place, home, away, screened):
    ih, ia = plane_slots(place)

    def block(which, back):
        def index(z, ih, ia):
            plane = lax.rem(NZ - z, NZ) if back else z
            return ((ih, ia)[which][plane], 0, 0, 0)

        return pl.BlockSpec((1, 8, 16, 256), index)

    return pl.pallas_call(
        response_kernel,
        grid_spec=pltpu.PrefetchScalarGridSpec(
            num_scalar_prefetch=2,
            grid=(HALF,),
            in_specs=[
                block(0, False),
                block(1, False),
                block(0, True),
                block(1, True),
                pl.BlockSpec((1, 512, 256), lambda z, ih, ia: (z, 0, 0)),
            ],
            out_specs=pl.BlockSpec((1024, 256), lambda z, ih, ia: (0, 0)),
            scratch_shapes=[pltpu.VMEM((1024, 512), BF)],
        ),
        out_shape=jax.ShapeDtypeStruct((1024, 256), F32),
        compiler_params=pltpu.CompilerParams(vmem_limit_bytes=56 * MIB),
        cost_estimate=pl.CostEstimate(
            flops=2 * 1024 * 512 * 256 * HALF, bytes_accessed=9 * MIB, transcendentals=0
        ),
        name="valence_response",
    )(ih, ia, home, away, home, away, screened)


def spectrum_kernel(cos_ref, sin_ref, x_ref, out_ref):
    first = lax.broadcasted_iota(jnp.int32, (1, 128), 1) < 64
    for k in range(8):
        x = x_ref[:, k * 128 : (k + 1) * 128]
        turned = pltpu.roll(x, 64, 1)
        turned = jnp.where(first, turned, -turned)
        cond = dot(cos_ref[...], x, precision=EXACT) + dot(sin_ref[...], turned, precision=EXACT)
        cond = (cond * NORM).astype(BF).astype(F32).T
        out_ref[k * 128 : (k + 1) * 128] = cond.astype(BF)


def cond_spectrum(cosine, sine, columns):
    return pl.pallas_call(
        spectrum_kernel,
        out_shape=jax.ShapeDtypeStruct((1024, 256), BF),
        in_specs=[pl.BlockSpec(memory_space=pltpu.VMEM)] * 3,
        out_specs=pl.BlockSpec(memory_space=pltpu.VMEM),
        compiler_params=pltpu.CompilerParams(vmem_limit_bytes=24 * MIB),
        cost_estimate=pl.CostEstimate(
            flops=24 * 256 * 256 * 1024, bytes_accessed=2 * MIB, transcendentals=0
        ),
        name="cond_spectrum",
    )(cosine, sine, columns)


def block_kernel(cond_ref, r_ref, out_ref):
    first = lax.broadcasted_iota(jnp.int32, (1, 128), 1) < 64
    for k in range(8):
        cond = cond_ref[k * 128 : (k + 1) * 128]
        rows = r_ref[k * 128 : (k + 1) * 128] * NORM
        top = rows.astype(BF)
        rest = (rows - top.astype(F32)).astype(BF)
        prod = dot(cond, top, ((1,), (1,))) + dot(cond, rest, ((1,), (1,)))
        swapped = pltpu.roll(prod[64:], 64, 1)
        both = prod[:64] + jnp.where(first, swapped, -swapped)
        even, odd = both[:32], both[32:]
        out_ref[:, 2 * k, :] = jnp.where(first, even, pltpu.roll(odd, 64, 1))
        out_ref[:, 2 * k + 1, :] = jnp.where(first, pltpu.roll(even, 64, 1), odd)


def kernel_blocks(cond, rows):
    return pl.pallas_call(
        block_kernel,
        out_shape=jax.ShapeDtypeStruct((32, 16, 128), F32),
        in_specs=[pl.BlockSpec(memory_space=pltpu.VMEM)] * 2,
        out_specs=pl.BlockSpec(memory_space=pltpu.VMEM),
        compiler_params=pltpu.CompilerParams(vmem_limit_bytes=24 * MIB),
        cost_estimate=pl.CostEstimate(
            flops=4 * 128 * 256 * 1024, bytes_accessed=2 * MIB, transcendentals=0
        ),
        name="kernel_blocks",
    )(cond, rows)


def line_tables(gmap, place):
    level = lax.dynamic_slice_in_dim(gmap, place * 256, 256) & (NZ - 1)
    column = jnp.arange(256, dtype=jnp.int32)
    angle = (level[:, None] * (column // 8)[None, :]) % NZ
    same = (column // NZ)[:, None] == (column % 8)[None, :]
    angle = angle.astype(F32) * (2.0 * math.pi / NZ)
    return jnp.where(same, jnp.cos(angle), 0.0), jnp.where(same, jnp.sin(angle), 0.0)


def on_device(wavefunctions, partner, gmap, screened):
    ka_place = lax.axis_index("ka")
    place = lax.axis_index("ga")
    owned = ka_place * 8 + jnp.arange(8, dtype=jnp.int32)
    source = (ka_place - jnp.arange(8, dtype=jnp.int32)) % 8
    slot_owner = (source[:, None] * 8 + jnp.arange(8, dtype=jnp.int32)[None, :]).reshape(64)

    waves = wavefunctions.reshape(8, 2, 2, 8, 256).transpose(0, 2, 1, 3, 4).reshape(8, 32, 256)
    slots = around_ka(waves)
    index = jnp.arange(PLANE, dtype=jnp.int32)
    negative = (NX - index // NY) % NX * NY + (NY - index % NY) % NY
    negative = jnp.where(place > NZ // 2, negative, index)
    flip = (index[:, None] == negative[None, :]).astype(BF)
    home_val = dot(waves[:, :16].reshape(128, 256), flip).astype(BF).reshape(8, 16, 256)
    home = gather_early(home_val)

    lines = line_transform(screened, gmap)

    wanted = partner[owned]
    wanted_slot = jnp.argmax(wanted[:, None] == slot_owner[None, :], axis=1).astype(jnp.int32)
    away_val, away_cond = choose(slots, wanted_slot, flip)
    lines, away_val, away_cond = lax.optimization_barrier((lines, away_val, away_cond))
    away = gather_planes(away_val)

    planes = cond_planes(waves[:, 16:], away_cond)
    columns = lax.all_to_all(planes, "ga", split_axis=0, concat_axis=0, tiled=True)
    wide = plane_transform(lines)
    cond = cond_spectrum(*line_tables(gmap, place), columns)

    blocks = kernel_blocks(cond, response(place, home, away, wide))

    parts = lax.all_to_all(blocks, "ga", split_axis=0, concat_axis=0, tiled=True)
    mine = jnp.sum(parts, axis=0)
    everyone = copies_to_all(mine, 8, "ka").reshape(64, 256)
    select = (partner[None, :] == owned[:, None]).astype(F32)
    mirror = jnp.dot(select, everyone, precision=EXACT).reshape(16, 128)
    lane = jnp.arange(128, dtype=jnp.int32)
    moved = lane // 64 * 64 + lane % 8 * 8 + lane // 8 % 8
    turn = (lane[:, None] == moved[None, :]).astype(F32)
    sign = jnp.where(jnp.arange(16) % 2 == 0, 1.0, -1.0).astype(F32)
    mirror = jnp.dot(mirror, turn, precision=EXACT) * sign[:, None]
    both = spread(jnp.stack([mine, mirror]), ZS)
    full = copies_to_all(both, 16, "ga", LEVELS)
    full = jnp.where(place % 2 == 0, full, full[:, ::-1])
    full = full.reshape(4, 8, 2, 8, 2, 2, 64)
    rows_out = full[:, :, 0].transpose(2, 3, 1, 0, 4, 5).reshape(8, 2, 4096)
    mirror_out = full[:, :, 1].transpose(2, 3, 0, 4, 1, 5).reshape(8, 2, 4096)
    return rows_out, mirror_out


def solution(mesh):
    in_specs = (P("ka", None, None, "ga", None), P(), P(), P("ga", None))
    out_specs = (P("ka", None, None), P("ka", None, None))
    return jax.shard_map(
        on_device, mesh=mesh, in_specs=in_specs, out_specs=out_specs, check_vma=False
    )
```

profile of v0, /device:TPU:8, one launch (start us, length us, event | category | flops | bytes accessed | tf_op | source)
XLA Modules:
  0.0 220.2 jit_solution(4473956074074416846)
XLA Ops:
  8.4 7.3 %collective-permute-start.7 = (bf16[8,16,256]{2,1,0:T(8,128)(2,1)S(1)}, bf16[8,16,256]{2,1,0:T(8,128)(2,1)S(1)}, u32[]{:S(2)}, u32[]{:S(2)}) collective-permute-start(bf16[8,16,256]{2,1,0:T(8,128)(2,1)S(1)} %bitcast.77), channel_id=1, source_target_pairs={{0,1},{1,0},{2,3},{3,2},{4,5},{5,4},{6,7},{7,6},{8,9},{9,8},{10,11... | collective-permute-start | bytes 196616 | tf_op jit(solution)/shard_map/ppermute | solution.py:56
  15.6 2.4 %collective-permute-done.7 = bf16[8,16,256]{2,1,0:T(8,128)(2,1)S(1)} collective-permute-done((bf16[8,16,256]{2,1,0:T(8,128)(2,1)S(1)}, bf16[8,16,256]{2,1,0:T(8,128)(2,1)S(1)}, u32[]{:S(2)}, u32[]{:S(2)}) %collective-permute-start.7) | collective-permute-done | bytes 65568 | tf_op jit(solution)/shard_map/ppermute | solution.py:56
  27.3 2.1 collective-permute-start.5
  30.7 2.2 copy-done.3
  35.4 8.5 %screened_line.1.y_ref = f32[2,17,256,256]{3,2,1,0:T(8,128)S(1)} custom-call(s32[32,1,256]{2,1,0:T(1,128)S(1)} %bitcast.65, bf16[272,32]{1,0:T(8,128)(2,1)S(1)} %copy-done.7, bf16[272,32]{1,0:T(8,128)(2,1)S(1)} %copy-done.8, bf16[256,8192]{1,0:T(8,128)(2,1)S(1)} %copy-done.3), custom_call_target="tpu_custom_call" | custom-call | flops 2281701376 | bytes 14680064 | tf_op jit(solution)/shard_map/screened_line/pallas_call | solution.py:127
  43.9 3.5 %copy-done = f32[2,17,256,256]{3,2,1,0:T(8,128)} copy-done((f32[2,17,256,256]{3,2,1,0:T(8,128)}, f32[2,17,256,256]{3,2,1,0:T(8,128)S(1)}, u32[]{:S(2)}) %copy-start) | copy-done | bytes 8912920
  49.3 4.5 %cond_planes.1 = f32[256,1024]{1,0:T(8,128)} custom-call(f32[256,512]{1,0:T(8,128)S(1)} %copy-done.10, bf16[8,16,256]{2,1,0:T(8,128)(2,1)S(1)} %get-tuple-element.27.home_ref, bf16[8,16,256]{2,1,0:T(8,128)(2,1)S(1)} %get-tuple-element.11.away_ref), custom_call_target="tpu_custom_call" | custom-call | flops 1610612736 | bytes 2097152 | tf_op jit(solution)/shard_map/cond_planes/pallas_call | solution.py:238
  53.8 12.1 %all-to-all-start = ((f32[32,8,1024]{2,1,0:T(8,128)}), f32[32,8,1024]{2,1,0:T(8,128)S(1)}, u32[]{:S(2)}, u32[]{:S(2)}) async-start(f32[32,8,1024]{2,1,0:T(8,128)} %bitcast.6), calls=%async_computation | async-start | bytes 2097152 | tf_op jit(solution)/shard_map/all_to_all | solution.py:416
  65.9 5.5 %collective-permute-start.8 = (bf16[8,16,256]{2,1,0:T(8,128)(2,1)S(1)}, bf16[8,16,256]{2,1,0:T(8,128)(2,1)S(1)}, u32[]{:S(2)}, u32[]{:S(2)}) collective-permute-start(bf16[8,16,256]{2,1,0:T(8,128)(2,1)S(1)} %get-tuple-element.12), channel_id=1, source_target_pairs={{0,1},{1,0},{2,3},{3,2},{4,5},{5,4},{6,7},{7,6},{8,9},{9,8},{10,11... | collective-permute-start | bytes 196616 | tf_op jit(solution)/shard_map/ppermute | solution.py:56
  71.4 18.7 %collective-permute-done.8 = bf16[8,16,256]{2,1,0:T(8,128)(2,1)S(1)} collective-permute-done((bf16[8,16,256]{2,1,0:T(8,128)(2,1)S(1)}, bf16[8,16,256]{2,1,0:T(8,128)(2,1)S(1)}, u32[]{:S(2)}, u32[]{:S(2)}) %collective-permute-start.8) | collective-permute-done | bytes 65568 | tf_op jit(solution)/shard_map/ppermute | solution.py:56
  97.4 2.4 %collective-permute-done.11 = bf16[2,8,16,256]{3,2,1,0:T(8,128)(2,1)S(1)} collective-permute-done((bf16[2,8,16,256]{3,2,1,0:T(8,128)(2,1)S(1)}, bf16[2,8,16,256]{3,2,1,0:T(8,128)(2,1)S(1)}, u32[]{:S(2)}, u32[]{:S(2)}) %collective-permute-start.11) | collective-permute-done | bytes 131104 | tf_op jit(solution)/shard_map/ppermute | solution.py:56
  101.5 4.4 %collective-permute-start.13 = (bf16[4,2,8,16,256]{4,3,2,1,0:T(8,128)(2,1)S(1)}, bf16[4,2,8,16,256]{4,3,2,1,0:T(8,128)(2,1)S(1)}, u32[]{:S(2)}, u32[]{:S(2)}) collective-permute-start(bf16[4,2,8,16,256]{4,3,2,1,0:T(8,128)(2,1)S(1)} %get-tuple-element.23), channel_id=1, source_target_pairs={{0,6},{1,7},{2,0},{3,1},{4,2},{5,3},{6,4},{7,5},{8,14},{9,15},{10,... | collective-permute-start | bytes 1572872 | tf_op jit(solution)/shard_map/ppermute | solution.py:56
  109.0 3.5 %copy-done.1 = f32[2,17,256,256]{3,2,1,0:T(8,128)S(1)} copy-done((f32[2,17,256,256]{3,2,1,0:T(8,128)S(1)}, f32[2,17,256,256]{3,2,1,0:T(8,128)}, u32[]{:S(2)}) %copy-start.1) | copy-done | bytes 8912920
  112.5 7.5 %screened_plane.1.refs_4_ = bf16[17,512,256]{2,1,0:T(8,128)(2,1)S(1)} custom-call(bf16[2,256,256]{2,1,0:T(8,128)(2,1)S(1)} %copy-done.5, bf16[2,256,256]{2,1,0:T(8,128)(2,1)S(1)} %copy-done.6, f32[2,17,256,256]{3,2,1,0:T(8,128)S(1)} %copy-done.1), custom_call_target="tpu_custom_call" | custom-call | flops 3422552064 | bytes 14680064 | tf_op jit(solution)/shard_map/screened_plane/pallas_call | solution.py:172
  122.1 3.0 %collective-permute-done.14 = bf16[4,2,8,16,256]{4,3,2,1,0:T(8,128)(2,1)S(1)} collective-permute-done((bf16[4,2,8,16,256]{4,3,2,1,0:T(8,128)(2,1)S(1)}, bf16[4,2,8,16,256]{4,3,2,1,0:T(8,128)(2,1)S(1)}, u32[]{:S(2)}, u32[]{:S(2)}) %collective-permute-start.14) | collective-permute-done | bytes 524320 | tf_op jit(solution)/shard_map/ppermute | solution.py:56
  126.7 3.7 %cond_spectrum.1.cond_ref = bf16[1024,256]{1,0:T(8,128)(2,1)S(1)} custom-call(f32[256,256]{1,0:T(8,128)S(1)} %get-tuple-element.31.cos_ref, f32[256,256]{1,0:T(8,128)S(1)} %get-tuple-element.30.sin_ref, f32[256,1024]{1,0:T(8,128)S(1)} %bitcast.63), custom_call_target="tpu_custom_call" | custom-call | flops 1610612736 | bytes 2097152 | tf_op jit(solution)/shard_map/cond_spectrum/pallas_call | solution.py:340
  130.4 19.7 %valence_response.1.r_ref = f32[1024,256]{1,0:T(8,128)} custom-call(s32[32]{0:T(128)} %get-tuple-element.32.ih_ref, s32[32]{0:T(128)} %get-tuple-element.33.ia_ref, bf16[32,8,16,256]{3,2,1,0:T(8,128)(2,1)} %all-gather.3.cloned.1.call-done.refs_0_.refs_2_, bf16[32,8,16,256]{3,2,1,0:T(8,128)(2,1)} %bitcast.66, ...), custom_call_target="tpu_custom_call" | custom-call | flops 4563402752 | bytes 9437184 | tf_op jit(solution)/shard_map/valence_response/pallas_call | solution.py:304
  152.6 5.9 %all-to-all-start.1 = ((f32[32,16,128]{2,1,0:T(8,128)}), f32[32,16,128]{2,1,0:T(8,128)S(1)}, u32[]{:S(2)}, u32[]{:S(2)}) async-start(f32[32,16,128]{2,1,0:T(8,128)} %kernel_blocks.1), calls=%async_computation.1 | async-start | bytes 524288 | tf_op jit(solution)/shard_map/all_to_all | solution.py:422
  158.5 12.3 %all-to-all-done.1 = f32[32,16,128]{2,1,0:T(8,128)S(1)} async-done(((f32[32,16,128]{2,1,0:T(8,128)}), f32[32,16,128]{2,1,0:T(8,128)S(1)}, u32[]{:S(2)}, u32[]{:S(2)}) %all-to-all-start.1) | async-done | bytes 262176 | tf_op jit(solution)/shard_map/all_to_all | solution.py:422
  171.5 9.1 %all-to-all-start.2 = ((f32[8,16,128]{2,1,0:T(8,128)}), f32[8,16,128]{2,1,0:T(8,128)S(1)}, u32[]{:S(2)}, u32[]{:S(2)}) async-start(f32[8,16,128]{2,1,0:T(8,128)} %broadcast_in_dim.16), calls=%async_computation.2 | async-start | bytes 131072 | tf_op jit(solution)/shard_map/all_to_all | solution.py:77
  180.6 5.9 %all-to-all-done.2 = f32[8,16,128]{2,1,0:T(8,128)S(1)} async-done(((f32[8,16,128]{2,1,0:T(8,128)}), f32[8,16,128]{2,1,0:T(8,128)S(1)}, u32[]{:S(2)}, u32[]{:S(2)}) %all-to-all-start.2) | async-done | bytes 65568 | tf_op jit(solution)/shard_map/all_to_all | solution.py:77
  187.6 7.0 %collective-permute-done.15 = f32[2,16,128]{2,1,0:T(8,128)S(1)} collective-permute-done((f32[2,16,128]{2,1,0:T(8,128)S(1)}, f32[2,16,128]{2,1,0:T(8,128)S(1)}, u32[]{:S(2)}, u32[]{:S(2)}) %collective-permute-start.15) | collective-permute-done | bytes 16416 | tf_op jit(solution)/shard_map/ppermute | solution.py:56
  195.5 4.8 %all-to-all-start.3 = ((f32[16,2,2,16,128]{4,3,2,1,0:T(8,128)}), f32[16,2,2,16,128]{4,3,2,1,0:T(8,128)S(1)}, u32[]{:S(2)}, u32[]{:S(2)}) async-start(f32[16,2,2,16,128]{4,3,2,1,0:T(8,128)} %broadcast_in_dim.19), calls=%async_computation.3 | async-start | bytes 1048576 | tf_op jit(solution)/shard_map/all_to_all | solution.py:77
  200.3 9.2 %all-to-all-done.3 = f32[16,2,2,16,128]{4,3,2,1,0:T(8,128)S(1)} async-done(((f32[16,2,2,16,128]{4,3,2,1,0:T(8,128)}), f32[16,2,2,16,128]{4,3,2,1,0:T(8,128)S(1)}, u32[]{:S(2)}, u32[]{:S(2)}) %all-to-all-start.3) | async-done | bytes 524320 | tf_op jit(solution)/shard_map/all_to_all | solution.py:77
  (89 shorter events, 40.9 us)
Async XLA Ops:
  7.2 123.2 %all-gather.3.cloned.1.call-start = ((), (), s32[]{:S(2)}) async-start(), calls=%async_computation.4 | async-start | bytes 2228224 | tf_op jit(solution)/shard_map/all_gather | solution.py:84
  8.4 9.7 %collective-permute-start.7 = (bf16[8,16,256]{2,1,0:T(8,128)(2,1)S(1)}, bf16[8,16,256]{2,1,0:T(8,128)(2,1)S(1)}, u32[]{:S(2)}, u32[]{:S(2)}) collective-permute-start(bf16[8,16,256]{2,1,0:T(8,128)(2,1)S(1)} %bitcast.77), channel_id=1, source_target_pairs={{0,1},{1,0},{2,3},{3,2},{4,5},{5,4},{6,7},{7,6},{8,9},{9,8},{10,11... | collective-permute-start | bytes 196616 | tf_op jit(solution)/shard_map/ppermute | solution.py:56
  18.8 8.5 %collective-permute-start = (bf16[8,32,256]{2,1,0:T(8,128)(2,1)S(1)}, bf16[8,32,256]{2,1,0:T(8,128)(2,1)S(1)}, u32[]{:S(2)}, u32[]{:S(2)}) collective-permute-start(bf16[8,32,256]{2,1,0:T(8,128)(2,1)S(1)} %bitcast.55), channel_id=1, source_target_pairs={{0,32},{32,64},{64,96},{96,128},{128,160},{160,192},{192,224},{224... | collective-permute-start | bytes 393224 | tf_op jit(solution)/shard_map/ppermute | solution.py:65
  18.8 10.5 %collective-permute-start.1 = (bf16[8,32,256]{2,1,0:T(8,128)(2,1)S(1)}, bf16[8,32,256]{2,1,0:T(8,128)(2,1)S(1)}, u32[]{:S(2)}, u32[]{:S(2)}) collective-permute-start(bf16[8,32,256]{2,1,0:T(8,128)(2,1)S(1)} %bitcast.56), channel_id=1, source_target_pairs={{0,64},{32,96},{64,128},{96,160},{128,192},{160,224},{192,0},{224,... | collective-permute-start | bytes 393224 | tf_op jit(solution)/shard_map/ppermute | solution.py:65
  20.7 26.7 %collective-permute-start.2 = (bf16[8,32,256]{2,1,0:T(8,128)(2,1)S(1)}, bf16[8,32,256]{2,1,0:T(8,128)(2,1)S(1)}, u32[]{:S(2)}, u32[]{:S(2)}) collective-permute-start(bf16[8,32,256]{2,1,0:T(8,128)(2,1)S(1)} %bitcast.57), channel_id=1, source_target_pairs={{0,96},{32,128},{64,160},{96,192},{128,224},{160,0},{192,32},{224,... | collective-permute-start | bytes 393224 | tf_op jit(solution)/shard_map/ppermute | solution.py:65
  22.6 24.8 %collective-permute-start.3 = (bf16[8,32,256]{2,1,0:T(8,128)(2,1)S(1)}, bf16[8,32,256]{2,1,0:T(8,128)(2,1)S(1)}, u32[]{:S(2)}, u32[]{:S(2)}) collective-permute-start(bf16[8,32,256]{2,1,0:T(8,128)(2,1)S(1)} %bitcast.58), channel_id=1, source_target_pairs={{0,128},{32,160},{64,192},{96,224},{128,0},{160,32},{192,64},{224,... | collective-permute-start | bytes 393224 | tf_op jit(solution)/shard_map/ppermute | solution.py:65
  24.4 22.9 %collective-permute-start.4 = (bf16[8,32,256]{2,1,0:T(8,128)(2,1)S(1)}, bf16[8,32,256]{2,1,0:T(8,128)(2,1)S(1)}, u32[]{:S(2)}, u32[]{:S(2)}) collective-permute-start(bf16[8,32,256]{2,1,0:T(8,128)(2,1)S(1)} %bitcast.59), channel_id=1, source_target_pairs={{0,160},{32,192},{64,224},{96,0},{128,32},{160,64},{192,96},{224,1... | collective-permute-start | bytes 393224 | tf_op jit(solution)/shard_map/ppermute | solution.py:65
  27.3 20.1 %collective-permute-start.5 = (bf16[8,32,256]{2,1,0:T(8,128)(2,1)S(1)}, bf16[8,32,256]{2,1,0:T(8,128)(2,1)S(1)}, u32[]{:S(2)}, u32[]{:S(2)}) collective-permute-start(bf16[8,32,256]{2,1,0:T(8,128)(2,1)S(1)} %bitcast.60), channel_id=1, source_target_pairs={{0,192},{32,224},{64,0},{96,32},{128,64},{160,96},{192,128},{224,1... | collective-permute-start | bytes 393224 | tf_op jit(solution)/shard_map/ppermute | solution.py:65
  29.3 18.1 %collective-permute-start.6 = (bf16[8,32,256]{2,1,0:T(8,128)(2,1)S(1)}, bf16[8,32,256]{2,1,0:T(8,128)(2,1)S(1)}, u32[]{:S(2)}, u32[]{:S(2)}) collective-permute-start(bf16[8,32,256]{2,1,0:T(8,128)(2,1)S(1)} %bitcast.61), channel_id=1, source_target_pairs={{0,224},{32,0},{64,32},{96,64},{128,96},{160,128},{192,160},{224,1... | collective-permute-start | bytes 393224 | tf_op jit(solution)/shard_map/ppermute | solution.py:65
  53.8 55.2 %copy-start.5 = (bf16[2,256,256]{2,1,0:T(8,128)(2,1)S(1)}, bf16[2,256,256]{2,1,0:T(8,128)(2,1)}, u32[]{:S(2)}) copy-start(bf16[2,256,256]{2,1,0:T(8,128)(2,1)} %constant.272.clone.high_ref) | copy-start | bytes 786436
  53.8 55.2 %copy-start.6 = (bf16[2,256,256]{2,1,0:T(8,128)(2,1)S(1)}, bf16[2,256,256]{2,1,0:T(8,128)(2,1)}, u32[]{:S(2)}) copy-start(bf16[2,256,256]{2,1,0:T(8,128)(2,1)} %constant.273.clone.low_ref) | copy-start | bytes 786436
  53.8 72.9 %all-to-all-start = ((f32[32,8,1024]{2,1,0:T(8,128)}), f32[32,8,1024]{2,1,0:T(8,128)S(1)}, u32[]{:S(2)}, u32[]{:S(2)}) async-start(f32[32,8,1024]{2,1,0:T(8,128)} %bitcast.6), calls=%async_computation | async-start | bytes 2097152 | tf_op jit(solution)/shard_map/all_to_all | solution.py:416
  65.9 24.1 %collective-permute-start.8 = (bf16[8,16,256]{2,1,0:T(8,128)(2,1)S(1)}, bf16[8,16,256]{2,1,0:T(8,128)(2,1)S(1)}, u32[]{:S(2)}, u32[]{:S(2)}) collective-permute-start(bf16[8,16,256]{2,1,0:T(8,128)(2,1)S(1)} %get-tuple-element.12), channel_id=1, source_target_pairs={{0,1},{1,0},{2,3},{3,2},{4,5},{5,4},{6,7},{7,6},{8,9},{9,8},{10,11... | collective-permute-start | bytes 196616 | tf_op jit(solution)/shard_map/ppermute | solution.py:56
  90.1 7.4 %collective-permute-start.9 = (bf16[2,8,16,256]{3,2,1,0:T(8,128)(2,1)S(1)}, bf16[2,8,16,256]{3,2,1,0:T(8,128)(2,1)S(1)}, u32[]{:S(2)}, u32[]{:S(2)}) collective-permute-start(bf16[2,8,16,256]{3,2,1,0:T(8,128)(2,1)S(1)} %get-tuple-element.25), channel_id=1, source_target_pairs={{0,8},{1,9},{2,10},{3,11},{4,12},{5,13},{6,14},{7,15},{8,16},{9,17... | collective-permute-start | bytes 393224 | tf_op jit(solution)/shard_map/ppermute | solution.py:56
  91.6 5.8 %collective-permute-start.10 = (bf16[2,8,16,256]{3,2,1,0:T(8,128)(2,1)S(1)}, bf16[2,8,16,256]{3,2,1,0:T(8,128)(2,1)S(1)}, u32[]{:S(2)}, u32[]{:S(2)}) collective-permute-start(bf16[2,8,16,256]{3,2,1,0:T(8,128)(2,1)S(1)} %get-tuple-element.25), channel_id=1, source_target_pairs={{0,24},{1,25},{2,26},{3,27},{4,28},{5,29},{6,30},{7,31},{8,0},{9,1... | collective-permute-start | bytes 393224 | tf_op jit(solution)/shard_map/ppermute | solution.py:56
  93.4 6.5 %collective-permute-start.11 = (bf16[2,8,16,256]{3,2,1,0:T(8,128)(2,1)S(1)}, bf16[2,8,16,256]{3,2,1,0:T(8,128)(2,1)S(1)}, u32[]{:S(2)}, u32[]{:S(2)}) collective-permute-start(bf16[2,8,16,256]{3,2,1,0:T(8,128)(2,1)S(1)} %get-tuple-element.25), channel_id=1, source_target_pairs={{0,16},{1,17},{2,18},{3,19},{4,20},{5,21},{6,22},{7,23},{8,24},{9,... | collective-permute-start | bytes 393224 | tf_op jit(solution)/shard_map/ppermute | solution.py:56
  99.9 22.1 %collective-permute-start.12 = (bf16[4,2,8,16,256]{4,3,2,1,0:T(8,128)(2,1)S(1)}, bf16[4,2,8,16,256]{4,3,2,1,0:T(8,128)(2,1)S(1)}, u32[]{:S(2)}, u32[]{:S(2)}) collective-permute-start(bf16[4,2,8,16,256]{4,3,2,1,0:T(8,128)(2,1)S(1)} %get-tuple-element.23), channel_id=1, source_target_pairs={{0,2},{1,3},{2,4},{3,5},{4,6},{5,7},{6,0},{7,1},{8,10},{9,11},{10,... | collective-permute-start | bytes 1572872 | tf_op jit(solution)/shard_map/ppermute | solution.py:56
  101.5 20.6 %collective-permute-start.13 = (bf16[4,2,8,16,256]{4,3,2,1,0:T(8,128)(2,1)S(1)}, bf16[4,2,8,16,256]{4,3,2,1,0:T(8,128)(2,1)S(1)}, u32[]{:S(2)}, u32[]{:S(2)}) collective-permute-start(bf16[4,2,8,16,256]{4,3,2,1,0:T(8,128)(2,1)S(1)} %get-tuple-element.23), channel_id=1, source_target_pairs={{0,6},{1,7},{2,0},{3,1},{4,2},{5,3},{6,4},{7,5},{8,14},{9,15},{10,... | collective-permute-start | bytes 1572872 | tf_op jit(solution)/shard_map/ppermute | solution.py:56
  105.9 19.2 %collective-permute-start.14 = (bf16[4,2,8,16,256]{4,3,2,1,0:T(8,128)(2,1)S(1)}, bf16[4,2,8,16,256]{4,3,2,1,0:T(8,128)(2,1)S(1)}, u32[]{:S(2)}, u32[]{:S(2)}) collective-permute-start(bf16[4,2,8,16,256]{4,3,2,1,0:T(8,128)(2,1)S(1)} %get-tuple-element.23), channel_id=1, source_target_pairs={{0,4},{1,5},{2,6},{3,7},{4,0},{5,1},{6,2},{7,3},{8,12},{9,13},{10,... | collective-permute-start | bytes 1572872 | tf_op jit(solution)/shard_map/ppermute | solution.py:56
  151.3 35.3 %copy-start.11 = (s32[64]{0:T(128)S(1)}, s32[64]{0:T(128)}, u32[]{:S(2)}) copy-start(s32[64]{0:T(128)} %param.11) | copy-start | bytes 772
  152.6 18.3 %all-to-all-start.1 = ((f32[32,16,128]{2,1,0:T(8,128)}), f32[32,16,128]{2,1,0:T(8,128)S(1)}, u32[]{:S(2)}, u32[]{:S(2)}) async-start(f32[32,16,128]{2,1,0:T(8,128)} %kernel_blocks.1), calls=%async_computation.1 | async-start | bytes 524288 | tf_op jit(solution)/shard_map/all_to_all | solution.py:422
  171.5 15.0 %all-to-all-start.2 = ((f32[8,16,128]{2,1,0:T(8,128)}), f32[8,16,128]{2,1,0:T(8,128)S(1)}, u32[]{:S(2)}, u32[]{:S(2)}) async-start(f32[8,16,128]{2,1,0:T(8,128)} %broadcast_in_dim.16), calls=%async_computation.2 | async-start | bytes 131072 | tf_op jit(solution)/shard_map/all_to_all | solution.py:77
  186.9 7.7 %collective-permute-start.15 = (f32[2,16,128]{2,1,0:T(8,128)S(1)}, f32[2,16,128]{2,1,0:T(8,128)S(1)}, u32[]{:S(2)}, u32[]{:S(2)}) collective-permute-start(f32[2,16,128]{2,1,0:T(8,128)S(1)} %get-tuple-element.29), channel_id=1, source_target_pairs={{0,1},{1,0},{2,3},{3,2},{4,5},{5,4},{6,7},{7,6},{8,9},{9,8},{10,11... | collective-permute-start | bytes 49160 | tf_op jit(solution)/shard_map/ppermute | solution.py:56
  195.5 14.0 %all-to-all-start.3 = ((f32[16,2,2,16,128]{4,3,2,1,0:T(8,128)}), f32[16,2,2,16,128]{4,3,2,1,0:T(8,128)S(1)}, u32[]{:S(2)}, u32[]{:S(2)}) async-start(f32[16,2,2,16,128]{4,3,2,1,0:T(8,128)} %broadcast_in_dim.19), calls=%async_computation.3 | async-start | bytes 1048576 | tf_op jit(solution)/shard_map/all_to_all | solution.py:77
  (9 other events, 28.8 us)
Sparse Core Ops, SparseCore 0:
  18.9 54.2 all-gather.2
where the time goes:
time: 221 us; the launch traced here: 220 us
  starting transfers between devices  68.1 us (31%)
  waiting for transfers between devices  61.9 us (28%)
  Pallas kernels  46.9 us (21%)
  local copies, waits for them, and re-layouts  22.6 us (10%)
  between operations  14.4 us (7%)
  other arithmetic  5.81 us (3%)
    ppermute x9, waiting for transfers between devices, shifted(): return lax.ppermute(value, 'ga', pairs)  34.4 us
    ppermute x9, starting transfers between devices, shifted(): return lax.ppermute(value, 'ga', pairs)  26.4 us
    pallas_call x1, Pallas kernels, response(): pl.pallas_call(response_kernel, grid_spec=pltpu.PrefetchScalarGridSpec(nu...  19.7 us
    unnamed x28, local copies, waits for them, and re-layouts  17.7 us
    all_to_all x2, waiting for transfers between devices, copies_to_all(): lax.all_to_all(copies, axis, split_axis=0, concat_axis=0, axis_index_grou...  15.1 us
    all_to_all x2, starting transfers between devices, copies_to_all(): lax.all_to_all(copies, axis, split_axis=0, concat_axis=0, axis_index_grou...  13.9 us
    all_to_all x1, waiting for transfers between devices, on_device(): lax.all_to_all(blocks, 'ga', split_axis=0, concat_axis=0, tiled=True)  12.3 us
    all_to_all x1, starting transfers between devices, on_device(): lax.all_to_all(planes, 'ga', split_axis=0, concat_axis=0, tiled=True)  12.1 us
  transfers between devices with their start and end apart: 21, of which 9 were waited for; matrix products, arithmetic and copies ran while one was open for 3% of the time, Pallas kernels for 12%

commit v1 on v0

v1 whole, which is shorter than its diff:
```python
import functools
import math

import jax
import jax.numpy as jnp
import numpy as np
from jax import lax
from jax.experimental import pallas as pl
from jax.experimental.pallas import tpu as pltpu
from jax.sharding import Mesh
from jax.sharding import PartitionSpec as P

NX = 16
NY = 16
NZ = 32
NG = 8192
PLANE = NX * NY
HALF = NZ // 2 + 1
LINE_BLOCKS = 4
NORM = 1.0 / math.sqrt(NG)
EXACT = lax.Precision.HIGHEST
BF = jnp.bfloat16
F32 = jnp.float32
MIB = 1 << 20

AXES = ("zl", "co", "x", "y", "zh")
SIZES = (4, 2, 4, 4, 2)
SIZE = dict(zip(AXES, SIZES))
KA = ("zl", "co")
GA = ("x", "y", "zh")
VMEM = 48 * MIB


def split_table(table):
    high = table.astype(np.float32).astype(BF)
    low = (table - high.astype(np.float64)).astype(np.float32).astype(BF)
    return high, low


def plane_angles():
    index = np.arange(PLANE)
    x, y = index // NY, index % NY
    turns = (np.outer(x, x) % NX) / NX + (np.outer(y, y) % NY) / NY
    return 2.0 * np.pi * turns


def line_angles():
    index = np.arange(NZ)
    return 2.0 * np.pi * (np.outer(index, index) % NZ) / NZ


def turned(value, axis, step):
    size = SIZE[axis]
    return lax.ppermute(value, axis, [(i, (i + step) % size) for i in range(size)])


def spread(value, axis):
    return jnp.stack([value] + [turned(value, axis, d) for d in range(1, SIZE[axis])])


def copies_to_all(value, axes):
    count = math.prod(SIZE[axis] for axis in axes)
    copies = jnp.broadcast_to(value[None], (count,) + value.shape)
    return lax.all_to_all(copies, axes, split_axis=0, concat_axis=0, tiled=True)


def dot(a, b, contract=((1,), (0,)), precision=None):
    return lax.dot_general(
        a, b, (contract, ((), ())), precision=precision, preferred_element_type=F32
    )


def line_kernel(gmap_ref, high_ref, low_ref, w_ref, y_ref):
    rows = 2 * HALF * 8
    keep = (lax.broadcasted_iota(jnp.int32, (rows, 256), 0) & 7) == (
        lax.broadcasted_iota(jnp.int32, (rows, 256), 1) >> 5
    )
    for b in range(LINE_BLOCKS):
        level = gmap_ref[b] & (NZ - 1)
        hot = (lax.broadcasted_iota(jnp.int32, (NZ, 256), 0) == level).astype(F32).astype(BF)
        block = w_ref[:, b * 256 : (b + 1) * 256]
        total = None
        for table in (high_ref, low_ref):
            picked = jnp.where(keep, dot(table[...], hot), 0.0).astype(BF)
            part = dot(picked, block, ((1,), (1,)))
            total = part if total is None else total + part
        y_ref[:, :, b * 8 : (b + 1) * 8, :] = total.reshape(2, HALF, 8, 256)


def line_transform(screened, gmap):
    angles = line_angles()[:HALF]
    table = np.stack([np.cos(angles), -np.sin(angles)])
    table = np.repeat(table.reshape(2 * HALF, NZ), 8, axis=0)
    high, low = split_table(table)
    rows = 2 * HALF * 8
    n = LINE_BLOCKS
    return pl.pallas_call(
        line_kernel,
        grid=(32 // n,),
        in_specs=[
            pl.BlockSpec((n, 1, 256), lambda b: (b, 0, 0)),
            pl.BlockSpec((rows, NZ), lambda b: (0, 0)),
            pl.BlockSpec((rows, NZ), lambda b: (0, 0)),
            pl.BlockSpec((256, n * 256), lambda b: (0, b)),
        ],
        out_specs=pl.BlockSpec((2, HALF, n * 8, 256), lambda b: (0, 0, b, 0)),
        out_shape=jax.ShapeDtypeStruct((2, HALF, PLANE, 256), F32),
        compiler_params=pltpu.CompilerParams(vmem_limit_bytes=VMEM),
        cost_estimate=pl.CostEstimate(
            flops=4 * rows * 256 * 8192, bytes_accessed=14 * MIB, transcendentals=0
        ),
        name="screened_line",
    )(gmap.reshape(32, 1, 256), jnp.asarray(high), jnp.asarray(low), screened)


def plane_kernel(high_ref, low_ref, y_ref, w_ref):
    real, imag = y_ref[0, 0], y_ref[1, 0]
    for odd in range(2):
        if odd:
            both = [real[:128] - real[128:], imag[:128] - imag[128:]]
        else:
            both = [real[:128] + real[128:], imag[:128] + imag[128:]]
        both = jnp.concatenate(both, axis=0)
        top = both.astype(BF)
        rest = (both - top.astype(F32)).astype(BF)
        high, low = high_ref[odd], low_ref[odd]
        prod = (dot(high, top) + (dot(high, rest) + dot(low, top))).astype(BF)
        for half in range(8):
            at = (2 * half + odd) * NY
            w_ref[0, at : at + NY] = prod[half * NY : (half + 1) * NY]
            w_ref[0, 256 + at : 256 + at + NY] = prod[128 + half * NY : 128 + (half + 1) * NY]


def plane_transform(lines):
    angles = plane_angles().reshape(NX, NY, PLANE)[:, :, :128]
    tables = []
    for odd in range(2):
        part = angles[odd::2].reshape(128, 128)
        cosine, sine = np.cos(part), np.sin(part)
        tables.append(np.block([[cosine, sine], [sine, -cosine]]))
    high, low = split_table(np.stack(tables))
    return pl.pallas_call(
        plane_kernel,
        grid=(HALF,),
        in_specs=[
            pl.BlockSpec((2, 256, 256), lambda z: (0, 0, 0)),
            pl.BlockSpec((2, 256, 256), lambda z: (0, 0, 0)),
            pl.BlockSpec((2, 1, 256, 256), lambda z: (0, z, 0, 0)),
        ],
        out_specs=pl.BlockSpec((1, 512, 256), lambda z: (z, 0, 0)),
        out_shape=jax.ShapeDtypeStruct((HALF, 512, 256), BF),
        compiler_params=pltpu.CompilerParams(vmem_limit_bytes=VMEM),
        cost_estimate=pl.CostEstimate(
            flops=12 * 256 * 256 * 256 * HALF, bytes_accessed=14 * MIB, transcendentals=0
        ),
        name="screened_plane",
    )(jnp.asarray(high), jnp.asarray(low), lines)


def choose_kernel(partner_ref, place_ref, flip_ref, near_ref, far_ref, val_ref, cond_ref):
    level, core = place_ref[0], place_ref[1]
    for m in range(8):
        wanted = partner_ref[(level * 2 + core) * 8 + m]
        back = (level - wanted // 16) & 3
        at = back * 8 + (wanted & 7)
        near = (wanted // 8) % 2 == core

        def take(ref, m=m, at=at):
            row = ref[at]
            val_ref[m] = dot(row[:16], flip_ref[...]).astype(BF)
            cond_ref[m] = row[16:]

        pl.when(near)(functools.partial(take, near_ref))
        pl.when(jnp.logical_not(near))(functools.partial(take, far_ref))


def choose(partner, near, far, flip):
    shape = jax.ShapeDtypeStruct((8, 16, 256), BF)
    place = jnp.stack([lax.axis_index("zl"), lax.axis_index("co")]).astype(jnp.int32)
    return pl.pallas_call(
        choose_kernel,
        in_specs=[pl.BlockSpec(memory_space=pltpu.SMEM)] * 2
        + [pl.BlockSpec(memory_space=pltpu.VMEM)] * 3,
        out_specs=[pl.BlockSpec(memory_space=pltpu.VMEM)] * 2,
        out_shape=[shape, shape],
        compiler_params=pltpu.CompilerParams(vmem_limit_bytes=16 * MIB),
        name="partner_choice",
    )(partner, place, flip, near, far)


def cond_kernel(table_ref, home_ref, away_ref, x_ref, rows_ref):
    for k in range(8):
        home, away = home_ref[k].astype(F32), away_ref[k].astype(F32)
        hr, hi = home[:8], home[8:]
        for place, band in enumerate((0, 2, 4, 6, 1, 3, 5, 7)):
            ar, ai = away[band : band + 1], away[8 + band : 9 + band]
            real = hr * ar + hi * ai
            imag = hr * ai - hi * ar
            at = k * 128 + place * 8
            rows_ref[at : at + 8, :256] = real
            rows_ref[at : at + 8, 256:] = imag
            rows_ref[at + 64 : at + 72, :256] = imag
            rows_ref[at + 64 : at + 72, 256:] = -real
    for k in range(8):
        x_ref[:, k * 128 : (k + 1) * 128] = dot(
            table_ref[...], rows_ref[k * 128 : (k + 1) * 128], ((1,), (1,)), EXACT
        )


def cond_planes(home, away):
    angles = plane_angles()
    table = np.concatenate([np.cos(angles), np.sin(angles)], axis=1).astype(np.float32)
    return pl.pallas_call(
        cond_kernel,
        out_shape=jax.ShapeDtypeStruct((256, 1024), F32),
        in_specs=[pl.BlockSpec(memory_space=pltpu.VMEM)] * 3,
        out_specs=pl.BlockSpec(memory_space=pltpu.VMEM),
        scratch_shapes=[pltpu.VMEM((1024, 512), F32)],
        compiler_params=pltpu.CompilerParams(vmem_limit_bytes=24 * MIB),
        cost_estimate=pl.CostEstimate(
            flops=12 * 256 * 512 * 1024, bytes_accessed=2 * MIB, transcendentals=0
        ),
        name="cond_planes",
    )(jnp.asarray(table), home, away)


def build_rows(rows_ref, waves, mirrored):
    home_ref, away_ref, home_back_ref, away_back_ref = waves

    def density(home, away, v):
        hr, hi = home[v : v + 1], home[8 + v : 9 + v]
        ar, ai = away[:8], away[8:]
        return hr * ar + hi * ai, hr * ai - hi * ar

    for k in range(8):
        home, away = home_ref[0, k].astype(F32), away_ref[0, k].astype(F32)
        home_back, away_back = home_back_ref[0, k].astype(F32), away_back_ref[0, k].astype(F32)
        if mirrored is not None:
            home_back = home_back * mirrored
        for pair in range(4):
            pieces = []
            for v in (2 * pair, 2 * pair + 1):
                real, imag = density(home, away, v)
                real_back, imag_back = density(home_back, away_back, v)
                pieces.append(
                    (real + real_back, imag - imag_back, imag + imag_back, real_back - real)
                )
            even_re, odd_im, even_im, odd_re = (
                jnp.concatenate(p, axis=0).astype(BF) for p in zip(*pieces)
            )
            at = k * 128 + pair * 16
            rows_ref[at : at + 16, :256] = even_re
            rows_ref[at : at + 16, 256:] = odd_im
            rows_ref[at + 64 : at + 80, :256] = even_im
            rows_ref[at + 64 : at + 80, 256:] = odd_re


def response_kernel(place_ref, *refs):
    first_waves, second_waves = refs[:4], refs[4:8]
    before_ref, w_ref, cond_ref, out_ref, sum_ref, first_ref, second_ref = refs[8:]
    step = pl.program_id(0)
    mirrored = jnp.where(step % 8 == 0, 0.0, 1.0)
    before = dot(second_ref[...], before_ref[0])
    build_rows(first_ref, first_waves, mirrored)
    total = jnp.where(step == 0, 0.0, sum_ref[...] + before)
    total = total + dot(first_ref[...], w_ref[0])
    build_rows(second_ref, second_waves, None)
    sum_ref[...] = total

    @pl.when(step == HALF // 2)
    def _():
        low = lax.broadcasted_iota(jnp.int32, (1, 128), 1) < 64
        for k in range(8):
            cond = cond_ref[k * 128 : (k + 1) * 128]
            rows = sum_ref[k * 128 : (k + 1) * 128] * NORM
            top = rows.astype(BF)
            rest = (rows - top.astype(F32)).astype(BF)
            prod = dot(cond, top, ((1,), (1,))) + dot(cond, rest, ((1,), (1,)))
            swapped = pltpu.roll(prod[64:], 64, 1)
            both = prod[:64] + jnp.where(low, swapped, -swapped)
            even, odd = both[:32], both[32:]
            real = jnp.where(low, even, pltpu.roll(odd, 64, 1))
            imag = jnp.where(low, pltpu.roll(even, 64, 1), odd)
            out_ref[:, 2 * k, :] = real
            out_ref[:, 2 * k + 1, :] = imag


def response(place, home, away, screened, cond):
    def block(which, second, back):
        def index(step, place_ref):
            z = jnp.minimum(2 * step + second, HALF - 1)
            z = (NZ - z) & (NZ - 1) if back else z
            place = place_ref[0]
            level = (place ^ z) & 1
            if which == 0:
                return ((z & 30) + level, 0, 0, 0)
            x = ((place >> 3) - (z >> 3)) & 3
            y = ((place >> 1) - (z >> 1)) & 3
            return ((y * 4 + x) * 2 + level, 0, 0, 0)

        return pl.BlockSpec((1, 8, 16, 256), index)

    waves = [block(w, s, b) for s in range(2) for b in (False, True) for w in range(2)]
    return pl.pallas_call(
        response_kernel,
        grid_spec=pltpu.PrefetchScalarGridSpec(
            num_scalar_prefetch=1,
            grid=(HALF // 2 + 1,),
            in_specs=waves
            + [
                pl.BlockSpec((1, 512, 256), lambda i, p: (jnp.maximum(2 * i - 1, 0), 0, 0)),
                pl.BlockSpec((1, 512, 256), lambda i, p: (2 * i, 0, 0)),
                pl.BlockSpec((1024, 256), lambda i, p: (0, 0)),
            ],
            out_specs=pl.BlockSpec((32, 16, 128), lambda i, p: (0, 0, 0)),
            scratch_shapes=[
                pltpu.VMEM((1024, 256), F32),
                pltpu.VMEM((1024, 512), BF),
                pltpu.VMEM((1024, 512), BF),
            ],
        ),
        out_shape=jax.ShapeDtypeStruct((32, 16, 128), F32),
        compiler_params=pltpu.CompilerParams(vmem_limit_bytes=VMEM),
        cost_estimate=pl.CostEstimate(
            flops=2 * 1024 * 512 * 256 * HALF, bytes_accessed=9 * MIB, transcendentals=0
        ),
        name="valence_response",
    )(place.reshape(1), *([home, away] * 4), screened, screened, cond)


def spectrum_kernel(cos_ref, sin_ref, x_ref, out_ref):
    first = lax.broadcasted_iota(jnp.int32, (1, 128), 1) < 64
    for k in range(8):
        x = x_ref[:, k * 128 : (k + 1) * 128]
        turned = pltpu.roll(x, 64, 1)
        turned = jnp.where(first, turned, -turned)
        cond = dot(cos_ref[...], x, precision=EXACT) + dot(sin_ref[...], turned, precision=EXACT)
        cond = (cond * NORM).astype(BF).astype(F32).T
        out_ref[k * 128 : (k + 1) * 128] = cond.astype(BF)


def cond_spectrum(cosine, sine, columns):
    return pl.pallas_call(
        spectrum_kernel,
        out_shape=jax.ShapeDtypeStruct((1024, 256), BF),
        in_specs=[pl.BlockSpec(memory_space=pltpu.VMEM)] * 3,
        out_specs=pl.BlockSpec(memory_space=pltpu.VMEM),
        compiler_params=pltpu.CompilerParams(vmem_limit_bytes=24 * MIB),
        cost_estimate=pl.CostEstimate(
            flops=24 * 256 * 256 * 1024, bytes_accessed=2 * MIB, transcendentals=0
        ),
        name="cond_spectrum",
    )(cosine, sine, columns)


def line_tables(gmap, place):
    level = lax.dynamic_slice_in_dim(gmap, place * 256, 256) & (NZ - 1)
    column = jnp.arange(256, dtype=jnp.int32)
    angle = (level[:, None] * (column // 8)[None, :]) % NZ
    same = (column // NZ)[:, None] == (column % 8)[None, :]
    angle = angle.astype(F32) * (2.0 * math.pi / NZ)
    return jnp.where(same, jnp.cos(angle), 0.0), jnp.where(same, jnp.sin(angle), 0.0)


def on_device(wavefunctions, partner, gmap, screened):
    ka_place = lax.axis_index(KA)
    place = lax.axis_index(GA)
    owned = ka_place * 8 + jnp.arange(8, dtype=jnp.int32)

    waves = wavefunctions.reshape(8, 2, 2, 8, 256).transpose(0, 2, 1, 3, 4).reshape(8, 32, 256)
    near = spread(waves, "zl").reshape(32, 32, 256)
    far = turned(near, "co", 1)

    index = jnp.arange(PLANE, dtype=jnp.int32)
    negative = (NX - index // NY) % NX * NY + (NY - index % NY) % NY
    negative = jnp.where(place > NZ // 2, negative, index)
    flip = (index[:, None] == negative[None, :]).astype(BF)
    home_val = dot(waves[:, :16].reshape(128, 256), flip).astype(BF).reshape(8, 16, 256)
    home = lax.all_gather(spread(home_val, "zh"), ("x", "y")).reshape(32, 8, 16, 256)

    lines = line_transform(screened, gmap)

    away_val, away_cond = choose(partner, near, far, flip)
    away = spread(spread(away_val, "zh"), "x")
    planes = cond_planes(waves[:, 16:], away_cond)
    away, planes, lines = lax.optimization_barrier((away, planes, lines))
    columns = lax.all_to_all(planes, GA, split_axis=0, concat_axis=0, tiled=True)
    away = spread(away, "y").reshape(32, 8, 16, 256)
    wide = plane_transform(lines)
    cond = cond_spectrum(*line_tables(gmap, place), columns)

    blocks = response(place, home, away, wide, cond)

    parts = lax.all_to_all(blocks, ("x", "y"), split_axis=0, concat_axis=0, tiled=True)
    mine = jnp.sum(parts.reshape(16, 2, 16, 128), axis=0)
    mine = mine + turned(mine, "zh", 1)
    everyone = copies_to_all(mine, KA)
    everyone = everyone.reshape(8, 2, 8, 256).transpose(0, 2, 1, 3).reshape(64, 512)
    select = (partner[None, :] == owned[:, None]).astype(F32)
    mirror = jnp.dot(select, everyone, precision=EXACT)
    mirror = mirror.reshape(8, 2, 2, 128).transpose(1, 0, 2, 3).reshape(32, 128)
    lane = jnp.arange(128, dtype=jnp.int32)
    moved = lane // 64 * 64 + lane % 8 * 8 + lane // 8 % 8
    turn = (lane[:, None] == moved[None, :]).astype(F32)
    sign = jnp.where(jnp.arange(32) % 2 == 0, 1.0, -1.0).astype(F32)
    mirror = jnp.dot(mirror, turn, precision=EXACT) * sign[:, None]
    full = copies_to_all(jnp.stack([mine.reshape(32, 128), mirror]), ("x", "y"))
    full = full.reshape(4, 4, 2, 2, 8, 2, 2, 64)
    rows_out = full[:, :, 0].transpose(3, 4, 1, 2, 0, 5, 6).reshape(8, 2, 4096)
    mirror_out = full[:, :, 1].transpose(3, 4, 0, 5, 1, 2, 6).reshape(8, 2, 4096)
    return rows_out, mirror_out


def solution(mesh):
    fine = Mesh(mesh.devices.reshape(SIZES), AXES)
    in_specs = (P(KA, None, None, GA, None), P(), P(), P(GA, None))
    out_specs = (P(KA, None, None), P(KA, None, None))
    return jax.shard_map(
        on_device, mesh=fine, in_specs=in_specs, out_specs=out_specs, check_vma=False
    )
```

time: 221 us -> 193 us (0.87)
  blocking collectives: 0 us -> 27.4 us
  waiting for transfers between devices: 61.9 us -> 34.7 us
  starting transfers between devices: 68.1 us -> 49.7 us
  local copies, waits for them, and re-layouts: 22.6 us -> 14.7 us
    all_to_all x0 -> x2, blocking collectives: none -> 27.4 us  [the longest x1 14.8 us: copies_to_all(): return lax.all_to_all(copies, axes, split_axis=0, concat_axis=0, tiled=True)]
    all_to_all x4 -> x2, waiting for transfers between devices: 27.4 us -> 6.74 us  [the longest x1 6.74 us: copies_to_all(): return lax.all_to_all(copies, axes, split_axis=0, concat_axis=0, tiled=True)]
    all_to_all x4 -> x2, starting transfers between devices: 31.9 us -> 14.3 us  [the longest x1 8.57 us: on_device(): lax.all_to_all(planes, GA, split_axis=0, concat_axis=0, tiled=True)]
    ppermute x16 -> x13, waiting for transfers between devices: 34.5 us -> 28 us  [turned(): lax.ppermute(value, axis, [(i, (i + step) % size) for i in range(size)])]
    pallas_call x1, Pallas kernels: 19.7 us -> 13.6 us  [response(): pl.pallas_call(response_kernel, grid_spec=pltpu.PrefetchScalarGridSpec(nu...]
    unnamed x28 -> x32, local copies, waits for them, and re-layouts: 17.7 us -> 11.7 us
    pallas_call x1, Pallas kernels: 7.47 us -> 13.2 us  [plane_transform(): pl.pallas_call(plane_kernel, grid=(HALF,), in_specs=[pl.BlockSpec((2, 256...]
    ppermute x16 -> x13, starting transfers between devices: 36.2 us -> 35.4 us  [turned(): lax.ppermute(value, axis, [(i, (i + step) % size) for i in range(size)])]
  transfers between devices with their start and end apart: 21 -> 16, of which waited for: 9 -> 10; matrix products, arithmetic and copies ran while one was open for 3% -> 2% of each run, Pallas kernels for 12% -> 17%
where the time goes in v1:
time: 193 us; the launch traced here: 192 us
  starting transfers between devices  49.7 us (26%)
  Pallas kernels  45.9 us (24%)
  waiting for transfers between devices  34.7 us (18%)
  blocking collectives  27.4 us (14%)
  local copies, waits for them, and re-layouts  14.7 us (8%)
  between operations  14.3 us (7%)
  other arithmetic  4.35 us (2%)
    ppermute x13, starting transfers between devices, turned(): lax.ppermute(value, axis, [(i, (i + step) % size) for i in range(size)])  35.4 us
    ppermute x13, waiting for transfers between devices, turned(): lax.ppermute(value, axis, [(i, (i + step) % size) for i in range(size)])  28 us
    all_to_all x1, blocking collectives, copies_to_all(): return lax.all_to_all(copies, axes, split_axis=0, concat_axis=0, tiled=True)  14.8 us
    pallas_call x1, Pallas kernels, response(): pl.pallas_call(response_kernel, grid_spec=pltpu.PrefetchScalarGridSpec(nu...  13.6 us
    pallas_call x1, Pallas kernels, plane_transform(): pl.pallas_call(plane_kernel, grid=(HALF,), in_specs=[pl.BlockSpec((2, 256...  13.2 us
    all_to_all x1, blocking collectives, on_device(): lax.all_to_all(blocks, ('x', 'y'), split_axis=0, concat_axis=0, tiled=True)  12.6 us
    unnamed x32, local copies, waits for them, and re-layouts  11.7 us
    pallas_call x1, Pallas kernels, line_transform(): pl.pallas_call(line_kernel, grid=(32 // n,), in_specs=[pl.BlockSpec((n, 1...  9.29 us
  transfers between devices with their start and end apart: 16, of which 10 were waited for; matrix products, arithmetic and copies ran while one was open for 2% of the time, Pallas kernels for 17%

profile of v1, /device:TPU:8, one launch (start us, length us, event | category | flops | bytes accessed | tf_op | source)
XLA Modules:
  0.0 191.6 jit_solution(11718837202078655625)
XLA Ops:
  8.4 7.3 %collective-permute-start = (bf16[8,16,256]{2,1,0:T(8,128)(2,1)S(1)}, bf16[8,16,256]{2,1,0:T(8,128)(2,1)S(1)}, u32[]{:S(2)}, u32[]{:S(2)}) collective-permute-start(bf16[8,16,256]{2,1,0:T(8,128)(2,1)S(1)} %bitcast.97), channel_id=1, source_target_pairs={{0,1},{1,0},{2,3},{3,2},{4,5},{5,4},{6,7},{7,6},{8,9},{9,8},{10,11... | collective-permute-start | bytes 196616 | tf_op jit(solution)/shard_map/ppermute | solution.py:54
  15.7 2.4 %collective-permute-done = bf16[8,16,256]{2,1,0:T(8,128)(2,1)S(1)} collective-permute-done((bf16[8,16,256]{2,1,0:T(8,128)(2,1)S(1)}, bf16[8,16,256]{2,1,0:T(8,128)(2,1)S(1)}, u32[]{:S(2)}, u32[]{:S(2)}) %collective-permute-start) | collective-permute-done | bytes 65568 | tf_op jit(solution)/shard_map/ppermute | solution.py:54
  22.6 2.1 %collective-permute-start.3 = (bf16[8,32,256]{2,1,0:T(8,128)(2,1)S(1)}, bf16[8,32,256]{2,1,0:T(8,128)(2,1)S(1)}, u32[]{:S(2)}, u32[]{:S(2)}) collective-permute-start(bf16[8,32,256]{2,1,0:T(8,128)(2,1)S(1)} %bitcast.81), channel_id=1, source_target_pairs={{0,192},{64,0},{128,64},{192,128},{1,193},{65,1},{129,65},{193,129... | collective-permute-start | bytes 393224 | tf_op jit(solution)/shard_map/ppermute | solution.py:54
  24.7 2.5 %collective-permute-done.1 = bf16[8,32,256]{2,1,0:T(8,128)(2,1)S(1)} collective-permute-done((bf16[8,32,256]{2,1,0:T(8,128)(2,1)S(1)}, bf16[8,32,256]{2,1,0:T(8,128)(2,1)S(1)}, u32[]{:S(2)}, u32[]{:S(2)}) %collective-permute-start.1) | collective-permute-done | bytes 131104 | tf_op jit(solution)/shard_map/ppermute | solution.py:54
  27.2 3.5 %collective-permute-done.2 = bf16[8,32,256]{2,1,0:T(8,128)(2,1)S(1)} collective-permute-done((bf16[8,32,256]{2,1,0:T(8,128)(2,1)S(1)}, bf16[8,32,256]{2,1,0:T(8,128)(2,1)S(1)}, u32[]{:S(2)}, u32[]{:S(2)}) %collective-permute-start.2) | collective-permute-done | bytes 131104 | tf_op jit(solution)/shard_map/ppermute | solution.py:54
  34.6 6.1 %collective-permute-start.5 = (bf16[8,16,256]{2,1,0:T(8,128)(2,1)S(1)}, bf16[8,16,256]{2,1,0:T(8,128)(2,1)S(1)}, u32[]{:S(2)}, u32[]{:S(2)}) collective-permute-start(bf16[8,16,256]{2,1,0:T(8,128)(2,1)S(1)} %get-tuple-element.7), channel_id=1, source_target_pairs={{0,1},{1,0},{2,3},{3,2},{4,5},{5,4},{6,7},{7,6},{8,9},{9,8},{10,11... | collective-permute-start | bytes 196616 | tf_op jit(solution)/shard_map/ppermute | solution.py:54
  40.6 2.2 %copy-done.2 = bf16[256,8192]{1,0:T(8,128)(2,1)S(1)} copy-done((bf16[256,8192]{1,0:T(8,128)(2,1)S(1)}, bf16[256,8192]{1,0:T(8,128)(2,1)}, u32[]{:S(2)}) %copy-start.2) | copy-done | bytes 4194328
  42.8 9.3 %screened_line.1.y_ref = f32[2,17,256,256]{3,2,1,0:T(8,128)} custom-call(s32[32,1,256]{2,1,0:T(1,128)S(1)} %bitcast.76, bf16[272,32]{1,0:T(8,128)(2,1)S(1)} %copy-done.8, bf16[272,32]{1,0:T(8,128)(2,1)S(1)} %copy-done.9, bf16[256,8192]{1,0:T(8,128)(2,1)S(1)} %copy-done.2), custom_call_target="tpu_custom_call" | custom-call | flops 2281701376 | bytes 14680064 | tf_op jit(solution)/shard_map/screened_line/pallas_call | solution.py:97
  53.8 2.7 %collective-permute-start.7 = (bf16[2,8,16,256]{3,2,1,0:T(8,128)(2,1)S(1)}, bf16[2,8,16,256]{3,2,1,0:T(8,128)(2,1)S(1)}, u32[]{:S(2)}, u32[]{:S(2)}) collective-permute-start(bf16[2,8,16,256]{3,2,1,0:T(8,128)(2,1)S(1)} %get-tuple-element.21), channel_id=1, source_target_pairs={{0,16},{8,24},{16,0},{24,8},{1,17},{9,25},{17,1},{25,9},{2,18},{10... | collective-permute-start | bytes 393224 | tf_op jit(solution)/shard_map/ppermute | solution.py:54
  57.9 4.5 %cond_planes.1 = f32[256,1024]{1,0:T(8,128)} custom-call(f32[256,512]{1,0:T(8,128)S(1)} %copy-done.12, bf16[8,16,256]{2,1,0:T(8,128)(2,1)S(1)} %get-tuple-element.18.home_ref, bf16[8,16,256]{2,1,0:T(8,128)(2,1)S(1)} %get-tuple-element.8.away_ref), custom_call_target="tpu_custom_call" | custom-call | flops 1610612736 | bytes 2097152 | tf_op jit(solution)/shard_map/cond_planes/pallas_call | solution.py:213
  62.4 3.6 %collective-permute-done.7 = bf16[2,8,16,256]{3,2,1,0:T(8,128)(2,1)S(1)} collective-permute-done((bf16[2,8,16,256]{3,2,1,0:T(8,128)(2,1)S(1)}, bf16[2,8,16,256]{3,2,1,0:T(8,128)(2,1)S(1)}, u32[]{:S(2)}, u32[]{:S(2)}) %collective-permute-start.7) | collective-permute-done | bytes 131104 | tf_op jit(solution)/shard_map/ppermute | solution.py:54
  66.1 8.6 %all-to-all-start = ((f32[32,8,1024]{2,1,0:T(8,128)}), f32[32,8,1024]{2,1,0:T(8,128)S(1)}, u32[]{:S(2)}, u32[]{:S(2)}) async-start(f32[32,8,1024]{2,1,0:T(8,128)} %bitcast.29), calls=%async_computation | async-start | bytes 2097152 | tf_op jit(solution)/shard_map/all_to_all | solution.py:387
  77.3 2.4 %collective-permute-start.11 = (bf16[4,2,8,16,256]{4,3,2,1,0:T(8,128)(2,1)S(1)}, bf16[4,2,8,16,256]{4,3,2,1,0:T(8,128)(2,1)S(1)}, u32[]{:S(2)}, u32[]{:S(2)}) collective-permute-start(bf16[4,2,8,16,256]{4,3,2,1,0:T(8,128)(2,1)S(1)} %pad_maximum_fusion.2), channel_id=1, source_target_pairs={{0,6},{2,0},{4,2},{6,4},{1,7},{3,1},{5,3},{7,5},{8,14},{10,8},{12,... | collective-permute-start | bytes 1572872 | tf_op jit(solution)/shard_map/ppermute | solution.py:54
  81.6 13.2 %screened_plane.1.refs_8_.refs_9_ = bf16[17,512,256]{2,1,0:T(8,128)(2,1)S(1)} custom-call(bf16[2,256,256]{2,1,0:T(8,128)(2,1)S(1)} %copy-done.5, bf16[2,256,256]{2,1,0:T(8,128)(2,1)S(1)} %copy-done.6, f32[2,17,256,256]{3,2,1,0:T(8,128)} %screened_line.1.y_ref), custom_call_target="tpu_custom_call" | custom-call | flops 3422552064 | bytes 14680064 | tf_op jit(solution)/shard_map/screened_plane/pallas_call | solution.py:142
  94.9 2.1 %copy-done = bf16[17,512,256]{2,1,0:T(8,128)(2,1)} copy-done((bf16[17,512,256]{2,1,0:T(8,128)(2,1)}, bf16[17,512,256]{2,1,0:T(8,128)(2,1)S(1)}, u32[]{:S(2)}) %copy-start) | copy-done | bytes 4456472
  98.9 9.8 %collective-permute-done.11 = bf16[4,2,8,16,256]{4,3,2,1,0:T(8,128)(2,1)S(1)} collective-permute-done((bf16[4,2,8,16,256]{4,3,2,1,0:T(8,128)(2,1)S(1)}, bf16[4,2,8,16,256]{4,3,2,1,0:T(8,128)(2,1)S(1)}, u32[]{:S(2)}, u32[]{:S(2)}) %collective-permute-start.11) | collective-permute-done | bytes 524320 | tf_op jit(solution)/shard_map/ppermute | solution.py:54
  111.0 3.7 %cond_spectrum.1.refs_10_ = bf16[1024,256]{1,0:T(8,128)(2,1)S(1)} custom-call(f32[256,256]{1,0:T(8,128)S(1)} %copy-done.7, f32[256,256]{1,0:T(8,128)S(1)} %get-tuple-element.22.sin_ref, f32[256,1024]{1,0:T(8,128)S(1)} %bitcast.74), custom_call_target="tpu_custom_call" | custom-call | flops 1610612736 | bytes 2097152 | tf_op jit(solution)/shard_map/cond_spectrum/pallas_call | solution.py:343
  118.1 13.6 %valence_response.1 = f32[32,16,128]{2,1,0:T(8,128)S(1)} custom-call(s32[1]{0:T(128)} %bitcast.place_ref, bf16[32,8,16,256]{3,2,1,0:T(8,128)(2,1)S(1)} %copy-done.1, bf16[32,8,16,256]{3,2,1,0:T(8,128)(2,1)S(1)} %bitcast.68, bf16[32,8,16,256]{3,2,1,0:T(8,128)(2,1)S(1)} %copy-done.1, bf16[32,8,16,256]{3,2,1,0:T(8,128)(2,1)S(1)} %bitcast.69, ...), custom_call_target="tpu_custom_call" | custom-call | flops 4563402752 | bytes 9437184 | tf_op jit(solution)/shard_map/valence_response/pallas_call | solution.py:304
  131.6 12.6 %all_to_all.26 = f32[32,16,128]{2,1,0:T(8,128)S(1)} all-to-all(f32[32,16,128]{2,1,0:T(8,128)S(1)} %valence_response.1), channel_id=1, replica_groups=mesh['zl'=4,'co'=2,'x'=4,'y'=4,'zh'=2] {'x','y'}, dimensions={0} | all-to-all | bytes 524288 | tf_op jit(solution)/shard_map/all_to_all | solution.py:394
  144.3 5.4 %collective-permute-start.12 = (f32[2,16,128]{2,1,0:T(8,128)S(1)}, f32[2,16,128]{2,1,0:T(8,128)S(1)}, u32[]{:S(2)}, u32[]{:S(2)}) collective-permute-start(f32[2,16,128]{2,1,0:T(8,128)S(1)} %reduce_sum.9), channel_id=1, source_target_pairs={{0,1},{1,0},{2,3},{3,2},{4,5},{5,4},{6,7},{7,6},{8,9},{9,8},{10,11... | collective-permute-start | bytes 49160 | tf_op jit(solution)/shard_map/ppermute | solution.py:54
  149.7 2.3 %collective-permute-done.12 = f32[2,16,128]{2,1,0:T(8,128)S(1)} collective-permute-done((f32[2,16,128]{2,1,0:T(8,128)S(1)}, f32[2,16,128]{2,1,0:T(8,128)S(1)}, u32[]{:S(2)}, u32[]{:S(2)}) %collective-permute-start.12) | collective-permute-done | bytes 16416 | tf_op jit(solution)/shard_map/ppermute | solution.py:54
  152.7 5.7 %all-to-all-start.2 = ((f32[8,2,16,128]{3,2,1,0:T(8,128)}), f32[8,2,16,128]{3,2,1,0:T(8,128)S(1)}, u32[]{:S(2)}, u32[]{:S(2)}) async-start(f32[8,2,16,128]{3,2,1,0:T(8,128)} %broadcast_in_dim.16), calls=%async_computation.2 | async-start | bytes 262144 | tf_op jit(solution)/shard_map/all_to_all | solution.py:64
  158.4 6.7 %all-to-all-done.2 = f32[8,2,16,128]{3,2,1,0:T(8,128)S(1)} async-done(((f32[8,2,16,128]{3,2,1,0:T(8,128)}), f32[8,2,16,128]{3,2,1,0:T(8,128)S(1)}, u32[]{:S(2)}, u32[]{:S(2)}) %all-to-all-start.2) | async-done | bytes 131104 | tf_op jit(solution)/shard_map/all_to_all | solution.py:64
  165.8 14.8 %all_to_all.27 = f32[16,2,32,128]{3,2,1,0:T(8,128)S(1)} all-to-all(f32[16,2,32,128]{3,2,1,0:T(8,128)S(1)} %broadcast_in_dim.21), channel_id=1, replica_groups=mesh['zl'=4,'co'=2,'x'=4,'y'=4,'zh'=2] {'x','y'}, dimensions={0} | all-to-all | bytes 1048576 | tf_op jit(solution)/shard_map/all_to_all | solution.py:64
  (78 shorter events, 30.2 us)
Async XLA Ops:
  7.2 33.5 %copy-start.8 = (bf16[272,32]{1,0:T(8,128)(2,1)S(1)}, bf16[272,32]{1,0:T(8,128)(2,1)}, u32[]{:S(2)}) copy-start(bf16[272,32]{1,0:T(8,128)(2,1)} %constant.189.clone.high_ref) | copy-start | bytes 52228
  7.2 33.5 %copy-start.9 = (bf16[272,32]{1,0:T(8,128)(2,1)S(1)}, bf16[272,32]{1,0:T(8,128)(2,1)}, u32[]{:S(2)}) copy-start(bf16[272,32]{1,0:T(8,128)(2,1)} %constant.190.clone.low_ref) | copy-start | bytes 52228
  7.2 25.6 %copy-start.11 = (s32[64]{0:T(128)S(1)}, s32[64]{0:T(128)}, u32[]{:S(2)}) copy-start(s32[64]{0:T(128)} %partner_ref.1) | copy-start | bytes 772
  7.2 33.4 %copy-start.10 = (s32[8192]{0:T(1024)S(1)}, s32[8192]{0:T(1024)}, u32[]{:S(2)}) copy-start(s32[8192]{0:T(1024)} %param.11) | copy-start | bytes 98308
  7.2 108.2 %all-gather.3.cloned.1.call-start = ((), (), s32[]{:S(2)}) async-start(), calls=%async_computation.4 | async-start | bytes 2228224 | tf_op jit(solution)/shard_map/all_gather | solution.py:379
  8.4 9.7 %collective-permute-start = (bf16[8,16,256]{2,1,0:T(8,128)(2,1)S(1)}, bf16[8,16,256]{2,1,0:T(8,128)(2,1)S(1)}, u32[]{:S(2)}, u32[]{:S(2)}) collective-permute-start(bf16[8,16,256]{2,1,0:T(8,128)(2,1)S(1)} %bitcast.97), channel_id=1, source_target_pairs={{0,1},{1,0},{2,3},{3,2},{4,5},{5,4},{6,7},{7,6},{8,9},{9,8},{10,11... | collective-permute-start | bytes 196616 | tf_op jit(solution)/shard_map/ppermute | solution.py:54
  18.8 8.4 %collective-permute-start.1 = (bf16[8,32,256]{2,1,0:T(8,128)(2,1)S(1)}, bf16[8,32,256]{2,1,0:T(8,128)(2,1)S(1)}, u32[]{:S(2)}, u32[]{:S(2)}) collective-permute-start(bf16[8,32,256]{2,1,0:T(8,128)(2,1)S(1)} %bitcast.79), channel_id=1, source_target_pairs={{0,64},{64,128},{128,192},{192,0},{1,65},{65,129},{129,193},{193,1... | collective-permute-start | bytes 393224 | tf_op jit(solution)/shard_map/ppermute | solution.py:54
  20.7 10.1 %collective-permute-start.2 = (bf16[8,32,256]{2,1,0:T(8,128)(2,1)S(1)}, bf16[8,32,256]{2,1,0:T(8,128)(2,1)S(1)}, u32[]{:S(2)}, u32[]{:S(2)}) collective-permute-start(bf16[8,32,256]{2,1,0:T(8,128)(2,1)S(1)} %bitcast.80), channel_id=1, source_target_pairs={{0,128},{64,192},{128,0},{192,64},{1,129},{65,193},{129,1},{193,65... | collective-permute-start | bytes 393224 | tf_op jit(solution)/shard_map/ppermute | solution.py:54
  22.6 8.1 %collective-permute-start.3 = (bf16[8,32,256]{2,1,0:T(8,128)(2,1)S(1)}, bf16[8,32,256]{2,1,0:T(8,128)(2,1)S(1)}, u32[]{:S(2)}, u32[]{:S(2)}) collective-permute-start(bf16[8,32,256]{2,1,0:T(8,128)(2,1)S(1)} %bitcast.81), channel_id=1, source_target_pairs={{0,192},{64,0},{128,64},{192,128},{1,193},{65,1},{129,65},{193,129... | collective-permute-start | bytes 393224 | tf_op jit(solution)/shard_map/ppermute | solution.py:54
  30.8 2.0 %collective-permute-start.4 = (bf16[32,32,256]{2,1,0:T(8,128)(2,1)S(1)}, bf16[32,32,256]{2,1,0:T(8,128)(2,1)S(1)}, u32[]{:S(2)}, u32[]{:S(2)}) collective-permute-start(bf16[32,32,256]{2,1,0:T(8,128)(2,1)S(1)} %bitcast.72), channel_id=1, source_target_pairs={{0,32},{32,0},{1,33},{33,1},{2,34},{34,2},{3,35},{35,3},{4,36},{36... | collective-permute-start | bytes 1572872 | tf_op jit(solution)/shard_map/ppermute | solution.py:54
  34.6 17.6 %collective-permute-start.5 = (bf16[8,16,256]{2,1,0:T(8,128)(2,1)S(1)}, bf16[8,16,256]{2,1,0:T(8,128)(2,1)S(1)}, u32[]{:S(2)}, u32[]{:S(2)}) collective-permute-start(bf16[8,16,256]{2,1,0:T(8,128)(2,1)S(1)} %get-tuple-element.7), channel_id=1, source_target_pairs={{0,1},{1,0},{2,3},{3,2},{4,5},{5,4},{6,7},{7,6},{8,9},{9,8},{10,11... | collective-permute-start | bytes 196616 | tf_op jit(solution)/shard_map/ppermute | solution.py:54
  42.8 15.1 %copy-start.12 = (f32[256,512]{1,0:T(8,128)S(1)}, f32[256,512]{1,0:T(8,128)}, u32[]{:S(2)}) copy-start(f32[256,512]{1,0:T(8,128)} %constant.191.clone.table_ref) | copy-start | bytes 1572868
  52.2 10.3 %collective-permute-start.6 = (bf16[2,8,16,256]{3,2,1,0:T(8,128)(2,1)S(1)}, bf16[2,8,16,256]{3,2,1,0:T(8,128)(2,1)S(1)}, u32[]{:S(2)}, u32[]{:S(2)}) collective-permute-start(bf16[2,8,16,256]{3,2,1,0:T(8,128)(2,1)S(1)} %get-tuple-element.21), channel_id=1, source_target_pairs={{0,8},{8,16},{16,24},{24,0},{1,9},{9,17},{17,25},{25,1},{2,10},{10... | collective-permute-start | bytes 393224 | tf_op jit(solution)/shard_map/ppermute | solution.py:54
  53.8 12.3 %collective-permute-start.7 = (bf16[2,8,16,256]{3,2,1,0:T(8,128)(2,1)S(1)}, bf16[2,8,16,256]{3,2,1,0:T(8,128)(2,1)S(1)}, u32[]{:S(2)}, u32[]{:S(2)}) collective-permute-start(bf16[2,8,16,256]{3,2,1,0:T(8,128)(2,1)S(1)} %get-tuple-element.21), channel_id=1, source_target_pairs={{0,16},{8,24},{16,0},{24,8},{1,17},{9,25},{17,1},{25,9},{2,18},{10... | collective-permute-start | bytes 393224 | tf_op jit(solution)/shard_map/ppermute | solution.py:54
  56.5 9.6 %collective-permute-start.8 = (bf16[2,8,16,256]{3,2,1,0:T(8,128)(2,1)S(1)}, bf16[2,8,16,256]{3,2,1,0:T(8,128)(2,1)S(1)}, u32[]{:S(2)}, u32[]{:S(2)}) collective-permute-start(bf16[2,8,16,256]{3,2,1,0:T(8,128)(2,1)S(1)} %get-tuple-element.21), channel_id=1, source_target_pairs={{0,24},{8,0},{16,8},{24,16},{1,25},{9,1},{17,9},{25,17},{2,26},{10... | collective-permute-start | bytes 393224 | tf_op jit(solution)/shard_map/ppermute | solution.py:54
  62.4 19.2 %copy-start.5 = (bf16[2,256,256]{2,1,0:T(8,128)(2,1)S(1)}, bf16[2,256,256]{2,1,0:T(8,128)(2,1)}, u32[]{:S(2)}) copy-start(bf16[2,256,256]{2,1,0:T(8,128)(2,1)} %constant.192.clone.high_ref) | copy-start | bytes 786436
  62.4 19.2 %copy-start.6 = (bf16[2,256,256]{2,1,0:T(8,128)(2,1)S(1)}, bf16[2,256,256]{2,1,0:T(8,128)(2,1)}, u32[]{:S(2)}) copy-start(bf16[2,256,256]{2,1,0:T(8,128)(2,1)} %constant.193.clone.low_ref) | copy-start | bytes 786436
  66.1 28.7 %copy-start.13 = (bf16[4,2,8,16,256]{4,3,2,1,0:T(8,128)(2,1)}, bf16[4,2,8,16,256]{4,3,2,1,0:T(8,128)(2,1)S(1)}, u32[]{:S(2)}) copy-start(bf16[4,2,8,16,256]{4,3,2,1,0:T(8,128)(2,1)S(1)} %pad_maximum_fusion.2) | copy-start | bytes 1572868
  66.1 43.9 %all-to-all-start = ((f32[32,8,1024]{2,1,0:T(8,128)}), f32[32,8,1024]{2,1,0:T(8,128)S(1)}, u32[]{:S(2)}, u32[]{:S(2)}) async-start(f32[32,8,1024]{2,1,0:T(8,128)} %bitcast.29), calls=%async_computation | async-start | bytes 2097152 | tf_op jit(solution)/shard_map/all_to_all | solution.py:387
  74.8 23.1 %collective-permute-start.9 = (bf16[4,2,8,16,256]{4,3,2,1,0:T(8,128)(2,1)S(1)}, bf16[4,2,8,16,256]{4,3,2,1,0:T(8,128)(2,1)S(1)}, u32[]{:S(2)}, u32[]{:S(2)}) collective-permute-start(bf16[4,2,8,16,256]{4,3,2,1,0:T(8,128)(2,1)S(1)} %pad_maximum_fusion.2), channel_id=1, source_target_pairs={{0,2},{2,4},{4,6},{6,0},{1,3},{3,5},{5,7},{7,1},{8,10},{10,12},{12... | collective-permute-start | bytes 1572872 | tf_op jit(solution)/shard_map/ppermute | solution.py:54
  76.5 22.4 %collective-permute-start.10 = (bf16[4,2,8,16,256]{4,3,2,1,0:T(8,128)(2,1)S(1)}, bf16[4,2,8,16,256]{4,3,2,1,0:T(8,128)(2,1)S(1)}, u32[]{:S(2)}, u32[]{:S(2)}) collective-permute-start(bf16[4,2,8,16,256]{4,3,2,1,0:T(8,128)(2,1)S(1)} %pad_maximum_fusion.2), channel_id=1, source_target_pairs={{0,4},{2,6},{4,0},{6,2},{1,5},{3,7},{5,1},{7,3},{8,12},{10,14},{12... | collective-permute-start | bytes 1572872 | tf_op jit(solution)/shard_map/ppermute | solution.py:54
  77.3 31.4 %collective-permute-start.11 = (bf16[4,2,8,16,256]{4,3,2,1,0:T(8,128)(2,1)S(1)}, bf16[4,2,8,16,256]{4,3,2,1,0:T(8,128)(2,1)S(1)}, u32[]{:S(2)}, u32[]{:S(2)}) collective-permute-start(bf16[4,2,8,16,256]{4,3,2,1,0:T(8,128)(2,1)S(1)} %pad_maximum_fusion.2), channel_id=1, source_target_pairs={{0,6},{2,0},{4,2},{6,4},{1,7},{3,1},{5,3},{7,5},{8,14},{10,8},{12,... | collective-permute-start | bytes 1572872 | tf_op jit(solution)/shard_map/ppermute | solution.py:54
  144.3 7.7 %collective-permute-start.12 = (f32[2,16,128]{2,1,0:T(8,128)S(1)}, f32[2,16,128]{2,1,0:T(8,128)S(1)}, u32[]{:S(2)}, u32[]{:S(2)}) collective-permute-start(f32[2,16,128]{2,1,0:T(8,128)S(1)} %reduce_sum.9), channel_id=1, source_target_pairs={{0,1},{1,0},{2,3},{3,2},{4,5},{5,4},{6,7},{7,6},{8,9},{9,8},{10,11... | collective-permute-start | bytes 49160 | tf_op jit(solution)/shard_map/ppermute | solution.py:54
  152.7 12.5 %all-to-all-start.2 = ((f32[8,2,16,128]{3,2,1,0:T(8,128)}), f32[8,2,16,128]{3,2,1,0:T(8,128)S(1)}, u32[]{:S(2)}, u32[]{:S(2)}) async-start(f32[8,2,16,128]{3,2,1,0:T(8,128)} %broadcast_in_dim.16), calls=%async_computation.2 | async-start | bytes 262144 | tf_op jit(solution)/shard_map/all_to_all | solution.py:64
  (6 other events, 8.6 us)
Sparse Core Ops, SparseCore 0:
  18.9 53.5 all-gather.2

commit v2 on v1

--- a/solution.py
+++ b/solution.py
@@ -17,6 +17,8 @@
 PLANE = NX * NY
 HALF = NZ // 2 + 1
 LINE_BLOCKS = 4
+LINE_STEPS = 32 // LINE_BLOCKS
+LINE_ROWS = 48
 NORM = 1.0 / math.sqrt(NG)
 EXACT = lax.Precision.HIGHEST
 BF = jnp.bfloat16
@@ -28,7 +30,6 @@
 SIZE = dict(zip(AXES, SIZES))
 KA = ("zl", "co")
 GA = ("x", "y", "zh")
-VMEM = 48 * MIB
 
 
 def split_table(table):
@@ -70,68 +71,54 @@
     )
 
 
-def line_kernel(gmap_ref, high_ref, low_ref, w_ref, y_ref):
-    rows = 2 * HALF * 8
-    keep = (lax.broadcasted_iota(jnp.int32, (rows, 256), 0) & 7) == (
-        lax.broadcasted_iota(jnp.int32, (rows, 256), 1) >> 5
-    )
-    for b in range(LINE_BLOCKS):
-        level = gmap_ref[b] & (NZ - 1)
-        hot = (lax.broadcasted_iota(jnp.int32, (NZ, 256), 0) == level).astype(F32).astype(BF)
-        block = w_ref[:, b * 256 : (b + 1) * 256]
-        total = None
-        for table in (high_ref, low_ref):
-            picked = jnp.where(keep, dot(table[...], hot), 0.0).astype(BF)
-            part = dot(picked, block, ((1,), (1,)))
-            total = part if total is None else total + part
-        y_ref[:, :, b * 8 : (b + 1) * 8, :] = total.reshape(2, HALF, 8, 256)
-
-
-def line_transform(screened, gmap):
+def screened_kernel(gmap_ref, line_ref, high_ref, low_ref, w_ref, out_ref, lines_ref):
+    step = pl.program_id(0)
+
+    @pl.when(step < LINE_STEPS)
+    def _():
+        rows = 2 * HALF
+        keep = lax.broadcasted_iota(jnp.int32, (1, 8, 256), 1) == (
+            lax.broadcasted_iota(jnp.int32, (1, 8, 256), 2) >> 5
+        )
+        for b in range(LINE_BLOCKS):
+            level = gmap_ref[b] & (NZ - 1)
+            hot = (lax.broadcasted_iota(jnp.int32, (NZ, 256), 0) == level).astype(F32).astype(BF)
+            picked = dot(line_ref[...], hot)
+            tables = []
+            for at in (0, LINE_ROWS):
+                wide = jnp.broadcast_to(picked[at : at + rows][:, None, :], (rows, 8, 256))
+                tables.append(jnp.where(keep, wide, 0.0).reshape(rows * 8, 256).astype(BF))
+            block = w_ref[:, b * 256 : (b + 1) * 256]
+            both = dot(jnp.concatenate(tables, axis=0), block, ((1,), (1,)))
+            total = both[: rows * 8] + both[rows * 8 :]
+            at = pl.multiple_of((step * LINE_BLOCKS + b) * 8, 8)
+            lines_ref[:, pl.ds(at, 8), :] = total.reshape(rows, 8, 256)
+
+    @pl.when(step >= LINE_STEPS)
+    def _():
+        z = step - LINE_STEPS
+        real, imag = lines_ref[z], lines_ref[HALF + z]
+        for odd in range(2):
+            if odd:
+                both = [real[:128] - real[128:], imag[:128] - imag[128:]]
+            else:
+                both = [real[:128] + real[128:], imag[:128] + imag[128:]]
+            both = jnp.concatenate(both, axis=0)
+            top = both.astype(BF)
+            rest = (both - top.astype(F32)).astype(BF)
+            high, low = high_ref[odd], low_ref[odd]
+            prod = (dot(high, top) + (dot(high, rest) + dot(low, top))).astype(BF)
+            for half in range(8):
+                at = (2 * half + odd) * NY
+                out_ref[0, at : at + NY] = prod[half * NY : (half + 1) * NY]
+                out_ref[0, 256 + at : 256 + at + NY] = prod[128 + half * NY : 144 + half * NY]
+
+
+def screened_transform(screened, gmap):
     angles = line_angles()[:HALF]
-    table = np.stack([np.cos(angles), -np.sin(angles)])
-    table = np.repeat(table.reshape(2 * HALF, NZ), 8, axis=0)
-    high, low = split_table(table)
-    rows = 2 * HALF * 8
-    n = LINE_BLOCKS
-    return pl.pallas_call(
-        line_kernel,
-        grid=(32 // n,),
-        in_specs=[
-            pl.BlockSpec((n, 1, 256), lambda b: (b, 0, 0)),
-            pl.BlockSpec((rows, NZ), lambda b: (0, 0)),
-            pl.BlockSpec((rows, NZ), lambda b: (0, 0)),
-            pl.BlockSpec((256, n * 256), lambda b: (0, b)),
-        ],
-        out_specs=pl.BlockSpec((2, HALF, n * 8, 256), lambda b: (0, 0, b, 0)),
-        out_shape=jax.ShapeDtypeStruct((2, HALF, PLANE, 256), F32),
-        compiler_params=pltpu.CompilerParams(vmem_limit_bytes=VMEM),
-        cost_estimate=pl.CostEstimate(
-            flops=4 * rows * 256 * 8192, bytes_accessed=14 * MIB, transcendentals=0
-        ),
-        name="screened_line",
-    )(gmap.reshape(32, 1, 256), jnp.asarray(high), jnp.asarray(low), screened)
-
-
-def plane_kernel(high_ref, low_ref, y_ref, w_ref):
-    real, imag = y_ref[0, 0], y_ref[1, 0]
-    for odd in range(2):
-        if odd:
-            both = [real[:128] - real[128:], imag[:128] - imag[128:]]
-        else:
-            both = [real[:128] + real[128:], imag[:128] + imag[128:]]
-        both = jnp.concatenate(both, axis=0)
-        top = both.astype(BF)
-        rest = (both - top.astype(F32)).astype(BF)
-        high, low = high_ref[odd], low_ref[odd]
-        prod = (dot(high, top) + (dot(high, rest) + dot(low, top))).astype(BF)
-        for half in range(8):
-            at = (2 * half + odd) * NY
-            w_ref[0, at : at + NY] = prod[half * NY : (half + 1) * NY]
-            w_ref[0, 256 + at : 256 + at + NY] = prod[128 + half * NY : 128 + (half + 1) * NY]
-
-
-def plane_transform(lines):
+    table = np.concatenate([np.cos(angles), -np.sin(angles)], axis=0)
+    padding = np.zeros((LINE_ROWS - 2 * HALF, NZ), BF)
+    line = np.concatenate([x for part in split_table(table) for x in (part, padding)], axis=0)
     angles = plane_angles().reshape(NX, NY, PLANE)[:, :, :128]
     tables = []
     for odd in range(2):
@@ -139,22 +126,27 @@
         cosine, sine = np.cos(part), np.sin(part)
         tables.append(np.block([[cosine, sine], [sine, -cosine]]))
     high, low = split_table(np.stack(tables))
-    return pl.pallas_call(
-        plane_kernel,
-        grid=(HALF,),
+    n = LINE_BLOCKS
+    last = LINE_STEPS - 1
+    return pl.pallas_call(
+        screened_kernel,
+        grid=(LINE_STEPS + HALF,),
         in_specs=[
-            pl.BlockSpec((2, 256, 256), lambda z: (0, 0, 0)),
-            pl.BlockSpec((2, 256, 256), lambda z: (0, 0, 0)),
-            pl.BlockSpec((2, 1, 256, 256), lambda z: (0, z, 0, 0)),
+            pl.BlockSpec((n, 1, 256), lambda i: (jnp.minimum(i, last), 0, 0)),
+            pl.BlockSpec((2 * LINE_ROWS, NZ), lambda i: (0, 0)),
+            pl.BlockSpec((2, 256, 256), lambda i: (0, 0, 0)),
+            pl.BlockSpec((2, 256, 256), lambda i: (0, 0, 0)),
+            pl.BlockSpec((256, n * 256), lambda i: (0, jnp.minimum(i, last))),
         ],
-        out_specs=pl.BlockSpec((1, 512, 256), lambda z: (z, 0, 0)),
+        out_specs=pl.BlockSpec((1, 512, 256), lambda i: (jnp.maximum(i - LINE_STEPS, 0), 0, 0)),
         out_shape=jax.ShapeDtypeStruct((HALF, 512, 256), BF),
-        compiler_params=pltpu.CompilerParams(vmem_limit_bytes=VMEM),
+        scratch_shapes=[pltpu.VMEM((2 * HALF, PLANE, 256), F32)],
+        compiler_params=pltpu.CompilerParams(vmem_limit_bytes=40 * MIB),
         cost_estimate=pl.CostEstimate(
-            flops=12 * 256 * 256 * 256 * HALF, bytes_accessed=14 * MIB, transcendentals=0
+            flops=12 * 256 * 256 * 256 * HALF, bytes_accessed=9 * MIB, transcendentals=0
         ),
-        name="screened_plane",
-    )(jnp.asarray(high), jnp.asarray(low), lines)
+        name="screened_transform",
+    )(gmap.reshape(32, 1, 256), jnp.asarray(line), jnp.asarray(high), jnp.asarray(low), screened)
 
 
 def choose_kernel(partner_ref, place_ref, flip_ref, near_ref, far_ref, val_ref, cond_ref):
@@ -286,21 +278,19 @@
 
 
 def response(place, home, away, screened, cond):
-    def block(which, second, back):
+    def block(second, back):
         def index(step, place_ref):
             z = jnp.minimum(2 * step + second, HALF - 1)
             z = (NZ - z) & (NZ - 1) if back else z
             place = place_ref[0]
             level = (place ^ z) & 1
-            if which == 0:
-                return ((z & 30) + level, 0, 0, 0)
             x = ((place >> 3) - (z >> 3)) & 3
             y = ((place >> 1) - (z >> 1)) & 3
             return ((y * 4 + x) * 2 + level, 0, 0, 0)
 
         return pl.BlockSpec((1, 8, 16, 256), index)
 
-    waves = [block(w, s, b) for s in range(2) for b in (False, True) for w in range(2)]
+    waves = [block(s, b) for s in range(2) for b in (False, True) for _ in range(2)]
     return pl.pallas_call(
         response_kernel,
         grid_spec=pltpu.PrefetchScalarGridSpec(
@@ -320,7 +310,7 @@
             ],
         ),
         out_shape=jax.ShapeDtypeStruct((32, 16, 128), F32),
-        compiler_params=pltpu.CompilerParams(vmem_limit_bytes=VMEM),
+        compiler_params=pltpu.CompilerParams(vmem_limit_bytes=20 * MIB),
         cost_estimate=pl.CostEstimate(
             flops=2 * 1024 * 512 * 256 * HALF, bytes_accessed=9 * MIB, transcendentals=0
         ),
@@ -362,6 +352,34 @@
     return jnp.where(same, jnp.cos(angle), 0.0), jnp.where(same, jnp.sin(angle), 0.0)
 
 
+def lay_out_kernel(full_ref, rows_ref, mirror_ref):
+    low = lax.broadcasted_iota(jnp.int32, (1, 128), 1) < 64
+    for m in range(4):
+        for n in range(4):
+            for c in (2 * n, 2 * n + 1):
+                piece = full_ref[m * 4 + n, 0, (c & 1) * 16 : (c & 1) * 16 + 16]
+                at = (c * 4 + m) * 128
+                rows_ref[:, :, at : at + 128] = piece.reshape(8, 2, 128)
+            even, odd = full_ref[m * 4 + n, 1, :16], full_ref[m * 4 + n, 1, 16:]
+            first = jnp.where(low, even, pltpu.roll(odd, 64, 1))
+            second = jnp.where(low, pltpu.roll(even, 64, 1), odd)
+            at = (2 * m * 4 + n) * 128
+            mirror_ref[:, :, at : at + 128] = first.reshape(8, 2, 128)
+            mirror_ref[:, :, at + 512 : at + 640] = second.reshape(8, 2, 128)
+
+
+def lay_out(full):
+    shape = jax.ShapeDtypeStruct((8, 2, 4096), F32)
+    return pl.pallas_call(
+        lay_out_kernel,
+        in_specs=[pl.BlockSpec(memory_space=pltpu.VMEM)],
+        out_specs=[pl.BlockSpec(memory_space=pltpu.VMEM)] * 2,
+        out_shape=[shape, shape],
+        compiler_params=pltpu.CompilerParams(vmem_limit_bytes=16 * MIB),
+        name="lay_out",
+    )(full)
+
+
 def on_device(wavefunctions, partner, gmap, screened):
     ka_place = lax.axis_index(KA)
     place = lax.axis_index(GA)
@@ -369,24 +387,24 @@
 
     waves = wavefunctions.reshape(8, 2, 2, 8, 256).transpose(0, 2, 1, 3, 4).reshape(8, 32, 256)
     near = spread(waves, "zl").reshape(32, 32, 256)
-    far = turned(near, "co", 1)
 
     index = jnp.arange(PLANE, dtype=jnp.int32)
     negative = (NX - index // NY) % NX * NY + (NY - index % NY) % NY
     negative = jnp.where(place > NZ // 2, negative, index)
     flip = (index[:, None] == negative[None, :]).astype(BF)
     home_val = dot(waves[:, :16].reshape(128, 256), flip).astype(BF).reshape(8, 16, 256)
-    home = lax.all_gather(spread(home_val, "zh"), ("x", "y")).reshape(32, 8, 16, 256)
-
-    lines = line_transform(screened, gmap)
+    home_val, near = lax.optimization_barrier((home_val, near))
+    far = turned(near, "co", 1)
 
     away_val, away_cond = choose(partner, near, far, flip)
+    home = spread(spread(home_val, "zh"), "x")
     away = spread(spread(away_val, "zh"), "x")
     planes = cond_planes(waves[:, 16:], away_cond)
-    away, planes, lines = lax.optimization_barrier((away, planes, lines))
+    away, planes, screened = lax.optimization_barrier((away, planes, screened))
+    home = spread(home, "y").reshape(32, 8, 16, 256)
     columns = lax.all_to_all(planes, GA, split_axis=0, concat_axis=0, tiled=True)
     away = spread(away, "y").reshape(32, 8, 16, 256)
-    wide = plane_transform(lines)
+    wide = screened_transform(screened, gmap)
     cond = cond_spectrum(*line_tables(gmap, place), columns)
 
     blocks = response(place, home, away, wide, cond)
@@ -405,10 +423,7 @@
     sign = jnp.where(jnp.arange(32) % 2 == 0, 1.0, -1.0).astype(F32)
     mirror = jnp.dot(mirror, turn, precision=EXACT) * sign[:, None]
     full = copies_to_all(jnp.stack([mine.reshape(32, 128), mirror]), ("x", "y"))
-    full = full.reshape(4, 4, 2, 2, 8, 2, 2, 64)
-    rows_out = full[:, :, 0].transpose(3, 4, 1, 2, 0, 5, 6).reshape(8, 2, 4096)
-    mirror_out = full[:, :, 1].transpose(3, 4, 0, 5, 1, 2, 6).reshape(8, 2, 4096)
-    return rows_out, mirror_out
+    return lay_out(full)
 
 
 def solution(mesh):

time: 193 us -> 220 us (1.14)
  starting transfers between devices: 49.7 us -> 84.5 us
  waiting for transfers between devices: 34.7 us -> 49.9 us
  between operations: 14.3 us -> 0.89 us
  Pallas kernels: 45.9 us -> 36.7 us
  local copies, waits for them, and re-layouts: 14.7 us -> 8.65 us
  other arithmetic: 4.35 us -> 8.71 us
    ppermute x13 -> x19, starting transfers between devices: 35.4 us -> 54.9 us  [turned(): lax.ppermute(value, axis, [(i, (i + step) % size) for i in range(size)])]
    ppermute x13 -> x19, waiting for transfers between devices: 28 us -> 43.2 us  [turned(): lax.ppermute(value, axis, [(i, (i + step) % size) for i in range(size)])]
    all_to_all x1, starting transfers between devices: 5.73 us -> 18.4 us  [copies_to_all(): return lax.all_to_all(copies, axes, split_axis=0, concat_axis=0, tiled=True)]
    pallas_call x2, Pallas kernels: 22.5 us -> 14.4 us  [the longest x1 13.4 us: screened_transform(): pl.pallas_call(screened_kernel, grid=(LINE_STEPS + HALF,), in_specs=[pl.B...]
    unnamed x32 -> x26, local copies, waits for them, and re-layouts: 11.7 us -> 6.81 us
    another operation x5 -> x7, other arithmetic: 2.13 us -> 6.48 us  [spread(): jnp.stack([value] + [turned(value, axis, d) for d in range(1, SIZE[axis])])]
    all_to_all x1, starting transfers between devices: 8.57 us -> 11.3 us  [on_device(): lax.all_to_all(planes, GA, split_axis=0, concat_axis=0, tiled=True)]
  transfers between devices with their start and end apart: 16 -> 21, of which waited for: 10 -> 10; matrix products, arithmetic and copies ran while one was open for 2% -> 4% of each run, Pallas kernels for 17% -> 8%
where the time goes in v2:
time: 220 us; the launch traced here: 219 us
  starting transfers between devices  84.5 us (38%)
  waiting for transfers between devices  49.9 us (23%)
  Pallas kernels  36.7 us (17%)
  blocking collectives  29 us (13%)
  other arithmetic  8.71 us (4%)
  local copies, waits for them, and re-layouts  8.65 us (4%)
    ppermute x19, starting transfers between devices, turned(): lax.ppermute(value, axis, [(i, (i + step) % size) for i in range(size)])  54.9 us
    ppermute x19, waiting for transfers between devices, turned(): lax.ppermute(value, axis, [(i, (i + step) % size) for i in range(size)])  43.2 us
    all_to_all x1, starting transfers between devices, copies_to_all(): return lax.all_to_all(copies, axes, split_axis=0, concat_axis=0, tiled=True)  18.4 us
    all_to_all x1, blocking collectives, copies_to_all(): return lax.all_to_all(copies, axes, split_axis=0, concat_axis=0, tiled=True)  14.8 us
    all_to_all x1, blocking collectives, on_device(): lax.all_to_all(blocks, ('x', 'y'), split_axis=0, concat_axis=0, tiled=True)  14.2 us
    pallas_call x1, Pallas kernels, screened_transform(): pl.pallas_call(screened_kernel, grid=(LINE_STEPS + HALF,), in_specs=[pl.B...  13.4 us
    pallas_call x1, Pallas kernels, response(): pl.pallas_call(response_kernel, grid_spec=pltpu.PrefetchScalarGridSpec(nu...  12.4 us
    all_to_all x1, starting transfers between devices, on_device(): lax.all_to_all(planes, GA, split_axis=0, concat_axis=0, tiled=True)  11.3 us
  transfers between devices with their start and end apart: 21, of which 10 were waited for; matrix products, arithmetic and copies ran while one was open for 4% of the time, Pallas kernels for 8%

profile of v2, /device:TPU:8, one launch (start us, length us, event | category | flops | bytes accessed | tf_op | source)
XLA Modules:
  0.0 218.9 jit_solution(343945642229959983)
XLA Ops:
  1.6 4.7 %collective-permute-start.2 = (bf16[8,32,256]{2,1,0:T(8,128)(2,1)S(1)}, bf16[8,32,256]{2,1,0:T(8,128)(2,1)S(1)}, u32[]{:S(2)}, u32[]{:S(2)}) collective-permute-start(bf16[8,32,256]{2,1,0:T(8,128)(2,1)S(1)} %bitcast.81), channel_id=1, source_target_pairs={{0,192},{64,0},{128,64},{192,128},{1,193},{65,1},{129,65},{193,129... | collective-permute-start | bytes 393224 | tf_op jit(solution)/shard_map/ppermute | solution.py:55
  7.2 3.0 %collective-permute-done.2 = bf16[8,32,256]{2,1,0:T(8,128)(2,1)S(1)} collective-permute-done((bf16[8,32,256]{2,1,0:T(8,128)(2,1)S(1)}, bf16[8,32,256]{2,1,0:T(8,128)(2,1)S(1)}, u32[]{:S(2)}, u32[]{:S(2)}) %collective-permute-start.2) | collective-permute-done | bytes 131104 | tf_op jit(solution)/shard_map/ppermute | solution.py:55
  10.2 7.3 %collective-permute-done.1 = bf16[8,32,256]{2,1,0:T(8,128)(2,1)S(1)} collective-permute-done((bf16[8,32,256]{2,1,0:T(8,128)(2,1)S(1)}, bf16[8,32,256]{2,1,0:T(8,128)(2,1)S(1)}, u32[]{:S(2)}, u32[]{:S(2)}) %collective-permute-start.1) | collective-permute-done | bytes 131104 | tf_op jit(solution)/shard_map/ppermute | solution.py:55
  22.0 5.5 %collective-permute-start.11 = (bf16[8,16,256]{2,1,0:T(8,128)(2,1)S(1)}, bf16[8,16,256]{2,1,0:T(8,128)(2,1)S(1)}, u32[]{:S(2)}, u32[]{:S(2)}) collective-permute-start(bf16[8,16,256]{2,1,0:T(8,128)(2,1)S(1)} %get-tuple-element.11), channel_id=1, source_target_pairs={{0,1},{1,0},{2,3},{3,2},{4,5},{5,4},{6,7},{7,6},{8,9},{9,8},{10,11... | collective-permute-start | bytes 196616 | tf_op jit(solution)/shard_map/ppermute | solution.py:55
  27.5 2.7 %collective-permute-done.11 = bf16[8,16,256]{2,1,0:T(8,128)(2,1)S(1)} collective-permute-done((bf16[8,16,256]{2,1,0:T(8,128)(2,1)S(1)}, bf16[8,16,256]{2,1,0:T(8,128)(2,1)S(1)}, u32[]{:S(2)}, u32[]{:S(2)}) %collective-permute-start.11) | collective-permute-done | bytes 65568 | tf_op jit(solution)/shard_map/ppermute | solution.py:55
  30.2 3.1 %collective-permute-start.13 = (bf16[2,8,16,256]{3,2,1,0:T(8,128)(2,1)S(1)}, bf16[2,8,16,256]{3,2,1,0:T(8,128)(2,1)S(1)}, u32[]{:S(2)}, u32[]{:S(2)}) collective-permute-start(bf16[2,8,16,256]{3,2,1,0:T(8,128)(2,1)S(1)} %get-tuple-element.21), channel_id=1, source_target_pairs={{0,16},{8,24},{16,0},{24,8},{1,17},{9,25},{17,1},{25,9},{2,18},{10... | collective-permute-start | bytes 393224 | tf_op jit(solution)/shard_map/ppermute | solution.py:55
  36.6 4.4 %cond_planes.1 = f32[256,1024]{1,0:T(8,128)} custom-call(f32[256,512]{1,0:T(8,128)S(1)} %copy-done.8, bf16[8,16,256]{2,1,0:T(8,128)(2,1)S(1)} %get-tuple-element.18.home_ref, bf16[8,16,256]{2,1,0:T(8,128)(2,1)S(1)} %get-tuple-element.12.away_ref), custom_call_target="tpu_custom_call" | custom-call | flops 1610612736 | bytes 2097152 | tf_op jit(solution)/shard_map/cond_planes/pallas_call | solution.py:205
  42.0 11.3 %all-to-all-start = ((f32[32,8,1024]{2,1,0:T(8,128)}), f32[32,8,1024]{2,1,0:T(8,128)S(1)}, u32[]{:S(2)}, u32[]{:S(2)}) async-start(f32[32,8,1024]{2,1,0:T(8,128)} %bitcast.38), calls=%async_computation | async-start | bytes 2097152 | tf_op jit(solution)/shard_map/all_to_all | solution.py:405
  53.2 5.5 %collective-permute-start.3 = (bf16[8,16,256]{2,1,0:T(8,128)(2,1)S(1)}, bf16[8,16,256]{2,1,0:T(8,128)(2,1)S(1)}, u32[]{:S(2)}, u32[]{:S(2)}) collective-permute-start(bf16[8,16,256]{2,1,0:T(8,128)(2,1)S(1)} %bitcast.103), channel_id=1, source_target_pairs={{0,1},{1,0},{2,3},{3,2},{4,5},{5,4},{6,7},{7,6},{8,9},{9,8},{10,11... | collective-permute-start | bytes 196616 | tf_op jit(solution)/shard_map/ppermute | solution.py:55
  58.7 11.5 %collective-permute-done.3 = bf16[8,16,256]{2,1,0:T(8,128)(2,1)S(1)} collective-permute-done((bf16[8,16,256]{2,1,0:T(8,128)(2,1)S(1)}, bf16[8,16,256]{2,1,0:T(8,128)(2,1)S(1)}, u32[]{:S(2)}, u32[]{:S(2)}) %collective-permute-start.3) | collective-permute-done | bytes 65568 | tf_op jit(solution)/shard_map/ppermute | solution.py:55
  70.2 3.1 %collective-permute-start.5 = (bf16[2,8,16,256]{3,2,1,0:T(8,128)(2,1)S(1)}, bf16[2,8,16,256]{3,2,1,0:T(8,128)(2,1)S(1)}, u32[]{:S(2)}, u32[]{:S(2)}) collective-permute-start(bf16[2,8,16,256]{3,2,1,0:T(8,128)(2,1)S(1)} %get-tuple-element.23), channel_id=1, source_target_pairs={{0,16},{8,24},{16,0},{24,8},{1,17},{9,25},{17,1},{25,9},{2,18},{10... | collective-permute-start | bytes 393224 | tf_op jit(solution)/shard_map/ppermute | solution.py:55
  76.8 2.7 %collective-permute-done.4 = bf16[2,8,16,256]{3,2,1,0:T(8,128)(2,1)S(1)} collective-permute-done((bf16[2,8,16,256]{3,2,1,0:T(8,128)(2,1)S(1)}, bf16[2,8,16,256]{3,2,1,0:T(8,128)(2,1)S(1)}, u32[]{:S(2)}, u32[]{:S(2)}) %collective-permute-start.4) | collective-permute-done | bytes 131104 | tf_op jit(solution)/shard_map/ppermute | solution.py:55
  82.4 10.9 %collective-permute-start.7 = (bf16[4,2,8,16,256]{4,3,2,1,0:T(8,128)(2,1)S(1)}, bf16[4,2,8,16,256]{4,3,2,1,0:T(8,128)(2,1)}, u32[]{:S(2)}, u32[]{:S(2)}) collective-permute-start(bf16[4,2,8,16,256]{4,3,2,1,0:T(8,128)(2,1)S(1)} %get-tuple-element.17), channel_id=1, source_target_pairs={{0,2},{2,4},{4,6},{6,0},{1,3},{3,5},{5,7},{7,1},{8,10},{10,12},{12... | collective-permute-start | bytes 1572872 | tf_op jit(solution)/shard_map/ppermute | solution.py:55
  96.9 9.3 %collective-permute-start.15 = (bf16[4,2,8,16,256]{4,3,2,1,0:T(8,128)(2,1)}, bf16[4,2,8,16,256]{4,3,2,1,0:T(8,128)(2,1)S(1)}, u32[]{:S(2)}, u32[]{:S(2)}) collective-permute-start(bf16[4,2,8,16,256]{4,3,2,1,0:T(8,128)(2,1)} %pad_maximum_fusion.4), channel_id=1, source_target_pairs={{0,2},{2,4},{4,6},{6,0},{1,3},{3,5},{5,7},{7,1},{8,10},{10,12},{12... | collective-permute-start | bytes 1572872 | tf_op jit(solution)/shard_map/ppermute | solution.py:55
  108.1 6.3 %collective-permute-done.7 = bf16[4,2,8,16,256]{4,3,2,1,0:T(8,128)(2,1)} collective-permute-done((bf16[4,2,8,16,256]{4,3,2,1,0:T(8,128)(2,1)S(1)}, bf16[4,2,8,16,256]{4,3,2,1,0:T(8,128)(2,1)}, u32[]{:S(2)}, u32[]{:S(2)}) %collective-permute-start.7) | collective-permute-done | bytes 524320 | tf_op jit(solution)/shard_map/ppermute | solution.py:55
  117.2 13.4 %screened_transform.1.refs_8_.refs_9_ = bf16[17,512,256]{2,1,0:T(8,128)(2,1)S(1)} custom-call(s32[32,1,256]{2,1,0:T(1,128)S(1)} %bitcast.80, bf16[96,32]{1,0:T(8,128)(2,1)S(1)} %copy-done.11, bf16[2,256,256]{2,1,0:T(8,128)(2,1)S(1)} %copy-done.10, bf16[2,256,256]{2,1,0:T(8,128)(2,1)S(1)} %copy-done.9, bf16[256,8192]{1,0:T(8,128)(2,1)S(1)} %copy-done.7), custom_call_target="tpu_custom_call" | custom-call | flops 3422552064 | bytes 9437184 | tf_op jit(solution)/shard_map/screened_transform/pallas_call | solution.py:131
  132.7 2.7 %pad_maximum_fusion.1 = bf16[4,4,2,8,16,256]{5,4,3,2,1,0:T(8,128)(2,1)} fusion(bf16[1,4,2,8,16,256]{5,4,3,2,1,0:T(8,128)(2,1)S(1)} %bitcast.89, bf16[1,4,2,8,16,256]{5,4,3,2,1,0:T(8,128)(2,1)S(1)} %bitcast.90, bf16[1,4,2,8,16,256]{5,4,3,2,1,0:T(8,128)(2,1)S(1)} %bitcast.91, bf16[1,4,2,8,16,256]{5,4,3,2,1,0:T(8,128)(2,1)} %bitcast.32), kind=kLoop, calls=%fused_computation.1 | loop fusion | flops 3145728 | bytes 4194304 | tf_op jit(solution)/shard_map/stack | solution.py:59
  136.4 3.7 %cond_spectrum.1.refs_10_ = bf16[1024,256]{1,0:T(8,128)(2,1)S(1)} custom-call(f32[256,256]{1,0:T(8,128)S(1)} %copy-done.3, f32[256,256]{1,0:T(8,128)S(1)} %get-tuple-element.24.sin_ref, f32[256,1024]{1,0:T(8,128)S(1)} %bitcast.78), custom_call_target="tpu_custom_call" | custom-call | flops 1610612736 | bytes 2097152 | tf_op jit(solution)/shard_map/cond_spectrum/pallas_call | solution.py:333
  142.3 12.4 %valence_response.1 = f32[32,16,128]{2,1,0:T(8,128)S(1)} custom-call(s32[1]{0:T(128)} %bitcast.place_ref, bf16[32,8,16,256]{3,2,1,0:T(8,128)(2,1)S(1)} %bitcast.68, bf16[32,8,16,256]{3,2,1,0:T(8,128)(2,1)S(1)} %bitcast.72, bf16[32,8,16,256]{3,2,1,0:T(8,128)(2,1)S(1)} %bitcast.69, bf16[32,8,16,256]{3,2,1,0:T(8,128)(2,1)S(1)} %bitcast.73, ...), custom_call_target="tpu_custom_call" | custom-call | flops 4563402752 | bytes 9437184 | tf_op jit(solution)/shard_map/valence_response/pallas_call | solution.py:294
  154.7 14.2 %all_to_all.26 = f32[32,16,128]{2,1,0:T(8,128)S(1)} all-to-all(f32[32,16,128]{2,1,0:T(8,128)S(1)} %valence_response.1), channel_id=1, replica_groups=mesh['zl'=4,'co'=2,'x'=4,'y'=4,'zh'=2] {'x','y'}, dimensions={0} | all-to-all | bytes 524288 | tf_op jit(solution)/shard_map/all_to_all | solution.py:412
  169.1 7.6 %collective-permute-done.18 = f32[2,16,128]{2,1,0:T(8,128)S(1)} collective-permute-done((f32[2,16,128]{2,1,0:T(8,128)S(1)}, f32[2,16,128]{2,1,0:T(8,128)S(1)}, u32[]{:S(2)}, u32[]{:S(2)}) %collective-permute-start.18) | collective-permute-done | bytes 16416 | tf_op jit(solution)/shard_map/ppermute | solution.py:55
  177.4 18.4 %all-to-all-start.2 = ((f32[8,2,16,128]{3,2,1,0:T(8,128)}), f32[8,2,16,128]{3,2,1,0:T(8,128)S(1)}, u32[]{:S(2)}, u32[]{:S(2)}) async-start(f32[8,2,16,128]{3,2,1,0:T(8,128)} %broadcast_in_dim.16), calls=%async_computation.2 | async-start | bytes 262144 | tf_op jit(solution)/shard_map/all_to_all | solution.py:65
  195.8 6.7 %all-to-all-done.2 = f32[8,2,16,128]{3,2,1,0:T(8,128)S(1)} async-done(((f32[8,2,16,128]{3,2,1,0:T(8,128)}), f32[8,2,16,128]{3,2,1,0:T(8,128)S(1)}, u32[]{:S(2)}, u32[]{:S(2)}) %all-to-all-start.2) | async-done | bytes 131104 | tf_op jit(solution)/shard_map/all_to_all | solution.py:65
  203.1 14.8 %all_to_all.27.full_ref = f32[16,2,32,128]{3,2,1,0:T(8,128)S(1)} all-to-all(f32[16,2,32,128]{3,2,1,0:T(8,128)S(1)} %broadcast_in_dim.21), channel_id=1, replica_groups=mesh['zl'=4,'co'=2,'x'=4,'y'=4,'zh'=2] {'x','y'}, dimensions={0} | all-to-all | bytes 1048576 | tf_op jit(solution)/shard_map/all_to_all | solution.py:65
  (81 shorter events, 32.9 us)
Async XLA Ops:
  1.6 8.6 %collective-permute-start.2 = (bf16[8,32,256]{2,1,0:T(8,128)(2,1)S(1)}, bf16[8,32,256]{2,1,0:T(8,128)(2,1)S(1)}, u32[]{:S(2)}, u32[]{:S(2)}) collective-permute-start(bf16[8,32,256]{2,1,0:T(8,128)(2,1)S(1)} %bitcast.81), channel_id=1, source_target_pairs={{0,192},{64,0},{128,64},{192,128},{1,193},{65,1},{129,65},{193,129... | collective-permute-start | bytes 393224 | tf_op jit(solution)/shard_map/ppermute | solution.py:55
  6.3 11.2 %collective-permute-start.1 = (bf16[8,32,256]{2,1,0:T(8,128)(2,1)S(1)}, bf16[8,32,256]{2,1,0:T(8,128)(2,1)S(1)}, u32[]{:S(2)}, u32[]{:S(2)}) collective-permute-start(bf16[8,32,256]{2,1,0:T(8,128)(2,1)S(1)} %bitcast.82), channel_id=1, source_target_pairs={{0,128},{64,192},{128,0},{192,64},{1,129},{65,193},{129,1},{193,65... | collective-permute-start | bytes 393224 | tf_op jit(solution)/shard_map/ppermute | solution.py:55
  6.3 11.2 %collective-permute-start = (bf16[8,32,256]{2,1,0:T(8,128)(2,1)S(1)}, bf16[8,32,256]{2,1,0:T(8,128)(2,1)S(1)}, u32[]{:S(2)}, u32[]{:S(2)}) collective-permute-start(bf16[8,32,256]{2,1,0:T(8,128)(2,1)S(1)} %bitcast.83), channel_id=1, source_target_pairs={{0,64},{64,128},{128,192},{192,0},{1,65},{65,129},{129,193},{193,1... | collective-permute-start | bytes 393224 | tf_op jit(solution)/shard_map/ppermute | solution.py:55
  17.6 2.0 collective-permute-start.10
  22.0 8.2 %collective-permute-start.11 = (bf16[8,16,256]{2,1,0:T(8,128)(2,1)S(1)}, bf16[8,16,256]{2,1,0:T(8,128)(2,1)S(1)}, u32[]{:S(2)}, u32[]{:S(2)}) collective-permute-start(bf16[8,16,256]{2,1,0:T(8,128)(2,1)S(1)} %get-tuple-element.11), channel_id=1, source_target_pairs={{0,1},{1,0},{2,3},{3,2},{4,5},{5,4},{6,7},{7,6},{8,9},{9,8},{10,11... | collective-permute-start | bytes 196616 | tf_op jit(solution)/shard_map/ppermute | solution.py:55
  30.2 10.8 %collective-permute-start.13 = (bf16[2,8,16,256]{3,2,1,0:T(8,128)(2,1)S(1)}, bf16[2,8,16,256]{3,2,1,0:T(8,128)(2,1)S(1)}, u32[]{:S(2)}, u32[]{:S(2)}) collective-permute-start(bf16[2,8,16,256]{3,2,1,0:T(8,128)(2,1)S(1)} %get-tuple-element.21), channel_id=1, source_target_pairs={{0,16},{8,24},{16,0},{24,8},{1,17},{9,25},{17,1},{25,9},{2,18},{10... | collective-permute-start | bytes 393224 | tf_op jit(solution)/shard_map/ppermute | solution.py:55
  33.3 7.7 %collective-permute-start.12 = (bf16[2,8,16,256]{3,2,1,0:T(8,128)(2,1)S(1)}, bf16[2,8,16,256]{3,2,1,0:T(8,128)(2,1)S(1)}, u32[]{:S(2)}, u32[]{:S(2)}) collective-permute-start(bf16[2,8,16,256]{3,2,1,0:T(8,128)(2,1)S(1)} %get-tuple-element.21), channel_id=1, source_target_pairs={{0,8},{8,16},{16,24},{24,0},{1,9},{9,17},{17,25},{25,1},{2,10},{10... | collective-permute-start | bytes 393224 | tf_op jit(solution)/shard_map/ppermute | solution.py:55
  33.9 7.1 %collective-permute-start.14 = (bf16[2,8,16,256]{3,2,1,0:T(8,128)(2,1)S(1)}, bf16[2,8,16,256]{3,2,1,0:T(8,128)(2,1)S(1)}, u32[]{:S(2)}, u32[]{:S(2)}) collective-permute-start(bf16[2,8,16,256]{3,2,1,0:T(8,128)(2,1)S(1)} %get-tuple-element.21), channel_id=1, source_target_pairs={{0,24},{8,0},{16,8},{24,16},{1,25},{9,1},{17,9},{25,17},{2,26},{10... | collective-permute-start | bytes 393224 | tf_op jit(solution)/shard_map/ppermute | solution.py:55
  42.0 51.4 %copy-start.6 = (s32[8192]{0:T(1024)S(1)}, s32[8192]{0:T(1024)}, u32[]{:S(2)}) copy-start(s32[8192]{0:T(1024)} %param.10) | copy-start | bytes 98308
  42.0 93.4 %all-to-all-start = ((f32[32,8,1024]{2,1,0:T(8,128)}), f32[32,8,1024]{2,1,0:T(8,128)S(1)}, u32[]{:S(2)}, u32[]{:S(2)}) async-start(f32[32,8,1024]{2,1,0:T(8,128)} %bitcast.38), calls=%async_computation | async-start | bytes 2097152 | tf_op jit(solution)/shard_map/all_to_all | solution.py:405
  53.2 16.9 %collective-permute-start.3 = (bf16[8,16,256]{2,1,0:T(8,128)(2,1)S(1)}, bf16[8,16,256]{2,1,0:T(8,128)(2,1)S(1)}, u32[]{:S(2)}, u32[]{:S(2)}) collective-permute-start(bf16[8,16,256]{2,1,0:T(8,128)(2,1)S(1)} %bitcast.103), channel_id=1, source_target_pairs={{0,1},{1,0},{2,3},{3,2},{4,5},{5,4},{6,7},{7,6},{8,9},{9,8},{10,11... | collective-permute-start | bytes 196616 | tf_op jit(solution)/shard_map/ppermute | solution.py:55
  70.2 6.6 %collective-permute-start.5 = (bf16[2,8,16,256]{3,2,1,0:T(8,128)(2,1)S(1)}, bf16[2,8,16,256]{3,2,1,0:T(8,128)(2,1)S(1)}, u32[]{:S(2)}, u32[]{:S(2)}) collective-permute-start(bf16[2,8,16,256]{3,2,1,0:T(8,128)(2,1)S(1)} %get-tuple-element.23), channel_id=1, source_target_pairs={{0,16},{8,24},{16,0},{24,8},{1,17},{9,25},{17,1},{25,9},{2,18},{10... | collective-permute-start | bytes 393224 | tf_op jit(solution)/shard_map/ppermute | solution.py:55
  73.3 6.2 %collective-permute-start.4 = (bf16[2,8,16,256]{3,2,1,0:T(8,128)(2,1)S(1)}, bf16[2,8,16,256]{3,2,1,0:T(8,128)(2,1)S(1)}, u32[]{:S(2)}, u32[]{:S(2)}) collective-permute-start(bf16[2,8,16,256]{3,2,1,0:T(8,128)(2,1)S(1)} %get-tuple-element.23), channel_id=1, source_target_pairs={{0,8},{8,16},{16,24},{24,0},{1,9},{9,17},{17,25},{25,1},{2,10},{10... | collective-permute-start | bytes 393224 | tf_op jit(solution)/shard_map/ppermute | solution.py:55
  73.9 5.6 %collective-permute-start.6 = (bf16[2,8,16,256]{3,2,1,0:T(8,128)(2,1)S(1)}, bf16[2,8,16,256]{3,2,1,0:T(8,128)(2,1)S(1)}, u32[]{:S(2)}, u32[]{:S(2)}) collective-permute-start(bf16[2,8,16,256]{3,2,1,0:T(8,128)(2,1)S(1)} %get-tuple-element.23), channel_id=1, source_target_pairs={{0,24},{8,0},{16,8},{24,16},{1,25},{9,1},{17,9},{25,17},{2,26},{10... | collective-permute-start | bytes 393224 | tf_op jit(solution)/shard_map/ppermute | solution.py:55
  79.4 36.9 %copy-start.11 = (bf16[96,32]{1,0:T(8,128)(2,1)S(1)}, bf16[96,32]{1,0:T(8,128)(2,1)}, u32[]{:S(2)}) copy-start(bf16[96,32]{1,0:T(8,128)(2,1)} %constant.188.clone.line_ref) | copy-start | bytes 18436
  80.3 16.6 %collective-permute-start.8 = (bf16[4,2,8,16,256]{4,3,2,1,0:T(8,128)(2,1)S(1)}, bf16[4,2,8,16,256]{4,3,2,1,0:T(8,128)(2,1)S(1)}, u32[]{:S(2)}, u32[]{:S(2)}) collective-permute-start(bf16[4,2,8,16,256]{4,3,2,1,0:T(8,128)(2,1)S(1)} %get-tuple-element.17), channel_id=1, source_target_pairs={{0,4},{2,6},{4,0},{6,2},{1,5},{3,7},{5,1},{7,3},{8,12},{10,14},{12... | collective-permute-start | bytes 1572872 | tf_op jit(solution)/shard_map/ppermute | solution.py:55
  82.4 32.0 %collective-permute-start.7 = (bf16[4,2,8,16,256]{4,3,2,1,0:T(8,128)(2,1)S(1)}, bf16[4,2,8,16,256]{4,3,2,1,0:T(8,128)(2,1)}, u32[]{:S(2)}, u32[]{:S(2)}) collective-permute-start(bf16[4,2,8,16,256]{4,3,2,1,0:T(8,128)(2,1)S(1)} %get-tuple-element.17), channel_id=1, source_target_pairs={{0,2},{2,4},{4,6},{6,0},{1,3},{3,5},{5,7},{7,1},{8,10},{10,12},{12... | collective-permute-start | bytes 1572872 | tf_op jit(solution)/shard_map/ppermute | solution.py:55
  93.3 21.1 %collective-permute-start.9 = (bf16[4,2,8,16,256]{4,3,2,1,0:T(8,128)(2,1)S(1)}, bf16[4,2,8,16,256]{4,3,2,1,0:T(8,128)(2,1)}, u32[]{:S(2)}, u32[]{:S(2)}) collective-permute-start(bf16[4,2,8,16,256]{4,3,2,1,0:T(8,128)(2,1)S(1)} %get-tuple-element.17), channel_id=1, source_target_pairs={{0,6},{2,0},{4,2},{6,4},{1,7},{3,1},{5,3},{7,5},{8,14},{10,8},{12,... | collective-permute-start | bytes 1572872 | tf_op jit(solution)/shard_map/ppermute | solution.py:55
  93.4 39.3 %collective-permute-start.17 = (bf16[4,2,8,16,256]{4,3,2,1,0:T(8,128)(2,1)}, bf16[4,2,8,16,256]{4,3,2,1,0:T(8,128)(2,1)S(1)}, u32[]{:S(2)}, u32[]{:S(2)}) collective-permute-start(bf16[4,2,8,16,256]{4,3,2,1,0:T(8,128)(2,1)} %pad_maximum_fusion.4), channel_id=1, source_target_pairs={{0,6},{2,0},{4,2},{6,4},{1,7},{3,1},{5,3},{7,5},{8,14},{10,8},{12,... | collective-permute-start | bytes 1572872 | tf_op jit(solution)/shard_map/ppermute | solution.py:55
  95.2 37.5 %collective-permute-start.16 = (bf16[4,2,8,16,256]{4,3,2,1,0:T(8,128)(2,1)}, bf16[4,2,8,16,256]{4,3,2,1,0:T(8,128)(2,1)S(1)}, u32[]{:S(2)}, u32[]{:S(2)}) collective-permute-start(bf16[4,2,8,16,256]{4,3,2,1,0:T(8,128)(2,1)} %pad_maximum_fusion.4), channel_id=1, source_target_pairs={{0,4},{2,6},{4,0},{6,2},{1,5},{3,7},{5,1},{7,3},{8,12},{10,14},{12... | collective-permute-start | bytes 1572872 | tf_op jit(solution)/shard_map/ppermute | solution.py:55
  96.9 35.8 %collective-permute-start.15 = (bf16[4,2,8,16,256]{4,3,2,1,0:T(8,128)(2,1)}, bf16[4,2,8,16,256]{4,3,2,1,0:T(8,128)(2,1)S(1)}, u32[]{:S(2)}, u32[]{:S(2)}) collective-permute-start(bf16[4,2,8,16,256]{4,3,2,1,0:T(8,128)(2,1)} %pad_maximum_fusion.4), channel_id=1, source_target_pairs={{0,2},{2,4},{4,6},{6,0},{1,3},{3,5},{5,7},{7,1},{8,10},{10,12},{12... | collective-permute-start | bytes 1572872 | tf_op jit(solution)/shard_map/ppermute | solution.py:55
  142.3 60.4 %copy-start.5 = (s32[64]{0:T(128)S(1)}, s32[64]{0:T(128)}, u32[]{:S(2)}) copy-start(s32[64]{0:T(128)} %partner_ref.1) | copy-start | bytes 772
  169.0 7.7 %collective-permute-start.18 = (f32[2,16,128]{2,1,0:T(8,128)S(1)}, f32[2,16,128]{2,1,0:T(8,128)S(1)}, u32[]{:S(2)}, u32[]{:S(2)}) collective-permute-start(f32[2,16,128]{2,1,0:T(8,128)S(1)} %reduce_sum.9), channel_id=1, source_target_pairs={{0,1},{1,0},{2,3},{3,2},{4,5},{5,4},{6,7},{7,6},{8,9},{9,8},{10,11... | collective-permute-start | bytes 49160 | tf_op jit(solution)/shard_map/ppermute | solution.py:55
  177.4 25.1 %all-to-all-start.2 = ((f32[8,2,16,128]{3,2,1,0:T(8,128)}), f32[8,2,16,128]{3,2,1,0:T(8,128)S(1)}, u32[]{:S(2)}, u32[]{:S(2)}) async-start(f32[8,2,16,128]{3,2,1,0:T(8,128)} %broadcast_in_dim.16), calls=%async_computation.2 | async-start | bytes 262144 | tf_op jit(solution)/shard_map/all_to_all | solution.py:65
  (10 other events, 86.2 us)

commit v3 on v1

--- a/solution.py
+++ b/solution.py
@@ -17,6 +17,7 @@
 PLANE = NX * NY
 HALF = NZ // 2 + 1
 LINE_BLOCKS = 4
+LINE_ROWS = 48
 NORM = 1.0 / math.sqrt(NG)
 EXACT = lax.Precision.HIGHEST
 BF = jnp.bfloat16
@@ -28,7 +29,6 @@
 SIZE = dict(zip(AXES, SIZES))
 KA = ("zl", "co")
 GA = ("x", "y", "zh")
-VMEM = 48 * MIB
 
 
 def split_table(table):
@@ -70,51 +70,51 @@
     )
 
 
-def line_kernel(gmap_ref, high_ref, low_ref, w_ref, y_ref):
-    rows = 2 * HALF * 8
-    keep = (lax.broadcasted_iota(jnp.int32, (rows, 256), 0) & 7) == (
-        lax.broadcasted_iota(jnp.int32, (rows, 256), 1) >> 5
+def line_kernel(gmap_ref, line_ref, w_ref, out_ref):
+    rows = 2 * HALF
+    keep = lax.broadcasted_iota(jnp.int32, (1, 8, 256), 1) == (
+        lax.broadcasted_iota(jnp.int32, (1, 8, 256), 2) >> 5
     )
     for b in range(LINE_BLOCKS):
         level = gmap_ref[b] & (NZ - 1)
         hot = (lax.broadcasted_iota(jnp.int32, (NZ, 256), 0) == level).astype(F32).astype(BF)
+        picked = dot(line_ref[...], hot)
+        tables = []
+        for at in (0, LINE_ROWS):
+            wide = jnp.broadcast_to(picked[at : at + rows][:, None, :], (rows, 8, 256))
+            tables.append(jnp.where(keep, wide, 0.0).reshape(rows * 8, 256).astype(BF))
         block = w_ref[:, b * 256 : (b + 1) * 256]
-        total = None
-        for table in (high_ref, low_ref):
-            picked = jnp.where(keep, dot(table[...], hot), 0.0).astype(BF)
-            part = dot(picked, block, ((1,), (1,)))
-            total = part if total is None else total + part
-        y_ref[:, :, b * 8 : (b + 1) * 8, :] = total.reshape(2, HALF, 8, 256)
+        both = dot(jnp.concatenate(tables, axis=0), block, ((1,), (1,)))
+        total = both[: rows * 8] + both[rows * 8 :]
+        out_ref[:, b * 8 : (b + 1) * 8, :] = total.reshape(rows, 8, 256)
 
 
 def line_transform(screened, gmap):
     angles = line_angles()[:HALF]
-    table = np.stack([np.cos(angles), -np.sin(angles)])
-    table = np.repeat(table.reshape(2 * HALF, NZ), 8, axis=0)
-    high, low = split_table(table)
-    rows = 2 * HALF * 8
+    table = np.concatenate([np.cos(angles), -np.sin(angles)], axis=0)
+    padding = np.zeros((LINE_ROWS - 2 * HALF, NZ), BF)
+    line = np.concatenate([x for part in split_table(table) for x in (part, padding)], axis=0)
     n = LINE_BLOCKS
     return pl.pallas_call(
         line_kernel,
         grid=(32 // n,),
         in_specs=[
-            pl.BlockSpec((n, 1, 256), lambda b: (b, 0, 0)),
-            pl.BlockSpec((rows, NZ), lambda b: (0, 0)),
-            pl.BlockSpec((rows, NZ), lambda b: (0, 0)),
-            pl.BlockSpec((256, n * 256), lambda b: (0, b)),
+            pl.BlockSpec((n, 1, 256), lambda i: (i, 0, 0)),
+            pl.BlockSpec((2 * LINE_ROWS, NZ), lambda i: (0, 0)),
+            pl.BlockSpec((256, n * 256), lambda i: (0, i)),
         ],
-        out_specs=pl.BlockSpec((2, HALF, n * 8, 256), lambda b: (0, 0, b, 0)),
-        out_shape=jax.ShapeDtypeStruct((2, HALF, PLANE, 256), F32),
-        compiler_params=pltpu.CompilerParams(vmem_limit_bytes=VMEM),
+        out_specs=pl.BlockSpec((2 * HALF, n * 8, 256), lambda i: (0, i, 0)),
+        out_shape=jax.ShapeDtypeStruct((2 * HALF, PLANE, 256), F32),
+        compiler_params=pltpu.CompilerParams(vmem_limit_bytes=16 * MIB),
         cost_estimate=pl.CostEstimate(
-            flops=4 * rows * 256 * 8192, bytes_accessed=14 * MIB, transcendentals=0
+            flops=4 * 272 * 256 * 8192, bytes_accessed=14 * MIB, transcendentals=0
         ),
         name="screened_line",
-    )(gmap.reshape(32, 1, 256), jnp.asarray(high), jnp.asarray(low), screened)
-
-
-def plane_kernel(high_ref, low_ref, y_ref, w_ref):
-    real, imag = y_ref[0, 0], y_ref[1, 0]
+    )(gmap.reshape(32, 1, 256), jnp.asarray(line), screened)
+
+
+def plane_kernel(high_ref, low_ref, real_ref, imag_ref, out_ref):
+    real, imag = real_ref[0], imag_ref[0]
     for odd in range(2):
         if odd:
             both = [real[:128] - real[128:], imag[:128] - imag[128:]]
@@ -127,8 +127,8 @@
         prod = (dot(high, top) + (dot(high, rest) + dot(low, top))).astype(BF)
         for half in range(8):
             at = (2 * half + odd) * NY
-            w_ref[0, at : at + NY] = prod[half * NY : (half + 1) * NY]
-            w_ref[0, 256 + at : 256 + at + NY] = prod[128 + half * NY : 128 + (half + 1) * NY]
+            out_ref[0, at : at + NY] = prod[half * NY : (half + 1) * NY]
+            out_ref[0, 256 + at : 256 + at + NY] = prod[128 + half * NY : 144 + half * NY]
 
 
 def plane_transform(lines):
@@ -145,21 +145,23 @@
         in_specs=[
             pl.BlockSpec((2, 256, 256), lambda z: (0, 0, 0)),
             pl.BlockSpec((2, 256, 256), lambda z: (0, 0, 0)),
-            pl.BlockSpec((2, 1, 256, 256), lambda z: (0, z, 0, 0)),
+            pl.BlockSpec((1, 256, 256), lambda z: (z, 0, 0)),
+            pl.BlockSpec((1, 256, 256), lambda z: (z + HALF, 0, 0)),
         ],
         out_specs=pl.BlockSpec((1, 512, 256), lambda z: (z, 0, 0)),
         out_shape=jax.ShapeDtypeStruct((HALF, 512, 256), BF),
-        compiler_params=pltpu.CompilerParams(vmem_limit_bytes=VMEM),
+        compiler_params=pltpu.CompilerParams(vmem_limit_bytes=16 * MIB),
         cost_estimate=pl.CostEstimate(
             flops=12 * 256 * 256 * 256 * HALF, bytes_accessed=14 * MIB, transcendentals=0
         ),
         name="screened_plane",
-    )(jnp.asarray(high), jnp.asarray(low), lines)
+    )(jnp.asarray(high), jnp.asarray(low), lines, lines)
 
 
 def choose_kernel(partner_ref, place_ref, flip_ref, near_ref, far_ref, val_ref, cond_ref):
     level, core = place_ref[0], place_ref[1]
     for m in range(8):
+        val_ref[0, m] = dot(near_ref[m, :16], flip_ref[...]).astype(BF)
         wanted = partner_ref[(level * 2 + core) * 8 + m]
         back = (level - wanted // 16) & 3
         at = back * 8 + (wanted & 7)
@@ -167,7 +169,7 @@
 
         def take(ref, m=m, at=at):
             row = ref[at]
-            val_ref[m] = dot(row[:16], flip_ref[...]).astype(BF)
+            val_ref[1, m] = dot(row[:16], flip_ref[...]).astype(BF)
             cond_ref[m] = row[16:]
 
         pl.when(near)(functools.partial(take, near_ref))
@@ -182,7 +184,7 @@
         in_specs=[pl.BlockSpec(memory_space=pltpu.SMEM)] * 2
         + [pl.BlockSpec(memory_space=pltpu.VMEM)] * 3,
         out_specs=[pl.BlockSpec(memory_space=pltpu.VMEM)] * 2,
-        out_shape=[shape, shape],
+        out_shape=[jax.ShapeDtypeStruct((2, 8, 16, 256), BF), shape],
         compiler_params=pltpu.CompilerParams(vmem_limit_bytes=16 * MIB),
         name="partner_choice",
     )(partner, place, flip, near, far)
@@ -292,10 +294,9 @@
             z = (NZ - z) & (NZ - 1) if back else z
             place = place_ref[0]
             level = (place ^ z) & 1
-            if which == 0:
-                return ((z & 30) + level, 0, 0, 0)
             x = ((place >> 3) - (z >> 3)) & 3
             y = ((place >> 1) - (z >> 1)) & 3
+            x, y = (x, y) if which == 0 else (y, x)
             return ((y * 4 + x) * 2 + level, 0, 0, 0)
 
         return pl.BlockSpec((1, 8, 16, 256), index)
@@ -320,7 +321,7 @@
             ],
         ),
         out_shape=jax.ShapeDtypeStruct((32, 16, 128), F32),
-        compiler_params=pltpu.CompilerParams(vmem_limit_bytes=VMEM),
+        compiler_params=pltpu.CompilerParams(vmem_limit_bytes=20 * MIB),
         cost_estimate=pl.CostEstimate(
             flops=2 * 1024 * 512 * 256 * HALF, bytes_accessed=9 * MIB, transcendentals=0
         ),
@@ -362,6 +363,34 @@
     return jnp.where(same, jnp.cos(angle), 0.0), jnp.where(same, jnp.sin(angle), 0.0)
 
 
+def lay_out_kernel(full_ref, rows_ref, mirror_ref):
+    low = lax.broadcasted_iota(jnp.int32, (1, 128), 1) < 64
+    for m in range(4):
+        for n in range(4):
+            for c in (2 * n, 2 * n + 1):
+                piece = full_ref[m * 4 + n, 0, (c & 1) * 16 : (c & 1) * 16 + 16]
+                at = (c * 4 + m) * 128
+                rows_ref[:, :, at : at + 128] = piece.reshape(8, 2, 128)
+            even, odd = full_ref[m * 4 + n, 1, :16], full_ref[m * 4 + n, 1, 16:]
+            first = jnp.where(low, even, pltpu.roll(odd, 64, 1))
+            second = jnp.where(low, pltpu.roll(even, 64, 1), odd)
+            at = (2 * m * 4 + n) * 128
+            mirror_ref[:, :, at : at + 128] = first.reshape(8, 2, 128)
+            mirror_ref[:, :, at + 512 : at + 640] = second.reshape(8, 2, 128)
+
+
+def lay_out(full):
+    shape = jax.ShapeDtypeStruct((8, 2, 4096), F32)
+    return pl.pallas_call(
+        lay_out_kernel,
+        in_specs=[pl.BlockSpec(memory_space=pltpu.VMEM)],
+        out_specs=[pl.BlockSpec(memory_space=pltpu.VMEM)] * 2,
+        out_shape=[shape, shape],
+        compiler_params=pltpu.CompilerParams(vmem_limit_bytes=16 * MIB),
+        name="lay_out",
+    )(full)
+
+
 def on_device(wavefunctions, partner, gmap, screened):
     ka_place = lax.axis_index(KA)
     place = lax.axis_index(GA)
@@ -369,24 +398,27 @@
 
     waves = wavefunctions.reshape(8, 2, 2, 8, 256).transpose(0, 2, 1, 3, 4).reshape(8, 32, 256)
     near = spread(waves, "zl").reshape(32, 32, 256)
-    far = turned(near, "co", 1)
 
     index = jnp.arange(PLANE, dtype=jnp.int32)
     negative = (NX - index // NY) % NX * NY + (NY - index % NY) % NY
     negative = jnp.where(place > NZ // 2, negative, index)
     flip = (index[:, None] == negative[None, :]).astype(BF)
-    home_val = dot(waves[:, :16].reshape(128, 256), flip).astype(BF).reshape(8, 16, 256)
-    home = lax.all_gather(spread(home_val, "zh"), ("x", "y")).reshape(32, 8, 16, 256)
-
     lines = line_transform(screened, gmap)
-
-    away_val, away_cond = choose(partner, near, far, flip)
-    away = spread(spread(away_val, "zh"), "x")
+    near, lines = lax.optimization_barrier((near, lines))
+    far = turned(near, "co", 1)
+
+    vals, away_cond = choose(partner, near, far, flip)
+    vals = spread(vals, "zh")
+    home, away = spread(vals[:, 0], "x"), spread(vals[:, 1], "y")
     planes = cond_planes(waves[:, 16:], away_cond)
-    away, planes, lines = lax.optimization_barrier((away, planes, lines))
+    home, away, planes, lines = lax.optimization_barrier((home, away, planes, lines))
+    homes = [home] + [turned(home, "y", d) for d in range(1, 4)]
+    aways = [away] + [turned(away, "x", d) for d in range(1, 4)]
+    homes[1], planes = lax.optimization_barrier((homes[1], planes))
     columns = lax.all_to_all(planes, GA, split_axis=0, concat_axis=0, tiled=True)
-    away = spread(away, "y").reshape(32, 8, 16, 256)
     wide = plane_transform(lines)
+    home = jnp.stack(homes).reshape(32, 8, 16, 256)
+    away = jnp.stack(aways).reshape(32, 8, 16, 256)
     cond = cond_spectrum(*line_tables(gmap, place), columns)
 
     blocks = response(place, home, away, wide, cond)
@@ -405,10 +437,7 @@
     sign = jnp.where(jnp.arange(32) % 2 == 0, 1.0, -1.0).astype(F32)
     mirror = jnp.dot(mirror, turn, precision=EXACT) * sign[:, None]
     full = copies_to_all(jnp.stack([mine.reshape(32, 128), mirror]), ("x", "y"))
-    full = full.reshape(4, 4, 2, 2, 8, 2, 2, 64)
-    rows_out = full[:, :, 0].transpose(3, 4, 1, 2, 0, 5, 6).reshape(8, 2, 4096)
-    mirror_out = full[:, :, 1].transpose(3, 4, 0, 5, 1, 2, 6).reshape(8, 2, 4096)
-    return rows_out, mirror_out
+    return lay_out(full)
 
 
 def solution(mesh):

time: 193 us -> 184 us (0.953)
  between operations: 14.3 us -> 0.93 us
  Pallas kernels: 45.9 us -> 37.6 us
  starting transfers between devices: 49.7 us -> 55.4 us
  other arithmetic: 4.35 us -> 8 us
  local copies, waits for them, and re-layouts: 14.7 us -> 17.7 us
    pallas_call x1, Pallas kernels: 13.2 us -> 6.77 us  [plane_transform(): pl.pallas_call(plane_kernel, grid=(HALF,), in_specs=[pl.BlockSpec((2, 256...]
    unnamed x32, local copies, waits for them, and re-layouts: 11.7 us -> 16 us
    another operation x0 -> x2, other arithmetic: none -> 4.02 us  [the longest x1 2.66 us: on_device(): home = jnp.stack(homes).reshape(32, 8, 16, 256)]
    all_to_all x1, starting transfers between devices: 5.73 us -> 8.73 us  [copies_to_all(): return lax.all_to_all(copies, axes, split_axis=0, concat_axis=0, tiled=True)]
    pallas_call x1, Pallas kernels: 9.29 us -> 6.63 us  [line_transform(): pl.pallas_call(line_kernel, grid=(32 // n,), in_specs=[pl.BlockSpec((n, 1...]
    all_to_all x1, starting transfers between devices: 8.57 us -> 10.5 us  [on_device(): lax.all_to_all(planes, GA, split_axis=0, concat_axis=0, tiled=True)]
    ppermute x13 -> x18, waiting for transfers between devices: 28 us -> 29.4 us  [turned(): lax.ppermute(value, axis, [(i, (i + step) % size) for i in range(size)])]
    ppermute x13 -> x18, starting transfers between devices: 35.4 us -> 36.2 us  [turned(): lax.ppermute(value, axis, [(i, (i + step) % size) for i in range(size)])]
  transfers between devices with their start and end apart: 16 -> 20, of which waited for: 10 -> 8; matrix products, arithmetic and copies ran while one was open for 2% -> 4% of each run, Pallas kernels for 17% -> 10%
where the time goes in v3:
time: 184 us; the launch traced here: 183 us
  starting transfers between devices  55.4 us (30%)
  Pallas kernels  37.6 us (20%)
  waiting for transfers between devices  36.2 us (20%)
  blocking collectives  27.1 us (15%)
  local copies, waits for them, and re-layouts  17.7 us (10%)
  other arithmetic  8 us (4%)
    ppermute x18, starting transfers between devices, turned(): lax.ppermute(value, axis, [(i, (i + step) % size) for i in range(size)])  36.2 us
    ppermute x18, waiting for transfers between devices, turned(): lax.ppermute(value, axis, [(i, (i + step) % size) for i in range(size)])  29.4 us
    unnamed x32, local copies, waits for them, and re-layouts  16 us
    all_to_all x1, blocking collectives, copies_to_all(): return lax.all_to_all(copies, axes, split_axis=0, concat_axis=0, tiled=True)  14.8 us
    pallas_call x1, Pallas kernels, response(): pl.pallas_call(response_kernel, grid_spec=pltpu.PrefetchScalarGridSpec(nu...  12.4 us
    all_to_all x1, blocking collectives, on_device(): lax.all_to_all(blocks, ('x', 'y'), split_axis=0, concat_axis=0, tiled=True)  12.4 us
    all_to_all x1, starting transfers between devices, on_device(): lax.all_to_all(planes, GA, split_axis=0, concat_axis=0, tiled=True)  10.5 us
    all_to_all x1, starting transfers between devices, copies_to_all(): return lax.all_to_all(copies, axes, split_axis=0, concat_axis=0, tiled=True)  8.73 us
  transfers between devices with their start and end apart: 20, of which 8 were waited for; matrix products, arithmetic and copies ran while one was open for 4% of the time, Pallas kernels for 10%

profile of v3, /device:TPU:8, one launch (start us, length us, event | category | flops | bytes accessed | tf_op | source)
XLA Modules:
  0.0 183.3 jit_solution(14643981681712451894)
XLA Ops:
  1.5 4.7 %collective-permute-start.2 = (bf16[8,32,256]{2,1,0:T(8,128)(2,1)S(1)}, bf16[8,32,256]{2,1,0:T(8,128)(2,1)S(1)}, u32[]{:S(2)}, u32[]{:S(2)}) collective-permute-start(bf16[8,32,256]{2,1,0:T(8,128)(2,1)S(1)} %bitcast.79), channel_id=1, source_target_pairs={{0,192},{64,0},{128,64},{192,128},{1,193},{65,1},{129,65},{193,129... | collective-permute-start | bytes 393224 | tf_op jit(solution)/shard_map/ppermute | solution.py:54
  10.6 6.6 %screened_line.1.real_ref.imag_ref = f32[34,256,256]{2,1,0:T(8,128)S(1)} custom-call(s32[32,1,256]{2,1,0:T(1,128)S(1)} %bitcast.76, bf16[96,32]{1,0:T(8,128)(2,1)S(1)} %copy-done.10, bf16[256,8192]{1,0:T(8,128)(2,1)S(1)} %copy-done.5), custom_call_target="tpu_custom_call" | custom-call | flops 2281701376 | bytes 14680064 | tf_op jit(solution)/shard_map/screened_line/pallas_call | solution.py:98
  17.3 3.5 %copy-done = f32[34,256,256]{2,1,0:T(8,128)} copy-done((f32[34,256,256]{2,1,0:T(8,128)}, f32[34,256,256]{2,1,0:T(8,128)S(1)}, u32[]{:S(2)}) %copy-start) | copy-done | bytes 8912920
  22.8 2.8 %partner_choice.1 = (bf16[2,8,16,256]{3,2,1,0:T(8,128)(2,1)S(1)}, bf16[8,16,256]{2,1,0:T(8,128)(2,1)S(1)}) custom-call(s32[64]{0:T(128)S(1)} %copy-done.11, s32[2]{0:T(128)S(1)} %pad_add_fusion.place_ref, bf16[256,256]{1,0:T(8,128)(2,1)S(1)} %fusion.4.flip_ref, bf16[32,32,256]{2,1,0:T(8,128)(2,1)S(1)} %bitcast.73, ...), custom_call_target="tpu_custom_call" | custom-call | tf_op jit(solution)/shard_map/partner_choice/pallas_call | solution.py:182
  25.6 5.4 %collective-permute-start.4 = (bf16[2,8,16,256]{3,2,1,0:T(8,128)(2,1)S(1)}, bf16[2,8,16,256]{3,2,1,0:T(8,128)(2,1)S(1)}, u32[]{:S(2)}, u32[]{:S(2)}) collective-permute-start(bf16[2,8,16,256]{3,2,1,0:T(8,128)(2,1)S(1)} %get-tuple-element.13), channel_id=1, source_target_pairs={{0,1},{1,0},{2,3},{3,2},{4,5},{5,4},{6,7},{7,6},{8,9},{9,8},{10,11... | collective-permute-start | bytes 393224 | tf_op jit(solution)/shard_map/ppermute | solution.py:54
  31.0 4.2 %collective-permute-done.4 = bf16[2,8,16,256]{3,2,1,0:T(8,128)(2,1)S(1)} collective-permute-done((bf16[2,8,16,256]{3,2,1,0:T(8,128)(2,1)S(1)}, bf16[2,8,16,256]{3,2,1,0:T(8,128)(2,1)S(1)}, u32[]{:S(2)}, u32[]{:S(2)}) %collective-permute-start.4) | collective-permute-done | bytes 131104 | tf_op jit(solution)/shard_map/ppermute | solution.py:54
  41.7 2.7 %collective-permute-start.6 = (bf16[2,8,16,256]{3,2,1,0:T(8,128)(2,1)S(1)}, bf16[2,8,16,256]{3,2,1,0:T(8,128)(2,1)S(1)}, u32[]{:S(2)}, u32[]{:S(2)}) collective-permute-start(bf16[2,8,16,256]{3,2,1,0:T(8,128)(2,1)S(1)} %get-tuple-element.23), channel_id=1, source_target_pairs={{0,16},{8,24},{16,0},{24,8},{1,17},{9,25},{17,1},{25,9},{2,18},{10... | collective-permute-start | bytes 393224 | tf_op jit(solution)/shard_map/ppermute | solution.py:54
  45.9 4.4 %cond_planes.1 = f32[256,1024]{1,0:T(8,128)} custom-call(f32[256,512]{1,0:T(8,128)S(1)} %copy-done.12, bf16[8,16,256]{2,1,0:T(8,128)(2,1)S(1)} %slice.14.home_ref, bf16[8,16,256]{2,1,0:T(8,128)(2,1)S(1)} %get-tuple-element.14.away_ref), custom_call_target="tpu_custom_call" | custom-call | flops 1610612736 | bytes 2097152 | tf_op jit(solution)/shard_map/cond_planes/pallas_call | solution.py:215
  51.6 11.4 %collective-permute-done.11 = bf16[4,2,8,16,256]{4,3,2,1,0:T(8,128)(2,1)S(1)} collective-permute-done((bf16[4,2,8,16,256]{4,3,2,1,0:T(8,128)(2,1)}, bf16[4,2,8,16,256]{4,3,2,1,0:T(8,128)(2,1)S(1)}, u32[]{:S(2)}, u32[]{:S(2)}) %collective-permute-start.11) | collective-permute-done | bytes 524320 | tf_op jit(solution)/shard_map/ppermute | solution.py:54
  62.9 10.5 %all-to-all-start = ((f32[32,8,1024]{2,1,0:T(8,128)}), f32[32,8,1024]{2,1,0:T(8,128)S(1)}, u32[]{:S(2)}, u32[]{:S(2)}) async-start(f32[32,8,1024]{2,1,0:T(8,128)} %bitcast.35), calls=%async_computation | async-start | bytes 2097152 | tf_op jit(solution)/shard_map/all_to_all | solution.py:418
  75.7 2.7 %collective-permute-start.15 = (bf16[4,2,8,16,256]{4,3,2,1,0:T(8,128)(2,1)S(1)}, bf16[4,2,8,16,256]{4,3,2,1,0:T(8,128)(2,1)S(1)}, u32[]{:S(2)}, u32[]{:S(2)}) collective-permute-start(bf16[4,2,8,16,256]{4,3,2,1,0:T(8,128)(2,1)S(1)} %pad_maximum_fusion.4), channel_id=1, source_target_pairs={{0,16},{8,24},{16,0},{24,8},{1,17},{9,25},{17,1},{25,9},{2,18},{10... | collective-permute-start | bytes 1572872 | tf_op jit(solution)/shard_map/ppermute | solution.py:54
  85.4 3.5 %copy-done.1 = f32[34,256,256]{2,1,0:T(8,128)S(1)} copy-done((f32[34,256,256]{2,1,0:T(8,128)S(1)}, f32[34,256,256]{2,1,0:T(8,128)}, u32[]{:S(2)}) %copy-start.1) | copy-done | bytes 8912920
  88.9 6.8 %screened_plane.1.refs_8_.refs_9_ = bf16[17,512,256]{2,1,0:T(8,128)(2,1)S(1)} custom-call(bf16[2,256,256]{2,1,0:T(8,128)(2,1)S(1)} %copy-done.6, bf16[2,256,256]{2,1,0:T(8,128)(2,1)S(1)} %copy-done.7, f32[34,256,256]{2,1,0:T(8,128)S(1)} %copy-done.1, f32[34,256,256]{2,1,0:T(8,128)S(1)} %copy-done.1), custom_call_target="tpu_custom_call" | custom-call | flops 3422552064 | bytes 14680064 | tf_op jit(solution)/shard_map/screened_plane/pallas_call | solution.py:142
  97.7 2.4 %collective-permute-done.14 = bf16[4,2,8,16,256]{4,3,2,1,0:T(8,128)(2,1)S(1)} collective-permute-done((bf16[4,2,8,16,256]{4,3,2,1,0:T(8,128)(2,1)S(1)}, bf16[4,2,8,16,256]{4,3,2,1,0:T(8,128)(2,1)S(1)}, u32[]{:S(2)}, u32[]{:S(2)}) %collective-permute-start.14) | collective-permute-done | bytes 524320 | tf_op jit(solution)/shard_map/ppermute | solution.py:54
  100.1 7.1 %collective-permute-done.15 = bf16[4,2,8,16,256]{4,3,2,1,0:T(8,128)(2,1)S(1)} collective-permute-done((bf16[4,2,8,16,256]{4,3,2,1,0:T(8,128)(2,1)S(1)}, bf16[4,2,8,16,256]{4,3,2,1,0:T(8,128)(2,1)S(1)}, u32[]{:S(2)}, u32[]{:S(2)}) %collective-permute-start.15) | collective-permute-done | bytes 524320 | tf_op jit(solution)/shard_map/ppermute | solution.py:54
  108.7 2.7 %pad_maximum_fusion = bf16[4,4,2,8,16,256]{5,4,3,2,1,0:T(8,128)(2,1)} fusion(bf16[1,4,2,8,16,256]{5,4,3,2,1,0:T(8,128)(2,1)S(1)} %bitcast.89, bf16[1,4,2,8,16,256]{5,4,3,2,1,0:T(8,128)(2,1)S(1)} %bitcast.87, bf16[1,4,2,8,16,256]{5,4,3,2,1,0:T(8,128)(2,1)S(1)} %bitcast.85, bf16[1,4,2,8,16,256]{5,4,3,2,1,0:T(8,128)(2,1)} %bitcast.25), kind=kLoop, calls=%fused_computation | loop fusion | flops 3145728 | bytes 4194304 | tf_op jit(solution)/shard_map/stack | solution.py:420
  112.3 3.7 %cond_spectrum.1.refs_10_ = bf16[1024,256]{1,0:T(8,128)(2,1)S(1)} custom-call(f32[256,256]{1,0:T(8,128)S(1)} %copy-done.8, f32[256,256]{1,0:T(8,128)S(1)} %get-tuple-element.26.sin_ref, f32[256,1024]{1,0:T(8,128)S(1)} %bitcast.74), custom_call_target="tpu_custom_call" | custom-call | flops 1610612736 | bytes 2097152 | tf_op jit(solution)/shard_map/cond_spectrum/pallas_call | solution.py:344
  118.3 12.4 %valence_response.1 = f32[32,16,128]{2,1,0:T(8,128)S(1)} custom-call(s32[1]{0:T(128)} %bitcast.place_ref, bf16[32,8,16,256]{3,2,1,0:T(8,128)(2,1)S(1)} %bitcast.68, bf16[32,8,16,256]{3,2,1,0:T(8,128)(2,1)S(1)} %bitcast.64, bf16[32,8,16,256]{3,2,1,0:T(8,128)(2,1)S(1)} %bitcast.69, bf16[32,8,16,256]{3,2,1,0:T(8,128)(2,1)S(1)} %bitcast.65, ...), custom_call_target="tpu_custom_call" | custom-call | flops 4563402752 | bytes 9437184 | tf_op jit(solution)/shard_map/valence_response/pallas_call | solution.py:305
  130.7 12.4 %all_to_all.26 = f32[32,16,128]{2,1,0:T(8,128)S(1)} all-to-all(f32[32,16,128]{2,1,0:T(8,128)S(1)} %valence_response.1), channel_id=1, replica_groups=mesh['zl'=4,'co'=2,'x'=4,'y'=4,'zh'=2] {'x','y'}, dimensions={0} | all-to-all | bytes 524288 | tf_op jit(solution)/shard_map/all_to_all | solution.py:426
  143.1 5.3 %collective-permute-start.17 = (f32[2,16,128]{2,1,0:T(8,128)S(1)}, f32[2,16,128]{2,1,0:T(8,128)S(1)}, u32[]{:S(2)}, u32[]{:S(2)}) collective-permute-start(f32[2,16,128]{2,1,0:T(8,128)S(1)} %reduce_sum.9), channel_id=1, source_target_pairs={{0,1},{1,0},{2,3},{3,2},{4,5},{5,4},{6,7},{7,6},{8,9},{9,8},{10,11... | collective-permute-start | bytes 49160 | tf_op jit(solution)/shard_map/ppermute | solution.py:54
  148.3 2.5 %collective-permute-done.17 = f32[2,16,128]{2,1,0:T(8,128)S(1)} collective-permute-done((f32[2,16,128]{2,1,0:T(8,128)S(1)}, f32[2,16,128]{2,1,0:T(8,128)S(1)}, u32[]{:S(2)}, u32[]{:S(2)}) %collective-permute-start.17) | collective-permute-done | bytes 16416 | tf_op jit(solution)/shard_map/ppermute | solution.py:54
  151.5 8.7 %all-to-all-start.2 = ((f32[8,2,16,128]{3,2,1,0:T(8,128)}), f32[8,2,16,128]{3,2,1,0:T(8,128)S(1)}, u32[]{:S(2)}, u32[]{:S(2)}) async-start(f32[8,2,16,128]{3,2,1,0:T(8,128)} %broadcast_in_dim.16), calls=%async_computation.2 | async-start | bytes 262144 | tf_op jit(solution)/shard_map/all_to_all | solution.py:64
  160.2 6.7 %all-to-all-done.2 = f32[8,2,16,128]{3,2,1,0:T(8,128)S(1)} async-done(((f32[8,2,16,128]{3,2,1,0:T(8,128)}), f32[8,2,16,128]{3,2,1,0:T(8,128)S(1)}, u32[]{:S(2)}, u32[]{:S(2)}) %all-to-all-start.2) | async-done | bytes 131104 | tf_op jit(solution)/shard_map/all_to_all | solution.py:64
  167.6 14.8 %all_to_all.27.full_ref = f32[16,2,32,128]{3,2,1,0:T(8,128)S(1)} all-to-all(f32[16,2,32,128]{3,2,1,0:T(8,128)S(1)} %broadcast_in_dim.21), channel_id=1, replica_groups=mesh['zl'=4,'co'=2,'x'=4,'y'=4,'zh'=2] {'x','y'}, dimensions={0} | all-to-all | bytes 1048576 | tf_op jit(solution)/shard_map/all_to_all | solution.py:64
  (84 shorter events, 34.6 us)
Async XLA Ops:
  1.5 19.2 %collective-permute-start.2 = (bf16[8,32,256]{2,1,0:T(8,128)(2,1)S(1)}, bf16[8,32,256]{2,1,0:T(8,128)(2,1)S(1)}, u32[]{:S(2)}, u32[]{:S(2)}) collective-permute-start(bf16[8,32,256]{2,1,0:T(8,128)(2,1)S(1)} %bitcast.79), channel_id=1, source_target_pairs={{0,192},{64,0},{128,64},{192,128},{1,193},{65,1},{129,65},{193,129... | collective-permute-start | bytes 393224 | tf_op jit(solution)/shard_map/ppermute | solution.py:54
  6.2 14.5 %collective-permute-start = (bf16[8,32,256]{2,1,0:T(8,128)(2,1)S(1)}, bf16[8,32,256]{2,1,0:T(8,128)(2,1)S(1)}, u32[]{:S(2)}, u32[]{:S(2)}) collective-permute-start(bf16[8,32,256]{2,1,0:T(8,128)(2,1)S(1)} %bitcast.80), channel_id=1, source_target_pairs={{0,64},{64,128},{128,192},{192,0},{1,65},{65,129},{129,193},{193,1... | collective-permute-start | bytes 393224 | tf_op jit(solution)/shard_map/ppermute | solution.py:54
  6.3 14.5 %collective-permute-start.1 = (bf16[8,32,256]{2,1,0:T(8,128)(2,1)S(1)}, bf16[8,32,256]{2,1,0:T(8,128)(2,1)S(1)}, u32[]{:S(2)}, u32[]{:S(2)}) collective-permute-start(bf16[8,32,256]{2,1,0:T(8,128)(2,1)S(1)} %bitcast.81), channel_id=1, source_target_pairs={{0,128},{64,192},{128,0},{192,64},{1,129},{65,193},{129,1},{193,65... | collective-permute-start | bytes 393224 | tf_op jit(solution)/shard_map/ppermute | solution.py:54
  20.8 2.0 %collective-permute-start.3 = (bf16[32,32,256]{2,1,0:T(8,128)(2,1)S(1)}, bf16[32,32,256]{2,1,0:T(8,128)(2,1)S(1)}, u32[]{:S(2)}, u32[]{:S(2)}) collective-permute-start(bf16[32,32,256]{2,1,0:T(8,128)(2,1)S(1)} %bitcast.72), channel_id=1, source_target_pairs={{0,32},{32,0},{1,33},{33,1},{2,34},{34,2},{3,35},{35,3},{4,36},{36... | collective-permute-start | bytes 1572872 | tf_op jit(solution)/shard_map/ppermute | solution.py:54
  25.6 9.6 %collective-permute-start.4 = (bf16[2,8,16,256]{3,2,1,0:T(8,128)(2,1)S(1)}, bf16[2,8,16,256]{3,2,1,0:T(8,128)(2,1)S(1)}, u32[]{:S(2)}, u32[]{:S(2)}) collective-permute-start(bf16[2,8,16,256]{3,2,1,0:T(8,128)(2,1)S(1)} %get-tuple-element.13), channel_id=1, source_target_pairs={{0,1},{1,0},{2,3},{3,2},{4,5},{5,4},{6,7},{7,6},{8,9},{9,8},{10,11... | collective-permute-start | bytes 393224 | tf_op jit(solution)/shard_map/ppermute | solution.py:54
  35.2 9.2 %collective-permute-start.8 = (bf16[2,8,16,256]{3,2,1,0:T(8,128)(2,1)S(1)}, bf16[2,8,16,256]{3,2,1,0:T(8,128)(2,1)S(1)}, u32[]{:S(2)}, u32[]{:S(2)}) collective-permute-start(bf16[2,8,16,256]{3,2,1,0:T(8,128)(2,1)S(1)} %get-tuple-element.24), channel_id=1, source_target_pairs={{0,2},{2,4},{4,6},{6,0},{1,3},{3,5},{5,7},{7,1},{8,10},{10,12},{12... | collective-permute-start | bytes 393224 | tf_op jit(solution)/shard_map/ppermute | solution.py:54
  36.9 13.4 %collective-permute-start.9 = (bf16[2,8,16,256]{3,2,1,0:T(8,128)(2,1)S(1)}, bf16[2,8,16,256]{3,2,1,0:T(8,128)(2,1)S(1)}, u32[]{:S(2)}, u32[]{:S(2)}) collective-permute-start(bf16[2,8,16,256]{3,2,1,0:T(8,128)(2,1)S(1)} %get-tuple-element.24), channel_id=1, source_target_pairs={{0,4},{2,6},{4,0},{6,2},{1,5},{3,7},{5,1},{7,3},{8,12},{10,14},{12... | collective-permute-start | bytes 393224 | tf_op jit(solution)/shard_map/ppermute | solution.py:54
  37.8 12.5 %collective-permute-start.10 = (bf16[2,8,16,256]{3,2,1,0:T(8,128)(2,1)S(1)}, bf16[2,8,16,256]{3,2,1,0:T(8,128)(2,1)S(1)}, u32[]{:S(2)}, u32[]{:S(2)}) collective-permute-start(bf16[2,8,16,256]{3,2,1,0:T(8,128)(2,1)S(1)} %get-tuple-element.24), channel_id=1, source_target_pairs={{0,6},{2,0},{4,2},{6,4},{1,7},{3,1},{5,3},{7,5},{8,14},{10,8},{12,... | collective-permute-start | bytes 393224 | tf_op jit(solution)/shard_map/ppermute | solution.py:54
  40.2 10.2 %collective-permute-start.5 = (bf16[2,8,16,256]{3,2,1,0:T(8,128)(2,1)S(1)}, bf16[2,8,16,256]{3,2,1,0:T(8,128)(2,1)S(1)}, u32[]{:S(2)}, u32[]{:S(2)}) collective-permute-start(bf16[2,8,16,256]{3,2,1,0:T(8,128)(2,1)S(1)} %get-tuple-element.23), channel_id=1, source_target_pairs={{0,8},{8,16},{16,24},{24,0},{1,9},{9,17},{17,25},{25,1},{2,10},{10... | collective-permute-start | bytes 393224 | tf_op jit(solution)/shard_map/ppermute | solution.py:54
  41.7 8.7 %collective-permute-start.6 = (bf16[2,8,16,256]{3,2,1,0:T(8,128)(2,1)S(1)}, bf16[2,8,16,256]{3,2,1,0:T(8,128)(2,1)S(1)}, u32[]{:S(2)}, u32[]{:S(2)}) collective-permute-start(bf16[2,8,16,256]{3,2,1,0:T(8,128)(2,1)S(1)} %get-tuple-element.23), channel_id=1, source_target_pairs={{0,16},{8,24},{16,0},{24,8},{1,17},{9,25},{17,1},{25,9},{2,18},{10... | collective-permute-start | bytes 393224 | tf_op jit(solution)/shard_map/ppermute | solution.py:54
  44.5 6.0 %collective-permute-start.7 = (bf16[2,8,16,256]{3,2,1,0:T(8,128)(2,1)S(1)}, bf16[2,8,16,256]{3,2,1,0:T(8,128)(2,1)S(1)}, u32[]{:S(2)}, u32[]{:S(2)}) collective-permute-start(bf16[2,8,16,256]{3,2,1,0:T(8,128)(2,1)S(1)} %get-tuple-element.23), channel_id=1, source_target_pairs={{0,24},{8,0},{16,8},{24,16},{1,25},{9,1},{17,9},{25,17},{2,26},{10... | collective-permute-start | bytes 393224 | tf_op jit(solution)/shard_map/ppermute | solution.py:54
  50.4 45.3 %copy-start.13 = (bf16[4,2,8,16,256]{4,3,2,1,0:T(8,128)(2,1)}, bf16[4,2,8,16,256]{4,3,2,1,0:T(8,128)(2,1)S(1)}, u32[]{:S(2)}) copy-start(bf16[4,2,8,16,256]{4,3,2,1,0:T(8,128)(2,1)S(1)} %pad_maximum_fusion.4) | copy-start | bytes 1572868
  50.4 35.0 %copy-start.6 = (bf16[2,256,256]{2,1,0:T(8,128)(2,1)S(1)}, bf16[2,256,256]{2,1,0:T(8,128)(2,1)}, u32[]{:S(2)}) copy-start(bf16[2,256,256]{2,1,0:T(8,128)(2,1)} %constant.189.clone.high_ref) | copy-start | bytes 786436
  50.4 34.9 %copy-start.7 = (bf16[2,256,256]{2,1,0:T(8,128)(2,1)S(1)}, bf16[2,256,256]{2,1,0:T(8,128)(2,1)}, u32[]{:S(2)}) copy-start(bf16[2,256,256]{2,1,0:T(8,128)(2,1)} %constant.190.clone.low_ref) | copy-start | bytes 786436
  51.3 11.6 %collective-permute-start.11 = (bf16[4,2,8,16,256]{4,3,2,1,0:T(8,128)(2,1)}, bf16[4,2,8,16,256]{4,3,2,1,0:T(8,128)(2,1)S(1)}, u32[]{:S(2)}, u32[]{:S(2)}) collective-permute-start(bf16[4,2,8,16,256]{4,3,2,1,0:T(8,128)(2,1)} %pad_maximum_fusion.3), channel_id=1, source_target_pairs={{0,2},{2,4},{4,6},{6,0},{1,3},{3,5},{5,7},{7,1},{8,10},{10,12},{12... | collective-permute-start | bytes 1572872 | tf_op jit(solution)/shard_map/ppermute | solution.py:54
  62.9 32.7 %copy-start.14 = (bf16[4,2,8,16,256]{4,3,2,1,0:T(8,128)(2,1)}, bf16[4,2,8,16,256]{4,3,2,1,0:T(8,128)(2,1)S(1)}, u32[]{:S(2)}) copy-start(bf16[4,2,8,16,256]{4,3,2,1,0:T(8,128)(2,1)S(1)} %collective-permute-done.11) | copy-start | bytes 1572868
  62.9 48.4 %all-to-all-start = ((f32[32,8,1024]{2,1,0:T(8,128)}), f32[32,8,1024]{2,1,0:T(8,128)S(1)}, u32[]{:S(2)}, u32[]{:S(2)}) async-start(f32[32,8,1024]{2,1,0:T(8,128)} %bitcast.35), calls=%async_computation | async-start | bytes 2097152 | tf_op jit(solution)/shard_map/all_to_all | solution.py:418
  74.3 25.9 %collective-permute-start.14 = (bf16[4,2,8,16,256]{4,3,2,1,0:T(8,128)(2,1)S(1)}, bf16[4,2,8,16,256]{4,3,2,1,0:T(8,128)(2,1)S(1)}, u32[]{:S(2)}, u32[]{:S(2)}) collective-permute-start(bf16[4,2,8,16,256]{4,3,2,1,0:T(8,128)(2,1)S(1)} %pad_maximum_fusion.4), channel_id=1, source_target_pairs={{0,8},{8,16},{16,24},{24,0},{1,9},{9,17},{17,25},{25,1},{2,10},{10... | collective-permute-start | bytes 1572872 | tf_op jit(solution)/shard_map/ppermute | solution.py:54
  75.7 31.5 %collective-permute-start.15 = (bf16[4,2,8,16,256]{4,3,2,1,0:T(8,128)(2,1)S(1)}, bf16[4,2,8,16,256]{4,3,2,1,0:T(8,128)(2,1)S(1)}, u32[]{:S(2)}, u32[]{:S(2)}) collective-permute-start(bf16[4,2,8,16,256]{4,3,2,1,0:T(8,128)(2,1)S(1)} %pad_maximum_fusion.4), channel_id=1, source_target_pairs={{0,16},{8,24},{16,0},{24,8},{1,17},{9,25},{17,1},{25,9},{2,18},{10... | collective-permute-start | bytes 1572872 | tf_op jit(solution)/shard_map/ppermute | solution.py:54
  78.5 28.8 %collective-permute-start.16 = (bf16[4,2,8,16,256]{4,3,2,1,0:T(8,128)(2,1)S(1)}, bf16[4,2,8,16,256]{4,3,2,1,0:T(8,128)(2,1)S(1)}, u32[]{:S(2)}, u32[]{:S(2)}) collective-permute-start(bf16[4,2,8,16,256]{4,3,2,1,0:T(8,128)(2,1)S(1)} %pad_maximum_fusion.4), channel_id=1, source_target_pairs={{0,24},{8,0},{16,8},{24,16},{1,25},{9,1},{17,9},{25,17},{2,26},{10... | collective-permute-start | bytes 1572872 | tf_op jit(solution)/shard_map/ppermute | solution.py:54
  79.9 28.7 %collective-permute-start.12 = (bf16[4,2,8,16,256]{4,3,2,1,0:T(8,128)(2,1)}, bf16[4,2,8,16,256]{4,3,2,1,0:T(8,128)(2,1)S(1)}, u32[]{:S(2)}, u32[]{:S(2)}) collective-permute-start(bf16[4,2,8,16,256]{4,3,2,1,0:T(8,128)(2,1)} %pad_maximum_fusion.3), channel_id=1, source_target_pairs={{0,4},{2,6},{4,0},{6,2},{1,5},{3,7},{5,1},{7,3},{8,12},{10,14},{12... | collective-permute-start | bytes 1572872 | tf_op jit(solution)/shard_map/ppermute | solution.py:54
  82.0 26.7 %collective-permute-start.13 = (bf16[4,2,8,16,256]{4,3,2,1,0:T(8,128)(2,1)}, bf16[4,2,8,16,256]{4,3,2,1,0:T(8,128)(2,1)S(1)}, u32[]{:S(2)}, u32[]{:S(2)}) collective-permute-start(bf16[4,2,8,16,256]{4,3,2,1,0:T(8,128)(2,1)} %pad_maximum_fusion.3), channel_id=1, source_target_pairs={{0,6},{2,0},{4,2},{6,4},{1,7},{3,1},{5,3},{7,5},{8,14},{10,8},{12,... | collective-permute-start | bytes 1572872 | tf_op jit(solution)/shard_map/ppermute | solution.py:54
  143.1 7.7 %collective-permute-start.17 = (f32[2,16,128]{2,1,0:T(8,128)S(1)}, f32[2,16,128]{2,1,0:T(8,128)S(1)}, u32[]{:S(2)}, u32[]{:S(2)}) collective-permute-start(f32[2,16,128]{2,1,0:T(8,128)S(1)} %reduce_sum.9), channel_id=1, source_target_pairs={{0,1},{1,0},{2,3},{3,2},{4,5},{5,4},{6,7},{7,6},{8,9},{9,8},{10,11... | collective-permute-start | bytes 49160 | tf_op jit(solution)/shard_map/ppermute | solution.py:54
  151.5 15.5 %all-to-all-start.2 = ((f32[8,2,16,128]{3,2,1,0:T(8,128)}), f32[8,2,16,128]{3,2,1,0:T(8,128)S(1)}, u32[]{:S(2)}, u32[]{:S(2)}) async-start(f32[8,2,16,128]{3,2,1,0:T(8,128)} %broadcast_in_dim.16), calls=%async_computation.2 | async-start | bytes 262144 | tf_op jit(solution)/shard_map/all_to_all | solution.py:64
  (12 other events, 58.5 us)

commit v4 on v2

--- a/solution.py
+++ b/solution.py
@@ -141,7 +141,7 @@
         out_specs=pl.BlockSpec((1, 512, 256), lambda i: (jnp.maximum(i - LINE_STEPS, 0), 0, 0)),
         out_shape=jax.ShapeDtypeStruct((HALF, 512, 256), BF),
         scratch_shapes=[pltpu.VMEM((2 * HALF, PLANE, 256), F32)],
-        compiler_params=pltpu.CompilerParams(vmem_limit_bytes=40 * MIB),
+        compiler_params=pltpu.CompilerParams(vmem_limit_bytes=54 * MIB),
         cost_estimate=pl.CostEstimate(
             flops=12 * 256 * 256 * 256 * HALF, bytes_accessed=9 * MIB, transcendentals=0
         ),
@@ -152,6 +152,7 @@
 def choose_kernel(partner_ref, place_ref, flip_ref, near_ref, far_ref, val_ref, cond_ref):
     level, core = place_ref[0], place_ref[1]
     for m in range(8):
+        val_ref[0, m] = dot(near_ref[m, :16], flip_ref[...]).astype(BF)
         wanted = partner_ref[(level * 2 + core) * 8 + m]
         back = (level - wanted // 16) & 3
         at = back * 8 + (wanted & 7)
@@ -159,7 +160,7 @@
 
         def take(ref, m=m, at=at):
             row = ref[at]
-            val_ref[m] = dot(row[:16], flip_ref[...]).astype(BF)
+            val_ref[1, m] = dot(row[:16], flip_ref[...]).astype(BF)
             cond_ref[m] = row[16:]
 
         pl.when(near)(functools.partial(take, near_ref))
@@ -174,7 +175,7 @@
         in_specs=[pl.BlockSpec(memory_space=pltpu.SMEM)] * 2
         + [pl.BlockSpec(memory_space=pltpu.VMEM)] * 3,
         out_specs=[pl.BlockSpec(memory_space=pltpu.VMEM)] * 2,
-        out_shape=[shape, shape],
+        out_shape=[jax.ShapeDtypeStruct((2, 8, 16, 256), BF), shape],
         compiler_params=pltpu.CompilerParams(vmem_limit_bytes=16 * MIB),
         name="partner_choice",
     )(partner, place, flip, near, far)
@@ -278,7 +279,7 @@
 
 
 def response(place, home, away, screened, cond):
-    def block(second, back):
+    def block(which, second, back):
         def index(step, place_ref):
             z = jnp.minimum(2 * step + second, HALF - 1)
             z = (NZ - z) & (NZ - 1) if back else z
@@ -286,11 +287,12 @@
             level = (place ^ z) & 1
             x = ((place >> 3) - (z >> 3)) & 3
             y = ((place >> 1) - (z >> 1)) & 3
+            x, y = (x, y) if which == 0 else (y, x)
             return ((y * 4 + x) * 2 + level, 0, 0, 0)
 
         return pl.BlockSpec((1, 8, 16, 256), index)
 
-    waves = [block(s, b) for s in range(2) for b in (False, True) for _ in range(2)]
+    waves = [block(w, s, b) for s in range(2) for b in (False, True) for w in range(2)]
     return pl.pallas_call(
         response_kernel,
         grid_spec=pltpu.PrefetchScalarGridSpec(
@@ -310,7 +312,7 @@
             ],
         ),
         out_shape=jax.ShapeDtypeStruct((32, 16, 128), F32),
-        compiler_params=pltpu.CompilerParams(vmem_limit_bytes=20 * MIB),
+        compiler_params=pltpu.CompilerParams(vmem_limit_bytes=40 * MIB),
         cost_estimate=pl.CostEstimate(
             flops=2 * 1024 * 512 * 256 * HALF, bytes_accessed=9 * MIB, transcendentals=0
         ),
@@ -335,7 +337,7 @@
         out_shape=jax.ShapeDtypeStruct((1024, 256), BF),
         in_specs=[pl.BlockSpec(memory_space=pltpu.VMEM)] * 3,
         out_specs=pl.BlockSpec(memory_space=pltpu.VMEM),
-        compiler_params=pltpu.CompilerParams(vmem_limit_bytes=24 * MIB),
+        compiler_params=pltpu.CompilerParams(vmem_limit_bytes=16 * MIB),
         cost_estimate=pl.CostEstimate(
             flops=24 * 256 * 256 * 1024, bytes_accessed=2 * MIB, transcendentals=0
         ),
@@ -392,27 +394,30 @@
     negative = (NX - index // NY) % NX * NY + (NY - index % NY) % NY
     negative = jnp.where(place > NZ // 2, negative, index)
     flip = (index[:, None] == negative[None, :]).astype(BF)
-    home_val = dot(waves[:, :16].reshape(128, 256), flip).astype(BF).reshape(8, 16, 256)
-    home_val, near = lax.optimization_barrier((home_val, near))
+    wide = screened_transform(screened, gmap)
+    near, wide = lax.optimization_barrier((near, wide))
     far = turned(near, "co", 1)
 
-    away_val, away_cond = choose(partner, near, far, flip)
-    home = spread(spread(home_val, "zh"), "x")
-    away = spread(spread(away_val, "zh"), "x")
+    vals, away_cond = choose(partner, near, far, flip)
     planes = cond_planes(waves[:, 16:], away_cond)
-    away, planes, screened = lax.optimization_barrier((away, planes, screened))
-    home = spread(home, "y").reshape(32, 8, 16, 256)
+    vals = spread(vals, "zh")
+    vals, planes = lax.optimization_barrier((vals, planes))
     columns = lax.all_to_all(planes, GA, split_axis=0, concat_axis=0, tiled=True)
-    away = spread(away, "y").reshape(32, 8, 16, 256)
-    wide = screened_transform(screened, gmap)
+    home, away = spread(vals[:, 0], "x"), spread(vals[:, 1], "y")
+    home, away = lax.optimization_barrier((home, away))
+    homes = [home] + [turned(home, "y", d) for d in range(1, 4)]
+    aways = [away] + [turned(away, "x", d) for d in range(1, 4)]
+    home = jnp.stack(homes).reshape(32, 8, 16, 256)
+    away = jnp.stack(aways).reshape(32, 8, 16, 256)
     cond = cond_spectrum(*line_tables(gmap, place), columns)
 
     blocks = response(place, home, away, wide, cond)
 
     parts = lax.all_to_all(blocks, ("x", "y"), split_axis=0, concat_axis=0, tiled=True)
     mine = jnp.sum(parts.reshape(16, 2, 16, 128), axis=0)
-    mine = mine + turned(mine, "zh", 1)
-    everyone = copies_to_all(mine, KA)
+    everyone = copies_to_all(mine, ("zl", "co", "zh")).reshape(8, 2, 2, 16, 128)
+    everyone = everyone[:, 0] + everyone[:, 1]
+    mine = lax.dynamic_index_in_dim(everyone, ka_place, keepdims=False)
     everyone = everyone.reshape(8, 2, 8, 256).transpose(0, 2, 1, 3).reshape(64, 512)
     select = (partner[None, :] == owned[:, None]).astype(F32)
     mirror = jnp.dot(select, everyone, precision=EXACT)

time: 220 us -> 179 us (0.81)
  starting transfers between devices: 84.5 us -> 46.9 us
  Pallas kernels: 36.7 us -> 42.5 us
  waiting for transfers between devices: 49.9 us -> 44.7 us
  local copies, waits for them, and re-layouts: 8.65 us -> 5.12 us
    ppermute x19 -> x17, starting transfers between devices: 54.9 us -> 28.5 us  [turned(): lax.ppermute(value, axis, [(i, (i + step) % size) for i in range(size)])]
    all_to_all x1, starting transfers between devices: 18.4 us -> 6.1 us  [copies_to_all(): return lax.all_to_all(copies, axes, split_axis=0, concat_axis=0, tiled=True)]
    ppermute x19 -> x17, waiting for transfers between devices: 43.2 us -> 32.4 us  [turned(): lax.ppermute(value, axis, [(i, (i + step) % size) for i in range(size)])]
    all_to_all x1, waiting for transfers between devices: 6.74 us -> 12.2 us  [copies_to_all(): return lax.all_to_all(copies, axes, split_axis=0, concat_axis=0, tiled=True)]
    another operation x7 -> x4, other arithmetic: 6.48 us -> 1.06 us  [spread(): jnp.stack([value] + [turned(value, axis, d) for d in range(1, SIZE[axis])])]
    pallas_call x1, Pallas kernels: 13.4 us -> 18.3 us  [screened_transform(): pl.pallas_call(screened_kernel, grid=(LINE_STEPS + HALF,), in_specs=[pl.B...]
    another operation x0 -> x2, other arithmetic: none -> 4.45 us  [the longest x1 2.67 us: on_device(): away = jnp.stack(aways).reshape(32, 8, 16, 256)]
    unnamed x26 -> x14, local copies, waits for them, and re-layouts: 6.81 us -> 3.22 us
  transfers between devices with their start and end apart: 21 -> 19, of which waited for: 10 -> 10; matrix products, arithmetic and copies ran while one was open for 4% -> 5% of each run, Pallas kernels for 8% -> 13%
where the time goes in v4:
time: 179 us; the launch traced here: 178 us
  starting transfers between devices  46.9 us (26%)
  waiting for transfers between devices  44.7 us (25%)
  Pallas kernels  42.5 us (24%)
  blocking collectives  29.4 us (16%)
  other arithmetic  8.43 us (5%)
  local copies, waits for them, and re-layouts  5.12 us (3%)
    ppermute x17, waiting for transfers between devices, turned(): lax.ppermute(value, axis, [(i, (i + step) % size) for i in range(size)])  32.4 us
    ppermute x17, starting transfers between devices, turned(): lax.ppermute(value, axis, [(i, (i + step) % size) for i in range(size)])  28.5 us
    pallas_call x1, Pallas kernels, screened_transform(): pl.pallas_call(screened_kernel, grid=(LINE_STEPS + HALF,), in_specs=[pl.B...  18.3 us
    all_to_all x1, blocking collectives, copies_to_all(): return lax.all_to_all(copies, axes, split_axis=0, concat_axis=0, tiled=True)  14.7 us
    all_to_all x1, blocking collectives, on_device(): lax.all_to_all(blocks, ('x', 'y'), split_axis=0, concat_axis=0, tiled=True)  14.6 us
    pallas_call x1, Pallas kernels, response(): pl.pallas_call(response_kernel, grid_spec=pltpu.PrefetchScalarGridSpec(nu...  12.4 us
    all_to_all x1, starting transfers between devices, on_device(): lax.all_to_all(planes, GA, split_axis=0, concat_axis=0, tiled=True)  12.3 us
    all_to_all x1, waiting for transfers between devices, copies_to_all(): return lax.all_to_all(copies, axes, split_axis=0, concat_axis=0, tiled=True)  12.2 us
  transfers between devices with their start and end apart: 19, of which 10 were waited for; matrix products, arithmetic and copies ran while one was open for 5% of the time, Pallas kernels for 13%

profile of v4, /device:TPU:8, one launch (start us, length us, event | category | flops | bytes accessed | tf_op | source)
XLA Modules:
  0.0 178.3 jit_solution(3638271233067841625)
XLA Ops:
  1.5 4.7 %collective-permute-start.2 = (bf16[8,32,256]{2,1,0:T(8,128)(2,1)S(1)}, bf16[8,32,256]{2,1,0:T(8,128)(2,1)S(1)}, u32[]{:S(2)}, u32[]{:S(2)}) collective-permute-start(bf16[8,32,256]{2,1,0:T(8,128)(2,1)S(1)} %bitcast.80), channel_id=1, source_target_pairs={{0,192},{64,0},{128,64},{192,128},{1,193},{65,1},{129,65},{193,129... | collective-permute-start | bytes 393224 | tf_op jit(solution)/shard_map/ppermute | solution.py:55
  6.9 18.3 %screened_transform.1.refs_8_.refs_9_ = bf16[17,512,256]{2,1,0:T(8,128)(2,1)} custom-call(s32[32,1,256]{2,1,0:T(1,128)} %bitcast.103, bf16[96,32]{1,0:T(8,128)(2,1)} %constant.192.clone.line_ref, bf16[2,256,256]{2,1,0:T(8,128)(2,1)} %constant.193.clone.high_ref, bf16[2,256,256]{2,1,0:T(8,128)(2,1)} %constant.194.clone.low_ref, bf16[256,8192]{1,0:T(8,128)(2,1)} %w_ref.1), custom_call_target="tpu_custom_call" | custom-call | flops 3422552064 | bytes 9437184 | tf_op jit(solution)/shard_map/screened_transform/pallas_call | solution.py:131
  27.3 2.7 %partner_choice.1 = (bf16[2,8,16,256]{3,2,1,0:T(8,128)(2,1)S(1)}, bf16[8,16,256]{2,1,0:T(8,128)(2,1)S(1)}) custom-call(s32[64]{0:T(128)S(1)} %copy-done.3, s32[2]{0:T(128)S(1)} %pad_add_fusion.place_ref, bf16[256,256]{1,0:T(8,128)(2,1)S(1)} %fusion.4.flip_ref, bf16[32,32,256]{2,1,0:T(8,128)(2,1)S(1)} %bitcast.74, ...), custom_call_target="tpu_custom_call" | custom-call | tf_op jit(solution)/shard_map/partner_choice/pallas_call | solution.py:173
  30.1 5.4 %collective-permute-start.4 = (bf16[2,8,16,256]{3,2,1,0:T(8,128)(2,1)S(1)}, bf16[2,8,16,256]{3,2,1,0:T(8,128)(2,1)S(1)}, u32[]{:S(2)}, u32[]{:S(2)}) collective-permute-start(bf16[2,8,16,256]{3,2,1,0:T(8,128)(2,1)S(1)} %get-tuple-element.11), channel_id=1, source_target_pairs={{0,1},{1,0},{2,3},{3,2},{4,5},{5,4},{6,7},{7,6},{8,9},{9,8},{10,11... | collective-permute-start | bytes 393224 | tf_op jit(solution)/shard_map/ppermute | solution.py:55
  35.5 4.4 %cond_planes.1 = f32[256,1024]{1,0:T(8,128)} custom-call(f32[256,512]{1,0:T(8,128)S(1)} %copy-done.4, bf16[8,16,256]{2,1,0:T(8,128)(2,1)S(1)} %slice.20.home_ref, bf16[8,16,256]{2,1,0:T(8,128)(2,1)S(1)} %get-tuple-element.12.away_ref), custom_call_target="tpu_custom_call" | custom-call | flops 1610612736 | bytes 2097152 | tf_op jit(solution)/shard_map/cond_planes/pallas_call | solution.py:206
  39.9 12.3 %all-to-all-start = ((f32[32,8,1024]{2,1,0:T(8,128)}), f32[32,8,1024]{2,1,0:T(8,128)S(1)}, u32[]{:S(2)}, u32[]{:S(2)}) async-start(f32[32,8,1024]{2,1,0:T(8,128)} %bitcast.35), calls=%async_computation | async-start | bytes 2097152 | tf_op jit(solution)/shard_map/all_to_all | solution.py:405
  52.3 2.8 %collective-permute-start.7 = (bf16[2,8,16,256]{3,2,1,0:T(8,128)(2,1)S(1)}, bf16[2,8,16,256]{3,2,1,0:T(8,128)(2,1)S(1)}, u32[]{:S(2)}, u32[]{:S(2)}) collective-permute-start(bf16[2,8,16,256]{3,2,1,0:T(8,128)(2,1)S(1)} %get-tuple-element.19), channel_id=1, source_target_pairs={{0,24},{8,0},{16,8},{24,16},{1,25},{9,1},{17,9},{25,17},{2,26},{10... | collective-permute-start | bytes 393224 | tf_op jit(solution)/shard_map/ppermute | solution.py:55
  57.3 2.4 %collective-permute-start.9 = (bf16[2,8,16,256]{3,2,1,0:T(8,128)(2,1)S(1)}, bf16[2,8,16,256]{3,2,1,0:T(8,128)(2,1)S(1)}, u32[]{:S(2)}, u32[]{:S(2)}) collective-permute-start(bf16[2,8,16,256]{3,2,1,0:T(8,128)(2,1)S(1)} %get-tuple-element.20), channel_id=1, source_target_pairs={{0,4},{2,6},{4,0},{6,2},{1,5},{3,7},{5,1},{7,3},{8,12},{10,14},{12... | collective-permute-start | bytes 393224 | tf_op jit(solution)/shard_map/ppermute | solution.py:55
  59.7 8.6 %collective-permute-done.7 = bf16[2,8,16,256]{3,2,1,0:T(8,128)(2,1)S(1)} collective-permute-done((bf16[2,8,16,256]{3,2,1,0:T(8,128)(2,1)S(1)}, bf16[2,8,16,256]{3,2,1,0:T(8,128)(2,1)S(1)}, u32[]{:S(2)}, u32[]{:S(2)}) %collective-permute-start.7) | collective-permute-done | bytes 131104 | tf_op jit(solution)/shard_map/ppermute | solution.py:55
  74.2 2.2 %collective-permute-start.13 = (bf16[4,2,8,16,256]{4,3,2,1,0:T(8,128)(2,1)S(1)}, bf16[4,2,8,16,256]{4,3,2,1,0:T(8,128)(2,1)S(1)}, u32[]{:S(2)}, u32[]{:S(2)}) collective-permute-start(bf16[4,2,8,16,256]{4,3,2,1,0:T(8,128)(2,1)S(1)} %pad_maximum_fusion.3), channel_id=1, source_target_pairs={{0,6},{2,0},{4,2},{6,4},{1,7},{3,1},{5,3},{7,5},{8,14},{10,8},{12,... | collective-permute-start | bytes 1572872 | tf_op jit(solution)/shard_map/ppermute | solution.py:55
  79.7 2.7 %collective-permute-start.15 = (bf16[4,2,8,16,256]{4,3,2,1,0:T(8,128)(2,1)}, bf16[4,2,8,16,256]{4,3,2,1,0:T(8,128)(2,1)S(1)}, u32[]{:S(2)}, u32[]{:S(2)}) collective-permute-start(bf16[4,2,8,16,256]{4,3,2,1,0:T(8,128)(2,1)} %pad_maximum_fusion.4), channel_id=1, source_target_pairs={{0,16},{8,24},{16,0},{24,8},{1,17},{9,25},{17,1},{25,9},{2,18},{10... | collective-permute-start | bytes 1572872 | tf_op jit(solution)/shard_map/ppermute | solution.py:55
  82.4 7.1 %collective-permute-done.13 = bf16[4,2,8,16,256]{4,3,2,1,0:T(8,128)(2,1)S(1)} collective-permute-done((bf16[4,2,8,16,256]{4,3,2,1,0:T(8,128)(2,1)S(1)}, bf16[4,2,8,16,256]{4,3,2,1,0:T(8,128)(2,1)S(1)}, u32[]{:S(2)}, u32[]{:S(2)}) %collective-permute-start.13) | collective-permute-done | bytes 524320 | tf_op jit(solution)/shard_map/ppermute | solution.py:55
  90.8 1.9 %compare_select_fusion = (f32[256,256]{1,0:T(8,128)S(1)}, f32[256,256]{1,0:T(8,128)}) fusion(s32[256]{0:T(256)S(1)} %get-tuple-element.24, s32[256]{0:T(256)S(1)} %get-tuple-element.27, s32[256]{0:T(256)S(1)} %get-tuple-element.25, s32[256]{0:T(256)S(1)} %get-tuple-element.26), kind=kLoop, calls=%fused_computation.13 | loop fusion | flops 1114112 | bytes 528384 | tf_op jit(solution)/shard_map/jit(_where)/select_n | solution.py:354
  92.7 4.8 %collective-permute-done.12 = bf16[4,2,8,16,256]{4,3,2,1,0:T(8,128)(2,1)} collective-permute-done((bf16[4,2,8,16,256]{4,3,2,1,0:T(8,128)(2,1)S(1)}, bf16[4,2,8,16,256]{4,3,2,1,0:T(8,128)(2,1)}, u32[]{:S(2)}, u32[]{:S(2)}) %collective-permute-start.12) | collective-permute-done | bytes 524320 | tf_op jit(solution)/shard_map/ppermute | solution.py:55
  99.2 1.8 pad_maximum_fusion
  101.0 5.1 %collective-permute-done.14 = bf16[4,2,8,16,256]{4,3,2,1,0:T(8,128)(2,1)S(1)} collective-permute-done((bf16[4,2,8,16,256]{4,3,2,1,0:T(8,128)(2,1)}, bf16[4,2,8,16,256]{4,3,2,1,0:T(8,128)(2,1)S(1)}, u32[]{:S(2)}, u32[]{:S(2)}) %collective-permute-start.14) | collective-permute-done | bytes 524320 | tf_op jit(solution)/shard_map/ppermute | solution.py:55
  106.1 2.7 %pad_maximum_fusion.1 = bf16[4,4,2,8,16,256]{5,4,3,2,1,0:T(8,128)(2,1)} fusion(bf16[1,4,2,8,16,256]{5,4,3,2,1,0:T(8,128)(2,1)S(1)} %bitcast.87, bf16[1,4,2,8,16,256]{5,4,3,2,1,0:T(8,128)(2,1)S(1)} %bitcast.88, bf16[1,4,2,8,16,256]{5,4,3,2,1,0:T(8,128)(2,1)S(1)} %bitcast.89, bf16[1,4,2,8,16,256]{5,4,3,2,1,0:T(8,128)(2,1)} %bitcast.30), kind=kLoop, calls=%fused_computation.1 | loop fusion | flops 3145728 | bytes 4194304 | tf_op jit(solution)/shard_map/stack | solution.py:411
  109.7 3.7 %cond_spectrum.1.refs_10_ = bf16[1024,256]{1,0:T(8,128)(2,1)S(1)} custom-call(f32[256,256]{1,0:T(8,128)S(1)} %copy-done.2, f32[256,256]{1,0:T(8,128)S(1)} %get-tuple-element.22.sin_ref, f32[256,1024]{1,0:T(8,128)S(1)} %bitcast.75), custom_call_target="tpu_custom_call" | custom-call | flops 1610612736 | bytes 2097152 | tf_op jit(solution)/shard_map/cond_spectrum/pallas_call | solution.py:335
  113.5 2.3 %copy-done.1 = bf16[17,512,256]{2,1,0:T(8,128)(2,1)S(1)} copy-done((bf16[17,512,256]{2,1,0:T(8,128)(2,1)S(1)}, bf16[17,512,256]{2,1,0:T(8,128)(2,1)}, u32[]{:S(2)}) %copy-start.1) | copy-done | bytes 4456472
  115.7 12.4 %valence_response.1 = f32[32,16,128]{2,1,0:T(8,128)S(1)} custom-call(s32[1]{0:T(128)} %bitcast.place_ref, bf16[32,8,16,256]{3,2,1,0:T(8,128)(2,1)S(1)} %bitcast.65, bf16[32,8,16,256]{3,2,1,0:T(8,128)(2,1)S(1)} %bitcast.69, bf16[32,8,16,256]{3,2,1,0:T(8,128)(2,1)S(1)} %bitcast.66, bf16[32,8,16,256]{3,2,1,0:T(8,128)(2,1)S(1)} %bitcast.70, ...), custom_call_target="tpu_custom_call" | custom-call | flops 4563402752 | bytes 9437184 | tf_op jit(solution)/shard_map/valence_response/pallas_call | solution.py:296
  128.1 14.6 %all_to_all.26 = f32[32,16,128]{2,1,0:T(8,128)S(1)} all-to-all(f32[32,16,128]{2,1,0:T(8,128)S(1)} %valence_response.1), channel_id=1, replica_groups=mesh['zl'=4,'co'=2,'x'=4,'y'=4,'zh'=2] {'x','y'}, dimensions={0} | all-to-all | bytes 524288 | tf_op jit(solution)/shard_map/all_to_all | solution.py:416
  143.5 6.1 %all-to-all-start.2 = ((f32[16,2,16,128]{3,2,1,0:T(8,128)}), f32[16,2,16,128]{3,2,1,0:T(8,128)S(1)}, u32[]{:S(2)}, u32[]{:S(2)}) async-start(f32[16,2,16,128]{3,2,1,0:T(8,128)} %broadcast_in_dim.16), calls=%async_computation.2 | async-start | bytes 524288 | tf_op jit(solution)/shard_map/all_to_all | solution.py:65
  149.7 12.2 %all-to-all-done.2 = f32[16,2,16,128]{3,2,1,0:T(8,128)S(1)} async-done(((f32[16,2,16,128]{3,2,1,0:T(8,128)}), f32[16,2,16,128]{3,2,1,0:T(8,128)S(1)}, u32[]{:S(2)}, u32[]{:S(2)}) %all-to-all-start.2) | async-done | bytes 262176 | tf_op jit(solution)/shard_map/all_to_all | solution.py:65
  162.6 14.7 %all_to_all.27.full_ref = f32[16,2,32,128]{3,2,1,0:T(8,128)S(1)} all-to-all(f32[16,2,32,128]{3,2,1,0:T(8,128)S(1)} %broadcast_in_dim.21), channel_id=1, replica_groups=mesh['zl'=4,'co'=2,'x'=4,'y'=4,'zh'=2] {'x','y'}, dimensions={0} | all-to-all | bytes 1048576 | tf_op jit(solution)/shard_map/all_to_all | solution.py:65
  (65 shorter events, 21.4 us)
Async XLA Ops:
  1.5 23.7 %collective-permute-start.2 = (bf16[8,32,256]{2,1,0:T(8,128)(2,1)S(1)}, bf16[8,32,256]{2,1,0:T(8,128)(2,1)S(1)}, u32[]{:S(2)}, u32[]{:S(2)}) collective-permute-start(bf16[8,32,256]{2,1,0:T(8,128)(2,1)S(1)} %bitcast.80), channel_id=1, source_target_pairs={{0,192},{64,0},{128,64},{192,128},{1,193},{65,1},{129,65},{193,129... | collective-permute-start | bytes 393224 | tf_op jit(solution)/shard_map/ppermute | solution.py:55
  6.2 19.0 %collective-permute-start.1 = (bf16[8,32,256]{2,1,0:T(8,128)(2,1)S(1)}, bf16[8,32,256]{2,1,0:T(8,128)(2,1)S(1)}, u32[]{:S(2)}, u32[]{:S(2)}) collective-permute-start(bf16[8,32,256]{2,1,0:T(8,128)(2,1)S(1)} %bitcast.81), channel_id=1, source_target_pairs={{0,128},{64,192},{128,0},{192,64},{1,129},{65,193},{129,1},{193,65... | collective-permute-start | bytes 393224 | tf_op jit(solution)/shard_map/ppermute | solution.py:55
  6.3 19.0 %collective-permute-start = (bf16[8,32,256]{2,1,0:T(8,128)(2,1)S(1)}, bf16[8,32,256]{2,1,0:T(8,128)(2,1)S(1)}, u32[]{:S(2)}, u32[]{:S(2)}) collective-permute-start(bf16[8,32,256]{2,1,0:T(8,128)(2,1)S(1)} %bitcast.82), channel_id=1, source_target_pairs={{0,64},{64,128},{128,192},{192,0},{1,65},{65,129},{129,193},{193,1... | collective-permute-start | bytes 393224 | tf_op jit(solution)/shard_map/ppermute | solution.py:55
  6.9 20.4 %copy-start.3 = (s32[64]{0:T(128)S(1)}, s32[64]{0:T(128)}, u32[]{:S(2)}) copy-start(s32[64]{0:T(128)} %partner_ref.1) | copy-start | bytes 772
  25.2 10.2 %copy-start.4 = (f32[256,512]{1,0:T(8,128)S(1)}, f32[256,512]{1,0:T(8,128)}, u32[]{:S(2)}) copy-start(f32[256,512]{1,0:T(8,128)} %constant.195.clone.table_ref) | copy-start | bytes 1572868
  25.3 2.0 %collective-permute-start.3 = (bf16[32,32,256]{2,1,0:T(8,128)(2,1)S(1)}, bf16[32,32,256]{2,1,0:T(8,128)(2,1)S(1)}, u32[]{:S(2)}, u32[]{:S(2)}) collective-permute-start(bf16[32,32,256]{2,1,0:T(8,128)(2,1)S(1)} %bitcast.73), channel_id=1, source_target_pairs={{0,32},{32,0},{1,33},{33,1},{2,34},{34,2},{3,35},{35,3},{4,36},{36... | collective-permute-start | bytes 1572872 | tf_op jit(solution)/shard_map/ppermute | solution.py:55
  30.1 9.9 %collective-permute-start.4 = (bf16[2,8,16,256]{3,2,1,0:T(8,128)(2,1)S(1)}, bf16[2,8,16,256]{3,2,1,0:T(8,128)(2,1)S(1)}, u32[]{:S(2)}, u32[]{:S(2)}) collective-permute-start(bf16[2,8,16,256]{3,2,1,0:T(8,128)(2,1)S(1)} %get-tuple-element.11), channel_id=1, source_target_pairs={{0,1},{1,0},{2,3},{3,2},{4,5},{5,4},{6,7},{7,6},{8,9},{9,8},{10,11... | collective-permute-start | bytes 393224 | tf_op jit(solution)/shard_map/ppermute | solution.py:55
  39.9 68.9 %all-to-all-start = ((f32[32,8,1024]{2,1,0:T(8,128)}), f32[32,8,1024]{2,1,0:T(8,128)S(1)}, u32[]{:S(2)}, u32[]{:S(2)}) async-start(f32[32,8,1024]{2,1,0:T(8,128)} %bitcast.35), calls=%async_computation | async-start | bytes 2097152 | tf_op jit(solution)/shard_map/all_to_all | solution.py:405
  52.3 16.0 %collective-permute-start.7 = (bf16[2,8,16,256]{3,2,1,0:T(8,128)(2,1)S(1)}, bf16[2,8,16,256]{3,2,1,0:T(8,128)(2,1)S(1)}, u32[]{:S(2)}, u32[]{:S(2)}) collective-permute-start(bf16[2,8,16,256]{3,2,1,0:T(8,128)(2,1)S(1)} %get-tuple-element.19), channel_id=1, source_target_pairs={{0,24},{8,0},{16,8},{24,16},{1,25},{9,1},{17,9},{25,17},{2,26},{10... | collective-permute-start | bytes 393224 | tf_op jit(solution)/shard_map/ppermute | solution.py:55
  55.1 15.1 %collective-permute-start.6 = (bf16[2,8,16,256]{3,2,1,0:T(8,128)(2,1)S(1)}, bf16[2,8,16,256]{3,2,1,0:T(8,128)(2,1)S(1)}, u32[]{:S(2)}, u32[]{:S(2)}) collective-permute-start(bf16[2,8,16,256]{3,2,1,0:T(8,128)(2,1)S(1)} %get-tuple-element.19), channel_id=1, source_target_pairs={{0,16},{8,24},{16,0},{24,8},{1,17},{9,25},{17,1},{25,9},{2,18},{10... | collective-permute-start | bytes 393224 | tf_op jit(solution)/shard_map/ppermute | solution.py:55
  55.9 15.8 %collective-permute-start.5 = (bf16[2,8,16,256]{3,2,1,0:T(8,128)(2,1)S(1)}, bf16[2,8,16,256]{3,2,1,0:T(8,128)(2,1)S(1)}, u32[]{:S(2)}, u32[]{:S(2)}) collective-permute-start(bf16[2,8,16,256]{3,2,1,0:T(8,128)(2,1)S(1)} %get-tuple-element.19), channel_id=1, source_target_pairs={{0,8},{8,16},{16,24},{24,0},{1,9},{9,17},{17,25},{25,1},{2,10},{10... | collective-permute-start | bytes 393224 | tf_op jit(solution)/shard_map/ppermute | solution.py:55
  56.8 15.0 %collective-permute-start.10 = (bf16[2,8,16,256]{3,2,1,0:T(8,128)(2,1)S(1)}, bf16[2,8,16,256]{3,2,1,0:T(8,128)(2,1)S(1)}, u32[]{:S(2)}, u32[]{:S(2)}) collective-permute-start(bf16[2,8,16,256]{3,2,1,0:T(8,128)(2,1)S(1)} %get-tuple-element.20), channel_id=1, source_target_pairs={{0,6},{2,0},{4,2},{6,4},{1,7},{3,1},{5,3},{7,5},{8,14},{10,8},{12,... | collective-permute-start | bytes 393224 | tf_op jit(solution)/shard_map/ppermute | solution.py:55
  57.3 14.4 %collective-permute-start.9 = (bf16[2,8,16,256]{3,2,1,0:T(8,128)(2,1)S(1)}, bf16[2,8,16,256]{3,2,1,0:T(8,128)(2,1)S(1)}, u32[]{:S(2)}, u32[]{:S(2)}) collective-permute-start(bf16[2,8,16,256]{3,2,1,0:T(8,128)(2,1)S(1)} %get-tuple-element.20), channel_id=1, source_target_pairs={{0,4},{2,6},{4,0},{6,2},{1,5},{3,7},{5,1},{7,3},{8,12},{10,14},{12... | collective-permute-start | bytes 393224 | tf_op jit(solution)/shard_map/ppermute | solution.py:55
  68.3 5.0 %collective-permute-start.8 = (bf16[2,8,16,256]{3,2,1,0:T(8,128)(2,1)S(1)}, bf16[2,8,16,256]{3,2,1,0:T(8,128)(2,1)S(1)}, u32[]{:S(2)}, u32[]{:S(2)}) collective-permute-start(bf16[2,8,16,256]{3,2,1,0:T(8,128)(2,1)S(1)} %get-tuple-element.20), channel_id=1, source_target_pairs={{0,2},{2,4},{4,6},{6,0},{1,3},{3,5},{5,7},{7,1},{8,10},{10,12},{12... | collective-permute-start | bytes 393224 | tf_op jit(solution)/shard_map/ppermute | solution.py:55
  71.8 27.4 %copy-start.5 = (bf16[4,2,8,16,256]{4,3,2,1,0:T(8,128)(2,1)}, bf16[4,2,8,16,256]{4,3,2,1,0:T(8,128)(2,1)S(1)}, u32[]{:S(2)}) copy-start(bf16[4,2,8,16,256]{4,3,2,1,0:T(8,128)(2,1)S(1)} %pad_maximum_fusion.3) | copy-start | bytes 1572868
  74.2 15.4 %collective-permute-start.13 = (bf16[4,2,8,16,256]{4,3,2,1,0:T(8,128)(2,1)S(1)}, bf16[4,2,8,16,256]{4,3,2,1,0:T(8,128)(2,1)S(1)}, u32[]{:S(2)}, u32[]{:S(2)}) collective-permute-start(bf16[4,2,8,16,256]{4,3,2,1,0:T(8,128)(2,1)S(1)} %pad_maximum_fusion.3), channel_id=1, source_target_pairs={{0,6},{2,0},{4,2},{6,4},{1,7},{3,1},{5,3},{7,5},{8,14},{10,8},{12,... | collective-permute-start | bytes 1572872 | tf_op jit(solution)/shard_map/ppermute | solution.py:55
  76.3 21.1 %collective-permute-start.12 = (bf16[4,2,8,16,256]{4,3,2,1,0:T(8,128)(2,1)S(1)}, bf16[4,2,8,16,256]{4,3,2,1,0:T(8,128)(2,1)}, u32[]{:S(2)}, u32[]{:S(2)}) collective-permute-start(bf16[4,2,8,16,256]{4,3,2,1,0:T(8,128)(2,1)S(1)} %pad_maximum_fusion.3), channel_id=1, source_target_pairs={{0,4},{2,6},{4,0},{6,2},{1,5},{3,7},{5,1},{7,3},{8,12},{10,14},{12... | collective-permute-start | bytes 1572872 | tf_op jit(solution)/shard_map/ppermute | solution.py:55
  77.1 22.1 %collective-permute-start.11 = (bf16[4,2,8,16,256]{4,3,2,1,0:T(8,128)(2,1)S(1)}, bf16[4,2,8,16,256]{4,3,2,1,0:T(8,128)(2,1)}, u32[]{:S(2)}, u32[]{:S(2)}) collective-permute-start(bf16[4,2,8,16,256]{4,3,2,1,0:T(8,128)(2,1)S(1)} %pad_maximum_fusion.3), channel_id=1, source_target_pairs={{0,2},{2,4},{4,6},{6,0},{1,3},{3,5},{5,7},{7,1},{8,10},{10,12},{12... | collective-permute-start | bytes 1572872 | tf_op jit(solution)/shard_map/ppermute | solution.py:55
  78.9 22.1 %collective-permute-start.16 = (bf16[4,2,8,16,256]{4,3,2,1,0:T(8,128)(2,1)}, bf16[4,2,8,16,256]{4,3,2,1,0:T(8,128)(2,1)S(1)}, u32[]{:S(2)}, u32[]{:S(2)}) collective-permute-start(bf16[4,2,8,16,256]{4,3,2,1,0:T(8,128)(2,1)} %pad_maximum_fusion.4), channel_id=1, source_target_pairs={{0,24},{8,0},{16,8},{24,16},{1,25},{9,1},{17,9},{25,17},{2,26},{10... | collective-permute-start | bytes 1572872 | tf_op jit(solution)/shard_map/ppermute | solution.py:55
  79.7 21.2 %collective-permute-start.15 = (bf16[4,2,8,16,256]{4,3,2,1,0:T(8,128)(2,1)}, bf16[4,2,8,16,256]{4,3,2,1,0:T(8,128)(2,1)S(1)}, u32[]{:S(2)}, u32[]{:S(2)}) collective-permute-start(bf16[4,2,8,16,256]{4,3,2,1,0:T(8,128)(2,1)} %pad_maximum_fusion.4), channel_id=1, source_target_pairs={{0,16},{8,24},{16,0},{24,8},{1,17},{9,25},{17,1},{25,9},{2,18},{10... | collective-permute-start | bytes 1572872 | tf_op jit(solution)/shard_map/ppermute | solution.py:55
  89.5 9.7 %copy-start.6 = (bf16[4,2,8,16,256]{4,3,2,1,0:T(8,128)(2,1)}, bf16[4,2,8,16,256]{4,3,2,1,0:T(8,128)(2,1)S(1)}, u32[]{:S(2)}) copy-start(bf16[4,2,8,16,256]{4,3,2,1,0:T(8,128)(2,1)S(1)} %collective-permute-done.13) | copy-start | bytes 1572868
  89.5 16.6 %collective-permute-start.14 = (bf16[4,2,8,16,256]{4,3,2,1,0:T(8,128)(2,1)}, bf16[4,2,8,16,256]{4,3,2,1,0:T(8,128)(2,1)S(1)}, u32[]{:S(2)}, u32[]{:S(2)}) collective-permute-start(bf16[4,2,8,16,256]{4,3,2,1,0:T(8,128)(2,1)} %pad_maximum_fusion.4), channel_id=1, source_target_pairs={{0,8},{8,16},{16,24},{24,0},{1,9},{9,17},{17,25},{25,1},{2,10},{10... | collective-permute-start | bytes 1572872 | tf_op jit(solution)/shard_map/ppermute | solution.py:55
  109.7 3.7 %copy-start = (bf16[4,4,2,8,16,256]{5,4,3,2,1,0:T(8,128)(2,1)S(1)}, bf16[4,4,2,8,16,256]{5,4,3,2,1,0:T(8,128)(2,1)}, u32[]{:S(2)}) copy-start(bf16[4,4,2,8,16,256]{5,4,3,2,1,0:T(8,128)(2,1)} %pad_maximum_fusion.1) | copy-start | bytes 6291460
  143.5 18.4 %all-to-all-start.2 = ((f32[16,2,16,128]{3,2,1,0:T(8,128)}), f32[16,2,16,128]{3,2,1,0:T(8,128)S(1)}, u32[]{:S(2)}, u32[]{:S(2)}) async-start(f32[16,2,16,128]{3,2,1,0:T(8,128)} %broadcast_in_dim.16), calls=%async_computation.2 | async-start | bytes 524288 | tf_op jit(solution)/shard_map/all_to_all | solution.py:65
  (2 other events, 3.2 us)

commit v5 on v4

--- a/solution.py
+++ b/solution.py
@@ -141,9 +141,9 @@
         out_specs=pl.BlockSpec((1, 512, 256), lambda i: (jnp.maximum(i - LINE_STEPS, 0), 0, 0)),
         out_shape=jax.ShapeDtypeStruct((HALF, 512, 256), BF),
         scratch_shapes=[pltpu.VMEM((2 * HALF, PLANE, 256), F32)],
-        compiler_params=pltpu.CompilerParams(vmem_limit_bytes=54 * MIB),
+        compiler_params=pltpu.CompilerParams(vmem_limit_bytes=40 * MIB),
         cost_estimate=pl.CostEstimate(
-            flops=12 * 256 * 256 * 256 * HALF, bytes_accessed=9 * MIB, transcendentals=0
+            flops=48 * 256 * 256 * 256 * HALF, bytes_accessed=9 * MIB, transcendentals=0
         ),
         name="screened_transform",
     )(gmap.reshape(32, 1, 256), jnp.asarray(line), jnp.asarray(high), jnp.asarray(low), screened)
@@ -250,7 +250,7 @@
 
 def response_kernel(place_ref, *refs):
     first_waves, second_waves = refs[:4], refs[4:8]
-    before_ref, w_ref, cond_ref, out_ref, sum_ref, first_ref, second_ref = refs[8:]
+    before_ref, w_ref, sum_ref, first_ref, second_ref = refs[8:]
     step = pl.program_id(0)
     mirrored = jnp.where(step % 8 == 0, 0.0, 1.0)
     before = dot(second_ref[...], before_ref[0])
@@ -260,64 +260,37 @@
     build_rows(second_ref, second_waves, None)
     sum_ref[...] = total
 
-    @pl.when(step == HALF // 2)
-    def _():
-        low = lax.broadcasted_iota(jnp.int32, (1, 128), 1) < 64
-        for k in range(8):
-            cond = cond_ref[k * 128 : (k + 1) * 128]
-            rows = sum_ref[k * 128 : (k + 1) * 128] * NORM
-            top = rows.astype(BF)
-            rest = (rows - top.astype(F32)).astype(BF)
-            prod = dot(cond, top, ((1,), (1,))) + dot(cond, rest, ((1,), (1,)))
-            swapped = pltpu.roll(prod[64:], 64, 1)
-            both = prod[:64] + jnp.where(low, swapped, -swapped)
-            even, odd = both[:32], both[32:]
-            real = jnp.where(low, even, pltpu.roll(odd, 64, 1))
-            imag = jnp.where(low, pltpu.roll(even, 64, 1), odd)
-            out_ref[:, 2 * k, :] = real
-            out_ref[:, 2 * k + 1, :] = imag
-
-
-def response(place, home, away, screened, cond):
+
+def response(place, waves, screened):
     def block(which, second, back):
         def index(step, place_ref):
             z = jnp.minimum(2 * step + second, HALF - 1)
             z = (NZ - z) & (NZ - 1) if back else z
-            place = place_ref[0]
-            level = (place ^ z) & 1
-            x = ((place >> 3) - (z >> 3)) & 3
-            y = ((place >> 1) - (z >> 1)) & 3
-            x, y = (x, y) if which == 0 else (y, x)
-            return ((y * 4 + x) * 2 + level, 0, 0, 0)
+            return (((z & 30) + ((place_ref[0] ^ z) & 1)) * 2 + which, 0, 0, 0)
 
         return pl.BlockSpec((1, 8, 16, 256), index)
 
-    waves = [block(w, s, b) for s in range(2) for b in (False, True) for w in range(2)]
+    blocks = [block(w, s, b) for s in range(2) for b in (False, True) for w in range(2)]
     return pl.pallas_call(
         response_kernel,
         grid_spec=pltpu.PrefetchScalarGridSpec(
             num_scalar_prefetch=1,
             grid=(HALF // 2 + 1,),
-            in_specs=waves
+            in_specs=blocks
             + [
                 pl.BlockSpec((1, 512, 256), lambda i, p: (jnp.maximum(2 * i - 1, 0), 0, 0)),
                 pl.BlockSpec((1, 512, 256), lambda i, p: (2 * i, 0, 0)),
-                pl.BlockSpec((1024, 256), lambda i, p: (0, 0)),
             ],
-            out_specs=pl.BlockSpec((32, 16, 128), lambda i, p: (0, 0, 0)),
-            scratch_shapes=[
-                pltpu.VMEM((1024, 256), F32),
-                pltpu.VMEM((1024, 512), BF),
-                pltpu.VMEM((1024, 512), BF),
-            ],
-        ),
-        out_shape=jax.ShapeDtypeStruct((32, 16, 128), F32),
-        compiler_params=pltpu.CompilerParams(vmem_limit_bytes=40 * MIB),
+            out_specs=pl.BlockSpec((1024, 256), lambda i, p: (0, 0)),
+            scratch_shapes=[pltpu.VMEM((1024, 512), BF), pltpu.VMEM((1024, 512), BF)],
+        ),
+        out_shape=jax.ShapeDtypeStruct((1024, 256), F32),
+        compiler_params=pltpu.CompilerParams(vmem_limit_bytes=20 * MIB),
         cost_estimate=pl.CostEstimate(
-            flops=2 * 1024 * 512 * 256 * HALF, bytes_accessed=9 * MIB, transcendentals=0
+            flops=16 * 1024 * 512 * 256 * HALF, bytes_accessed=9 * MIB, transcendentals=0
         ),
         name="valence_response",
-    )(place.reshape(1), *([home, away] * 4), screened, screened, cond)
+    )(place.reshape(1), *([waves] * 8), screened, screened)
 
 
 def spectrum_kernel(cos_ref, sin_ref, x_ref, out_ref):
@@ -343,6 +316,35 @@
         ),
         name="cond_spectrum",
     )(cosine, sine, columns)
+
+
+def block_kernel(cond_ref, r_ref, out_ref):
+    first = lax.broadcasted_iota(jnp.int32, (1, 128), 1) < 64
+    for k in range(8):
+        cond = cond_ref[k * 128 : (k + 1) * 128]
+        rows = r_ref[k * 128 : (k + 1) * 128] * NORM
+        top = rows.astype(BF)
+        rest = (rows - top.astype(F32)).astype(BF)
+        prod = dot(cond, top, ((1,), (1,))) + dot(cond, rest, ((1,), (1,)))
+        swapped = pltpu.roll(prod[64:], 64, 1)
+        both = prod[:64] + jnp.where(first, swapped, -swapped)
+        even, odd = both[:32], both[32:]
+        out_ref[:, 2 * k, :] = jnp.where(first, even, pltpu.roll(odd, 64, 1))
+        out_ref[:, 2 * k + 1, :] = jnp.where(first, pltpu.roll(even, 64, 1), odd)
+
+
+def kernel_blocks(cond, rows):
+    return pl.pallas_call(
+        block_kernel,
+        out_shape=jax.ShapeDtypeStruct((32, 16, 128), F32),
+        in_specs=[pl.BlockSpec(memory_space=pltpu.VMEM)] * 2,
+        out_specs=pl.BlockSpec(memory_space=pltpu.VMEM),
+        compiler_params=pltpu.CompilerParams(vmem_limit_bytes=16 * MIB),
+        cost_estimate=pl.CostEstimate(
+            flops=4 * 128 * 256 * 1024, bytes_accessed=2 * MIB, transcendentals=0
+        ),
+        name="kernel_blocks",
+    )(cond, rows)
 
 
 def line_tables(gmap, place):
@@ -394,24 +396,20 @@
     negative = (NX - index // NY) % NX * NY + (NY - index % NY) % NY
     negative = jnp.where(place > NZ // 2, negative, index)
     flip = (index[:, None] == negative[None, :]).astype(BF)
-    wide = screened_transform(screened, gmap)
-    near, wide = lax.optimization_barrier((near, wide))
     far = turned(near, "co", 1)
 
     vals, away_cond = choose(partner, near, far, flip)
     planes = cond_planes(waves[:, 16:], away_cond)
     vals = spread(vals, "zh")
+    vals, screened = lax.optimization_barrier((vals, screened))
+    wide = screened_transform(screened, gmap)
+    vals = copies_to_all(vals, ("x", "y")).reshape(64, 8, 16, 256)
+
     vals, planes = lax.optimization_barrier((vals, planes))
     columns = lax.all_to_all(planes, GA, split_axis=0, concat_axis=0, tiled=True)
-    home, away = spread(vals[:, 0], "x"), spread(vals[:, 1], "y")
-    home, away = lax.optimization_barrier((home, away))
-    homes = [home] + [turned(home, "y", d) for d in range(1, 4)]
-    aways = [away] + [turned(away, "x", d) for d in range(1, 4)]
-    home = jnp.stack(homes).reshape(32, 8, 16, 256)
-    away = jnp.stack(aways).reshape(32, 8, 16, 256)
+    rows = response(place, vals, wide)
     cond = cond_spectrum(*line_tables(gmap, place), columns)
-
-    blocks = response(place, home, away, wide, cond)
+    blocks = kernel_blocks(cond, rows)
 
     parts = lax.all_to_all(blocks, ("x", "y"), split_axis=0, concat_axis=0, tiled=True)
     mine = jnp.sum(parts.reshape(16, 2, 16, 128), axis=0)

time: 179 us -> 196 us (1.095)
  waiting for transfers between devices: 44.7 us -> 63.3 us
  starting transfers between devices: 46.9 us -> 53.9 us
  other arithmetic: 8.43 us -> 1.55 us
  local copies, waits for them, and re-layouts: 5.12 us -> 9.34 us
  blocking collectives: 29.4 us -> 26.1 us
  Pallas kernels: 42.5 us -> 39.6 us
    all_to_all x1 -> x2, waiting for transfers between devices: 12.2 us -> 44.3 us  [copies_to_all(): return lax.all_to_all(copies, axes, split_axis=0, concat_axis=0, tiled=True)]
    all_to_all x1 -> x2, starting transfers between devices: 6.1 us -> 24.4 us  [copies_to_all(): return lax.all_to_all(copies, axes, split_axis=0, concat_axis=0, tiled=True)]
    ppermute x17 -> x5, starting transfers between devices: 28.5 us -> 10.9 us  [turned(): lax.ppermute(value, axis, [(i, (i + step) % size) for i in range(size)])]
    ppermute x17 -> x5, waiting for transfers between devices: 32.4 us -> 16.4 us  [turned(): lax.ppermute(value, axis, [(i, (i + step) % size) for i in range(size)])]
    all_to_all x1, starting transfers between devices: 12.3 us -> 18.5 us  [on_device(): lax.all_to_all(planes, GA, split_axis=0, concat_axis=0, tiled=True)]
    pallas_call x1, Pallas kernels: 18.3 us -> 13.5 us  [screened_transform(): pl.pallas_call(screened_kernel, grid=(LINE_STEPS + HALF,), in_specs=[pl.B...]
    another operation x2 -> x0, other arithmetic: 4.45 us -> none  [the longest x1 2.67 us: on_device(): away = jnp.stack(aways).reshape(32, 8, 16, 256)]
    all_to_all x1, blocking collectives: 14.6 us -> 11.4 us  [on_device(): lax.all_to_all(blocks, ('x', 'y'), split_axis=0, concat_axis=0, tiled=True)]
  transfers between devices with their start and end apart: 19 -> 8, of which waited for: 10 -> 7; matrix products, arithmetic and copies ran while one was open for 5% -> 1% of each run, Pallas kernels for 13% -> 16%
where the time goes in v5:
time: 196 us; the launch traced here: 195 us
  waiting for transfers between devices  63.3 us (32%)
  starting transfers between devices  53.9 us (28%)
  Pallas kernels  39.6 us (20%)
  blocking collectives  26.1 us (13%)
  local copies, waits for them, and re-layouts  9.34 us (5%)
    all_to_all x2, waiting for transfers between devices, copies_to_all(): return lax.all_to_all(copies, axes, split_axis=0, concat_axis=0, tiled=True)  44.3 us
    all_to_all x2, starting transfers between devices, copies_to_all(): return lax.all_to_all(copies, axes, split_axis=0, concat_axis=0, tiled=True)  24.4 us
    all_to_all x1, starting transfers between devices, on_device(): lax.all_to_all(planes, GA, split_axis=0, concat_axis=0, tiled=True)  18.5 us
    ppermute x5, waiting for transfers between devices, turned(): lax.ppermute(value, axis, [(i, (i + step) % size) for i in range(size)])  16.4 us
    all_to_all x1, blocking collectives, copies_to_all(): return lax.all_to_all(copies, axes, split_axis=0, concat_axis=0, tiled=True)  14.7 us
    pallas_call x1, Pallas kernels, response(): pl.pallas_call(response_kernel, grid_spec=pltpu.PrefetchScalarGridSpec(nu...  13.8 us
    pallas_call x1, Pallas kernels, screened_transform(): pl.pallas_call(screened_kernel, grid=(LINE_STEPS + HALF,), in_specs=[pl.B...  13.5 us
    all_to_all x1, blocking collectives, on_device(): lax.all_to_all(blocks, ('x', 'y'), split_axis=0, concat_axis=0, tiled=True)  11.4 us
  transfers between devices with their start and end apart: 8, of which 7 were waited for; matrix products, arithmetic and copies ran while one was open for 1% of the time, Pallas kernels for 16%

profile of v5, /device:TPU:8, one launch (start us, length us, event | category | flops | bytes accessed | tf_op | source)
XLA Modules:
  0.0 195.0 jit_solution(4169025912539502321)
XLA Ops:
  1.5 4.7 %collective-permute-start.2 = (bf16[8,32,256]{2,1,0:T(8,128)(2,1)S(1)}, bf16[8,32,256]{2,1,0:T(8,128)(2,1)S(1)}, u32[]{:S(2)}, u32[]{:S(2)}) collective-permute-start(bf16[8,32,256]{2,1,0:T(8,128)(2,1)S(1)} %bitcast.49), channel_id=1, source_target_pairs={{0,192},{64,0},{128,64},{192,128},{1,193},{65,1},{129,65},{193,129... | collective-permute-start | bytes 393224 | tf_op jit(solution)/shard_map/ppermute | solution.py:55
  6.9 3.2 %collective-permute-done.2 = bf16[8,32,256]{2,1,0:T(8,128)(2,1)S(1)} collective-permute-done((bf16[8,32,256]{2,1,0:T(8,128)(2,1)S(1)}, bf16[8,32,256]{2,1,0:T(8,128)(2,1)S(1)}, u32[]{:S(2)}, u32[]{:S(2)}) %collective-permute-start.2) | collective-permute-done | bytes 131104 | tf_op jit(solution)/shard_map/ppermute | solution.py:55
  10.2 7.3 %collective-permute-done.1 = bf16[8,32,256]{2,1,0:T(8,128)(2,1)S(1)} collective-permute-done((bf16[8,32,256]{2,1,0:T(8,128)(2,1)S(1)}, bf16[8,32,256]{2,1,0:T(8,128)(2,1)S(1)}, u32[]{:S(2)}, u32[]{:S(2)}) %collective-permute-start.1) | collective-permute-done | bytes 131104 | tf_op jit(solution)/shard_map/ppermute | solution.py:55
  17.8 1.8 collective-permute-done.3.far_ref
  20.2 2.8 %partner_choice.1 = (bf16[2,8,16,256]{3,2,1,0:T(8,128)(2,1)S(1)}, bf16[8,16,256]{2,1,0:T(8,128)(2,1)S(1)}) custom-call(s32[64]{0:T(128)S(1)} %copy-done, s32[2]{0:T(128)S(1)} %pad_add_fusion.place_ref, bf16[256,256]{1,0:T(8,128)(2,1)S(1)} %fusion.4.flip_ref, bf16[32,32,256]{2,1,0:T(8,128)(2,1)S(1)} %bitcast.43, ...), custom_call_target="tpu_custom_call" | custom-call | tf_op jit(solution)/shard_map/partner_choice/pallas_call | solution.py:173
  23.0 5.5 %collective-permute-start.4 = (bf16[2,8,16,256]{3,2,1,0:T(8,128)(2,1)S(1)}, bf16[2,8,16,256]{3,2,1,0:T(8,128)(2,1)S(1)}, u32[]{:S(2)}, u32[]{:S(2)}) collective-permute-start(bf16[2,8,16,256]{3,2,1,0:T(8,128)(2,1)S(1)} %get-tuple-element.8), channel_id=1, source_target_pairs={{0,1},{1,0},{2,3},{3,2},{4,5},{5,4},{6,7},{7,6},{8,9},{9,8},{10,11... | collective-permute-start | bytes 393224 | tf_op jit(solution)/shard_map/ppermute | solution.py:55
  28.4 4.1 %collective-permute-done.4 = bf16[2,8,16,256]{3,2,1,0:T(8,128)(2,1)S(1)} collective-permute-done((bf16[2,8,16,256]{3,2,1,0:T(8,128)(2,1)S(1)}, bf16[2,8,16,256]{3,2,1,0:T(8,128)(2,1)S(1)}, u32[]{:S(2)}, u32[]{:S(2)}) %collective-permute-start.4) | collective-permute-done | bytes 131104 | tf_op jit(solution)/shard_map/ppermute | solution.py:55
  32.6 2.5 %broadcast_in_dim.18 = bf16[16,2,2,8,16,256]{5,4,3,2,1,0:T(8,128)(2,1)} broadcast(bf16[2,2,8,16,256]{4,3,2,1,0:T(8,128)(2,1)S(1)} %pad_maximum_fusion.1), dimensions={1,2,3,4,5} | broadcast | bytes 4456448 | tf_op jit(solution)/shard_map/broadcast_in_dim | solution.py:64
  35.1 7.5 %all-to-all-start = ((bf16[16,2,2,8,16,256]{5,4,3,2,1,0:T(8,128)(2,1)}), bf16[16,2,2,8,16,256]{5,4,3,2,1,0:T(8,128)(2,1)}, u32[]{:S(2)}, u32[]{:S(2)}) async-start(bf16[16,2,2,8,16,256]{5,4,3,2,1,0:T(8,128)(2,1)} %broadcast_in_dim.18), calls=%async_computation | async-start | bytes 8388608 | tf_op jit(solution)/shard_map/all_to_all | solution.py:65
  42.8 1.1 compare_select_fusion
  43.9 4.4 %cond_planes.1 = f32[256,1024]{1,0:T(8,128)} custom-call(f32[256,512]{1,0:T(8,128)S(1)} %copy-done.4, bf16[8,16,256]{2,1,0:T(8,128)(2,1)S(1)} %slice.12.home_ref, bf16[8,16,256]{2,1,0:T(8,128)(2,1)S(1)} %get-tuple-element.10.away_ref), custom_call_target="tpu_custom_call" | custom-call | flops 1610612736 | bytes 2097152 | tf_op jit(solution)/shard_map/cond_planes/pallas_call | solution.py:206
  48.4 13.5 %screened_transform.1.refs_8_.refs_9_ = bf16[17,512,256]{2,1,0:T(8,128)(2,1)S(1)} custom-call(s32[32,1,256]{2,1,0:T(1,128)S(1)} %bitcast.46, bf16[96,32]{1,0:T(8,128)(2,1)S(1)} %copy-done.7, bf16[2,256,256]{2,1,0:T(8,128)(2,1)S(1)} %copy-done.5, bf16[2,256,256]{2,1,0:T(8,128)(2,1)S(1)} %copy-done.6, bf16[256,8192]{1,0:T(8,128)(2,1)S(1)} %copy-done.3), custom_call_target="tpu_custom_call" | custom-call | flops 13690208256 | bytes 9437184 | tf_op jit(solution)/shard_map/screened_transform/pallas_call | solution.py:131
  61.8 2.0 %copy-done.8 = bf16[17,512,256]{2,1,0:T(8,128)(2,1)} copy-done((bf16[17,512,256]{2,1,0:T(8,128)(2,1)}, bf16[17,512,256]{2,1,0:T(8,128)(2,1)S(1)}, u32[]{:S(2)}) %copy-start.8) | copy-done | bytes 4456472
  63.9 32.0 %all-to-all-done = bf16[16,2,2,8,16,256]{5,4,3,2,1,0:T(8,128)(2,1)} async-done(((bf16[16,2,2,8,16,256]{5,4,3,2,1,0:T(8,128)(2,1)}), bf16[16,2,2,8,16,256]{5,4,3,2,1,0:T(8,128)(2,1)}, u32[]{:S(2)}, u32[]{:S(2)}) %all-to-all-start) | async-done | bytes 4194336 | tf_op jit(solution)/shard_map/all_to_all | solution.py:65
  95.9 18.5 %all-to-all-start.1 = ((f32[32,8,1024]{2,1,0:T(8,128)}), f32[32,8,1024]{2,1,0:T(8,128)S(1)}, u32[]{:S(2)}, u32[]{:S(2)}) async-start(f32[32,8,1024]{2,1,0:T(8,128)} %bitcast.14), calls=%async_computation.1 | async-start | bytes 2097152 | tf_op jit(solution)/shard_map/all_to_all | solution.py:409
  114.4 2.3 %copy-done.9 = bf16[17,512,256]{2,1,0:T(8,128)(2,1)S(1)} copy-done((bf16[17,512,256]{2,1,0:T(8,128)(2,1)S(1)}, bf16[17,512,256]{2,1,0:T(8,128)(2,1)}, u32[]{:S(2)}) %copy-start.9) | copy-done | bytes 4456472
  116.6 13.8 %valence_response.1.r_ref = f32[1024,256]{1,0:T(8,128)S(1)} custom-call(s32[1]{0:T(128)} %bitcast.16.place_ref, bf16[64,8,16,256]{3,2,1,0:T(8,128)(2,1)} %bitcast.13.refs_0_.refs_1_.refs_2_.refs_3_.refs_4_.refs_5_.refs_6_.refs_7_, bf16[64,8,16,256]{3,2,1,0:T(8,128)(2,1)} %bitcast.13.refs_0_.refs_1_.refs_2_.refs_3_.refs_4_.refs_5_.refs_6_.refs_7_, ...), custom_call_target="tpu_custom_call" | custom-call | flops 36507222016 | bytes 9437184 | tf_op jit(solution)/shard_map/valence_response/pallas_call | solution.py:274
  130.4 2.7 %all-to-all-done.1 = f32[32,8,1024]{2,1,0:T(8,128)S(1)} async-done(((f32[32,8,1024]{2,1,0:T(8,128)}), f32[32,8,1024]{2,1,0:T(8,128)S(1)}, u32[]{:S(2)}, u32[]{:S(2)}) %all-to-all-start.1) | async-done | bytes 1048608 | tf_op jit(solution)/shard_map/all_to_all | solution.py:409
  133.1 3.7 %cond_spectrum.1.cond_ref = bf16[1024,256]{1,0:T(8,128)(2,1)S(1)} custom-call(f32[256,256]{1,0:T(8,128)S(1)} %get-tuple-element.15.cos_ref, f32[256,256]{1,0:T(8,128)S(1)} %get-tuple-element.14.sin_ref, f32[256,1024]{1,0:T(8,128)S(1)} %bitcast.44), custom_call_target="tpu_custom_call" | custom-call | flops 1610612736 | bytes 2097152 | tf_op jit(solution)/shard_map/cond_spectrum/pallas_call | solution.py:308
  137.4 11.4 %all_to_all.31 = f32[32,16,128]{2,1,0:T(8,128)S(1)} all-to-all(f32[32,16,128]{2,1,0:T(8,128)S(1)} %kernel_blocks.1), channel_id=1, replica_groups=mesh['zl'=4,'co'=2,'x'=4,'y'=4,'zh'=2] {'x','y'}, dimensions={0} | all-to-all | bytes 524288 | tf_op jit(solution)/shard_map/all_to_all | solution.py:414
  149.5 16.9 %all-to-all-start.3 = ((f32[16,2,16,128]{3,2,1,0:T(8,128)}), f32[16,2,16,128]{3,2,1,0:T(8,128)S(1)}, u32[]{:S(2)}, u32[]{:S(2)}) async-start(f32[16,2,16,128]{3,2,1,0:T(8,128)} %broadcast_in_dim.19), calls=%async_computation.3 | async-start | bytes 524288 | tf_op jit(solution)/shard_map/all_to_all | solution.py:65
  166.5 12.2 %all-to-all-done.3 = f32[16,2,16,128]{3,2,1,0:T(8,128)S(1)} async-done(((f32[16,2,16,128]{3,2,1,0:T(8,128)}), f32[16,2,16,128]{3,2,1,0:T(8,128)S(1)}, u32[]{:S(2)}, u32[]{:S(2)}) %all-to-all-start.3) | async-done | bytes 262176 | tf_op jit(solution)/shard_map/all_to_all | solution.py:65
  179.3 14.7 %all_to_all.32.full_ref = f32[16,2,32,128]{3,2,1,0:T(8,128)S(1)} all-to-all(f32[16,2,32,128]{3,2,1,0:T(8,128)S(1)} %broadcast_in_dim.24), channel_id=1, replica_groups=mesh['zl'=4,'co'=2,'x'=4,'y'=4,'zh'=2] {'x','y'}, dimensions={0} | all-to-all | bytes 1048576 | tf_op jit(solution)/shard_map/all_to_all | solution.py:65
  194.1 1.0 lay_out.1
  (46 shorter events, 4.6 us)
Async XLA Ops:
  1.5 8.6 %collective-permute-start.2 = (bf16[8,32,256]{2,1,0:T(8,128)(2,1)S(1)}, bf16[8,32,256]{2,1,0:T(8,128)(2,1)S(1)}, u32[]{:S(2)}, u32[]{:S(2)}) collective-permute-start(bf16[8,32,256]{2,1,0:T(8,128)(2,1)S(1)} %bitcast.49), channel_id=1, source_target_pairs={{0,192},{64,0},{128,64},{192,128},{1,193},{65,1},{129,65},{193,129... | collective-permute-start | bytes 393224 | tf_op jit(solution)/shard_map/ppermute | solution.py:55
  6.2 11.2 %collective-permute-start.1 = (bf16[8,32,256]{2,1,0:T(8,128)(2,1)S(1)}, bf16[8,32,256]{2,1,0:T(8,128)(2,1)S(1)}, u32[]{:S(2)}, u32[]{:S(2)}) collective-permute-start(bf16[8,32,256]{2,1,0:T(8,128)(2,1)S(1)} %bitcast.50), channel_id=1, source_target_pairs={{0,128},{64,192},{128,0},{192,64},{1,129},{65,193},{129,1},{193,65... | collective-permute-start | bytes 393224 | tf_op jit(solution)/shard_map/ppermute | solution.py:55
  6.3 11.2 %collective-permute-start = (bf16[8,32,256]{2,1,0:T(8,128)(2,1)S(1)}, bf16[8,32,256]{2,1,0:T(8,128)(2,1)S(1)}, u32[]{:S(2)}, u32[]{:S(2)}) collective-permute-start(bf16[8,32,256]{2,1,0:T(8,128)(2,1)S(1)} %bitcast.51), channel_id=1, source_target_pairs={{0,64},{64,128},{128,192},{192,0},{1,65},{65,129},{129,193},{193,1... | collective-permute-start | bytes 393224 | tf_op jit(solution)/shard_map/ppermute | solution.py:55
  17.5 2.0 %collective-permute-start.3 = (bf16[32,32,256]{2,1,0:T(8,128)(2,1)S(1)}, bf16[32,32,256]{2,1,0:T(8,128)(2,1)S(1)}, u32[]{:S(2)}, u32[]{:S(2)}) collective-permute-start(bf16[32,32,256]{2,1,0:T(8,128)(2,1)S(1)} %bitcast.42), channel_id=1, source_target_pairs={{0,32},{32,0},{1,33},{33,1},{2,34},{34,2},{3,35},{35,3},{4,36},{36... | collective-permute-start | bytes 1572872 | tf_op jit(solution)/shard_map/ppermute | solution.py:55
  19.5 0.7 copy-start
  23.0 9.6 %collective-permute-start.4 = (bf16[2,8,16,256]{3,2,1,0:T(8,128)(2,1)S(1)}, bf16[2,8,16,256]{3,2,1,0:T(8,128)(2,1)S(1)}, u32[]{:S(2)}, u32[]{:S(2)}) collective-permute-start(bf16[2,8,16,256]{3,2,1,0:T(8,128)(2,1)S(1)} %get-tuple-element.8), channel_id=1, source_target_pairs={{0,1},{1,0},{2,3},{3,2},{4,5},{5,4},{6,7},{7,6},{8,9},{9,8},{10,11... | collective-permute-start | bytes 393224 | tf_op jit(solution)/shard_map/ppermute | solution.py:55
  35.1 7.6 %copy-start.2 = (s32[8192]{0:T(1024)S(1)}, s32[8192]{0:T(1024)}, u32[]{:S(2)}) copy-start(s32[8192]{0:T(1024)} %param.10) | copy-start | bytes 98308
  35.1 8.8 %copy-start.4 = (f32[256,512]{1,0:T(8,128)S(1)}, f32[256,512]{1,0:T(8,128)}, u32[]{:S(2)}) copy-start(f32[256,512]{1,0:T(8,128)} %constant.192.clone.table_ref) | copy-start | bytes 1572868
  35.1 60.8 %all-to-all-start = ((bf16[16,2,2,8,16,256]{5,4,3,2,1,0:T(8,128)(2,1)}), bf16[16,2,2,8,16,256]{5,4,3,2,1,0:T(8,128)(2,1)}, u32[]{:S(2)}, u32[]{:S(2)}) async-start(bf16[16,2,2,8,16,256]{5,4,3,2,1,0:T(8,128)(2,1)} %broadcast_in_dim.18), calls=%async_computation | async-start | bytes 8388608 | tf_op jit(solution)/shard_map/all_to_all | solution.py:65
  42.6 5.7 %copy-start.5 = (bf16[2,256,256]{2,1,0:T(8,128)(2,1)S(1)}, bf16[2,256,256]{2,1,0:T(8,128)(2,1)}, u32[]{:S(2)}) copy-start(bf16[2,256,256]{2,1,0:T(8,128)(2,1)} %constant.194.clone.high_ref) | copy-start | bytes 786436
  42.6 5.7 %copy-start.6 = (bf16[2,256,256]{2,1,0:T(8,128)(2,1)S(1)}, bf16[2,256,256]{2,1,0:T(8,128)(2,1)}, u32[]{:S(2)}) copy-start(bf16[2,256,256]{2,1,0:T(8,128)(2,1)} %constant.195.clone.low_ref) | copy-start | bytes 786436
  42.6 5.7 %copy-start.7 = (bf16[96,32]{1,0:T(8,128)(2,1)S(1)}, bf16[96,32]{1,0:T(8,128)(2,1)}, u32[]{:S(2)}) copy-start(bf16[96,32]{1,0:T(8,128)(2,1)} %constant.193.clone.line_ref) | copy-start | bytes 18436
  42.7 5.7 %copy-start.3 = (bf16[256,8192]{1,0:T(8,128)(2,1)S(1)}, bf16[256,8192]{1,0:T(8,128)(2,1)}, u32[]{:S(2)}) copy-start(bf16[256,8192]{1,0:T(8,128)(2,1)} %w_ref) | copy-start | bytes 12582916
  61.8 2.0 %copy-start.8 = (bf16[17,512,256]{2,1,0:T(8,128)(2,1)}, bf16[17,512,256]{2,1,0:T(8,128)(2,1)S(1)}, u32[]{:S(2)}) copy-start(bf16[17,512,256]{2,1,0:T(8,128)(2,1)S(1)} %screened_transform.1.refs_8_.refs_9_) | copy-start | bytes 13369348
  95.9 37.2 %all-to-all-start.1 = ((f32[32,8,1024]{2,1,0:T(8,128)}), f32[32,8,1024]{2,1,0:T(8,128)S(1)}, u32[]{:S(2)}, u32[]{:S(2)}) async-start(f32[32,8,1024]{2,1,0:T(8,128)} %bitcast.14), calls=%async_computation.1 | async-start | bytes 2097152 | tf_op jit(solution)/shard_map/all_to_all | solution.py:409
  114.4 2.3 %copy-start.9 = (bf16[17,512,256]{2,1,0:T(8,128)(2,1)S(1)}, bf16[17,512,256]{2,1,0:T(8,128)(2,1)}, u32[]{:S(2)}) copy-start(bf16[17,512,256]{2,1,0:T(8,128)(2,1)} %copy-done.8) | copy-start | bytes 13369348
  133.1 45.8 %copy-start.1 = (s32[64]{0:T(128)S(1)}, s32[64]{0:T(128)}, u32[]{:S(2)}) copy-start(s32[64]{0:T(128)} %partner_ref.1) | copy-start | bytes 772
  149.5 29.2 %all-to-all-start.3 = ((f32[16,2,16,128]{3,2,1,0:T(8,128)}), f32[16,2,16,128]{3,2,1,0:T(8,128)S(1)}, u32[]{:S(2)}, u32[]{:S(2)}) async-start(f32[16,2,16,128]{3,2,1,0:T(8,128)} %broadcast_in_dim.19), calls=%async_computation.3 | async-start | bytes 524288 | tf_op jit(solution)/shard_map/all_to_all | solution.py:65

commit v6 on v5

--- a/solution.py
+++ b/solution.py
@@ -261,12 +261,15 @@
     sum_ref[...] = total
 
 
-def response(place, waves, screened):
+def response(place, home, away, screened):
     def block(which, second, back):
         def index(step, place_ref):
             z = jnp.minimum(2 * step + second, HALF - 1)
             z = (NZ - z) & (NZ - 1) if back else z
-            return (((z & 30) + ((place_ref[0] ^ z) & 1)) * 2 + which, 0, 0, 0)
+            x = ((place_ref[0] >> 3) - (z >> 3)) & 3
+            y = ((place_ref[0] >> 1) - (z >> 1)) & 3
+            x, y = (x, y) if which == 0 else (y, x)
+            return ((y * 4 + x) * 2 + ((place_ref[0] ^ z) & 1), 0, 0, 0)
 
         return pl.BlockSpec((1, 8, 16, 256), index)
 
@@ -290,7 +293,7 @@
             flops=16 * 1024 * 512 * 256 * HALF, bytes_accessed=9 * MIB, transcendentals=0
         ),
         name="valence_response",
-    )(place.reshape(1), *([waves] * 8), screened, screened)
+    )(place.reshape(1), *([home, away] * 4), screened, screened)
 
 
 def spectrum_kernel(cos_ref, sin_ref, x_ref, out_ref):
@@ -401,13 +404,17 @@
     vals, away_cond = choose(partner, near, far, flip)
     planes = cond_planes(waves[:, 16:], away_cond)
     vals = spread(vals, "zh")
-    vals, screened = lax.optimization_barrier((vals, screened))
+    home, away = spread(vals[:, 0], "x"), spread(vals[:, 1], "y")
+    home, away, planes, screened = lax.optimization_barrier((home, away, planes, screened))
+    homes = [home] + [turned(home, "y", d) for d in range(1, 4)]
+    aways = [away] + [turned(away, "x", d) for d in range(1, 4)]
     wide = screened_transform(screened, gmap)
-    vals = copies_to_all(vals, ("x", "y")).reshape(64, 8, 16, 256)
-
-    vals, planes = lax.optimization_barrier((vals, planes))
+
+    wide, planes = lax.optimization_barrier((wide, planes))
     columns = lax.all_to_all(planes, GA, split_axis=0, concat_axis=0, tiled=True)
-    rows = response(place, vals, wide)
+    home = jnp.stack(homes).reshape(32, 8, 16, 256)
+    away = jnp.stack(aways).reshape(32, 8, 16, 256)
+    rows = response(place, home, away, wide)
     cond = cond_spectrum(*line_tables(gmap, place), columns)
     blocks = kernel_blocks(cond, rows)
 

time: 196 us -> 172 us (0.88)
  waiting for transfers between devices: 63.3 us -> 48.1 us
  starting transfers between devices: 53.9 us -> 45.3 us
  other arithmetic: 1.55 us -> 5.89 us
  local copies, waits for them, and re-layouts: 9.34 us -> 6.82 us
    all_to_all x2 -> x1, waiting for transfers between devices: 44.3 us -> 12.2 us  [copies_to_all(): return lax.all_to_all(copies, axes, split_axis=0, concat_axis=0, tiled=True)]
    ppermute x5 -> x17, starting transfers between devices: 10.9 us -> 30.1 us  [turned(): lax.ppermute(value, axis, [(i, (i + step) % size) for i in range(size)])]
    all_to_all x2 -> x1, starting transfers between devices: 24.4 us -> 5.74 us  [copies_to_all(): return lax.all_to_all(copies, axes, split_axis=0, concat_axis=0, tiled=True)]
    ppermute x5 -> x17, waiting for transfers between devices: 16.4 us -> 32.1 us  [turned(): lax.ppermute(value, axis, [(i, (i + step) % size) for i in range(size)])]
    all_to_all x1, starting transfers between devices: 18.5 us -> 9.5 us  [on_device(): lax.all_to_all(planes, GA, split_axis=0, concat_axis=0, tiled=True)]
    another operation x0 -> x2, other arithmetic: none -> 3.39 us  [the longest x1 1.78 us: on_device(): home = jnp.stack(homes).reshape(32, 8, 16, 256)]
    broadcast_in_dim x3 -> x2, local copies, waits for them, and re-layouts: 3.28 us -> 0.78 us  [copies_to_all(): copies = jnp.broadcast_to(value[None], (count,) + value.shape)]
    pallas_call x1, Pallas kernels: 13.8 us -> 11.8 us  [response(): pl.pallas_call(response_kernel, grid_spec=pltpu.PrefetchScalarGridSpec(nu...]
  transfers between devices with their start and end apart: 8 -> 19, of which waited for: 7 -> 8; matrix products, arithmetic and copies ran while one was open for 1% -> 3% of each run, Pallas kernels for 16% -> 17%
where the time goes in v6:
time: 172 us; the launch traced here: 171 us
  waiting for transfers between devices  48.1 us (28%)
  starting transfers between devices  45.3 us (26%)
  Pallas kernels  37.7 us (22%)
  blocking collectives  26 us (15%)
  local copies, waits for them, and re-layouts  6.82 us (4%)
  other arithmetic  5.89 us (3%)
    ppermute x17, waiting for transfers between devices, turned(): lax.ppermute(value, axis, [(i, (i + step) % size) for i in range(size)])  32.1 us
    ppermute x17, starting transfers between devices, turned(): lax.ppermute(value, axis, [(i, (i + step) % size) for i in range(size)])  30.1 us
    all_to_all x1, blocking collectives, copies_to_all(): return lax.all_to_all(copies, axes, split_axis=0, concat_axis=0, tiled=True)  14.7 us
    pallas_call x1, Pallas kernels, screened_transform(): pl.pallas_call(screened_kernel, grid=(LINE_STEPS + HALF,), in_specs=[pl.B...  13.4 us
    all_to_all x1, waiting for transfers between devices, copies_to_all(): return lax.all_to_all(copies, axes, split_axis=0, concat_axis=0, tiled=True)  12.2 us
    pallas_call x1, Pallas kernels, response(): pl.pallas_call(response_kernel, grid_spec=pltpu.PrefetchScalarGridSpec(nu...  11.8 us
    all_to_all x1, blocking collectives, on_device(): lax.all_to_all(blocks, ('x', 'y'), split_axis=0, concat_axis=0, tiled=True)  11.2 us
    all_to_all x1, starting transfers between devices, on_device(): lax.all_to_all(planes, GA, split_axis=0, concat_axis=0, tiled=True)  9.5 us
  transfers between devices with their start and end apart: 19, of which 8 were waited for; matrix products, arithmetic and copies ran while one was open for 3% of the time, Pallas kernels for 17%

profile of v6, /device:TPU:8, one launch (start us, length us, event | category | flops | bytes accessed | tf_op | source)
XLA Modules:
  0.0 171.1 jit_solution(6976709470591356282)
XLA Ops:
  1.6 4.7 %collective-permute-start.2 = (bf16[8,32,256]{2,1,0:T(8,128)(2,1)S(1)}, bf16[8,32,256]{2,1,0:T(8,128)(2,1)S(1)}, u32[]{:S(2)}, u32[]{:S(2)}) collective-permute-start(bf16[8,32,256]{2,1,0:T(8,128)(2,1)S(1)} %bitcast.81), channel_id=1, source_target_pairs={{0,192},{64,0},{128,64},{192,128},{1,193},{65,1},{129,65},{193,129... | collective-permute-start | bytes 393224 | tf_op jit(solution)/shard_map/ppermute | solution.py:55
  7.0 3.2 %collective-permute-done.2 = bf16[8,32,256]{2,1,0:T(8,128)(2,1)S(1)} collective-permute-done((bf16[8,32,256]{2,1,0:T(8,128)(2,1)S(1)}, bf16[8,32,256]{2,1,0:T(8,128)(2,1)S(1)}, u32[]{:S(2)}, u32[]{:S(2)}) %collective-permute-start.2) | collective-permute-done | bytes 131104 | tf_op jit(solution)/shard_map/ppermute | solution.py:55
  10.2 4.4 %collective-permute-done = bf16[8,32,256]{2,1,0:T(8,128)(2,1)S(1)} collective-permute-done((bf16[8,32,256]{2,1,0:T(8,128)(2,1)S(1)}, bf16[8,32,256]{2,1,0:T(8,128)(2,1)S(1)}, u32[]{:S(2)}, u32[]{:S(2)}) %collective-permute-start) | collective-permute-done | bytes 131104 | tf_op jit(solution)/shard_map/ppermute | solution.py:55
  14.6 3.2 %collective-permute-done.1 = bf16[8,32,256]{2,1,0:T(8,128)(2,1)S(1)} collective-permute-done((bf16[8,32,256]{2,1,0:T(8,128)(2,1)S(1)}, bf16[8,32,256]{2,1,0:T(8,128)(2,1)S(1)}, u32[]{:S(2)}, u32[]{:S(2)}) %collective-permute-start.1) | collective-permute-done | bytes 131104 | tf_op jit(solution)/shard_map/ppermute | solution.py:55
  20.5 2.8 %partner_choice.1 = (bf16[2,8,16,256]{3,2,1,0:T(8,128)(2,1)S(1)}, bf16[8,16,256]{2,1,0:T(8,128)(2,1)S(1)}) custom-call(s32[64]{0:T(128)S(1)} %copy-done, s32[2]{0:T(128)S(1)} %pad_add_fusion.place_ref, bf16[256,256]{1,0:T(8,128)(2,1)S(1)} %fusion.4.flip_ref, bf16[32,32,256]{2,1,0:T(8,128)(2,1)S(1)} %bitcast.74, ...), custom_call_target="tpu_custom_call" | custom-call | tf_op jit(solution)/shard_map/partner_choice/pallas_call | solution.py:173
  23.3 5.2 %collective-permute-start.4 = (bf16[2,8,16,256]{3,2,1,0:T(8,128)(2,1)S(1)}, bf16[2,8,16,256]{3,2,1,0:T(8,128)(2,1)S(1)}, u32[]{:S(2)}, u32[]{:S(2)}) collective-permute-start(bf16[2,8,16,256]{3,2,1,0:T(8,128)(2,1)S(1)} %get-tuple-element.10), channel_id=1, source_target_pairs={{0,1},{1,0},{2,3},{3,2},{4,5},{5,4},{6,7},{7,6},{8,9},{9,8},{10,11... | collective-permute-start | bytes 393224 | tf_op jit(solution)/shard_map/ppermute | solution.py:55
  28.5 7.1 %collective-permute-done.4 = bf16[2,8,16,256]{3,2,1,0:T(8,128)(2,1)S(1)} collective-permute-done((bf16[2,8,16,256]{3,2,1,0:T(8,128)(2,1)S(1)}, bf16[2,8,16,256]{3,2,1,0:T(8,128)(2,1)S(1)}, u32[]{:S(2)}, u32[]{:S(2)}) %collective-permute-start.4) | collective-permute-done | bytes 131104 | tf_op jit(solution)/shard_map/ppermute | solution.py:55
  38.2 2.4 %collective-permute-start.10 = (bf16[2,8,16,256]{3,2,1,0:T(8,128)(2,1)S(1)}, bf16[2,8,16,256]{3,2,1,0:T(8,128)(2,1)S(1)}, u32[]{:S(2)}, u32[]{:S(2)}) collective-permute-start(bf16[2,8,16,256]{3,2,1,0:T(8,128)(2,1)S(1)} %get-tuple-element.20), channel_id=1, source_target_pairs={{0,6},{2,0},{4,2},{6,4},{1,7},{3,1},{5,3},{7,5},{8,14},{10,8},{12,... | collective-permute-start | bytes 393224 | tf_op jit(solution)/shard_map/ppermute | solution.py:55
  42.1 2.7 %collective-permute-start.6 = (bf16[2,8,16,256]{3,2,1,0:T(8,128)(2,1)S(1)}, bf16[2,8,16,256]{3,2,1,0:T(8,128)(2,1)S(1)}, u32[]{:S(2)}, u32[]{:S(2)}) collective-permute-start(bf16[2,8,16,256]{3,2,1,0:T(8,128)(2,1)S(1)} %get-tuple-element.19), channel_id=1, source_target_pairs={{0,16},{8,24},{16,0},{24,8},{1,17},{9,25},{17,1},{25,9},{2,18},{10... | collective-permute-start | bytes 393224 | tf_op jit(solution)/shard_map/ppermute | solution.py:55
  46.3 4.5 %cond_planes.1 = f32[256,1024]{1,0:T(8,128)} custom-call(f32[256,512]{1,0:T(8,128)S(1)} %copy-done.4, bf16[8,16,256]{2,1,0:T(8,128)(2,1)S(1)} %slice.22.home_ref, bf16[8,16,256]{2,1,0:T(8,128)(2,1)S(1)} %get-tuple-element.11.away_ref), custom_call_target="tpu_custom_call" | custom-call | flops 1610612736 | bytes 2097152 | tf_op jit(solution)/shard_map/cond_planes/pallas_call | solution.py:206
  53.6 2.5 %collective-permute-start.15 = (bf16[4,2,8,16,256]{4,3,2,1,0:T(8,128)(2,1)S(1)}, bf16[4,2,8,16,256]{4,3,2,1,0:T(8,128)(2,1)}, u32[]{:S(2)}, u32[]{:S(2)}) collective-permute-start(bf16[4,2,8,16,256]{4,3,2,1,0:T(8,128)(2,1)S(1)} %pad_maximum_fusion.4), channel_id=1, source_target_pairs={{0,16},{8,24},{16,0},{24,8},{1,17},{9,25},{17,1},{25,9},{2,18},{10... | collective-permute-start | bytes 1572872 | tf_op jit(solution)/shard_map/ppermute | solution.py:55
  57.0 3.4 %collective-permute-start.12 = (bf16[4,2,8,16,256]{4,3,2,1,0:T(8,128)(2,1)}, bf16[4,2,8,16,256]{4,3,2,1,0:T(8,128)(2,1)}, u32[]{:S(2)}, u32[]{:S(2)}) collective-permute-start(bf16[4,2,8,16,256]{4,3,2,1,0:T(8,128)(2,1)} %pad_maximum_fusion.3), channel_id=1, source_target_pairs={{0,4},{2,6},{4,0},{6,2},{1,5},{3,7},{5,1},{7,3},{8,12},{10,14},{12... | collective-permute-start | bytes 1572872 | tf_op jit(solution)/shard_map/ppermute | solution.py:55
  60.4 12.4 %collective-permute-done.14 = bf16[4,2,8,16,256]{4,3,2,1,0:T(8,128)(2,1)S(1)} collective-permute-done((bf16[4,2,8,16,256]{4,3,2,1,0:T(8,128)(2,1)S(1)}, bf16[4,2,8,16,256]{4,3,2,1,0:T(8,128)(2,1)S(1)}, u32[]{:S(2)}, u32[]{:S(2)}) %collective-permute-start.14) | collective-permute-done | bytes 524320 | tf_op jit(solution)/shard_map/ppermute | solution.py:55
  74.2 2.2 %copy-done.3 = bf16[256,8192]{1,0:T(8,128)(2,1)S(1)} copy-done((bf16[256,8192]{1,0:T(8,128)(2,1)S(1)}, bf16[256,8192]{1,0:T(8,128)(2,1)}, u32[]{:S(2)}) %copy-start.3) | copy-done | bytes 4194328
  76.3 13.4 %screened_transform.1.refs_8_.refs_9_ = bf16[17,512,256]{2,1,0:T(8,128)(2,1)S(1)} custom-call(s32[32,1,256]{2,1,0:T(1,128)S(1)} %bitcast.77, bf16[96,32]{1,0:T(8,128)(2,1)S(1)} %copy-done.7, bf16[2,256,256]{2,1,0:T(8,128)(2,1)S(1)} %copy-done.5, bf16[2,256,256]{2,1,0:T(8,128)(2,1)S(1)} %copy-done.6, bf16[256,8192]{1,0:T(8,128)(2,1)S(1)} %copy-done.3), custom_call_target="tpu_custom_call" | custom-call | flops 13690208256 | bytes 9437184 | tf_op jit(solution)/shard_map/screened_transform/pallas_call | solution.py:131
  89.8 2.0 %copy-done.8 = bf16[17,512,256]{2,1,0:T(8,128)(2,1)} copy-done((bf16[17,512,256]{2,1,0:T(8,128)(2,1)}, bf16[17,512,256]{2,1,0:T(8,128)(2,1)S(1)}, u32[]{:S(2)}) %copy-start.8) | copy-done | bytes 4456472
  91.8 9.5 %all-to-all-start = ((f32[32,8,1024]{2,1,0:T(8,128)}), f32[32,8,1024]{2,1,0:T(8,128)S(1)}, u32[]{:S(2)}, u32[]{:S(2)}) async-start(f32[32,8,1024]{2,1,0:T(8,128)} %bitcast.24), calls=%async_computation | async-start | bytes 2097152 | tf_op jit(solution)/shard_map/all_to_all | solution.py:414
  104.8 11.8 %valence_response.1.r_ref = f32[1024,256]{1,0:T(8,128)S(1)} custom-call(s32[1]{0:T(128)} %bitcast.26.place_ref, bf16[32,8,16,256]{3,2,1,0:T(8,128)(2,1)S(1)} %bitcast.69, bf16[32,8,16,256]{3,2,1,0:T(8,128)(2,1)S(1)} %bitcast.65, bf16[32,8,16,256]{3,2,1,0:T(8,128)(2,1)S(1)} %bitcast.70, bf16[32,8,16,256]{3,2,1,0:T(8,128)(2,1)S(1)} %bitcast.66, ...), custom_call_target="tpu_custom_call" | custom-call | flops 36507222016 | bytes 9437184 | tf_op jit(solution)/shard_map/valence_response/pallas_call | solution.py:277
  116.6 3.8 %all-to-all-done = f32[32,8,1024]{2,1,0:T(8,128)S(1)} async-done(((f32[32,8,1024]{2,1,0:T(8,128)}), f32[32,8,1024]{2,1,0:T(8,128)S(1)}, u32[]{:S(2)}, u32[]{:S(2)}) %all-to-all-start) | async-done | bytes 1048608 | tf_op jit(solution)/shard_map/all_to_all | solution.py:414
  120.5 3.7 %cond_spectrum.1.cond_ref = bf16[1024,256]{1,0:T(8,128)(2,1)S(1)} custom-call(f32[256,256]{1,0:T(8,128)S(1)} %get-tuple-element.23.cos_ref, f32[256,256]{1,0:T(8,128)S(1)} %get-tuple-element.22.sin_ref, f32[256,1024]{1,0:T(8,128)S(1)} %bitcast.75), custom_call_target="tpu_custom_call" | custom-call | flops 1610612736 | bytes 2097152 | tf_op jit(solution)/shard_map/cond_spectrum/pallas_call | solution.py:311
  124.7 11.2 %all_to_all.26 = f32[32,16,128]{2,1,0:T(8,128)S(1)} all-to-all(f32[32,16,128]{2,1,0:T(8,128)S(1)} %kernel_blocks.1), channel_id=1, replica_groups=mesh['zl'=4,'co'=2,'x'=4,'y'=4,'zh'=2] {'x','y'}, dimensions={0} | all-to-all | bytes 524288 | tf_op jit(solution)/shard_map/all_to_all | solution.py:421
  136.7 5.7 %all-to-all-start.2 = ((f32[16,2,16,128]{3,2,1,0:T(8,128)}), f32[16,2,16,128]{3,2,1,0:T(8,128)S(1)}, u32[]{:S(2)}, u32[]{:S(2)}) async-start(f32[16,2,16,128]{3,2,1,0:T(8,128)} %broadcast_in_dim.16), calls=%async_computation.2 | async-start | bytes 524288 | tf_op jit(solution)/shard_map/all_to_all | solution.py:65
  142.5 12.2 %all-to-all-done.2 = f32[16,2,16,128]{3,2,1,0:T(8,128)S(1)} async-done(((f32[16,2,16,128]{3,2,1,0:T(8,128)}), f32[16,2,16,128]{3,2,1,0:T(8,128)S(1)}, u32[]{:S(2)}, u32[]{:S(2)}) %all-to-all-start.2) | async-done | bytes 262176 | tf_op jit(solution)/shard_map/all_to_all | solution.py:65
  155.4 14.7 %all_to_all.27.full_ref = f32[16,2,32,128]{3,2,1,0:T(8,128)S(1)} all-to-all(f32[16,2,32,128]{3,2,1,0:T(8,128)S(1)} %broadcast_in_dim.21), channel_id=1, replica_groups=mesh['zl'=4,'co'=2,'x'=4,'y'=4,'zh'=2] {'x','y'}, dimensions={0} | all-to-all | bytes 1048576 | tf_op jit(solution)/shard_map/all_to_all | solution.py:65
  (75 shorter events, 21.2 us)
Async XLA Ops:
  0.6 45.7 %copy-start.4 = (f32[256,512]{1,0:T(8,128)S(1)}, f32[256,512]{1,0:T(8,128)}, u32[]{:S(2)}) copy-start(f32[256,512]{1,0:T(8,128)} %constant.192.clone.table_ref) | copy-start | bytes 1572868
  1.6 8.6 %collective-permute-start.2 = (bf16[8,32,256]{2,1,0:T(8,128)(2,1)S(1)}, bf16[8,32,256]{2,1,0:T(8,128)(2,1)S(1)}, u32[]{:S(2)}, u32[]{:S(2)}) collective-permute-start(bf16[8,32,256]{2,1,0:T(8,128)(2,1)S(1)} %bitcast.81), channel_id=1, source_target_pairs={{0,192},{64,0},{128,64},{192,128},{1,193},{65,1},{129,65},{193,129... | collective-permute-start | bytes 393224 | tf_op jit(solution)/shard_map/ppermute | solution.py:55
  6.3 8.3 %collective-permute-start = (bf16[8,32,256]{2,1,0:T(8,128)(2,1)S(1)}, bf16[8,32,256]{2,1,0:T(8,128)(2,1)S(1)}, u32[]{:S(2)}, u32[]{:S(2)}) collective-permute-start(bf16[8,32,256]{2,1,0:T(8,128)(2,1)S(1)} %bitcast.82), channel_id=1, source_target_pairs={{0,64},{64,128},{128,192},{192,0},{1,65},{65,129},{129,193},{193,1... | collective-permute-start | bytes 393224 | tf_op jit(solution)/shard_map/ppermute | solution.py:55
  6.3 11.5 %collective-permute-start.1 = (bf16[8,32,256]{2,1,0:T(8,128)(2,1)S(1)}, bf16[8,32,256]{2,1,0:T(8,128)(2,1)S(1)}, u32[]{:S(2)}, u32[]{:S(2)}) collective-permute-start(bf16[8,32,256]{2,1,0:T(8,128)(2,1)S(1)} %bitcast.83), channel_id=1, source_target_pairs={{0,128},{64,192},{128,0},{192,64},{1,129},{65,193},{129,1},{193,65... | collective-permute-start | bytes 393224 | tf_op jit(solution)/shard_map/ppermute | solution.py:55
  17.9 2.0 %collective-permute-start.3 = (bf16[32,32,256]{2,1,0:T(8,128)(2,1)S(1)}, bf16[32,32,256]{2,1,0:T(8,128)(2,1)S(1)}, u32[]{:S(2)}, u32[]{:S(2)}) collective-permute-start(bf16[32,32,256]{2,1,0:T(8,128)(2,1)S(1)} %bitcast.73), channel_id=1, source_target_pairs={{0,32},{32,0},{1,33},{33,1},{2,34},{34,2},{3,35},{35,3},{4,36},{36... | collective-permute-start | bytes 1572872 | tf_op jit(solution)/shard_map/ppermute | solution.py:55
  23.3 12.3 %collective-permute-start.4 = (bf16[2,8,16,256]{3,2,1,0:T(8,128)(2,1)S(1)}, bf16[2,8,16,256]{3,2,1,0:T(8,128)(2,1)S(1)}, u32[]{:S(2)}, u32[]{:S(2)}) collective-permute-start(bf16[2,8,16,256]{3,2,1,0:T(8,128)(2,1)S(1)} %get-tuple-element.10), channel_id=1, source_target_pairs={{0,1},{1,0},{2,3},{3,2},{4,5},{5,4},{6,7},{7,6},{8,9},{9,8},{10,11... | collective-permute-start | bytes 393224 | tf_op jit(solution)/shard_map/ppermute | solution.py:55
  35.6 9.2 %collective-permute-start.8 = (bf16[2,8,16,256]{3,2,1,0:T(8,128)(2,1)S(1)}, bf16[2,8,16,256]{3,2,1,0:T(8,128)(2,1)S(1)}, u32[]{:S(2)}, u32[]{:S(2)}) collective-permute-start(bf16[2,8,16,256]{3,2,1,0:T(8,128)(2,1)S(1)} %get-tuple-element.20), channel_id=1, source_target_pairs={{0,2},{2,4},{4,6},{6,0},{1,3},{3,5},{5,7},{7,1},{8,10},{10,12},{12... | collective-permute-start | bytes 393224 | tf_op jit(solution)/shard_map/ppermute | solution.py:55
  37.3 13.5 %collective-permute-start.9 = (bf16[2,8,16,256]{3,2,1,0:T(8,128)(2,1)S(1)}, bf16[2,8,16,256]{3,2,1,0:T(8,128)(2,1)S(1)}, u32[]{:S(2)}, u32[]{:S(2)}) collective-permute-start(bf16[2,8,16,256]{3,2,1,0:T(8,128)(2,1)S(1)} %get-tuple-element.20), channel_id=1, source_target_pairs={{0,4},{2,6},{4,0},{6,2},{1,5},{3,7},{5,1},{7,3},{8,12},{10,14},{12... | collective-permute-start | bytes 393224 | tf_op jit(solution)/shard_map/ppermute | solution.py:55
  38.2 12.6 %collective-permute-start.10 = (bf16[2,8,16,256]{3,2,1,0:T(8,128)(2,1)S(1)}, bf16[2,8,16,256]{3,2,1,0:T(8,128)(2,1)S(1)}, u32[]{:S(2)}, u32[]{:S(2)}) collective-permute-start(bf16[2,8,16,256]{3,2,1,0:T(8,128)(2,1)S(1)} %get-tuple-element.20), channel_id=1, source_target_pairs={{0,6},{2,0},{4,2},{6,4},{1,7},{3,1},{5,3},{7,5},{8,14},{10,8},{12,... | collective-permute-start | bytes 393224 | tf_op jit(solution)/shard_map/ppermute | solution.py:55
  40.6 10.2 %collective-permute-start.5 = (bf16[2,8,16,256]{3,2,1,0:T(8,128)(2,1)S(1)}, bf16[2,8,16,256]{3,2,1,0:T(8,128)(2,1)S(1)}, u32[]{:S(2)}, u32[]{:S(2)}) collective-permute-start(bf16[2,8,16,256]{3,2,1,0:T(8,128)(2,1)S(1)} %get-tuple-element.19), channel_id=1, source_target_pairs={{0,8},{8,16},{16,24},{24,0},{1,9},{9,17},{17,25},{25,1},{2,10},{10... | collective-permute-start | bytes 393224 | tf_op jit(solution)/shard_map/ppermute | solution.py:55
  42.1 8.8 %collective-permute-start.6 = (bf16[2,8,16,256]{3,2,1,0:T(8,128)(2,1)S(1)}, bf16[2,8,16,256]{3,2,1,0:T(8,128)(2,1)S(1)}, u32[]{:S(2)}, u32[]{:S(2)}) collective-permute-start(bf16[2,8,16,256]{3,2,1,0:T(8,128)(2,1)S(1)} %get-tuple-element.19), channel_id=1, source_target_pairs={{0,16},{8,24},{16,0},{24,8},{1,17},{9,25},{17,1},{25,9},{2,18},{10... | collective-permute-start | bytes 393224 | tf_op jit(solution)/shard_map/ppermute | solution.py:55
  44.9 6.0 %collective-permute-start.7 = (bf16[2,8,16,256]{3,2,1,0:T(8,128)(2,1)S(1)}, bf16[2,8,16,256]{3,2,1,0:T(8,128)(2,1)S(1)}, u32[]{:S(2)}, u32[]{:S(2)}) collective-permute-start(bf16[2,8,16,256]{3,2,1,0:T(8,128)(2,1)S(1)} %get-tuple-element.19), channel_id=1, source_target_pairs={{0,24},{8,0},{16,8},{24,16},{1,25},{9,1},{17,9},{25,17},{2,26},{10... | collective-permute-start | bytes 393224 | tf_op jit(solution)/shard_map/ppermute | solution.py:55
  50.8 23.4 %copy-start.5 = (bf16[2,256,256]{2,1,0:T(8,128)(2,1)S(1)}, bf16[2,256,256]{2,1,0:T(8,128)(2,1)}, u32[]{:S(2)}) copy-start(bf16[2,256,256]{2,1,0:T(8,128)(2,1)} %constant.194.clone.high_ref) | copy-start | bytes 786436
  50.8 23.4 %copy-start.6 = (bf16[2,256,256]{2,1,0:T(8,128)(2,1)S(1)}, bf16[2,256,256]{2,1,0:T(8,128)(2,1)}, u32[]{:S(2)}) copy-start(bf16[2,256,256]{2,1,0:T(8,128)(2,1)} %constant.195.clone.low_ref) | copy-start | bytes 786436
  50.8 23.4 %copy-start.7 = (bf16[96,32]{1,0:T(8,128)(2,1)S(1)}, bf16[96,32]{1,0:T(8,128)(2,1)}, u32[]{:S(2)}) copy-start(bf16[96,32]{1,0:T(8,128)(2,1)} %constant.193.clone.line_ref) | copy-start | bytes 18436
  51.8 21.0 %collective-permute-start.14 = (bf16[4,2,8,16,256]{4,3,2,1,0:T(8,128)(2,1)S(1)}, bf16[4,2,8,16,256]{4,3,2,1,0:T(8,128)(2,1)S(1)}, u32[]{:S(2)}, u32[]{:S(2)}) collective-permute-start(bf16[4,2,8,16,256]{4,3,2,1,0:T(8,128)(2,1)S(1)} %pad_maximum_fusion.4), channel_id=1, source_target_pairs={{0,8},{8,16},{16,24},{24,0},{1,9},{9,17},{17,25},{25,1},{2,10},{10... | collective-permute-start | bytes 1572872 | tf_op jit(solution)/shard_map/ppermute | solution.py:55
  53.6 47.7 %collective-permute-start.15 = (bf16[4,2,8,16,256]{4,3,2,1,0:T(8,128)(2,1)S(1)}, bf16[4,2,8,16,256]{4,3,2,1,0:T(8,128)(2,1)}, u32[]{:S(2)}, u32[]{:S(2)}) collective-permute-start(bf16[4,2,8,16,256]{4,3,2,1,0:T(8,128)(2,1)S(1)} %pad_maximum_fusion.4), channel_id=1, source_target_pairs={{0,16},{8,24},{16,0},{24,8},{1,17},{9,25},{17,1},{25,9},{2,18},{10... | collective-permute-start | bytes 1572872 | tf_op jit(solution)/shard_map/ppermute | solution.py:55
  56.1 45.2 %collective-permute-start.16 = (bf16[4,2,8,16,256]{4,3,2,1,0:T(8,128)(2,1)S(1)}, bf16[4,2,8,16,256]{4,3,2,1,0:T(8,128)(2,1)}, u32[]{:S(2)}, u32[]{:S(2)}) collective-permute-start(bf16[4,2,8,16,256]{4,3,2,1,0:T(8,128)(2,1)S(1)} %pad_maximum_fusion.4), channel_id=1, source_target_pairs={{0,24},{8,0},{16,8},{24,16},{1,25},{9,1},{17,9},{25,17},{2,26},{10... | collective-permute-start | bytes 1572872 | tf_op jit(solution)/shard_map/ppermute | solution.py:55
  57.0 46.0 %collective-permute-start.11 = (bf16[4,2,8,16,256]{4,3,2,1,0:T(8,128)(2,1)}, bf16[4,2,8,16,256]{4,3,2,1,0:T(8,128)(2,1)}, u32[]{:S(2)}, u32[]{:S(2)}) collective-permute-start(bf16[4,2,8,16,256]{4,3,2,1,0:T(8,128)(2,1)} %pad_maximum_fusion.3), channel_id=1, source_target_pairs={{0,2},{2,4},{4,6},{6,0},{1,3},{3,5},{5,7},{7,1},{8,10},{10,12},{12... | collective-permute-start | bytes 1572872 | tf_op jit(solution)/shard_map/ppermute | solution.py:55
  57.0 46.1 %collective-permute-start.12 = (bf16[4,2,8,16,256]{4,3,2,1,0:T(8,128)(2,1)}, bf16[4,2,8,16,256]{4,3,2,1,0:T(8,128)(2,1)}, u32[]{:S(2)}, u32[]{:S(2)}) collective-permute-start(bf16[4,2,8,16,256]{4,3,2,1,0:T(8,128)(2,1)} %pad_maximum_fusion.3), channel_id=1, source_target_pairs={{0,4},{2,6},{4,0},{6,2},{1,5},{3,7},{5,1},{7,3},{8,12},{10,14},{12... | collective-permute-start | bytes 1572872 | tf_op jit(solution)/shard_map/ppermute | solution.py:55
  72.8 30.2 %collective-permute-start.13 = (bf16[4,2,8,16,256]{4,3,2,1,0:T(8,128)(2,1)}, bf16[4,2,8,16,256]{4,3,2,1,0:T(8,128)(2,1)}, u32[]{:S(2)}, u32[]{:S(2)}) collective-permute-start(bf16[4,2,8,16,256]{4,3,2,1,0:T(8,128)(2,1)} %pad_maximum_fusion.3), channel_id=1, source_target_pairs={{0,6},{2,0},{4,2},{6,4},{1,7},{3,1},{5,3},{7,5},{8,14},{10,8},{12,... | collective-permute-start | bytes 1572872 | tf_op jit(solution)/shard_map/ppermute | solution.py:55
  91.8 28.6 %all-to-all-start = ((f32[32,8,1024]{2,1,0:T(8,128)}), f32[32,8,1024]{2,1,0:T(8,128)S(1)}, u32[]{:S(2)}, u32[]{:S(2)}) async-start(f32[32,8,1024]{2,1,0:T(8,128)} %bitcast.24), calls=%async_computation | async-start | bytes 2097152 | tf_op jit(solution)/shard_map/all_to_all | solution.py:414
  124.1 30.8 %copy-start.1 = (s32[64]{0:T(128)S(1)}, s32[64]{0:T(128)}, u32[]{:S(2)}) copy-start(s32[64]{0:T(128)} %partner_ref.1) | copy-start | bytes 772
  136.7 18.0 %all-to-all-start.2 = ((f32[16,2,16,128]{3,2,1,0:T(8,128)}), f32[16,2,16,128]{3,2,1,0:T(8,128)S(1)}, u32[]{:S(2)}, u32[]{:S(2)}) async-start(f32[16,2,16,128]{3,2,1,0:T(8,128)} %broadcast_in_dim.16), calls=%async_computation.2 | async-start | bytes 524288 | tf_op jit(solution)/shard_map/all_to_all | solution.py:65
  (7 other events, 36.5 us)

commit v7 on v6

--- a/solution.py
+++ b/solution.py
@@ -71,8 +71,9 @@
     )
 
 
-def screened_kernel(gmap_ref, line_ref, high_ref, low_ref, w_ref, out_ref, lines_ref):
+def screened_kernel(gmap_ref, line_ref, high_ref, low_ref, w_ref, out_ref, end_ref, lines_ref):
     step = pl.program_id(0)
+    end_ref[...] = jnp.zeros_like(end_ref)
 
     @pl.when(step < LINE_STEPS)
     def _():
@@ -138,8 +139,14 @@
             pl.BlockSpec((2, 256, 256), lambda i: (0, 0, 0)),
             pl.BlockSpec((256, n * 256), lambda i: (0, jnp.minimum(i, last))),
         ],
-        out_specs=pl.BlockSpec((1, 512, 256), lambda i: (jnp.maximum(i - LINE_STEPS, 0), 0, 0)),
-        out_shape=jax.ShapeDtypeStruct((HALF, 512, 256), BF),
+        out_specs=[
+            pl.BlockSpec((1, 512, 256), lambda i: (jnp.maximum(i - LINE_STEPS, 0), 0, 0)),
+            pl.BlockSpec((8, 128), lambda i: (0, 0)),
+        ],
+        out_shape=[
+            jax.ShapeDtypeStruct((HALF, 512, 256), BF),
+            jax.ShapeDtypeStruct((8, 128), F32),
+        ],
         scratch_shapes=[pltpu.VMEM((2 * HALF, PLANE, 256), F32)],
         compiler_params=pltpu.CompilerParams(vmem_limit_bytes=40 * MIB),
         cost_estimate=pl.CostEstimate(
@@ -407,10 +414,10 @@
     home, away = spread(vals[:, 0], "x"), spread(vals[:, 1], "y")
     home, away, planes, screened = lax.optimization_barrier((home, away, planes, screened))
     homes = [home] + [turned(home, "y", d) for d in range(1, 4)]
-    aways = [away] + [turned(away, "x", d) for d in range(1, 4)]
-    wide = screened_transform(screened, gmap)
-
-    wide, planes = lax.optimization_barrier((wide, planes))
+    aways = [away] + [turned(away, "x", d) for d in range(1, 3)]
+    wide, end = screened_transform(screened, gmap)
+    away, planes, end = lax.optimization_barrier((away, planes, end))
+    aways.append(turned(away, "x", 3))
     columns = lax.all_to_all(planes, GA, split_axis=0, concat_axis=0, tiled=True)
     home = jnp.stack(homes).reshape(32, 8, 16, 256)
     away = jnp.stack(aways).reshape(32, 8, 16, 256)

time: 172 us -> 162 us (0.942)
  waiting for transfers between devices: 48.1 us -> 28.7 us
  starting transfers between devices: 45.3 us -> 55.1 us
  local copies, waits for them, and re-layouts: 6.82 us -> 4.78 us
    ppermute x17, waiting for transfers between devices: 32.1 us -> 16.5 us  [turned(): lax.ppermute(value, axis, [(i, (i + step) % size) for i in range(size)])]
    all_to_all x1, starting transfers between devices: 5.74 us -> 12.1 us  [copies_to_all(): return lax.all_to_all(copies, axes, split_axis=0, concat_axis=0, tiled=True)]
    all_to_all x1, waiting for transfers between devices: 3.82 us -> 0.01 us  [on_device(): lax.all_to_all(planes, GA, split_axis=0, concat_axis=0, tiled=True)]
    all_to_all x1, starting transfers between devices: 9.5 us -> 11.6 us  [on_device(): lax.all_to_all(planes, GA, split_axis=0, concat_axis=0, tiled=True)]
    unnamed x24 -> x16, local copies, waits for them, and re-layouts: 4.92 us -> 2.88 us
  transfers between devices with their start and end apart: 19 -> 19, of which waited for: 8 -> 6; matrix products, arithmetic and copies ran while one was open for 3% -> 3% of each run, Pallas kernels for 17% -> 19%
where the time goes in v7:
time: 162 us
  starting transfers between devices  55.1 us (34%)
  Pallas kernels  38.2 us (24%)
  waiting for transfers between devices  28.7 us (18%)
  blocking collectives  27.6 us (17%)
  other arithmetic  5.74 us (4%)
  local copies, waits for them, and re-layouts  4.78 us (3%)
    ppermute x17, starting transfers between devices, turned(): lax.ppermute(value, axis, [(i, (i + step) % size) for i in range(size)])  31.4 us
    ppermute x17, waiting for transfers between devices, turned(): lax.ppermute(value, axis, [(i, (i + step) % size) for i in range(size)])  16.5 us
    all_to_all x1, blocking collectives, copies_to_all(): return lax.all_to_all(copies, axes, split_axis=0, concat_axis=0, tiled=True)  14.7 us
    pallas_call x1, Pallas kernels, screened_transform(): pl.pallas_call(screened_kernel, grid=(LINE_STEPS + HALF,), in_specs=[pl.B...  13.9 us
    all_to_all x1, blocking collectives, on_device(): lax.all_to_all(blocks, ('x', 'y'), split_axis=0, concat_axis=0, tiled=True)  12.9 us
    all_to_all x1, waiting for transfers between devices, copies_to_all(): return lax.all_to_all(copies, axes, split_axis=0, concat_axis=0, tiled=True)  12.2 us
    all_to_all x1, starting transfers between devices, copies_to_all(): return lax.all_to_all(copies, axes, split_axis=0, concat_axis=0, tiled=True)  12.1 us
    pallas_call x1, Pallas kernels, response(): pl.pallas_call(response_kernel, grid_spec=pltpu.PrefetchScalarGridSpec(nu...  11.8 us
  transfers between devices with their start and end apart: 19, of which 6 were waited for; matrix products, arithmetic and copies ran while one was open for 3% of the time, Pallas kernels for 19%

profile of v7, /device:TPU:8, one launch (start us, length us, event | category | flops | bytes accessed | tf_op | source)
XLA Modules:
  0.0 161.5 jit_solution(7947477995121183442)
XLA Ops:
  1.6 4.7 %collective-permute-start.2 = (bf16[8,32,256]{2,1,0:T(8,128)(2,1)S(1)}, bf16[8,32,256]{2,1,0:T(8,128)(2,1)S(1)}, u32[]{:S(2)}, u32[]{:S(2)}) collective-permute-start(bf16[8,32,256]{2,1,0:T(8,128)(2,1)S(1)} %bitcast.81), channel_id=1, source_target_pairs={{0,192},{64,0},{128,64},{192,128},{1,193},{65,1},{129,65},{193,129... | collective-permute-start | bytes 393224 | tf_op jit(solution)/shard_map/ppermute | solution.py:55
  7.0 3.2 %collective-permute-done.2 = bf16[8,32,256]{2,1,0:T(8,128)(2,1)S(1)} collective-permute-done((bf16[8,32,256]{2,1,0:T(8,128)(2,1)S(1)}, bf16[8,32,256]{2,1,0:T(8,128)(2,1)S(1)}, u32[]{:S(2)}, u32[]{:S(2)}) %collective-permute-start.2) | collective-permute-done | bytes 131104 | tf_op jit(solution)/shard_map/ppermute | solution.py:55
  10.2 7.3 %collective-permute-done.1 = bf16[8,32,256]{2,1,0:T(8,128)(2,1)S(1)} collective-permute-done((bf16[8,32,256]{2,1,0:T(8,128)(2,1)S(1)}, bf16[8,32,256]{2,1,0:T(8,128)(2,1)S(1)}, u32[]{:S(2)}, u32[]{:S(2)}) %collective-permute-start.1) | collective-permute-done | bytes 131104 | tf_op jit(solution)/shard_map/ppermute | solution.py:55
  17.9 1.8 %collective-permute-done.3.far_ref = bf16[32,32,256]{2,1,0:T(8,128)(2,1)S(1)} collective-permute-done((bf16[32,32,256]{2,1,0:T(8,128)(2,1)S(1)}, bf16[32,32,256]{2,1,0:T(8,128)(2,1)S(1)}, u32[]{:S(2)}, u32[]{:S(2)}) %collective-permute-start.3) | collective-permute-done | bytes 524320 | tf_op jit(solution)/shard_map/ppermute | solution.py:55
  20.3 2.8 %partner_choice.1 = (bf16[2,8,16,256]{3,2,1,0:T(8,128)(2,1)S(1)}, bf16[8,16,256]{2,1,0:T(8,128)(2,1)S(1)}) custom-call(s32[64]{0:T(128)S(1)} %copy-done, s32[2]{0:T(128)S(1)} %pad_add_fusion.place_ref, bf16[256,256]{1,0:T(8,128)(2,1)S(1)} %fusion.4.flip_ref, bf16[32,32,256]{2,1,0:T(8,128)(2,1)S(1)} %bitcast.74, ...), custom_call_target="tpu_custom_call" | custom-call | tf_op jit(solution)/shard_map/partner_choice/pallas_call | solution.py:180
  23.1 5.5 %collective-permute-start.4 = (bf16[2,8,16,256]{3,2,1,0:T(8,128)(2,1)S(1)}, bf16[2,8,16,256]{3,2,1,0:T(8,128)(2,1)S(1)}, u32[]{:S(2)}, u32[]{:S(2)}) collective-permute-start(bf16[2,8,16,256]{3,2,1,0:T(8,128)(2,1)S(1)} %get-tuple-element.11), channel_id=1, source_target_pairs={{0,1},{1,0},{2,3},{3,2},{4,5},{5,4},{6,7},{7,6},{8,9},{9,8},{10,11... | collective-permute-start | bytes 393224 | tf_op jit(solution)/shard_map/ppermute | solution.py:55
  28.6 4.0 %collective-permute-done.4 = bf16[2,8,16,256]{3,2,1,0:T(8,128)(2,1)S(1)} collective-permute-done((bf16[2,8,16,256]{3,2,1,0:T(8,128)(2,1)S(1)}, bf16[2,8,16,256]{3,2,1,0:T(8,128)(2,1)S(1)}, u32[]{:S(2)}, u32[]{:S(2)}) %collective-permute-start.4) | collective-permute-done | bytes 131104 | tf_op jit(solution)/shard_map/ppermute | solution.py:55
  32.6 2.8 %collective-permute-start.7 = (bf16[2,8,16,256]{3,2,1,0:T(8,128)(2,1)S(1)}, bf16[2,8,16,256]{3,2,1,0:T(8,128)(2,1)S(1)}, u32[]{:S(2)}, u32[]{:S(2)}) collective-permute-start(bf16[2,8,16,256]{3,2,1,0:T(8,128)(2,1)S(1)} %get-tuple-element.21), channel_id=1, source_target_pairs={{0,24},{8,0},{16,8},{24,16},{1,25},{9,1},{17,9},{25,17},{2,26},{10... | collective-permute-start | bytes 393224 | tf_op jit(solution)/shard_map/ppermute | solution.py:55
  37.6 2.6 %collective-permute-start.9 = (bf16[2,8,16,256]{3,2,1,0:T(8,128)(2,1)S(1)}, bf16[2,8,16,256]{3,2,1,0:T(8,128)(2,1)S(1)}, u32[]{:S(2)}, u32[]{:S(2)}) collective-permute-start(bf16[2,8,16,256]{3,2,1,0:T(8,128)(2,1)S(1)} %get-tuple-element.22), channel_id=1, source_target_pairs={{0,4},{2,6},{4,0},{6,2},{1,5},{3,7},{5,1},{7,3},{8,12},{10,14},{12... | collective-permute-start | bytes 393224 | tf_op jit(solution)/shard_map/ppermute | solution.py:55
  40.3 1.7 %collective-permute-start.8 = (bf16[2,8,16,256]{3,2,1,0:T(8,128)(2,1)S(1)}, bf16[2,8,16,256]{3,2,1,0:T(8,128)(2,1)S(1)}, u32[]{:S(2)}, u32[]{:S(2)}) collective-permute-start(bf16[2,8,16,256]{3,2,1,0:T(8,128)(2,1)S(1)} %get-tuple-element.22), channel_id=1, source_target_pairs={{0,2},{2,4},{4,6},{6,0},{1,3},{3,5},{5,7},{7,1},{8,10},{10,12},{12... | collective-permute-start | bytes 393224 | tf_op jit(solution)/shard_map/ppermute | solution.py:55
  42.1 4.4 %cond_planes.1 = f32[256,1024]{1,0:T(8,128)} custom-call(f32[256,512]{1,0:T(8,128)S(1)} %copy-done.4, bf16[8,16,256]{2,1,0:T(8,128)(2,1)S(1)} %slice.22.home_ref, bf16[8,16,256]{2,1,0:T(8,128)(2,1)S(1)} %get-tuple-element.12.away_ref), custom_call_target="tpu_custom_call" | custom-call | flops 1610612736 | bytes 2097152 | tf_op jit(solution)/shard_map/cond_planes/pallas_call | solution.py:213
  47.6 1.8 %collective-permute-start.13 = (bf16[4,2,8,16,256]{4,3,2,1,0:T(8,128)(2,1)S(1)}, bf16[4,2,8,16,256]{4,3,2,1,0:T(8,128)(2,1)}, u32[]{:S(2)}, u32[]{:S(2)}) collective-permute-start(bf16[4,2,8,16,256]{4,3,2,1,0:T(8,128)(2,1)S(1)} %pad_maximum_fusion.3), channel_id=1, source_target_pairs={{0,6},{2,0},{4,2},{6,4},{1,7},{3,1},{5,3},{7,5},{8,14},{10,8},{12,... | collective-permute-start | bytes 1572872 | tf_op jit(solution)/shard_map/ppermute | solution.py:55
  52.7 1.9 %collective-permute-start.15 = (bf16[4,2,8,16,256]{4,3,2,1,0:T(8,128)(2,1)}, bf16[4,2,8,16,256]{4,3,2,1,0:T(8,128)(2,1)}, u32[]{:S(2)}, u32[]{:S(2)}) collective-permute-start(bf16[4,2,8,16,256]{4,3,2,1,0:T(8,128)(2,1)} %pad_maximum_fusion.4), channel_id=1, source_target_pairs={{0,16},{8,24},{16,0},{24,8},{1,17},{9,25},{17,1},{25,9},{2,18},{10... | collective-permute-start | bytes 1572872 | tf_op jit(solution)/shard_map/ppermute | solution.py:55
  54.7 2.3 %collective-permute-start.14 = (bf16[4,2,8,16,256]{4,3,2,1,0:T(8,128)(2,1)}, bf16[4,2,8,16,256]{4,3,2,1,0:T(8,128)(2,1)}, u32[]{:S(2)}, u32[]{:S(2)}) collective-permute-start(bf16[4,2,8,16,256]{4,3,2,1,0:T(8,128)(2,1)} %pad_maximum_fusion.4), channel_id=1, source_target_pairs={{0,8},{8,16},{16,24},{24,0},{1,9},{9,17},{17,25},{25,1},{2,10},{10... | collective-permute-start | bytes 1572872 | tf_op jit(solution)/shard_map/ppermute | solution.py:55
  56.9 11.6 %all-to-all-start = ((f32[32,8,1024]{2,1,0:T(8,128)}), f32[32,8,1024]{2,1,0:T(8,128)S(1)}, u32[]{:S(2)}, u32[]{:S(2)}) async-start(f32[32,8,1024]{2,1,0:T(8,128)} %bitcast.23), calls=%async_computation | async-start | bytes 2097152 | tf_op jit(solution)/shard_map/all_to_all | solution.py:421
  68.6 3.0 %collective-permute-start.16 = (bf16[4,2,8,16,256]{4,3,2,1,0:T(8,128)(2,1)}, bf16[4,2,8,16,256]{4,3,2,1,0:T(8,128)(2,1)S(1)}, u32[]{:S(2)}, u32[]{:S(2)}) collective-permute-start(bf16[4,2,8,16,256]{4,3,2,1,0:T(8,128)(2,1)} %pad_maximum_fusion.4), channel_id=1, source_target_pairs={{0,24},{8,0},{16,8},{24,16},{1,25},{9,1},{17,9},{25,17},{2,26},{10... | collective-permute-start | bytes 1572872 | tf_op jit(solution)/shard_map/ppermute | solution.py:55
  71.6 2.2 %copy-done.3 = bf16[256,8192]{1,0:T(8,128)(2,1)S(1)} copy-done((bf16[256,8192]{1,0:T(8,128)(2,1)S(1)}, bf16[256,8192]{1,0:T(8,128)(2,1)}, u32[]{:S(2)}) %copy-start.3) | copy-done | bytes 4194328
  73.8 13.9 %screened_transform.1 = (bf16[17,512,256]{2,1,0:T(8,128)(2,1)S(1)}, f32[8,128]{1,0:T(8,128)}) custom-call(s32[32,1,256]{2,1,0:T(1,128)S(1)} %bitcast.77, bf16[96,32]{1,0:T(8,128)(2,1)S(1)} %copy-done.7, bf16[2,256,256]{2,1,0:T(8,128)(2,1)S(1)} %copy-done.5, bf16[2,256,256]{2,1,0:T(8,128)(2,1)S(1)} %copy-done.6, bf16[256,8192]{1,0:T(8,128)(2,1)S(1)} %copy-done.3), custom_call_target="tpu_custom_call" | custom-call | flops 13690208256 | bytes 9437184 | tf_op jit(solution)/shard_map/screened_transform/pallas_call | solution.py:132
  91.0 11.8 %valence_response.1.r_ref = f32[1024,256]{1,0:T(8,128)S(1)} custom-call(s32[1]{0:T(128)} %bitcast.25.place_ref, bf16[32,8,16,256]{3,2,1,0:T(8,128)(2,1)S(1)} %bitcast.65, bf16[32,8,16,256]{3,2,1,0:T(8,128)(2,1)S(1)} %bitcast.69, bf16[32,8,16,256]{3,2,1,0:T(8,128)(2,1)S(1)} %bitcast.66, bf16[32,8,16,256]{3,2,1,0:T(8,128)(2,1)S(1)} %bitcast.70, ...), custom_call_target="tpu_custom_call" | custom-call | flops 36507222016 | bytes 9437184 | tf_op jit(solution)/shard_map/valence_response/pallas_call | solution.py:284
  102.8 3.7 %cond_spectrum.1.cond_ref = bf16[1024,256]{1,0:T(8,128)(2,1)S(1)} custom-call(f32[256,256]{1,0:T(8,128)S(1)} %get-tuple-element.25.cos_ref, f32[256,256]{1,0:T(8,128)S(1)} %get-tuple-element.24.sin_ref, f32[256,1024]{1,0:T(8,128)S(1)} %bitcast.75), custom_call_target="tpu_custom_call" | custom-call | flops 1610612736 | bytes 2097152 | tf_op jit(solution)/shard_map/cond_spectrum/pallas_call | solution.py:318
  107.1 12.9 %all_to_all.26 = f32[32,16,128]{2,1,0:T(8,128)S(1)} all-to-all(f32[32,16,128]{2,1,0:T(8,128)S(1)} %kernel_blocks.1), channel_id=1, replica_groups=mesh['zl'=4,'co'=2,'x'=4,'y'=4,'zh'=2] {'x','y'}, dimensions={0} | all-to-all | bytes 524288 | tf_op jit(solution)/shard_map/all_to_all | solution.py:428
  120.8 12.1 %all-to-all-start.2 = ((f32[16,2,16,128]{3,2,1,0:T(8,128)}), f32[16,2,16,128]{3,2,1,0:T(8,128)S(1)}, u32[]{:S(2)}, u32[]{:S(2)}) async-start(f32[16,2,16,128]{3,2,1,0:T(8,128)} %broadcast_in_dim.16), calls=%async_computation.2 | async-start | bytes 524288 | tf_op jit(solution)/shard_map/all_to_all | solution.py:65
  132.9 12.2 %all-to-all-done.2 = f32[16,2,16,128]{3,2,1,0:T(8,128)S(1)} async-done(((f32[16,2,16,128]{3,2,1,0:T(8,128)}), f32[16,2,16,128]{3,2,1,0:T(8,128)S(1)}, u32[]{:S(2)}, u32[]{:S(2)}) %all-to-all-start.2) | async-done | bytes 262176 | tf_op jit(solution)/shard_map/all_to_all | solution.py:65
  145.8 14.7 %all_to_all.27.full_ref = f32[16,2,32,128]{3,2,1,0:T(8,128)S(1)} all-to-all(f32[16,2,32,128]{3,2,1,0:T(8,128)S(1)} %broadcast_in_dim.21), channel_id=1, replica_groups=mesh['zl'=4,'co'=2,'x'=4,'y'=4,'zh'=2] {'x','y'}, dimensions={0} | all-to-all | bytes 1048576 | tf_op jit(solution)/shard_map/all_to_all | solution.py:65
  (67 shorter events, 15.5 us)
Async XLA Ops:
  0.6 41.5 %copy-start.4 = (f32[256,512]{1,0:T(8,128)S(1)}, f32[256,512]{1,0:T(8,128)}, u32[]{:S(2)}) copy-start(f32[256,512]{1,0:T(8,128)} %constant.192.clone.table_ref) | copy-start | bytes 1572868
  1.6 8.6 %collective-permute-start.2 = (bf16[8,32,256]{2,1,0:T(8,128)(2,1)S(1)}, bf16[8,32,256]{2,1,0:T(8,128)(2,1)S(1)}, u32[]{:S(2)}, u32[]{:S(2)}) collective-permute-start(bf16[8,32,256]{2,1,0:T(8,128)(2,1)S(1)} %bitcast.81), channel_id=1, source_target_pairs={{0,192},{64,0},{128,64},{192,128},{1,193},{65,1},{129,65},{193,129... | collective-permute-start | bytes 393224 | tf_op jit(solution)/shard_map/ppermute | solution.py:55
  6.3 11.2 %collective-permute-start.1 = (bf16[8,32,256]{2,1,0:T(8,128)(2,1)S(1)}, bf16[8,32,256]{2,1,0:T(8,128)(2,1)S(1)}, u32[]{:S(2)}, u32[]{:S(2)}) collective-permute-start(bf16[8,32,256]{2,1,0:T(8,128)(2,1)S(1)} %bitcast.82), channel_id=1, source_target_pairs={{0,128},{64,192},{128,0},{192,64},{1,129},{65,193},{129,1},{193,65... | collective-permute-start | bytes 393224 | tf_op jit(solution)/shard_map/ppermute | solution.py:55
  6.3 11.2 %collective-permute-start = (bf16[8,32,256]{2,1,0:T(8,128)(2,1)S(1)}, bf16[8,32,256]{2,1,0:T(8,128)(2,1)S(1)}, u32[]{:S(2)}, u32[]{:S(2)}) collective-permute-start(bf16[8,32,256]{2,1,0:T(8,128)(2,1)S(1)} %bitcast.83), channel_id=1, source_target_pairs={{0,64},{64,128},{128,192},{192,0},{1,65},{65,129},{129,193},{193,1... | collective-permute-start | bytes 393224 | tf_op jit(solution)/shard_map/ppermute | solution.py:55
  17.6 2.0 %collective-permute-start.3 = (bf16[32,32,256]{2,1,0:T(8,128)(2,1)S(1)}, bf16[32,32,256]{2,1,0:T(8,128)(2,1)S(1)}, u32[]{:S(2)}, u32[]{:S(2)}) collective-permute-start(bf16[32,32,256]{2,1,0:T(8,128)(2,1)S(1)} %bitcast.73), channel_id=1, source_target_pairs={{0,32},{32,0},{1,33},{33,1},{2,34},{34,2},{3,35},{35,3},{4,36},{36... | collective-permute-start | bytes 1572872 | tf_op jit(solution)/shard_map/ppermute | solution.py:55
  23.1 9.5 %collective-permute-start.4 = (bf16[2,8,16,256]{3,2,1,0:T(8,128)(2,1)S(1)}, bf16[2,8,16,256]{3,2,1,0:T(8,128)(2,1)S(1)}, u32[]{:S(2)}, u32[]{:S(2)}) collective-permute-start(bf16[2,8,16,256]{3,2,1,0:T(8,128)(2,1)S(1)} %get-tuple-element.11), channel_id=1, source_target_pairs={{0,1},{1,0},{2,3},{3,2},{4,5},{5,4},{6,7},{7,6},{8,9},{9,8},{10,11... | collective-permute-start | bytes 393224 | tf_op jit(solution)/shard_map/ppermute | solution.py:55
  32.6 7.7 %collective-permute-start.7 = (bf16[2,8,16,256]{3,2,1,0:T(8,128)(2,1)S(1)}, bf16[2,8,16,256]{3,2,1,0:T(8,128)(2,1)S(1)}, u32[]{:S(2)}, u32[]{:S(2)}) collective-permute-start(bf16[2,8,16,256]{3,2,1,0:T(8,128)(2,1)S(1)} %get-tuple-element.21), channel_id=1, source_target_pairs={{0,24},{8,0},{16,8},{24,16},{1,25},{9,1},{17,9},{25,17},{2,26},{10... | collective-permute-start | bytes 393224 | tf_op jit(solution)/shard_map/ppermute | solution.py:55
  35.5 11.1 %collective-permute-start.6 = (bf16[2,8,16,256]{3,2,1,0:T(8,128)(2,1)S(1)}, bf16[2,8,16,256]{3,2,1,0:T(8,128)(2,1)S(1)}, u32[]{:S(2)}, u32[]{:S(2)}) collective-permute-start(bf16[2,8,16,256]{3,2,1,0:T(8,128)(2,1)S(1)} %get-tuple-element.21), channel_id=1, source_target_pairs={{0,16},{8,24},{16,0},{24,8},{1,17},{9,25},{17,1},{25,9},{2,18},{10... | collective-permute-start | bytes 393224 | tf_op jit(solution)/shard_map/ppermute | solution.py:55
  36.3 10.3 %collective-permute-start.5 = (bf16[2,8,16,256]{3,2,1,0:T(8,128)(2,1)S(1)}, bf16[2,8,16,256]{3,2,1,0:T(8,128)(2,1)S(1)}, u32[]{:S(2)}, u32[]{:S(2)}) collective-permute-start(bf16[2,8,16,256]{3,2,1,0:T(8,128)(2,1)S(1)} %get-tuple-element.21), channel_id=1, source_target_pairs={{0,8},{8,16},{16,24},{24,0},{1,9},{9,17},{17,25},{25,1},{2,10},{10... | collective-permute-start | bytes 393224 | tf_op jit(solution)/shard_map/ppermute | solution.py:55
  37.2 9.5 %collective-permute-start.10 = (bf16[2,8,16,256]{3,2,1,0:T(8,128)(2,1)S(1)}, bf16[2,8,16,256]{3,2,1,0:T(8,128)(2,1)S(1)}, u32[]{:S(2)}, u32[]{:S(2)}) collective-permute-start(bf16[2,8,16,256]{3,2,1,0:T(8,128)(2,1)S(1)} %get-tuple-element.22), channel_id=1, source_target_pairs={{0,6},{2,0},{4,2},{6,4},{1,7},{3,1},{5,3},{7,5},{8,14},{10,8},{12,... | collective-permute-start | bytes 393224 | tf_op jit(solution)/shard_map/ppermute | solution.py:55
  37.6 9.1 %collective-permute-start.9 = (bf16[2,8,16,256]{3,2,1,0:T(8,128)(2,1)S(1)}, bf16[2,8,16,256]{3,2,1,0:T(8,128)(2,1)S(1)}, u32[]{:S(2)}, u32[]{:S(2)}) collective-permute-start(bf16[2,8,16,256]{3,2,1,0:T(8,128)(2,1)S(1)} %get-tuple-element.22), channel_id=1, source_target_pairs={{0,4},{2,6},{4,0},{6,2},{1,5},{3,7},{5,1},{7,3},{8,12},{10,14},{12... | collective-permute-start | bytes 393224 | tf_op jit(solution)/shard_map/ppermute | solution.py:55
  40.3 6.3 %collective-permute-start.8 = (bf16[2,8,16,256]{3,2,1,0:T(8,128)(2,1)S(1)}, bf16[2,8,16,256]{3,2,1,0:T(8,128)(2,1)S(1)}, u32[]{:S(2)}, u32[]{:S(2)}) collective-permute-start(bf16[2,8,16,256]{3,2,1,0:T(8,128)(2,1)S(1)} %get-tuple-element.22), channel_id=1, source_target_pairs={{0,2},{2,4},{4,6},{6,0},{1,3},{3,5},{5,7},{7,1},{8,10},{10,12},{12... | collective-permute-start | bytes 393224 | tf_op jit(solution)/shard_map/ppermute | solution.py:55
  46.6 25.0 %copy-start.5 = (bf16[2,256,256]{2,1,0:T(8,128)(2,1)S(1)}, bf16[2,256,256]{2,1,0:T(8,128)(2,1)}, u32[]{:S(2)}) copy-start(bf16[2,256,256]{2,1,0:T(8,128)(2,1)} %constant.194.clone.high_ref) | copy-start | bytes 786436
  46.6 25.0 %copy-start.6 = (bf16[2,256,256]{2,1,0:T(8,128)(2,1)S(1)}, bf16[2,256,256]{2,1,0:T(8,128)(2,1)}, u32[]{:S(2)}) copy-start(bf16[2,256,256]{2,1,0:T(8,128)(2,1)} %constant.195.clone.low_ref) | copy-start | bytes 786436
  46.6 25.0 %copy-start.7 = (bf16[96,32]{1,0:T(8,128)(2,1)S(1)}, bf16[96,32]{1,0:T(8,128)(2,1)}, u32[]{:S(2)}) copy-start(bf16[96,32]{1,0:T(8,128)(2,1)} %constant.193.clone.line_ref) | copy-start | bytes 18436
  47.6 21.0 %collective-permute-start.13 = (bf16[4,2,8,16,256]{4,3,2,1,0:T(8,128)(2,1)S(1)}, bf16[4,2,8,16,256]{4,3,2,1,0:T(8,128)(2,1)}, u32[]{:S(2)}, u32[]{:S(2)}) collective-permute-start(bf16[4,2,8,16,256]{4,3,2,1,0:T(8,128)(2,1)S(1)} %pad_maximum_fusion.3), channel_id=1, source_target_pairs={{0,6},{2,0},{4,2},{6,4},{1,7},{3,1},{5,3},{7,5},{8,14},{10,8},{12,... | collective-permute-start | bytes 1572872 | tf_op jit(solution)/shard_map/ppermute | solution.py:55
  50.6 37.1 %collective-permute-start.12 = (bf16[4,2,8,16,256]{4,3,2,1,0:T(8,128)(2,1)S(1)}, bf16[4,2,8,16,256]{4,3,2,1,0:T(8,128)(2,1)}, u32[]{:S(2)}, u32[]{:S(2)}) collective-permute-start(bf16[4,2,8,16,256]{4,3,2,1,0:T(8,128)(2,1)S(1)} %pad_maximum_fusion.3), channel_id=1, source_target_pairs={{0,4},{2,6},{4,0},{6,2},{1,5},{3,7},{5,1},{7,3},{8,12},{10,14},{12... | collective-permute-start | bytes 1572872 | tf_op jit(solution)/shard_map/ppermute | solution.py:55
  51.5 36.3 %collective-permute-start.11 = (bf16[4,2,8,16,256]{4,3,2,1,0:T(8,128)(2,1)S(1)}, bf16[4,2,8,16,256]{4,3,2,1,0:T(8,128)(2,1)}, u32[]{:S(2)}, u32[]{:S(2)}) collective-permute-start(bf16[4,2,8,16,256]{4,3,2,1,0:T(8,128)(2,1)S(1)} %pad_maximum_fusion.3), channel_id=1, source_target_pairs={{0,2},{2,4},{4,6},{6,0},{1,3},{3,5},{5,7},{7,1},{8,10},{10,12},{12... | collective-permute-start | bytes 1572872 | tf_op jit(solution)/shard_map/ppermute | solution.py:55
  52.7 36.6 %collective-permute-start.15 = (bf16[4,2,8,16,256]{4,3,2,1,0:T(8,128)(2,1)}, bf16[4,2,8,16,256]{4,3,2,1,0:T(8,128)(2,1)}, u32[]{:S(2)}, u32[]{:S(2)}) collective-permute-start(bf16[4,2,8,16,256]{4,3,2,1,0:T(8,128)(2,1)} %pad_maximum_fusion.4), channel_id=1, source_target_pairs={{0,16},{8,24},{16,0},{24,8},{1,17},{9,25},{17,1},{25,9},{2,18},{10... | collective-permute-start | bytes 1572872 | tf_op jit(solution)/shard_map/ppermute | solution.py:55
  54.7 34.7 %collective-permute-start.14 = (bf16[4,2,8,16,256]{4,3,2,1,0:T(8,128)(2,1)}, bf16[4,2,8,16,256]{4,3,2,1,0:T(8,128)(2,1)}, u32[]{:S(2)}, u32[]{:S(2)}) collective-permute-start(bf16[4,2,8,16,256]{4,3,2,1,0:T(8,128)(2,1)} %pad_maximum_fusion.4), channel_id=1, source_target_pairs={{0,8},{8,16},{16,24},{24,0},{1,9},{9,17},{17,25},{25,1},{2,10},{10... | collective-permute-start | bytes 1572872 | tf_op jit(solution)/shard_map/ppermute | solution.py:55
  56.9 45.9 %all-to-all-start = ((f32[32,8,1024]{2,1,0:T(8,128)}), f32[32,8,1024]{2,1,0:T(8,128)S(1)}, u32[]{:S(2)}, u32[]{:S(2)}) async-start(f32[32,8,1024]{2,1,0:T(8,128)} %bitcast.23), calls=%async_computation | async-start | bytes 2097152 | tf_op jit(solution)/shard_map/all_to_all | solution.py:421
  68.6 20.8 %collective-permute-start.16 = (bf16[4,2,8,16,256]{4,3,2,1,0:T(8,128)(2,1)}, bf16[4,2,8,16,256]{4,3,2,1,0:T(8,128)(2,1)S(1)}, u32[]{:S(2)}, u32[]{:S(2)}) collective-permute-start(bf16[4,2,8,16,256]{4,3,2,1,0:T(8,128)(2,1)} %pad_maximum_fusion.4), channel_id=1, source_target_pairs={{0,24},{8,0},{16,8},{24,16},{1,25},{9,1},{17,9},{25,17},{2,26},{10... | collective-permute-start | bytes 1572872 | tf_op jit(solution)/shard_map/ppermute | solution.py:55
  106.5 38.8 %copy-start.1 = (s32[64]{0:T(128)S(1)}, s32[64]{0:T(128)}, u32[]{:S(2)}) copy-start(s32[64]{0:T(128)} %partner_ref.1) | copy-start | bytes 772
  120.8 24.4 %all-to-all-start.2 = ((f32[16,2,16,128]{3,2,1,0:T(8,128)}), f32[16,2,16,128]{3,2,1,0:T(8,128)S(1)}, u32[]{:S(2)}, u32[]{:S(2)}) async-start(f32[16,2,16,128]{3,2,1,0:T(8,128)} %broadcast_in_dim.16), calls=%async_computation.2 | async-start | bytes 524288 | tf_op jit(solution)/shard_map/all_to_all | solution.py:65
  (3 other events, 5.7 us)

commit v8 on v7

--- a/solution.py
+++ b/solution.py
@@ -18,7 +18,7 @@
 HALF = NZ // 2 + 1
 LINE_BLOCKS = 4
 LINE_STEPS = 32 // LINE_BLOCKS
-LINE_ROWS = 48
+LINE_ROWS = 32
 NORM = 1.0 / math.sqrt(NG)
 EXACT = lax.Precision.HIGHEST
 BF = jnp.bfloat16
@@ -71,13 +71,13 @@
     )
 
 
-def screened_kernel(gmap_ref, line_ref, high_ref, low_ref, w_ref, out_ref, end_ref, lines_ref):
+def screened_kernel(n, gmap_ref, line_ref, high_ref, low_ref, w_ref, out_ref, end_ref, lines_ref):
     step = pl.program_id(0)
     end_ref[...] = jnp.zeros_like(end_ref)
 
     @pl.when(step < LINE_STEPS)
     def _():
-        rows = 2 * HALF
+        rows = 2 * n
         keep = lax.broadcasted_iota(jnp.int32, (1, 8, 256), 1) == (
             lax.broadcasted_iota(jnp.int32, (1, 8, 256), 2) >> 5
         )
@@ -98,7 +98,7 @@
     @pl.when(step >= LINE_STEPS)
     def _():
         z = step - LINE_STEPS
-        real, imag = lines_ref[z], lines_ref[HALF + z]
+        real, imag = lines_ref[z], lines_ref[n + z]
         for odd in range(2):
             if odd:
                 both = [real[:128] - real[128:], imag[:128] - imag[128:]]
@@ -115,10 +115,11 @@
                 out_ref[0, 256 + at : 256 + at + NY] = prod[128 + half * NY : 144 + half * NY]
 
 
-def screened_transform(screened, gmap):
-    angles = line_angles()[:HALF]
+def screened_transform(screened, gmap, first):
+    angles = line_angles()[first:HALF:2]
+    n = angles.shape[0]
     table = np.concatenate([np.cos(angles), -np.sin(angles)], axis=0)
-    padding = np.zeros((LINE_ROWS - 2 * HALF, NZ), BF)
+    padding = np.zeros((LINE_ROWS - 2 * n, NZ), BF)
     line = np.concatenate([x for part in split_table(table) for x in (part, padding)], axis=0)
     angles = plane_angles().reshape(NX, NY, PLANE)[:, :, :128]
     tables = []
@@ -127,36 +128,36 @@
         cosine, sine = np.cos(part), np.sin(part)
         tables.append(np.block([[cosine, sine], [sine, -cosine]]))
     high, low = split_table(np.stack(tables))
-    n = LINE_BLOCKS
+    m = LINE_BLOCKS
     last = LINE_STEPS - 1
     return pl.pallas_call(
-        screened_kernel,
-        grid=(LINE_STEPS + HALF,),
+        functools.partial(screened_kernel, n),
+        grid=(LINE_STEPS + n,),
         in_specs=[
-            pl.BlockSpec((n, 1, 256), lambda i: (jnp.minimum(i, last), 0, 0)),
+            pl.BlockSpec((m, 1, 256), lambda i: (jnp.minimum(i, last), 0, 0)),
             pl.BlockSpec((2 * LINE_ROWS, NZ), lambda i: (0, 0)),
             pl.BlockSpec((2, 256, 256), lambda i: (0, 0, 0)),
             pl.BlockSpec((2, 256, 256), lambda i: (0, 0, 0)),
-            pl.BlockSpec((256, n * 256), lambda i: (0, jnp.minimum(i, last))),
+            pl.BlockSpec((256, m * 256), lambda i: (0, jnp.minimum(i, last))),
         ],
         out_specs=[
             pl.BlockSpec((1, 512, 256), lambda i: (jnp.maximum(i - LINE_STEPS, 0), 0, 0)),
             pl.BlockSpec((8, 128), lambda i: (0, 0)),
         ],
         out_shape=[
-            jax.ShapeDtypeStruct((HALF, 512, 256), BF),
+            jax.ShapeDtypeStruct((n, 512, 256), BF),
             jax.ShapeDtypeStruct((8, 128), F32),
         ],
-        scratch_shapes=[pltpu.VMEM((2 * HALF, PLANE, 256), F32)],
-        compiler_params=pltpu.CompilerParams(vmem_limit_bytes=40 * MIB),
+        scratch_shapes=[pltpu.VMEM((2 * n, PLANE, 256), F32)],
+        compiler_params=pltpu.CompilerParams(vmem_limit_bytes=24 * MIB),
         cost_estimate=pl.CostEstimate(
-            flops=48 * 256 * 256 * 256 * HALF, bytes_accessed=9 * MIB, transcendentals=0
+            flops=24 * 256 * 256 * 256 * HALF, bytes_accessed=7 * MIB, transcendentals=0
         ),
         name="screened_transform",
     )(gmap.reshape(32, 1, 256), jnp.asarray(line), jnp.asarray(high), jnp.asarray(low), screened)
 
 
-def choose_kernel(partner_ref, place_ref, flip_ref, near_ref, far_ref, val_ref, cond_ref):
+def choose_kernel(partner_ref, place_ref, flip_ref, near_ref, far_ref, end_ref, val_ref, cond_ref):
     level, core = place_ref[0], place_ref[1]
     for m in range(8):
         val_ref[0, m] = dot(near_ref[m, :16], flip_ref[...]).astype(BF)
@@ -174,18 +175,18 @@
         pl.when(jnp.logical_not(near))(functools.partial(take, far_ref))
 
 
-def choose(partner, near, far, flip):
+def choose(partner, near, far, flip, end):
     shape = jax.ShapeDtypeStruct((8, 16, 256), BF)
     place = jnp.stack([lax.axis_index("zl"), lax.axis_index("co")]).astype(jnp.int32)
     return pl.pallas_call(
         choose_kernel,
         in_specs=[pl.BlockSpec(memory_space=pltpu.SMEM)] * 2
-        + [pl.BlockSpec(memory_space=pltpu.VMEM)] * 3,
+        + [pl.BlockSpec(memory_space=pltpu.VMEM)] * 4,
         out_specs=[pl.BlockSpec(memory_space=pltpu.VMEM)] * 2,
         out_shape=[jax.ShapeDtypeStruct((2, 8, 16, 256), BF), shape],
         compiler_params=pltpu.CompilerParams(vmem_limit_bytes=16 * MIB),
         name="partner_choice",
-    )(partner, place, flip, near, far)
+    )(partner, place, flip, near, far, end)
 
 
 def cond_kernel(table_ref, home_ref, away_ref, x_ref, rows_ref):
@@ -268,7 +269,7 @@
     sum_ref[...] = total
 
 
-def response(place, home, away, screened):
+def response(place, home, away, even, odd):
     def block(which, second, back):
         def index(step, place_ref):
             z = jnp.minimum(2 * step + second, HALF - 1)
@@ -288,8 +289,8 @@
             grid=(HALF // 2 + 1,),
             in_specs=blocks
             + [
-                pl.BlockSpec((1, 512, 256), lambda i, p: (jnp.maximum(2 * i - 1, 0), 0, 0)),
-                pl.BlockSpec((1, 512, 256), lambda i, p: (2 * i, 0, 0)),
+                pl.BlockSpec((1, 512, 256), lambda i, p: (jnp.maximum(i - 1, 0), 0, 0)),
+                pl.BlockSpec((1, 512, 256), lambda i, p: (i, 0, 0)),
             ],
             out_specs=pl.BlockSpec((1024, 256), lambda i, p: (0, 0)),
             scratch_shapes=[pltpu.VMEM((1024, 512), BF), pltpu.VMEM((1024, 512), BF)],
@@ -300,7 +301,7 @@
             flops=16 * 1024 * 512 * 256 * HALF, bytes_accessed=9 * MIB, transcendentals=0
         ),
         name="valence_response",
-    )(place.reshape(1), *([home, away] * 4), screened, screened)
+    )(place.reshape(1), *([home, away] * 4), odd, even)
 
 
 def spectrum_kernel(cos_ref, sin_ref, x_ref, out_ref):
@@ -406,22 +407,24 @@
     negative = (NX - index // NY) % NX * NY + (NY - index % NY) % NY
     negative = jnp.where(place > NZ // 2, negative, index)
     flip = (index[:, None] == negative[None, :]).astype(BF)
+    even, end = screened_transform(screened, gmap, 0)
+    near, end = lax.optimization_barrier((near, end))
     far = turned(near, "co", 1)
 
-    vals, away_cond = choose(partner, near, far, flip)
+    vals, away_cond = choose(partner, near, far, flip, end)
     planes = cond_planes(waves[:, 16:], away_cond)
     vals = spread(vals, "zh")
     home, away = spread(vals[:, 0], "x"), spread(vals[:, 1], "y")
     home, away, planes, screened = lax.optimization_barrier((home, away, planes, screened))
     homes = [home] + [turned(home, "y", d) for d in range(1, 4)]
     aways = [away] + [turned(away, "x", d) for d in range(1, 3)]
-    wide, end = screened_transform(screened, gmap)
-    away, planes, end = lax.optimization_barrier((away, planes, end))
+    odd, _ = screened_transform(screened, gmap, 1)
+    away, planes = lax.optimization_barrier((away, planes))
     aways.append(turned(away, "x", 3))
     columns = lax.all_to_all(planes, GA, split_axis=0, concat_axis=0, tiled=True)
     home = jnp.stack(homes).reshape(32, 8, 16, 256)
     away = jnp.stack(aways).reshape(32, 8, 16, 256)
-    rows = response(place, home, away, wide)
+    rows = response(place, home, away, even, odd)
     cond = cond_spectrum(*line_tables(gmap, place), columns)
     blocks = kernel_blocks(cond, rows)
 

time: 162 us -> 167 us (1.031)
  local copies, waits for them, and re-layouts: 4.78 us -> 11.4 us
  waiting for transfers between devices: 28.7 us -> 22.6 us
  Pallas kernels: 38.2 us -> 42 us
    unnamed x16 -> x28, local copies, waits for them, and re-layouts: 2.88 us -> 9.55 us
    ppermute x17, waiting for transfers between devices: 16.5 us -> 10.3 us  [turned(): lax.ppermute(value, axis, [(i, (i + step) % size) for i in range(size)])]
    pallas_call x1 -> x2, Pallas kernels: 13.9 us -> 17.7 us  [screened_transform(): pl.pallas_call(functools.partial(screened_kernel, n), grid=(LINE_STEPS +...]
  transfers between devices with their start and end apart: 19 -> 19, of which waited for: 6 -> 5; matrix products, arithmetic and copies ran while one was open for 3% -> 3% of each run, Pallas kernels for 19% -> 20%
where the time goes in v8:
time: 167 us; the launch traced here: 166 us
  starting transfers between devices  54.3 us (33%)
  Pallas kernels  42 us (25%)
  blocking collectives  28.5 us (17%)
  waiting for transfers between devices  22.6 us (14%)
  local copies, waits for them, and re-layouts  11.4 us (7%)
  other arithmetic  5.88 us (4%)
    ppermute x17, starting transfers between devices, turned(): lax.ppermute(value, axis, [(i, (i + step) % size) for i in range(size)])  31.4 us
    pallas_call x2, Pallas kernels, screened_transform(): pl.pallas_call(functools.partial(screened_kernel, n), grid=(LINE_STEPS +...  17.7 us
    all_to_all x1, blocking collectives, copies_to_all(): return lax.all_to_all(copies, axes, split_axis=0, concat_axis=0, tiled=True)  14.7 us
    all_to_all x1, blocking collectives, on_device(): lax.all_to_all(blocks, ('x', 'y'), split_axis=0, concat_axis=0, tiled=True)  13.8 us
    all_to_all x1, waiting for transfers between devices, copies_to_all(): return lax.all_to_all(copies, axes, split_axis=0, concat_axis=0, tiled=True)  12.2 us
    pallas_call x1, Pallas kernels, response(): pl.pallas_call(response_kernel, grid_spec=pltpu.PrefetchScalarGridSpec(nu...  11.7 us
    all_to_all x1, starting transfers between devices, on_device(): lax.all_to_all(planes, GA, split_axis=0, concat_axis=0, tiled=True)  11.6 us
    all_to_all x1, starting transfers between devices, copies_to_all(): return lax.all_to_all(copies, axes, split_axis=0, concat_axis=0, tiled=True)  11.4 us
  transfers between devices with their start and end apart: 19, of which 5 were waited for; matrix products, arithmetic and copies ran while one was open for 3% of the time, Pallas kernels for 20%

profile of v8, /device:TPU:8, one launch (start us, length us, event | category | flops | bytes accessed | tf_op | source)
XLA Modules:
  0.0 165.9 jit_solution(3058599813031797384)
XLA Ops:
  1.5 4.7 %collective-permute-start.2 = (bf16[8,32,256]{2,1,0:T(8,128)(2,1)S(1)}, bf16[8,32,256]{2,1,0:T(8,128)(2,1)S(1)}, u32[]{:S(2)}, u32[]{:S(2)}) collective-permute-start(bf16[8,32,256]{2,1,0:T(8,128)(2,1)S(1)} %bitcast.82), channel_id=1, source_target_pairs={{0,192},{64,0},{128,64},{192,128},{1,193},{65,1},{129,65},{193,129... | collective-permute-start | bytes 393224 | tf_op jit(solution)/shard_map/ppermute | solution.py:55
  7.7 2.2 %copy-done.3 = bf16[256,8192]{1,0:T(8,128)(2,1)S(1)} copy-done((bf16[256,8192]{1,0:T(8,128)(2,1)S(1)}, bf16[256,8192]{1,0:T(8,128)(2,1)}, u32[]{:S(2)}) %copy-start.3) | copy-done | bytes 4194328
  12.5 8.9 %screened_transform.2 = (bf16[9,512,256]{2,1,0:T(8,128)(2,1)S(1)}, f32[8,128]{1,0:T(8,128)S(1)}) custom-call(s32[32,1,256]{2,1,0:T(1,128)S(1)} %bitcast.77, bf16[64,32]{1,0:T(8,128)(2,1)S(1)} %copy-done.11, bf16[2,256,256]{2,1,0:T(8,128)(2,1)S(1)} %copy-done.6, bf16[2,256,256]{2,1,0:T(8,128)(2,1)S(1)} %copy-done.8, bf16[256,8192]{1,0:T(8,128)(2,1)S(1)} %copy-done.3), custom_call_target="tpu_custom_call" | custom-call | flops 6845104128 | bytes 7340032 | tf_op jit(solution)/shard_map/screened_transform/pallas_call | solution.py:133
  24.9 2.8 %partner_choice.1 = (bf16[2,8,16,256]{3,2,1,0:T(8,128)(2,1)S(1)}, bf16[8,16,256]{2,1,0:T(8,128)(2,1)S(1)}) custom-call(s32[64]{0:T(128)S(1)} %copy-done, s32[2]{0:T(128)S(1)} %pad_add_fusion.place_ref, bf16[256,256]{1,0:T(8,128)(2,1)S(1)} %fusion.4.flip_ref, bf16[32,32,256]{2,1,0:T(8,128)(2,1)S(1)} %bitcast.74, ...), custom_call_target="tpu_custom_call" | custom-call | tf_op jit(solution)/shard_map/partner_choice/pallas_call | solution.py:181
  27.7 5.4 %collective-permute-start.4 = (bf16[2,8,16,256]{3,2,1,0:T(8,128)(2,1)S(1)}, bf16[2,8,16,256]{3,2,1,0:T(8,128)(2,1)S(1)}, u32[]{:S(2)}, u32[]{:S(2)}) collective-permute-start(bf16[2,8,16,256]{3,2,1,0:T(8,128)(2,1)S(1)} %get-tuple-element.18), channel_id=1, source_target_pairs={{0,1},{1,0},{2,3},{3,2},{4,5},{5,4},{6,7},{7,6},{8,9},{9,8},{10,11... | collective-permute-start | bytes 393224 | tf_op jit(solution)/shard_map/ppermute | solution.py:55
  33.2 4.1 %collective-permute-done.4 = bf16[2,8,16,256]{3,2,1,0:T(8,128)(2,1)S(1)} collective-permute-done((bf16[2,8,16,256]{3,2,1,0:T(8,128)(2,1)S(1)}, bf16[2,8,16,256]{3,2,1,0:T(8,128)(2,1)S(1)}, u32[]{:S(2)}, u32[]{:S(2)}) %collective-permute-start.4) | collective-permute-done | bytes 131104 | tf_op jit(solution)/shard_map/ppermute | solution.py:55
  37.3 2.8 %collective-permute-start.7 = (bf16[2,8,16,256]{3,2,1,0:T(8,128)(2,1)S(1)}, bf16[2,8,16,256]{3,2,1,0:T(8,128)(2,1)S(1)}, u32[]{:S(2)}, u32[]{:S(2)}) collective-permute-start(bf16[2,8,16,256]{3,2,1,0:T(8,128)(2,1)S(1)} %get-tuple-element.29), channel_id=1, source_target_pairs={{0,24},{8,0},{16,8},{24,16},{1,25},{9,1},{17,9},{25,17},{2,26},{10... | collective-permute-start | bytes 393224 | tf_op jit(solution)/shard_map/ppermute | solution.py:55
  42.3 2.6 %collective-permute-start.9 = (bf16[2,8,16,256]{3,2,1,0:T(8,128)(2,1)S(1)}, bf16[2,8,16,256]{3,2,1,0:T(8,128)(2,1)S(1)}, u32[]{:S(2)}, u32[]{:S(2)}) collective-permute-start(bf16[2,8,16,256]{3,2,1,0:T(8,128)(2,1)S(1)} %get-tuple-element.30), channel_id=1, source_target_pairs={{0,4},{2,6},{4,0},{6,2},{1,5},{3,7},{5,1},{7,3},{8,12},{10,14},{12... | collective-permute-start | bytes 393224 | tf_op jit(solution)/shard_map/ppermute | solution.py:55
  46.8 4.5 %cond_planes.1 = f32[256,1024]{1,0:T(8,128)} custom-call(f32[256,512]{1,0:T(8,128)S(1)} %copy-done.5, bf16[8,16,256]{2,1,0:T(8,128)(2,1)S(1)} %slice.22.home_ref, bf16[8,16,256]{2,1,0:T(8,128)(2,1)S(1)} %get-tuple-element.19.away_ref), custom_call_target="tpu_custom_call" | custom-call | flops 1610612736 | bytes 2097152 | tf_op jit(solution)/shard_map/cond_planes/pallas_call | solution.py:214
  52.3 1.8 %collective-permute-start.13 = (bf16[4,2,8,16,256]{4,3,2,1,0:T(8,128)(2,1)S(1)}, bf16[4,2,8,16,256]{4,3,2,1,0:T(8,128)(2,1)}, u32[]{:S(2)}, u32[]{:S(2)}) collective-permute-start(bf16[4,2,8,16,256]{4,3,2,1,0:T(8,128)(2,1)S(1)} %pad_maximum_fusion.3), channel_id=1, source_target_pairs={{0,6},{2,0},{4,2},{6,4},{1,7},{3,1},{5,3},{7,5},{8,14},{10,8},{12,... | collective-permute-start | bytes 1572872 | tf_op jit(solution)/shard_map/ppermute | solution.py:55
  57.4 2.0 %collective-permute-start.15 = (bf16[4,2,8,16,256]{4,3,2,1,0:T(8,128)(2,1)}, bf16[4,2,8,16,256]{4,3,2,1,0:T(8,128)(2,1)}, u32[]{:S(2)}, u32[]{:S(2)}) collective-permute-start(bf16[4,2,8,16,256]{4,3,2,1,0:T(8,128)(2,1)} %pad_maximum_fusion.4), channel_id=1, source_target_pairs={{0,16},{8,24},{16,0},{24,8},{1,17},{9,25},{17,1},{25,9},{2,18},{10... | collective-permute-start | bytes 1572872 | tf_op jit(solution)/shard_map/ppermute | solution.py:55
  59.4 2.3 %collective-permute-start.14 = (bf16[4,2,8,16,256]{4,3,2,1,0:T(8,128)(2,1)}, bf16[4,2,8,16,256]{4,3,2,1,0:T(8,128)(2,1)}, u32[]{:S(2)}, u32[]{:S(2)}) collective-permute-start(bf16[4,2,8,16,256]{4,3,2,1,0:T(8,128)(2,1)} %pad_maximum_fusion.4), channel_id=1, source_target_pairs={{0,8},{8,16},{16,24},{24,0},{1,9},{9,17},{17,25},{25,1},{2,10},{10... | collective-permute-start | bytes 1572872 | tf_op jit(solution)/shard_map/ppermute | solution.py:55
  61.7 11.6 %all-to-all-start = ((f32[32,8,1024]{2,1,0:T(8,128)}), f32[32,8,1024]{2,1,0:T(8,128)S(1)}, u32[]{:S(2)}, u32[]{:S(2)}) async-start(f32[32,8,1024]{2,1,0:T(8,128)} %bitcast.24), calls=%async_computation | async-start | bytes 2097152 | tf_op jit(solution)/shard_map/all_to_all | solution.py:424
  73.3 3.0 %collective-permute-start.16 = (bf16[4,2,8,16,256]{4,3,2,1,0:T(8,128)(2,1)}, bf16[4,2,8,16,256]{4,3,2,1,0:T(8,128)(2,1)S(1)}, u32[]{:S(2)}, u32[]{:S(2)}) collective-permute-start(bf16[4,2,8,16,256]{4,3,2,1,0:T(8,128)(2,1)} %pad_maximum_fusion.4), channel_id=1, source_target_pairs={{0,24},{8,0},{16,8},{24,16},{1,25},{9,1},{17,9},{25,17},{2,26},{10... | collective-permute-start | bytes 1572872 | tf_op jit(solution)/shard_map/ppermute | solution.py:55
  76.3 2.2 %copy-done.4 = bf16[256,8192]{1,0:T(8,128)(2,1)S(1)} copy-done((bf16[256,8192]{1,0:T(8,128)(2,1)S(1)}, bf16[256,8192]{1,0:T(8,128)(2,1)}, u32[]{:S(2)}) %copy-start.4) | copy-done | bytes 4194328
  78.5 8.8 %screened_transform.3 = (bf16[8,512,256]{2,1,0:T(8,128)(2,1)S(1)}, f32[8,128]{1,0:T(8,128)}) custom-call(s32[32,1,256]{2,1,0:T(1,128)S(1)} %bitcast.78, bf16[64,32]{1,0:T(8,128)(2,1)S(1)} %copy-done.10, bf16[2,256,256]{2,1,0:T(8,128)(2,1)S(1)} %copy-done.7, bf16[2,256,256]{2,1,0:T(8,128)(2,1)S(1)} %copy-done.9, bf16[256,8192]{1,0:T(8,128)(2,1)S(1)} %copy-done.4), custom_call_target="tpu_custom_call" | custom-call | flops 6845104128 | bytes 7340032 | tf_op jit(solution)/shard_map/screened_transform/pallas_call | solution.py:133
  88.9 4.2 %collective-permute-done.16 = bf16[4,2,8,16,256]{4,3,2,1,0:T(8,128)(2,1)S(1)} collective-permute-done((bf16[4,2,8,16,256]{4,3,2,1,0:T(8,128)(2,1)}, bf16[4,2,8,16,256]{4,3,2,1,0:T(8,128)(2,1)S(1)}, u32[]{:S(2)}, u32[]{:S(2)}) %collective-permute-start.16) | collective-permute-done | bytes 524320 | tf_op jit(solution)/shard_map/ppermute | solution.py:55
  93.2 1.8 %pad_maximum_fusion.1 = bf16[4,4,2,8,16,256]{5,4,3,2,1,0:T(8,128)(2,1)S(1)} fusion(bf16[1,4,2,8,16,256]{5,4,3,2,1,0:T(8,128)(2,1)S(1)} %bitcast.88, bf16[1,4,2,8,16,256]{5,4,3,2,1,0:T(8,128)(2,1)} %bitcast.34, bf16[1,4,2,8,16,256]{5,4,3,2,1,0:T(8,128)(2,1)} %bitcast.33, bf16[1,4,2,8,16,256]{5,4,3,2,1,0:T(8,128)(2,1)} %bitcast.32), kind=kLoop, calls=%fused_computation.1 | loop fusion | flops 3145728 | bytes 4194304 | tf_op jit(solution)/shard_map/stack | solution.py:426
  95.3 11.7 %valence_response.1.r_ref = f32[1024,256]{1,0:T(8,128)S(1)} custom-call(s32[1]{0:T(128)} %bitcast.26.place_ref, bf16[32,8,16,256]{3,2,1,0:T(8,128)(2,1)S(1)} %bitcast.65, bf16[32,8,16,256]{3,2,1,0:T(8,128)(2,1)S(1)} %bitcast.69, bf16[32,8,16,256]{3,2,1,0:T(8,128)(2,1)S(1)} %bitcast.66, bf16[32,8,16,256]{3,2,1,0:T(8,128)(2,1)S(1)} %bitcast.70, ...), custom_call_target="tpu_custom_call" | custom-call | flops 36507222016 | bytes 9437184 | tf_op jit(solution)/shard_map/valence_response/pallas_call | solution.py:285
  107.1 3.7 %cond_spectrum.1.cond_ref = bf16[1024,256]{1,0:T(8,128)(2,1)S(1)} custom-call(f32[256,256]{1,0:T(8,128)S(1)} %get-tuple-element.33.cos_ref, f32[256,256]{1,0:T(8,128)S(1)} %get-tuple-element.32.sin_ref, f32[256,1024]{1,0:T(8,128)S(1)} %bitcast.75), custom_call_target="tpu_custom_call" | custom-call | flops 1610612736 | bytes 2097152 | tf_op jit(solution)/shard_map/cond_spectrum/pallas_call | solution.py:319
  111.4 13.8 %all_to_all.26 = f32[32,16,128]{2,1,0:T(8,128)S(1)} all-to-all(f32[32,16,128]{2,1,0:T(8,128)S(1)} %kernel_blocks.1), channel_id=1, replica_groups=mesh['zl'=4,'co'=2,'x'=4,'y'=4,'zh'=2] {'x','y'}, dimensions={0} | all-to-all | bytes 524288 | tf_op jit(solution)/shard_map/all_to_all | solution.py:431
  125.9 11.4 %all-to-all-start.2 = ((f32[16,2,16,128]{3,2,1,0:T(8,128)}), f32[16,2,16,128]{3,2,1,0:T(8,128)S(1)}, u32[]{:S(2)}, u32[]{:S(2)}) async-start(f32[16,2,16,128]{3,2,1,0:T(8,128)} %broadcast_in_dim.16), calls=%async_computation.2 | async-start | bytes 524288 | tf_op jit(solution)/shard_map/all_to_all | solution.py:65
  137.3 12.2 %all-to-all-done.2 = f32[16,2,16,128]{3,2,1,0:T(8,128)S(1)} async-done(((f32[16,2,16,128]{3,2,1,0:T(8,128)}), f32[16,2,16,128]{3,2,1,0:T(8,128)S(1)}, u32[]{:S(2)}, u32[]{:S(2)}) %all-to-all-start.2) | async-done | bytes 262176 | tf_op jit(solution)/shard_map/all_to_all | solution.py:65
  150.2 14.7 %all_to_all.27.full_ref = f32[16,2,32,128]{3,2,1,0:T(8,128)S(1)} all-to-all(f32[16,2,32,128]{3,2,1,0:T(8,128)S(1)} %broadcast_in_dim.21), channel_id=1, replica_groups=mesh['zl'=4,'co'=2,'x'=4,'y'=4,'zh'=2] {'x','y'}, dimensions={0} | all-to-all | bytes 1048576 | tf_op jit(solution)/shard_map/all_to_all | solution.py:65
  (80 shorter events, 21.8 us)
Async XLA Ops:
  1.5 21.3 %collective-permute-start.2 = (bf16[8,32,256]{2,1,0:T(8,128)(2,1)S(1)}, bf16[8,32,256]{2,1,0:T(8,128)(2,1)S(1)}, u32[]{:S(2)}, u32[]{:S(2)}) collective-permute-start(bf16[8,32,256]{2,1,0:T(8,128)(2,1)S(1)} %bitcast.82), channel_id=1, source_target_pairs={{0,192},{64,0},{128,64},{192,128},{1,193},{65,1},{129,65},{193,129... | collective-permute-start | bytes 393224 | tf_op jit(solution)/shard_map/ppermute | solution.py:55
  6.2 16.6 %collective-permute-start.1 = (bf16[8,32,256]{2,1,0:T(8,128)(2,1)S(1)}, bf16[8,32,256]{2,1,0:T(8,128)(2,1)S(1)}, u32[]{:S(2)}, u32[]{:S(2)}) collective-permute-start(bf16[8,32,256]{2,1,0:T(8,128)(2,1)S(1)} %bitcast.83), channel_id=1, source_target_pairs={{0,128},{64,192},{128,0},{192,64},{1,129},{65,193},{129,1},{193,65... | collective-permute-start | bytes 393224 | tf_op jit(solution)/shard_map/ppermute | solution.py:55
  6.3 16.6 %collective-permute-start = (bf16[8,32,256]{2,1,0:T(8,128)(2,1)S(1)}, bf16[8,32,256]{2,1,0:T(8,128)(2,1)S(1)}, u32[]{:S(2)}, u32[]{:S(2)}) collective-permute-start(bf16[8,32,256]{2,1,0:T(8,128)(2,1)S(1)} %bitcast.84), channel_id=1, source_target_pairs={{0,64},{64,128},{128,192},{192,0},{1,65},{65,129},{129,193},{193,1... | collective-permute-start | bytes 393224 | tf_op jit(solution)/shard_map/ppermute | solution.py:55
  12.5 12.4 %copy-start = (s32[64]{0:T(128)S(1)}, s32[64]{0:T(128)}, u32[]{:S(2)}) copy-start(s32[64]{0:T(128)} %partner_ref.1) | copy-start | bytes 772
  22.8 24.0 %copy-start.5 = (f32[256,512]{1,0:T(8,128)S(1)}, f32[256,512]{1,0:T(8,128)}, u32[]{:S(2)}) copy-start(f32[256,512]{1,0:T(8,128)} %constant.197.clone.table_ref) | copy-start | bytes 1572868
  22.9 2.0 %collective-permute-start.3 = (bf16[32,32,256]{2,1,0:T(8,128)(2,1)S(1)}, bf16[32,32,256]{2,1,0:T(8,128)(2,1)S(1)}, u32[]{:S(2)}, u32[]{:S(2)}) collective-permute-start(bf16[32,32,256]{2,1,0:T(8,128)(2,1)S(1)} %bitcast.73), channel_id=1, source_target_pairs={{0,32},{32,0},{1,33},{33,1},{2,34},{34,2},{3,35},{35,3},{4,36},{36... | collective-permute-start | bytes 1572872 | tf_op jit(solution)/shard_map/ppermute | solution.py:55
  27.7 9.5 %collective-permute-start.4 = (bf16[2,8,16,256]{3,2,1,0:T(8,128)(2,1)S(1)}, bf16[2,8,16,256]{3,2,1,0:T(8,128)(2,1)S(1)}, u32[]{:S(2)}, u32[]{:S(2)}) collective-permute-start(bf16[2,8,16,256]{3,2,1,0:T(8,128)(2,1)S(1)} %get-tuple-element.18), channel_id=1, source_target_pairs={{0,1},{1,0},{2,3},{3,2},{4,5},{5,4},{6,7},{7,6},{8,9},{9,8},{10,11... | collective-permute-start | bytes 393224 | tf_op jit(solution)/shard_map/ppermute | solution.py:55
  37.3 7.8 %collective-permute-start.7 = (bf16[2,8,16,256]{3,2,1,0:T(8,128)(2,1)S(1)}, bf16[2,8,16,256]{3,2,1,0:T(8,128)(2,1)S(1)}, u32[]{:S(2)}, u32[]{:S(2)}) collective-permute-start(bf16[2,8,16,256]{3,2,1,0:T(8,128)(2,1)S(1)} %get-tuple-element.29), channel_id=1, source_target_pairs={{0,24},{8,0},{16,8},{24,16},{1,25},{9,1},{17,9},{25,17},{2,26},{10... | collective-permute-start | bytes 393224 | tf_op jit(solution)/shard_map/ppermute | solution.py:55
  40.2 11.1 %collective-permute-start.6 = (bf16[2,8,16,256]{3,2,1,0:T(8,128)(2,1)S(1)}, bf16[2,8,16,256]{3,2,1,0:T(8,128)(2,1)S(1)}, u32[]{:S(2)}, u32[]{:S(2)}) collective-permute-start(bf16[2,8,16,256]{3,2,1,0:T(8,128)(2,1)S(1)} %get-tuple-element.29), channel_id=1, source_target_pairs={{0,16},{8,24},{16,0},{24,8},{1,17},{9,25},{17,1},{25,9},{2,18},{10... | collective-permute-start | bytes 393224 | tf_op jit(solution)/shard_map/ppermute | solution.py:55
  41.0 10.3 %collective-permute-start.5 = (bf16[2,8,16,256]{3,2,1,0:T(8,128)(2,1)S(1)}, bf16[2,8,16,256]{3,2,1,0:T(8,128)(2,1)S(1)}, u32[]{:S(2)}, u32[]{:S(2)}) collective-permute-start(bf16[2,8,16,256]{3,2,1,0:T(8,128)(2,1)S(1)} %get-tuple-element.29), channel_id=1, source_target_pairs={{0,8},{8,16},{16,24},{24,0},{1,9},{9,17},{17,25},{25,1},{2,10},{10... | collective-permute-start | bytes 393224 | tf_op jit(solution)/shard_map/ppermute | solution.py:55
  41.8 9.5 %collective-permute-start.10 = (bf16[2,8,16,256]{3,2,1,0:T(8,128)(2,1)S(1)}, bf16[2,8,16,256]{3,2,1,0:T(8,128)(2,1)S(1)}, u32[]{:S(2)}, u32[]{:S(2)}) collective-permute-start(bf16[2,8,16,256]{3,2,1,0:T(8,128)(2,1)S(1)} %get-tuple-element.30), channel_id=1, source_target_pairs={{0,6},{2,0},{4,2},{6,4},{1,7},{3,1},{5,3},{7,5},{8,14},{10,8},{12,... | collective-permute-start | bytes 393224 | tf_op jit(solution)/shard_map/ppermute | solution.py:55
  42.3 9.1 %collective-permute-start.9 = (bf16[2,8,16,256]{3,2,1,0:T(8,128)(2,1)S(1)}, bf16[2,8,16,256]{3,2,1,0:T(8,128)(2,1)S(1)}, u32[]{:S(2)}, u32[]{:S(2)}) collective-permute-start(bf16[2,8,16,256]{3,2,1,0:T(8,128)(2,1)S(1)} %get-tuple-element.30), channel_id=1, source_target_pairs={{0,4},{2,6},{4,0},{6,2},{1,5},{3,7},{5,1},{7,3},{8,12},{10,14},{12... | collective-permute-start | bytes 393224 | tf_op jit(solution)/shard_map/ppermute | solution.py:55
  45.1 6.3 %collective-permute-start.8 = (bf16[2,8,16,256]{3,2,1,0:T(8,128)(2,1)S(1)}, bf16[2,8,16,256]{3,2,1,0:T(8,128)(2,1)S(1)}, u32[]{:S(2)}, u32[]{:S(2)}) collective-permute-start(bf16[2,8,16,256]{3,2,1,0:T(8,128)(2,1)S(1)} %get-tuple-element.30), channel_id=1, source_target_pairs={{0,2},{2,4},{4,6},{6,0},{1,3},{3,5},{5,7},{7,1},{8,10},{10,12},{12... | collective-permute-start | bytes 393224 | tf_op jit(solution)/shard_map/ppermute | solution.py:55
  51.3 25.0 %copy-start.7 = (bf16[2,256,256]{2,1,0:T(8,128)(2,1)S(1)}, bf16[2,256,256]{2,1,0:T(8,128)(2,1)}, u32[]{:S(2)}) copy-start(bf16[2,256,256]{2,1,0:T(8,128)(2,1)} %constant.195.clone.high_ref) | copy-start | bytes 786436
  51.3 25.0 %copy-start.9 = (bf16[2,256,256]{2,1,0:T(8,128)(2,1)S(1)}, bf16[2,256,256]{2,1,0:T(8,128)(2,1)}, u32[]{:S(2)}) copy-start(bf16[2,256,256]{2,1,0:T(8,128)(2,1)} %constant.196.clone.low_ref) | copy-start | bytes 786436
  51.4 24.9 %copy-start.10 = (bf16[64,32]{1,0:T(8,128)(2,1)S(1)}, bf16[64,32]{1,0:T(8,128)(2,1)}, u32[]{:S(2)}) copy-start(bf16[64,32]{1,0:T(8,128)(2,1)} %constant.198.clone.line_ref) | copy-start | bytes 12292
  52.3 21.0 %collective-permute-start.13 = (bf16[4,2,8,16,256]{4,3,2,1,0:T(8,128)(2,1)S(1)}, bf16[4,2,8,16,256]{4,3,2,1,0:T(8,128)(2,1)}, u32[]{:S(2)}, u32[]{:S(2)}) collective-permute-start(bf16[4,2,8,16,256]{4,3,2,1,0:T(8,128)(2,1)S(1)} %pad_maximum_fusion.3), channel_id=1, source_target_pairs={{0,6},{2,0},{4,2},{6,4},{1,7},{3,1},{5,3},{7,5},{8,14},{10,8},{12,... | collective-permute-start | bytes 1572872 | tf_op jit(solution)/shard_map/ppermute | solution.py:55
  55.3 32.0 %collective-permute-start.12 = (bf16[4,2,8,16,256]{4,3,2,1,0:T(8,128)(2,1)S(1)}, bf16[4,2,8,16,256]{4,3,2,1,0:T(8,128)(2,1)}, u32[]{:S(2)}, u32[]{:S(2)}) collective-permute-start(bf16[4,2,8,16,256]{4,3,2,1,0:T(8,128)(2,1)S(1)} %pad_maximum_fusion.3), channel_id=1, source_target_pairs={{0,4},{2,6},{4,0},{6,2},{1,5},{3,7},{5,1},{7,3},{8,12},{10,14},{12... | collective-permute-start | bytes 1572872 | tf_op jit(solution)/shard_map/ppermute | solution.py:55
  56.2 31.1 %collective-permute-start.11 = (bf16[4,2,8,16,256]{4,3,2,1,0:T(8,128)(2,1)S(1)}, bf16[4,2,8,16,256]{4,3,2,1,0:T(8,128)(2,1)}, u32[]{:S(2)}, u32[]{:S(2)}) collective-permute-start(bf16[4,2,8,16,256]{4,3,2,1,0:T(8,128)(2,1)S(1)} %pad_maximum_fusion.3), channel_id=1, source_target_pairs={{0,2},{2,4},{4,6},{6,0},{1,3},{3,5},{5,7},{7,1},{8,10},{10,12},{12... | collective-permute-start | bytes 1572872 | tf_op jit(solution)/shard_map/ppermute | solution.py:55
  57.4 35.7 %collective-permute-start.15 = (bf16[4,2,8,16,256]{4,3,2,1,0:T(8,128)(2,1)}, bf16[4,2,8,16,256]{4,3,2,1,0:T(8,128)(2,1)}, u32[]{:S(2)}, u32[]{:S(2)}) collective-permute-start(bf16[4,2,8,16,256]{4,3,2,1,0:T(8,128)(2,1)} %pad_maximum_fusion.4), channel_id=1, source_target_pairs={{0,16},{8,24},{16,0},{24,8},{1,17},{9,25},{17,1},{25,9},{2,18},{10... | collective-permute-start | bytes 1572872 | tf_op jit(solution)/shard_map/ppermute | solution.py:55
  59.4 33.8 %collective-permute-start.14 = (bf16[4,2,8,16,256]{4,3,2,1,0:T(8,128)(2,1)}, bf16[4,2,8,16,256]{4,3,2,1,0:T(8,128)(2,1)}, u32[]{:S(2)}, u32[]{:S(2)}) collective-permute-start(bf16[4,2,8,16,256]{4,3,2,1,0:T(8,128)(2,1)} %pad_maximum_fusion.4), channel_id=1, source_target_pairs={{0,8},{8,16},{16,24},{24,0},{1,9},{9,17},{17,25},{25,1},{2,10},{10... | collective-permute-start | bytes 1572872 | tf_op jit(solution)/shard_map/ppermute | solution.py:55
  61.7 45.4 %all-to-all-start = ((f32[32,8,1024]{2,1,0:T(8,128)}), f32[32,8,1024]{2,1,0:T(8,128)S(1)}, u32[]{:S(2)}, u32[]{:S(2)}) async-start(f32[32,8,1024]{2,1,0:T(8,128)} %bitcast.24), calls=%async_computation | async-start | bytes 2097152 | tf_op jit(solution)/shard_map/all_to_all | solution.py:424
  73.3 19.9 %collective-permute-start.16 = (bf16[4,2,8,16,256]{4,3,2,1,0:T(8,128)(2,1)}, bf16[4,2,8,16,256]{4,3,2,1,0:T(8,128)(2,1)S(1)}, u32[]{:S(2)}, u32[]{:S(2)}) collective-permute-start(bf16[4,2,8,16,256]{4,3,2,1,0:T(8,128)(2,1)} %pad_maximum_fusion.4), channel_id=1, source_target_pairs={{0,24},{8,0},{16,8},{24,16},{1,25},{9,1},{17,9},{25,17},{2,26},{10... | collective-permute-start | bytes 1572872 | tf_op jit(solution)/shard_map/ppermute | solution.py:55
  125.9 23.7 %all-to-all-start.2 = ((f32[16,2,16,128]{3,2,1,0:T(8,128)}), f32[16,2,16,128]{3,2,1,0:T(8,128)S(1)}, u32[]{:S(2)}, u32[]{:S(2)}) async-start(f32[16,2,16,128]{3,2,1,0:T(8,128)} %broadcast_in_dim.16), calls=%async_computation.2 | async-start | bytes 524288 | tf_op jit(solution)/shard_map/all_to_all | solution.py:65
  (9 other events, 14.1 us)

commit v9 on v8

--- a/solution.py
+++ b/solution.py
@@ -115,7 +115,7 @@
                 out_ref[0, 256 + at : 256 + at + NY] = prod[128 + half * NY : 144 + half * NY]
 
 
-def screened_transform(screened, gmap, first):
+def screened_transform(screened, gmap, first, room):
     angles = line_angles()[first:HALF:2]
     n = angles.shape[0]
     table = np.concatenate([np.cos(angles), -np.sin(angles)], axis=0)
@@ -149,7 +149,7 @@
             jax.ShapeDtypeStruct((8, 128), F32),
         ],
         scratch_shapes=[pltpu.VMEM((2 * n, PLANE, 256), F32)],
-        compiler_params=pltpu.CompilerParams(vmem_limit_bytes=24 * MIB),
+        compiler_params=pltpu.CompilerParams(vmem_limit_bytes=room * MIB),
         cost_estimate=pl.CostEstimate(
             flops=24 * 256 * 256 * 256 * HALF, bytes_accessed=7 * MIB, transcendentals=0
         ),
@@ -407,7 +407,7 @@
     negative = (NX - index // NY) % NX * NY + (NY - index % NY) % NY
     negative = jnp.where(place > NZ // 2, negative, index)
     flip = (index[:, None] == negative[None, :]).astype(BF)
-    even, end = screened_transform(screened, gmap, 0)
+    even, end = screened_transform(screened, gmap, 0, 54)
     near, end = lax.optimization_barrier((near, end))
     far = turned(near, "co", 1)
 
@@ -418,14 +418,15 @@
     home, away, planes, screened = lax.optimization_barrier((home, away, planes, screened))
     homes = [home] + [turned(home, "y", d) for d in range(1, 4)]
     aways = [away] + [turned(away, "x", d) for d in range(1, 3)]
-    odd, _ = screened_transform(screened, gmap, 1)
+    odd, _ = screened_transform(screened, gmap, 1, 24)
     away, planes = lax.optimization_barrier((away, planes))
     aways.append(turned(away, "x", 3))
     columns = lax.all_to_all(planes, GA, split_axis=0, concat_axis=0, tiled=True)
     home = jnp.stack(homes).reshape(32, 8, 16, 256)
     away = jnp.stack(aways).reshape(32, 8, 16, 256)
+    cond = cond_spectrum(*line_tables(gmap, place), columns)
+    home, cond = lax.optimization_barrier((home, cond))
     rows = response(place, home, away, even, odd)
-    cond = cond_spectrum(*line_tables(gmap, place), columns)
     blocks = kernel_blocks(cond, rows)
 
     parts = lax.all_to_all(blocks, ("x", "y"), split_axis=0, concat_axis=0, tiled=True)

time: 167 us -> 183 us (1.096)
  waiting for transfers between devices: 22.6 us -> 31 us
  blocking collectives: 28.5 us -> 34.2 us
  Pallas kernels: 42 us -> 46.4 us
  local copies, waits for them, and re-layouts: 11.4 us -> 7.3 us
  other arithmetic: 5.88 us -> 8.21 us
    ppermute x17, waiting for transfers between devices: 10.3 us -> 18.7 us  [turned(): lax.ppermute(value, axis, [(i, (i + step) % size) for i in range(size)])]
    all_to_all x1, blocking collectives: 13.8 us -> 19.5 us  [on_device(): lax.all_to_all(blocks, ('x', 'y'), split_axis=0, concat_axis=0, tiled=True)]
    pallas_call x2, Pallas kernels: 17.7 us -> 22 us  [screened_transform(): pl.pallas_call(functools.partial(screened_kernel, n), grid=(LINE_STEPS +...]
    unnamed x28 -> x30, local copies, waits for them, and re-layouts: 9.55 us -> 5.46 us
  transfers between devices with their start and end apart: 19 -> 19, of which waited for: 5 -> 5; matrix products, arithmetic and copies ran while one was open for 3% -> 4% of each run, Pallas kernels for 20% -> 14%
where the time goes in v9:
time: 183 us; the launch traced here: 182 us
  starting transfers between devices  53.8 us (29%)
  Pallas kernels  46.4 us (25%)
  blocking collectives  34.2 us (19%)
  waiting for transfers between devices  31 us (17%)
  other arithmetic  8.21 us (4%)
  local copies, waits for them, and re-layouts  7.3 us (4%)
    ppermute x17, starting transfers between devices, turned(): lax.ppermute(value, axis, [(i, (i + step) % size) for i in range(size)])  31.2 us
    pallas_call x2, Pallas kernels, screened_transform(): pl.pallas_call(functools.partial(screened_kernel, n), grid=(LINE_STEPS +...  22 us
    all_to_all x1, blocking collectives, on_device(): lax.all_to_all(blocks, ('x', 'y'), split_axis=0, concat_axis=0, tiled=True)  19.5 us
    ppermute x17, waiting for transfers between devices, turned(): lax.ppermute(value, axis, [(i, (i + step) % size) for i in range(size)])  18.7 us
    all_to_all x1, blocking collectives, copies_to_all(): return lax.all_to_all(copies, axes, split_axis=0, concat_axis=0, tiled=True)  14.7 us
    all_to_all x1, starting transfers between devices, on_device(): lax.all_to_all(planes, GA, split_axis=0, concat_axis=0, tiled=True)  12.8 us
    all_to_all x1, waiting for transfers between devices, copies_to_all(): return lax.all_to_all(copies, axes, split_axis=0, concat_axis=0, tiled=True)  12.2 us
    pallas_call x1, Pallas kernels, response(): pl.pallas_call(response_kernel, grid_spec=pltpu.PrefetchScalarGridSpec(nu...  12 us
  transfers between devices with their start and end apart: 19, of which 5 were waited for; matrix products, arithmetic and copies ran while one was open for 4% of the time, Pallas kernels for 14%

profile of v9, /device:TPU:8, one launch (start us, length us, event | category | flops | bytes accessed | tf_op | source)
XLA Modules:
  0.0 182.2 jit_solution(211224715176993648)
XLA Ops:
  1.5 4.7 %collective-permute-start.2 = (bf16[8,32,256]{2,1,0:T(8,128)(2,1)S(1)}, bf16[8,32,256]{2,1,0:T(8,128)(2,1)S(1)}, u32[]{:S(2)}, u32[]{:S(2)}) collective-permute-start(bf16[8,32,256]{2,1,0:T(8,128)(2,1)S(1)} %bitcast.82), channel_id=1, source_target_pairs={{0,192},{64,0},{128,64},{192,128},{1,193},{65,1},{129,65},{193,129... | collective-permute-start | bytes 393224 | tf_op jit(solution)/shard_map/ppermute | solution.py:55
  6.9 13.1 %screened_transform.2 = (bf16[9,512,256]{2,1,0:T(8,128)(2,1)}, f32[8,128]{1,0:T(8,128)}) custom-call(s32[32,1,256]{2,1,0:T(1,128)} %bitcast.77, bf16[64,32]{1,0:T(8,128)(2,1)} %constant.194.clone.line_ref, bf16[2,256,256]{2,1,0:T(8,128)(2,1)} %constant.195.clone.high_ref, bf16[2,256,256]{2,1,0:T(8,128)(2,1)} %constant.196.clone.low_ref, bf16[256,8192]{1,0:T(8,128)(2,1)} %w_ref.2), custom_call_target="tpu_custom_call" | custom-call | flops 6845104128 | bytes 7340032 | tf_op jit(solution)/shard_map/screened_transform/pallas_call | solution.py:133
  22.9 2.8 %partner_choice.1 = (bf16[2,8,16,256]{3,2,1,0:T(8,128)(2,1)S(1)}, bf16[8,16,256]{2,1,0:T(8,128)(2,1)S(1)}) custom-call(s32[64]{0:T(128)S(1)} %copy-done.3, s32[2]{0:T(128)S(1)} %pad_add_fusion.place_ref, bf16[256,256]{1,0:T(8,128)(2,1)S(1)} %fusion.4.flip_ref, bf16[32,32,256]{2,1,0:T(8,128)(2,1)S(1)} %bitcast.74, ...), custom_call_target="tpu_custom_call" | custom-call | tf_op jit(solution)/shard_map/partner_choice/pallas_call | solution.py:181
  25.6 5.4 %collective-permute-start.4 = (bf16[2,8,16,256]{3,2,1,0:T(8,128)(2,1)S(1)}, bf16[2,8,16,256]{3,2,1,0:T(8,128)(2,1)S(1)}, u32[]{:S(2)}, u32[]{:S(2)}) collective-permute-start(bf16[2,8,16,256]{3,2,1,0:T(8,128)(2,1)S(1)} %get-tuple-element.20), channel_id=1, source_target_pairs={{0,1},{1,0},{2,3},{3,2},{4,5},{5,4},{6,7},{7,6},{8,9},{9,8},{10,11... | collective-permute-start | bytes 393224 | tf_op jit(solution)/shard_map/ppermute | solution.py:55
  31.0 4.2 %collective-permute-done.4 = bf16[2,8,16,256]{3,2,1,0:T(8,128)(2,1)S(1)} collective-permute-done((bf16[2,8,16,256]{3,2,1,0:T(8,128)(2,1)S(1)}, bf16[2,8,16,256]{3,2,1,0:T(8,128)(2,1)S(1)}, u32[]{:S(2)}, u32[]{:S(2)}) %collective-permute-start.4) | collective-permute-done | bytes 131104 | tf_op jit(solution)/shard_map/ppermute | solution.py:55
  35.2 2.8 %collective-permute-start.7 = (bf16[2,8,16,256]{3,2,1,0:T(8,128)(2,1)S(1)}, bf16[2,8,16,256]{3,2,1,0:T(8,128)(2,1)S(1)}, u32[]{:S(2)}, u32[]{:S(2)}) collective-permute-start(bf16[2,8,16,256]{3,2,1,0:T(8,128)(2,1)S(1)} %get-tuple-element.33), channel_id=1, source_target_pairs={{0,24},{8,0},{16,8},{24,16},{1,25},{9,1},{17,9},{25,17},{2,26},{10... | collective-permute-start | bytes 393224 | tf_op jit(solution)/shard_map/ppermute | solution.py:55
  40.2 2.6 %collective-permute-start.9 = (bf16[2,8,16,256]{3,2,1,0:T(8,128)(2,1)S(1)}, bf16[2,8,16,256]{3,2,1,0:T(8,128)(2,1)S(1)}, u32[]{:S(2)}, u32[]{:S(2)}) collective-permute-start(bf16[2,8,16,256]{3,2,1,0:T(8,128)(2,1)S(1)} %get-tuple-element.34), channel_id=1, source_target_pairs={{0,4},{2,6},{4,0},{6,2},{1,5},{3,7},{5,1},{7,3},{8,12},{10,14},{12... | collective-permute-start | bytes 393224 | tf_op jit(solution)/shard_map/ppermute | solution.py:55
  44.7 4.4 %cond_planes.1 = f32[256,1024]{1,0:T(8,128)} custom-call(f32[256,512]{1,0:T(8,128)S(1)} %copy-done.6, bf16[8,16,256]{2,1,0:T(8,128)(2,1)S(1)} %slice.22.home_ref, bf16[8,16,256]{2,1,0:T(8,128)(2,1)S(1)} %get-tuple-element.21.away_ref), custom_call_target="tpu_custom_call" | custom-call | flops 1610612736 | bytes 2097152 | tf_op jit(solution)/shard_map/cond_planes/pallas_call | solution.py:214
  50.2 12.8 %all-to-all-start = ((f32[32,8,1024]{2,1,0:T(8,128)}), f32[32,8,1024]{2,1,0:T(8,128)S(1)}, u32[]{:S(2)}, u32[]{:S(2)}) async-start(f32[32,8,1024]{2,1,0:T(8,128)} %bitcast.29), calls=%async_computation | async-start | bytes 2097152 | tf_op jit(solution)/shard_map/all_to_all | solution.py:424
  63.4 1.9 %compare_select_fusion = (f32[256,256]{1,0:T(8,128)S(1)}, f32[256,256]{1,0:T(8,128)}) fusion(s32[256]{0:T(256)S(1)} %get-tuple-element.38, s32[256]{0:T(256)S(1)} %get-tuple-element.41, s32[256]{0:T(256)S(1)} %get-tuple-element.39, s32[256]{0:T(256)S(1)} %get-tuple-element.40), kind=kLoop, calls=%fused_computation.13 | loop fusion | flops 1114112 | bytes 528384 | tf_op jit(solution)/shard_map/jit(_where)/select_n | solution.py:367
  65.3 2.7 %collective-permute-start.12 = (bf16[4,2,8,16,256]{4,3,2,1,0:T(8,128)(2,1)S(1)}, bf16[4,2,8,16,256]{4,3,2,1,0:T(8,128)(2,1)S(1)}, u32[]{:S(2)}, u32[]{:S(2)}) collective-permute-start(bf16[4,2,8,16,256]{4,3,2,1,0:T(8,128)(2,1)S(1)} %pad_maximum_fusion.3), channel_id=1, source_target_pairs={{0,4},{2,6},{4,0},{6,2},{1,5},{3,7},{5,1},{7,3},{8,12},{10,14},{12... | collective-permute-start | bytes 1572872 | tf_op jit(solution)/shard_map/ppermute | solution.py:55
  69.8 3.0 %collective-permute-start.15 = (bf16[4,2,8,16,256]{4,3,2,1,0:T(8,128)(2,1)}, bf16[4,2,8,16,256]{4,3,2,1,0:T(8,128)(2,1)S(1)}, u32[]{:S(2)}, u32[]{:S(2)}) collective-permute-start(bf16[4,2,8,16,256]{4,3,2,1,0:T(8,128)(2,1)} %pad_maximum_fusion.4), channel_id=1, source_target_pairs={{0,16},{8,24},{16,0},{24,8},{1,17},{9,25},{17,1},{25,9},{2,18},{10... | collective-permute-start | bytes 1572872 | tf_op jit(solution)/shard_map/ppermute | solution.py:55
  73.4 12.5 %collective-permute-done.13 = bf16[4,2,8,16,256]{4,3,2,1,0:T(8,128)(2,1)S(1)} collective-permute-done((bf16[4,2,8,16,256]{4,3,2,1,0:T(8,128)(2,1)S(1)}, bf16[4,2,8,16,256]{4,3,2,1,0:T(8,128)(2,1)S(1)}, u32[]{:S(2)}, u32[]{:S(2)}) %collective-permute-start.13) | collective-permute-done | bytes 524320 | tf_op jit(solution)/shard_map/ppermute | solution.py:55
  85.9 2.7 %collective-permute-start.16 = (bf16[4,2,8,16,256]{4,3,2,1,0:T(8,128)(2,1)}, bf16[4,2,8,16,256]{4,3,2,1,0:T(8,128)(2,1)S(1)}, u32[]{:S(2)}, u32[]{:S(2)}) collective-permute-start(bf16[4,2,8,16,256]{4,3,2,1,0:T(8,128)(2,1)} %pad_maximum_fusion.4), channel_id=1, source_target_pairs={{0,24},{8,0},{16,8},{24,16},{1,25},{9,1},{17,9},{25,17},{2,26},{10... | collective-permute-start | bytes 1572872 | tf_op jit(solution)/shard_map/ppermute | solution.py:55
  88.7 2.2 %copy-done.5 = bf16[256,8192]{1,0:T(8,128)(2,1)S(1)} copy-done((bf16[256,8192]{1,0:T(8,128)(2,1)S(1)}, bf16[256,8192]{1,0:T(8,128)(2,1)}, u32[]{:S(2)}) %copy-start.5) | copy-done | bytes 4194328
  90.9 8.8 %screened_transform.3 = (bf16[8,512,256]{2,1,0:T(8,128)(2,1)S(1)}, f32[8,128]{1,0:T(8,128)}) custom-call(s32[32,1,256]{2,1,0:T(1,128)S(1)} %bitcast.78, bf16[64,32]{1,0:T(8,128)(2,1)S(1)} %copy-done.9, bf16[2,256,256]{2,1,0:T(8,128)(2,1)S(1)} %copy-done.7, bf16[2,256,256]{2,1,0:T(8,128)(2,1)S(1)} %copy-done.8, bf16[256,8192]{1,0:T(8,128)(2,1)S(1)} %copy-done.5), custom_call_target="tpu_custom_call" | custom-call | flops 6845104128 | bytes 7340032 | tf_op jit(solution)/shard_map/screened_transform/pallas_call | solution.py:133
  99.7 2.2 %pad_maximum_fusion = bf16[4,4,2,8,16,256]{5,4,3,2,1,0:T(8,128)(2,1)S(1)} fusion(bf16[1,4,2,8,16,256]{5,4,3,2,1,0:T(8,128)(2,1)} %bitcast.88, bf16[1,4,2,8,16,256]{5,4,3,2,1,0:T(8,128)(2,1)S(1)} %bitcast.91, bf16[1,4,2,8,16,256]{5,4,3,2,1,0:T(8,128)(2,1)S(1)} %bitcast.92, bf16[1,4,2,8,16,256]{5,4,3,2,1,0:T(8,128)(2,1)} %bitcast.79), kind=kLoop, calls=%fused_computation | loop fusion | flops 3145728 | bytes 4194304 | tf_op jit(solution)/shard_map/stack | solution.py:425
  102.0 2.7 %pad_maximum_fusion.1 = bf16[4,4,2,8,16,256]{5,4,3,2,1,0:T(8,128)(2,1)} fusion(bf16[1,4,2,8,16,256]{5,4,3,2,1,0:T(8,128)(2,1)S(1)} %bitcast.93, bf16[1,4,2,8,16,256]{5,4,3,2,1,0:T(8,128)(2,1)S(1)} %bitcast.89, bf16[1,4,2,8,16,256]{5,4,3,2,1,0:T(8,128)(2,1)S(1)} %bitcast.90, bf16[1,4,2,8,16,256]{5,4,3,2,1,0:T(8,128)(2,1)} %bitcast.32), kind=kLoop, calls=%fused_computation.1 | loop fusion | flops 3145728 | bytes 4194304 | tf_op jit(solution)/shard_map/stack | solution.py:426
  105.6 3.7 %cond_spectrum.1.cond_ref = bf16[1024,256]{1,0:T(8,128)(2,1)S(1)} custom-call(f32[256,256]{1,0:T(8,128)S(1)} %copy-done.1, f32[256,256]{1,0:T(8,128)S(1)} %get-tuple-element.36.sin_ref, f32[256,1024]{1,0:T(8,128)S(1)} %bitcast.75), custom_call_target="tpu_custom_call" | custom-call | flops 1610612736 | bytes 2097152 | tf_op jit(solution)/shard_map/cond_spectrum/pallas_call | solution.py:319
  110.9 12.0 %valence_response.1.r_ref = f32[1024,256]{1,0:T(8,128)S(1)} custom-call(s32[1]{0:T(128)} %bitcast.31.place_ref, bf16[32,8,16,256]{3,2,1,0:T(8,128)(2,1)S(1)} %bitcast.65, bf16[32,8,16,256]{3,2,1,0:T(8,128)(2,1)S(1)} %bitcast.69, bf16[32,8,16,256]{3,2,1,0:T(8,128)(2,1)S(1)} %bitcast.66, bf16[32,8,16,256]{3,2,1,0:T(8,128)(2,1)S(1)} %bitcast.70, ...), custom_call_target="tpu_custom_call" | custom-call | flops 36507222016 | bytes 9437184 | tf_op jit(solution)/shard_map/valence_response/pallas_call | solution.py:285
  123.6 19.5 %all_to_all.26 = f32[32,16,128]{2,1,0:T(8,128)S(1)} all-to-all(f32[32,16,128]{2,1,0:T(8,128)S(1)} %kernel_blocks.1), channel_id=1, replica_groups=mesh['zl'=4,'co'=2,'x'=4,'y'=4,'zh'=2] {'x','y'}, dimensions={0} | all-to-all | bytes 524288 | tf_op jit(solution)/shard_map/all_to_all | solution.py:432
  143.8 9.8 %all-to-all-start.2 = ((f32[16,2,16,128]{3,2,1,0:T(8,128)}), f32[16,2,16,128]{3,2,1,0:T(8,128)S(1)}, u32[]{:S(2)}, u32[]{:S(2)}) async-start(f32[16,2,16,128]{3,2,1,0:T(8,128)} %broadcast_in_dim.16), calls=%async_computation.2 | async-start | bytes 524288 | tf_op jit(solution)/shard_map/all_to_all | solution.py:65
  153.6 12.2 %all-to-all-done.2 = f32[16,2,16,128]{3,2,1,0:T(8,128)S(1)} async-done(((f32[16,2,16,128]{3,2,1,0:T(8,128)}), f32[16,2,16,128]{3,2,1,0:T(8,128)S(1)}, u32[]{:S(2)}, u32[]{:S(2)}) %all-to-all-start.2) | async-done | bytes 262176 | tf_op jit(solution)/shard_map/all_to_all | solution.py:65
  166.5 14.7 %all_to_all.27.full_ref = f32[16,2,32,128]{3,2,1,0:T(8,128)S(1)} all-to-all(f32[16,2,32,128]{3,2,1,0:T(8,128)S(1)} %broadcast_in_dim.21), channel_id=1, replica_groups=mesh['zl'=4,'co'=2,'x'=4,'y'=4,'zh'=2] {'x','y'}, dimensions={0} | all-to-all | bytes 1048576 | tf_op jit(solution)/shard_map/all_to_all | solution.py:65
  (82 shorter events, 17.7 us)
Async XLA Ops:
  1.5 18.5 %collective-permute-start.2 = (bf16[8,32,256]{2,1,0:T(8,128)(2,1)S(1)}, bf16[8,32,256]{2,1,0:T(8,128)(2,1)S(1)}, u32[]{:S(2)}, u32[]{:S(2)}) collective-permute-start(bf16[8,32,256]{2,1,0:T(8,128)(2,1)S(1)} %bitcast.82), channel_id=1, source_target_pairs={{0,192},{64,0},{128,64},{192,128},{1,193},{65,1},{129,65},{193,129... | collective-permute-start | bytes 393224 | tf_op jit(solution)/shard_map/ppermute | solution.py:55
  6.2 13.8 %collective-permute-start.1 = (bf16[8,32,256]{2,1,0:T(8,128)(2,1)S(1)}, bf16[8,32,256]{2,1,0:T(8,128)(2,1)S(1)}, u32[]{:S(2)}, u32[]{:S(2)}) collective-permute-start(bf16[8,32,256]{2,1,0:T(8,128)(2,1)S(1)} %bitcast.83), channel_id=1, source_target_pairs={{0,128},{64,192},{128,0},{192,64},{1,129},{65,193},{129,1},{193,65... | collective-permute-start | bytes 393224 | tf_op jit(solution)/shard_map/ppermute | solution.py:55
  6.3 13.8 %collective-permute-start = (bf16[8,32,256]{2,1,0:T(8,128)(2,1)S(1)}, bf16[8,32,256]{2,1,0:T(8,128)(2,1)S(1)}, u32[]{:S(2)}, u32[]{:S(2)}) collective-permute-start(bf16[8,32,256]{2,1,0:T(8,128)(2,1)S(1)} %bitcast.84), channel_id=1, source_target_pairs={{0,64},{64,128},{128,192},{192,0},{1,65},{65,129},{129,193},{193,1... | collective-permute-start | bytes 393224 | tf_op jit(solution)/shard_map/ppermute | solution.py:55
  20.1 24.6 %copy-start.6 = (f32[256,512]{1,0:T(8,128)S(1)}, f32[256,512]{1,0:T(8,128)}, u32[]{:S(2)}) copy-start(f32[256,512]{1,0:T(8,128)} %constant.197.clone.table_ref) | copy-start | bytes 1572868
  20.2 2.0 %collective-permute-start.3 = (bf16[32,32,256]{2,1,0:T(8,128)(2,1)S(1)}, bf16[32,32,256]{2,1,0:T(8,128)(2,1)S(1)}, u32[]{:S(2)}, u32[]{:S(2)}) collective-permute-start(bf16[32,32,256]{2,1,0:T(8,128)(2,1)S(1)} %bitcast.73), channel_id=1, source_target_pairs={{0,32},{32,0},{1,33},{33,1},{2,34},{34,2},{3,35},{35,3},{4,36},{36... | collective-permute-start | bytes 1572872 | tf_op jit(solution)/shard_map/ppermute | solution.py:55
  25.6 9.6 %collective-permute-start.4 = (bf16[2,8,16,256]{3,2,1,0:T(8,128)(2,1)S(1)}, bf16[2,8,16,256]{3,2,1,0:T(8,128)(2,1)S(1)}, u32[]{:S(2)}, u32[]{:S(2)}) collective-permute-start(bf16[2,8,16,256]{3,2,1,0:T(8,128)(2,1)S(1)} %get-tuple-element.20), channel_id=1, source_target_pairs={{0,1},{1,0},{2,3},{3,2},{4,5},{5,4},{6,7},{7,6},{8,9},{9,8},{10,11... | collective-permute-start | bytes 393224 | tf_op jit(solution)/shard_map/ppermute | solution.py:55
  35.2 7.8 %collective-permute-start.7 = (bf16[2,8,16,256]{3,2,1,0:T(8,128)(2,1)S(1)}, bf16[2,8,16,256]{3,2,1,0:T(8,128)(2,1)S(1)}, u32[]{:S(2)}, u32[]{:S(2)}) collective-permute-start(bf16[2,8,16,256]{3,2,1,0:T(8,128)(2,1)S(1)} %get-tuple-element.33), channel_id=1, source_target_pairs={{0,24},{8,0},{16,8},{24,16},{1,25},{9,1},{17,9},{25,17},{2,26},{10... | collective-permute-start | bytes 393224 | tf_op jit(solution)/shard_map/ppermute | solution.py:55
  38.1 11.0 %collective-permute-start.6 = (bf16[2,8,16,256]{3,2,1,0:T(8,128)(2,1)S(1)}, bf16[2,8,16,256]{3,2,1,0:T(8,128)(2,1)S(1)}, u32[]{:S(2)}, u32[]{:S(2)}) collective-permute-start(bf16[2,8,16,256]{3,2,1,0:T(8,128)(2,1)S(1)} %get-tuple-element.33), channel_id=1, source_target_pairs={{0,16},{8,24},{16,0},{24,8},{1,17},{9,25},{17,1},{25,9},{2,18},{10... | collective-permute-start | bytes 393224 | tf_op jit(solution)/shard_map/ppermute | solution.py:55
  38.9 10.2 %collective-permute-start.5 = (bf16[2,8,16,256]{3,2,1,0:T(8,128)(2,1)S(1)}, bf16[2,8,16,256]{3,2,1,0:T(8,128)(2,1)S(1)}, u32[]{:S(2)}, u32[]{:S(2)}) collective-permute-start(bf16[2,8,16,256]{3,2,1,0:T(8,128)(2,1)S(1)} %get-tuple-element.33), channel_id=1, source_target_pairs={{0,8},{8,16},{16,24},{24,0},{1,9},{9,17},{17,25},{25,1},{2,10},{10... | collective-permute-start | bytes 393224 | tf_op jit(solution)/shard_map/ppermute | solution.py:55
  39.7 9.5 %collective-permute-start.10 = (bf16[2,8,16,256]{3,2,1,0:T(8,128)(2,1)S(1)}, bf16[2,8,16,256]{3,2,1,0:T(8,128)(2,1)S(1)}, u32[]{:S(2)}, u32[]{:S(2)}) collective-permute-start(bf16[2,8,16,256]{3,2,1,0:T(8,128)(2,1)S(1)} %get-tuple-element.34), channel_id=1, source_target_pairs={{0,6},{2,0},{4,2},{6,4},{1,7},{3,1},{5,3},{7,5},{8,14},{10,8},{12,... | collective-permute-start | bytes 393224 | tf_op jit(solution)/shard_map/ppermute | solution.py:55
  40.2 9.1 %collective-permute-start.9 = (bf16[2,8,16,256]{3,2,1,0:T(8,128)(2,1)S(1)}, bf16[2,8,16,256]{3,2,1,0:T(8,128)(2,1)S(1)}, u32[]{:S(2)}, u32[]{:S(2)}) collective-permute-start(bf16[2,8,16,256]{3,2,1,0:T(8,128)(2,1)S(1)} %get-tuple-element.34), channel_id=1, source_target_pairs={{0,4},{2,6},{4,0},{6,2},{1,5},{3,7},{5,1},{7,3},{8,12},{10,14},{12... | collective-permute-start | bytes 393224 | tf_op jit(solution)/shard_map/ppermute | solution.py:55
  43.0 6.2 %collective-permute-start.8 = (bf16[2,8,16,256]{3,2,1,0:T(8,128)(2,1)S(1)}, bf16[2,8,16,256]{3,2,1,0:T(8,128)(2,1)S(1)}, u32[]{:S(2)}, u32[]{:S(2)}) collective-permute-start(bf16[2,8,16,256]{3,2,1,0:T(8,128)(2,1)S(1)} %get-tuple-element.34), channel_id=1, source_target_pairs={{0,2},{2,4},{4,6},{6,0},{1,3},{3,5},{5,7},{7,1},{8,10},{10,12},{12... | collective-permute-start | bytes 393224 | tf_op jit(solution)/shard_map/ppermute | solution.py:55
  49.2 50.5 %copy-start.13 = (bf16[4,2,8,16,256]{4,3,2,1,0:T(8,128)(2,1)}, bf16[4,2,8,16,256]{4,3,2,1,0:T(8,128)(2,1)S(1)}, u32[]{:S(2)}) copy-start(bf16[4,2,8,16,256]{4,3,2,1,0:T(8,128)(2,1)S(1)} %pad_maximum_fusion.3) | copy-start | bytes 1572868
  49.2 39.5 %copy-start.7 = (bf16[2,256,256]{2,1,0:T(8,128)(2,1)S(1)}, bf16[2,256,256]{2,1,0:T(8,128)(2,1)}, u32[]{:S(2)}) copy-start(bf16[2,256,256]{2,1,0:T(8,128)(2,1)} %constant.195.clone.high_ref) | copy-start | bytes 786436
  49.2 39.5 %copy-start.8 = (bf16[2,256,256]{2,1,0:T(8,128)(2,1)S(1)}, bf16[2,256,256]{2,1,0:T(8,128)(2,1)}, u32[]{:S(2)}) copy-start(bf16[2,256,256]{2,1,0:T(8,128)(2,1)} %constant.196.clone.low_ref) | copy-start | bytes 786436
  49.2 39.5 %copy-start.9 = (bf16[64,32]{1,0:T(8,128)(2,1)S(1)}, bf16[64,32]{1,0:T(8,128)(2,1)}, u32[]{:S(2)}) copy-start(bf16[64,32]{1,0:T(8,128)(2,1)} %constant.198.clone.line_ref) | copy-start | bytes 12292
  50.2 54.5 %all-to-all-start = ((f32[32,8,1024]{2,1,0:T(8,128)}), f32[32,8,1024]{2,1,0:T(8,128)S(1)}, u32[]{:S(2)}, u32[]{:S(2)}) async-start(f32[32,8,1024]{2,1,0:T(8,128)} %bitcast.29), calls=%async_computation | async-start | bytes 2097152 | tf_op jit(solution)/shard_map/all_to_all | solution.py:424
  63.0 22.9 %collective-permute-start.13 = (bf16[4,2,8,16,256]{4,3,2,1,0:T(8,128)(2,1)S(1)}, bf16[4,2,8,16,256]{4,3,2,1,0:T(8,128)(2,1)S(1)}, u32[]{:S(2)}, u32[]{:S(2)}) collective-permute-start(bf16[4,2,8,16,256]{4,3,2,1,0:T(8,128)(2,1)S(1)} %pad_maximum_fusion.3), channel_id=1, source_target_pairs={{0,6},{2,0},{4,2},{6,4},{1,7},{3,1},{5,3},{7,5},{8,14},{10,8},{12,... | collective-permute-start | bytes 1572872 | tf_op jit(solution)/shard_map/ppermute | solution.py:55
  65.3 34.4 %collective-permute-start.12 = (bf16[4,2,8,16,256]{4,3,2,1,0:T(8,128)(2,1)S(1)}, bf16[4,2,8,16,256]{4,3,2,1,0:T(8,128)(2,1)S(1)}, u32[]{:S(2)}, u32[]{:S(2)}) collective-permute-start(bf16[4,2,8,16,256]{4,3,2,1,0:T(8,128)(2,1)S(1)} %pad_maximum_fusion.3), channel_id=1, source_target_pairs={{0,4},{2,6},{4,0},{6,2},{1,5},{3,7},{5,1},{7,3},{8,12},{10,14},{12... | collective-permute-start | bytes 1572872 | tf_op jit(solution)/shard_map/ppermute | solution.py:55
  68.0 31.7 %collective-permute-start.11 = (bf16[4,2,8,16,256]{4,3,2,1,0:T(8,128)(2,1)S(1)}, bf16[4,2,8,16,256]{4,3,2,1,0:T(8,128)(2,1)S(1)}, u32[]{:S(2)}, u32[]{:S(2)}) collective-permute-start(bf16[4,2,8,16,256]{4,3,2,1,0:T(8,128)(2,1)S(1)} %pad_maximum_fusion.3), channel_id=1, source_target_pairs={{0,2},{2,4},{4,6},{6,0},{1,3},{3,5},{5,7},{7,1},{8,10},{10,12},{12... | collective-permute-start | bytes 1572872 | tf_op jit(solution)/shard_map/ppermute | solution.py:55
  69.8 32.2 %collective-permute-start.15 = (bf16[4,2,8,16,256]{4,3,2,1,0:T(8,128)(2,1)}, bf16[4,2,8,16,256]{4,3,2,1,0:T(8,128)(2,1)S(1)}, u32[]{:S(2)}, u32[]{:S(2)}) collective-permute-start(bf16[4,2,8,16,256]{4,3,2,1,0:T(8,128)(2,1)} %pad_maximum_fusion.4), channel_id=1, source_target_pairs={{0,16},{8,24},{16,0},{24,8},{1,17},{9,25},{17,1},{25,9},{2,18},{10... | collective-permute-start | bytes 1572872 | tf_op jit(solution)/shard_map/ppermute | solution.py:55
  72.8 29.2 %collective-permute-start.14 = (bf16[4,2,8,16,256]{4,3,2,1,0:T(8,128)(2,1)}, bf16[4,2,8,16,256]{4,3,2,1,0:T(8,128)(2,1)S(1)}, u32[]{:S(2)}, u32[]{:S(2)}) collective-permute-start(bf16[4,2,8,16,256]{4,3,2,1,0:T(8,128)(2,1)} %pad_maximum_fusion.4), channel_id=1, source_target_pairs={{0,8},{8,16},{16,24},{24,0},{1,9},{9,17},{17,25},{25,1},{2,10},{10... | collective-permute-start | bytes 1572872 | tf_op jit(solution)/shard_map/ppermute | solution.py:55
  85.9 16.0 %collective-permute-start.16 = (bf16[4,2,8,16,256]{4,3,2,1,0:T(8,128)(2,1)}, bf16[4,2,8,16,256]{4,3,2,1,0:T(8,128)(2,1)S(1)}, u32[]{:S(2)}, u32[]{:S(2)}) collective-permute-start(bf16[4,2,8,16,256]{4,3,2,1,0:T(8,128)(2,1)} %pad_maximum_fusion.4), channel_id=1, source_target_pairs={{0,24},{8,0},{16,8},{24,16},{1,25},{9,1},{17,9},{25,17},{2,26},{10... | collective-permute-start | bytes 1572872 | tf_op jit(solution)/shard_map/ppermute | solution.py:55
  143.8 22.1 %all-to-all-start.2 = ((f32[16,2,16,128]{3,2,1,0:T(8,128)}), f32[16,2,16,128]{3,2,1,0:T(8,128)S(1)}, u32[]{:S(2)}, u32[]{:S(2)}) async-start(f32[16,2,16,128]{3,2,1,0:T(8,128)} %broadcast_in_dim.16), calls=%async_computation.2 | async-start | bytes 524288 | tf_op jit(solution)/shard_map/all_to_all | solution.py:65
  (10 other events, 58.3 us)

commit v10 on v7

--- a/solution.py
+++ b/solution.py
@@ -156,6 +156,15 @@
     )(gmap.reshape(32, 1, 256), jnp.asarray(line), jnp.asarray(high), jnp.asarray(low), screened)
 
 
+def halves(value):
+    high = value.astype(BF)
+    return high, (value - high.astype(F32)).astype(BF)
+
+
+def dot_halves(a, b, contract=((1,), (0,))):
+    return dot(a[0], b[0], contract) + (dot(a[0], b[1], contract) + dot(a[1], b[0], contract))
+
+
 def choose_kernel(partner_ref, place_ref, flip_ref, near_ref, far_ref, val_ref, cond_ref):
     level, core = place_ref[0], place_ref[1]
     for m in range(8):
@@ -188,7 +197,7 @@
     )(partner, place, flip, near, far)
 
 
-def cond_kernel(table_ref, home_ref, away_ref, x_ref, rows_ref):
+def cond_kernel(high_ref, low_ref, home_ref, away_ref, x_ref, rows_ref):
     for k in range(8):
         home, away = home_ref[k].astype(F32), away_ref[k].astype(F32)
         hr, hi = home[:8], home[8:]
@@ -201,19 +210,19 @@
             rows_ref[at : at + 8, 256:] = imag
             rows_ref[at + 64 : at + 72, :256] = imag
             rows_ref[at + 64 : at + 72, 256:] = -real
-    for k in range(8):
-        x_ref[:, k * 128 : (k + 1) * 128] = dot(
-            table_ref[...], rows_ref[k * 128 : (k + 1) * 128], ((1,), (1,)), EXACT
-        )
+    table = high_ref[...], low_ref[...]
+    for k in range(4):
+        rows = halves(rows_ref[k * 256 : (k + 1) * 256])
+        x_ref[:, k * 256 : (k + 1) * 256] = dot_halves(table, rows, ((1,), (1,)))
 
 
 def cond_planes(home, away):
     angles = plane_angles()
-    table = np.concatenate([np.cos(angles), np.sin(angles)], axis=1).astype(np.float32)
+    high, low = split_table(np.concatenate([np.cos(angles), np.sin(angles)], axis=1))
     return pl.pallas_call(
         cond_kernel,
         out_shape=jax.ShapeDtypeStruct((256, 1024), F32),
-        in_specs=[pl.BlockSpec(memory_space=pltpu.VMEM)] * 3,
+        in_specs=[pl.BlockSpec(memory_space=pltpu.VMEM)] * 4,
         out_specs=pl.BlockSpec(memory_space=pltpu.VMEM),
         scratch_shapes=[pltpu.VMEM((1024, 512), F32)],
         compiler_params=pltpu.CompilerParams(vmem_limit_bytes=24 * MIB),
@@ -221,7 +230,7 @@
             flops=12 * 256 * 512 * 1024, bytes_accessed=2 * MIB, transcendentals=0
         ),
         name="cond_planes",
-    )(jnp.asarray(table), home, away)
+    )(jnp.asarray(high), jnp.asarray(low), home, away)
 
 
 def build_rows(rows_ref, waves, mirrored):
@@ -305,13 +314,18 @@
 
 def spectrum_kernel(cos_ref, sin_ref, x_ref, out_ref):
     first = lax.broadcasted_iota(jnp.int32, (1, 128), 1) < 64
-    for k in range(8):
-        x = x_ref[:, k * 128 : (k + 1) * 128]
-        turned = pltpu.roll(x, 64, 1)
-        turned = jnp.where(first, turned, -turned)
-        cond = dot(cos_ref[...], x, precision=EXACT) + dot(sin_ref[...], turned, precision=EXACT)
+    table = halves(jnp.concatenate([cos_ref[...], sin_ref[...]], axis=1))
+    for pair in range(4):
+        straight, crossed = [], []
+        for k in (2 * pair, 2 * pair + 1):
+            x = x_ref[:, k * 128 : (k + 1) * 128]
+            other = pltpu.roll(x, 64, 1)
+            straight.append(x)
+            crossed.append(jnp.where(first, other, -other))
+        both = [jnp.concatenate(part, axis=1) for part in (straight, crossed)]
+        cond = dot_halves(table, halves(jnp.concatenate(both, axis=0)))
         cond = (cond * NORM).astype(BF).astype(F32).T
-        out_ref[k * 128 : (k + 1) * 128] = cond.astype(BF)
+        out_ref[pair * 256 : (pair + 1) * 256] = cond.astype(BF)
 
 
 def cond_spectrum(cosine, sine, columns):
@@ -371,10 +385,11 @@
     for m in range(4):
         for n in range(4):
             for c in (2 * n, 2 * n + 1):
-                piece = full_ref[m * 4 + n, 0, (c & 1) * 16 : (c & 1) * 16 + 16]
+                piece = full_ref[m * 4 + n, 0, (c & 1) * 16 : (c & 1) * 16 + 16].astype(F32)
                 at = (c * 4 + m) * 128
                 rows_ref[:, :, at : at + 128] = piece.reshape(8, 2, 128)
-            even, odd = full_ref[m * 4 + n, 1, :16], full_ref[m * 4 + n, 1, 16:]
+            even = full_ref[m * 4 + n, 1, :16].astype(F32)
+            odd = full_ref[m * 4 + n, 1, 16:].astype(F32)
             first = jnp.where(low, even, pltpu.roll(odd, 64, 1))
             second = jnp.where(low, pltpu.roll(even, 64, 1), odd)
             at = (2 * m * 4 + n) * 128
@@ -439,7 +454,8 @@
     turn = (lane[:, None] == moved[None, :]).astype(F32)
     sign = jnp.where(jnp.arange(32) % 2 == 0, 1.0, -1.0).astype(F32)
     mirror = jnp.dot(mirror, turn, precision=EXACT) * sign[:, None]
-    full = copies_to_all(jnp.stack([mine.reshape(32, 128), mirror]), ("x", "y"))
+    both = jnp.stack([mine.reshape(32, 128), mirror]).astype(BF)
+    full = copies_to_all(both, ("x", "y"))
     return lay_out(full)
 
 

time: 162 us -> 157 us (0.969)
  Pallas kernels: 38.2 us -> 33.2 us
  waiting for transfers between devices: 28.7 us -> 31 us
  blocking collectives: 27.6 us -> 25.7 us
    all_to_all x1, blocking collectives: 14.7 us -> 11.9 us  [copies_to_all(): return lax.all_to_all(copies, axes, split_axis=0, concat_axis=0, tiled=True)]
    pallas_call x1, Pallas kernels: 3.65 us -> 1.22 us  [cond_spectrum(): pl.pallas_call(spectrum_kernel, out_shape=jax.ShapeDtypeStruct((1024, 256...]
    pallas_call x1, Pallas kernels: 4.44 us -> 2.03 us  [cond_planes(): pl.pallas_call(cond_kernel, out_shape=jax.ShapeDtypeStruct((256, 1024), F...]
    ppermute x17, waiting for transfers between devices: 16.5 us -> 18.7 us  [turned(): lax.ppermute(value, axis, [(i, (i + step) % size) for i in range(size)])]
  transfers between devices with their start and end apart: 19 -> 19, of which waited for: 6 -> 9; matrix products, arithmetic and copies ran while one was open for 3% -> 3% of each run, Pallas kernels for 19% -> 18%
where the time goes in v10:
time: 157 us; the launch traced here: 156 us
  starting transfers between devices  54.5 us (35%)
  Pallas kernels  33.2 us (21%)
  waiting for transfers between devices  31 us (20%)
  blocking collectives  25.7 us (16%)
  other arithmetic  5.69 us (4%)
  local copies, waits for them, and re-layouts  4.78 us (3%)
    ppermute x17, starting transfers between devices, turned(): lax.ppermute(value, axis, [(i, (i + step) % size) for i in range(size)])  32.3 us
    ppermute x17, waiting for transfers between devices, turned(): lax.ppermute(value, axis, [(i, (i + step) % size) for i in range(size)])  18.7 us
    pallas_call x1, Pallas kernels, screened_transform(): pl.pallas_call(screened_kernel, grid=(LINE_STEPS + HALF,), in_specs=[pl.B...  13.9 us
    all_to_all x1, blocking collectives, on_device(): lax.all_to_all(blocks, ('x', 'y'), split_axis=0, concat_axis=0, tiled=True)  13.8 us
    all_to_all x1, waiting for transfers between devices, copies_to_all(): return lax.all_to_all(copies, axes, split_axis=0, concat_axis=0, tiled=True)  12.2 us
    all_to_all x1, blocking collectives, copies_to_all(): return lax.all_to_all(copies, axes, split_axis=0, concat_axis=0, tiled=True)  11.9 us
    pallas_call x1, Pallas kernels, response(): pl.pallas_call(response_kernel, grid_spec=pltpu.PrefetchScalarGridSpec(nu...  11.8 us
    all_to_all x1, starting transfers between devices, on_device(): lax.all_to_all(planes, GA, split_axis=0, concat_axis=0, tiled=True)  11.6 us
  transfers between devices with their start and end apart: 19, of which 9 were waited for; matrix products, arithmetic and copies ran while one was open for 3% of the time, Pallas kernels for 18%

profile of v10, /device:TPU:8, one launch (start us, length us, event | category | flops | bytes accessed | tf_op | source)
XLA Modules:
  0.0 156.1 jit_solution(2459240900485599942)
XLA Ops:
  1.6 4.7 %collective-permute-start.2 = (bf16[8,32,256]{2,1,0:T(8,128)(2,1)S(1)}, bf16[8,32,256]{2,1,0:T(8,128)(2,1)S(1)}, u32[]{:S(2)}, u32[]{:S(2)}) collective-permute-start(bf16[8,32,256]{2,1,0:T(8,128)(2,1)S(1)} %bitcast.81), channel_id=1, source_target_pairs={{0,192},{64,0},{128,64},{192,128},{1,193},{65,1},{129,65},{193,129... | collective-permute-start | bytes 393224 | tf_op jit(solution)/shard_map/ppermute | solution.py:55
  7.0 3.2 %collective-permute-done.2 = bf16[8,32,256]{2,1,0:T(8,128)(2,1)S(1)} collective-permute-done((bf16[8,32,256]{2,1,0:T(8,128)(2,1)S(1)}, bf16[8,32,256]{2,1,0:T(8,128)(2,1)S(1)}, u32[]{:S(2)}, u32[]{:S(2)}) %collective-permute-start.2) | collective-permute-done | bytes 131104 | tf_op jit(solution)/shard_map/ppermute | solution.py:55
  10.2 7.3 %collective-permute-done.1 = bf16[8,32,256]{2,1,0:T(8,128)(2,1)S(1)} collective-permute-done((bf16[8,32,256]{2,1,0:T(8,128)(2,1)S(1)}, bf16[8,32,256]{2,1,0:T(8,128)(2,1)S(1)}, u32[]{:S(2)}, u32[]{:S(2)}) %collective-permute-start.1) | collective-permute-done | bytes 131104 | tf_op jit(solution)/shard_map/ppermute | solution.py:55
  17.9 1.8 %collective-permute-done.3.far_ref = bf16[32,32,256]{2,1,0:T(8,128)(2,1)S(1)} collective-permute-done((bf16[32,32,256]{2,1,0:T(8,128)(2,1)S(1)}, bf16[32,32,256]{2,1,0:T(8,128)(2,1)S(1)}, u32[]{:S(2)}, u32[]{:S(2)}) %collective-permute-start.3) | collective-permute-done | bytes 524320 | tf_op jit(solution)/shard_map/ppermute | solution.py:55
  20.3 2.7 %partner_choice.1 = (bf16[2,8,16,256]{3,2,1,0:T(8,128)(2,1)S(1)}, bf16[8,16,256]{2,1,0:T(8,128)(2,1)S(1)}) custom-call(s32[64]{0:T(128)S(1)} %copy-done, s32[2]{0:T(128)S(1)} %pad_add_fusion.place_ref, bf16[256,256]{1,0:T(8,128)(2,1)S(1)} %fusion.5.flip_ref, bf16[32,32,256]{2,1,0:T(8,128)(2,1)S(1)} %bitcast.74, ...), custom_call_target="tpu_custom_call" | custom-call | tf_op jit(solution)/shard_map/partner_choice/pallas_call | solution.py:189
  23.0 5.5 %collective-permute-start.4 = (bf16[2,8,16,256]{3,2,1,0:T(8,128)(2,1)S(1)}, bf16[2,8,16,256]{3,2,1,0:T(8,128)(2,1)S(1)}, u32[]{:S(2)}, u32[]{:S(2)}) collective-permute-start(bf16[2,8,16,256]{3,2,1,0:T(8,128)(2,1)S(1)} %get-tuple-element.11), channel_id=1, source_target_pairs={{0,1},{1,0},{2,3},{3,2},{4,5},{5,4},{6,7},{7,6},{8,9},{9,8},{10,11... | collective-permute-start | bytes 393224 | tf_op jit(solution)/shard_map/ppermute | solution.py:55
  28.4 4.1 %collective-permute-done.4 = bf16[2,8,16,256]{3,2,1,0:T(8,128)(2,1)S(1)} collective-permute-done((bf16[2,8,16,256]{3,2,1,0:T(8,128)(2,1)S(1)}, bf16[2,8,16,256]{3,2,1,0:T(8,128)(2,1)S(1)}, u32[]{:S(2)}, u32[]{:S(2)}) %collective-permute-start.4) | collective-permute-done | bytes 131104 | tf_op jit(solution)/shard_map/ppermute | solution.py:55
  32.6 2.8 %collective-permute-start.7 = (bf16[2,8,16,256]{3,2,1,0:T(8,128)(2,1)S(1)}, bf16[2,8,16,256]{3,2,1,0:T(8,128)(2,1)S(1)}, u32[]{:S(2)}, u32[]{:S(2)}) collective-permute-start(bf16[2,8,16,256]{3,2,1,0:T(8,128)(2,1)S(1)} %get-tuple-element.21), channel_id=1, source_target_pairs={{0,24},{8,0},{16,8},{24,16},{1,25},{9,1},{17,9},{25,17},{2,26},{10... | collective-permute-start | bytes 393224 | tf_op jit(solution)/shard_map/ppermute | solution.py:55
  37.6 2.6 %collective-permute-start.9 = (bf16[2,8,16,256]{3,2,1,0:T(8,128)(2,1)S(1)}, bf16[2,8,16,256]{3,2,1,0:T(8,128)(2,1)S(1)}, u32[]{:S(2)}, u32[]{:S(2)}) collective-permute-start(bf16[2,8,16,256]{3,2,1,0:T(8,128)(2,1)S(1)} %get-tuple-element.22), channel_id=1, source_target_pairs={{0,4},{2,6},{4,0},{6,2},{1,5},{3,7},{5,1},{7,3},{8,12},{10,14},{12... | collective-permute-start | bytes 393224 | tf_op jit(solution)/shard_map/ppermute | solution.py:55
  42.1 2.0 %cond_planes.1 = f32[256,1024]{1,0:T(8,128)} custom-call(bf16[256,512]{1,0:T(8,128)(2,1)S(1)} %copy-done.6, bf16[256,512]{1,0:T(8,128)(2,1)S(1)} %copy-done.7, bf16[8,16,256]{2,1,0:T(8,128)(2,1)S(1)} %slice.22.home_ref, bf16[8,16,256]{2,1,0:T(8,128)(2,1)S(1)} %get-tuple-element.12.away_ref), custom_call_target="tpu_custom_call" | custom-call | flops 1610612736 | bytes 2097152 | tf_op jit(solution)/shard_map/cond_planes/pallas_call | solution.py:222
  46.4 2.9 %collective-permute-start.13 = (bf16[4,2,8,16,256]{4,3,2,1,0:T(8,128)(2,1)S(1)}, bf16[4,2,8,16,256]{4,3,2,1,0:T(8,128)(2,1)}, u32[]{:S(2)}, u32[]{:S(2)}) collective-permute-start(bf16[4,2,8,16,256]{4,3,2,1,0:T(8,128)(2,1)S(1)} %pad_maximum_fusion.3), channel_id=1, source_target_pairs={{0,6},{2,0},{4,2},{6,4},{1,7},{3,1},{5,3},{7,5},{8,14},{10,8},{12,... | collective-permute-start | bytes 1572872 | tf_op jit(solution)/shard_map/ppermute | solution.py:55
  50.7 2.0 %collective-permute-start.11 = (bf16[4,2,8,16,256]{4,3,2,1,0:T(8,128)(2,1)S(1)}, bf16[4,2,8,16,256]{4,3,2,1,0:T(8,128)(2,1)}, u32[]{:S(2)}, u32[]{:S(2)}) collective-permute-start(bf16[4,2,8,16,256]{4,3,2,1,0:T(8,128)(2,1)S(1)} %pad_maximum_fusion.3), channel_id=1, source_target_pairs={{0,2},{2,4},{4,6},{6,0},{1,3},{3,5},{5,7},{7,1},{8,10},{10,12},{12... | collective-permute-start | bytes 1572872 | tf_op jit(solution)/shard_map/ppermute | solution.py:55
  52.7 2.1 %collective-permute-start.15 = (bf16[4,2,8,16,256]{4,3,2,1,0:T(8,128)(2,1)}, bf16[4,2,8,16,256]{4,3,2,1,0:T(8,128)(2,1)}, u32[]{:S(2)}, u32[]{:S(2)}) collective-permute-start(bf16[4,2,8,16,256]{4,3,2,1,0:T(8,128)(2,1)} %pad_maximum_fusion.4), channel_id=1, source_target_pairs={{0,16},{8,24},{16,0},{24,8},{1,17},{9,25},{17,1},{25,9},{2,18},{10... | collective-permute-start | bytes 1572872 | tf_op jit(solution)/shard_map/ppermute | solution.py:55
  54.8 2.3 %collective-permute-start.14 = (bf16[4,2,8,16,256]{4,3,2,1,0:T(8,128)(2,1)}, bf16[4,2,8,16,256]{4,3,2,1,0:T(8,128)(2,1)}, u32[]{:S(2)}, u32[]{:S(2)}) collective-permute-start(bf16[4,2,8,16,256]{4,3,2,1,0:T(8,128)(2,1)} %pad_maximum_fusion.4), channel_id=1, source_target_pairs={{0,8},{8,16},{16,24},{24,0},{1,9},{9,17},{17,25},{25,1},{2,10},{10... | collective-permute-start | bytes 1572872 | tf_op jit(solution)/shard_map/ppermute | solution.py:55
  57.0 11.6 %all-to-all-start = ((f32[32,8,1024]{2,1,0:T(8,128)}), f32[32,8,1024]{2,1,0:T(8,128)S(1)}, u32[]{:S(2)}, u32[]{:S(2)}) async-start(f32[32,8,1024]{2,1,0:T(8,128)} %bitcast.23), calls=%async_computation | async-start | bytes 2097152 | tf_op jit(solution)/shard_map/all_to_all | solution.py:436
  68.7 2.8 %collective-permute-start.16 = (bf16[4,2,8,16,256]{4,3,2,1,0:T(8,128)(2,1)}, bf16[4,2,8,16,256]{4,3,2,1,0:T(8,128)(2,1)S(1)}, u32[]{:S(2)}, u32[]{:S(2)}) collective-permute-start(bf16[4,2,8,16,256]{4,3,2,1,0:T(8,128)(2,1)} %pad_maximum_fusion.4), channel_id=1, source_target_pairs={{0,24},{8,0},{16,8},{24,16},{1,25},{9,1},{17,9},{25,17},{2,26},{10... | collective-permute-start | bytes 1572872 | tf_op jit(solution)/shard_map/ppermute | solution.py:55
  71.5 2.2 %copy-done.3 = bf16[256,8192]{1,0:T(8,128)(2,1)S(1)} copy-done((bf16[256,8192]{1,0:T(8,128)(2,1)S(1)}, bf16[256,8192]{1,0:T(8,128)(2,1)}, u32[]{:S(2)}) %copy-start.3) | copy-done | bytes 4194328
  73.7 13.9 %screened_transform.1 = (bf16[17,512,256]{2,1,0:T(8,128)(2,1)S(1)}, f32[8,128]{1,0:T(8,128)}) custom-call(s32[32,1,256]{2,1,0:T(1,128)S(1)} %bitcast.77, bf16[96,32]{1,0:T(8,128)(2,1)S(1)} %copy-done.8, bf16[2,256,256]{2,1,0:T(8,128)(2,1)S(1)} %copy-done.4, bf16[2,256,256]{2,1,0:T(8,128)(2,1)S(1)} %copy-done.5, bf16[256,8192]{1,0:T(8,128)(2,1)S(1)} %copy-done.3), custom_call_target="tpu_custom_call" | custom-call | flops 13690208256 | bytes 9437184 | tf_op jit(solution)/shard_map/screened_transform/pallas_call | solution.py:132
  89.8 1.6 %pad_maximum_fusion.1 = bf16[4,4,2,8,16,256]{5,4,3,2,1,0:T(8,128)(2,1)S(1)} fusion(bf16[1,4,2,8,16,256]{5,4,3,2,1,0:T(8,128)(2,1)S(1)} %bitcast.87, bf16[1,4,2,8,16,256]{5,4,3,2,1,0:T(8,128)(2,1)} %bitcast.33, bf16[1,4,2,8,16,256]{5,4,3,2,1,0:T(8,128)(2,1)} %bitcast.32, bf16[1,4,2,8,16,256]{5,4,3,2,1,0:T(8,128)(2,1)} %bitcast.31), kind=kLoop, calls=%fused_computation.1 | loop fusion | flops 3145728 | bytes 4194304 | tf_op jit(solution)/shard_map/stack | solution.py:438
  91.5 11.8 %valence_response.1.r_ref = f32[1024,256]{1,0:T(8,128)S(1)} custom-call(s32[1]{0:T(128)} %bitcast.25.place_ref, bf16[32,8,16,256]{3,2,1,0:T(8,128)(2,1)S(1)} %bitcast.65, bf16[32,8,16,256]{3,2,1,0:T(8,128)(2,1)S(1)} %bitcast.69, bf16[32,8,16,256]{3,2,1,0:T(8,128)(2,1)S(1)} %bitcast.66, bf16[32,8,16,256]{3,2,1,0:T(8,128)(2,1)S(1)} %bitcast.70, ...), custom_call_target="tpu_custom_call" | custom-call | flops 36507222016 | bytes 9437184 | tf_op jit(solution)/shard_map/valence_response/pallas_call | solution.py:293
  105.2 13.8 %all_to_all.26 = f32[32,16,128]{2,1,0:T(8,128)S(1)} all-to-all(f32[32,16,128]{2,1,0:T(8,128)S(1)} %kernel_blocks.1), channel_id=1, replica_groups=mesh['zl'=4,'co'=2,'x'=4,'y'=4,'zh'=2] {'x','y'}, dimensions={0} | all-to-all | bytes 524288 | tf_op jit(solution)/shard_map/all_to_all | solution.py:443
  119.7 10.6 %all-to-all-start.2 = ((f32[16,2,16,128]{3,2,1,0:T(8,128)}), f32[16,2,16,128]{3,2,1,0:T(8,128)S(1)}, u32[]{:S(2)}, u32[]{:S(2)}) async-start(f32[16,2,16,128]{3,2,1,0:T(8,128)} %broadcast_in_dim.16), calls=%async_computation.2 | async-start | bytes 524288 | tf_op jit(solution)/shard_map/all_to_all | solution.py:65
  130.4 12.2 %all-to-all-done.2 = f32[16,2,16,128]{3,2,1,0:T(8,128)S(1)} async-done(((f32[16,2,16,128]{3,2,1,0:T(8,128)}), f32[16,2,16,128]{3,2,1,0:T(8,128)S(1)}, u32[]{:S(2)}, u32[]{:S(2)}) %all-to-all-start.2) | async-done | bytes 262176 | tf_op jit(solution)/shard_map/all_to_all | solution.py:65
  143.2 11.9 %all_to_all.27.full_ref = bf16[16,2,32,128]{3,2,1,0:T(8,128)(2,1)S(1)} all-to-all(bf16[16,2,32,128]{3,2,1,0:T(8,128)(2,1)S(1)} %broadcast_in_dim.21), channel_id=1, replica_groups=mesh['zl'=4,'co'=2,'x'=4,'y'=4,'zh'=2] {'x','y'}, dimensions={0} | all-to-all | bytes 524288 | tf_op jit(solution)/shard_map/all_to_all | solution.py:65
  (69 shorter events, 16.7 us)
Async XLA Ops:
  0.6 41.4 %copy-start.6 = (bf16[256,512]{1,0:T(8,128)(2,1)S(1)}, bf16[256,512]{1,0:T(8,128)(2,1)}, u32[]{:S(2)}) copy-start(bf16[256,512]{1,0:T(8,128)(2,1)} %constant.194.clone.high_ref) | copy-start | bytes 786436
  0.6 41.4 %copy-start.7 = (bf16[256,512]{1,0:T(8,128)(2,1)S(1)}, bf16[256,512]{1,0:T(8,128)(2,1)}, u32[]{:S(2)}) copy-start(bf16[256,512]{1,0:T(8,128)(2,1)} %constant.195.clone.low_ref) | copy-start | bytes 786436
  1.6 8.6 %collective-permute-start.2 = (bf16[8,32,256]{2,1,0:T(8,128)(2,1)S(1)}, bf16[8,32,256]{2,1,0:T(8,128)(2,1)S(1)}, u32[]{:S(2)}, u32[]{:S(2)}) collective-permute-start(bf16[8,32,256]{2,1,0:T(8,128)(2,1)S(1)} %bitcast.81), channel_id=1, source_target_pairs={{0,192},{64,0},{128,64},{192,128},{1,193},{65,1},{129,65},{193,129... | collective-permute-start | bytes 393224 | tf_op jit(solution)/shard_map/ppermute | solution.py:55
  6.3 11.2 %collective-permute-start.1 = (bf16[8,32,256]{2,1,0:T(8,128)(2,1)S(1)}, bf16[8,32,256]{2,1,0:T(8,128)(2,1)S(1)}, u32[]{:S(2)}, u32[]{:S(2)}) collective-permute-start(bf16[8,32,256]{2,1,0:T(8,128)(2,1)S(1)} %bitcast.82), channel_id=1, source_target_pairs={{0,128},{64,192},{128,0},{192,64},{1,129},{65,193},{129,1},{193,65... | collective-permute-start | bytes 393224 | tf_op jit(solution)/shard_map/ppermute | solution.py:55
  6.3 11.2 %collective-permute-start = (bf16[8,32,256]{2,1,0:T(8,128)(2,1)S(1)}, bf16[8,32,256]{2,1,0:T(8,128)(2,1)S(1)}, u32[]{:S(2)}, u32[]{:S(2)}) collective-permute-start(bf16[8,32,256]{2,1,0:T(8,128)(2,1)S(1)} %bitcast.83), channel_id=1, source_target_pairs={{0,64},{64,128},{128,192},{192,0},{1,65},{65,129},{129,193},{193,1... | collective-permute-start | bytes 393224 | tf_op jit(solution)/shard_map/ppermute | solution.py:55
  17.6 2.0 %collective-permute-start.3 = (bf16[32,32,256]{2,1,0:T(8,128)(2,1)S(1)}, bf16[32,32,256]{2,1,0:T(8,128)(2,1)S(1)}, u32[]{:S(2)}, u32[]{:S(2)}) collective-permute-start(bf16[32,32,256]{2,1,0:T(8,128)(2,1)S(1)} %bitcast.73), channel_id=1, source_target_pairs={{0,32},{32,0},{1,33},{33,1},{2,34},{34,2},{3,35},{35,3},{4,36},{36... | collective-permute-start | bytes 1572872 | tf_op jit(solution)/shard_map/ppermute | solution.py:55
  23.0 9.6 %collective-permute-start.4 = (bf16[2,8,16,256]{3,2,1,0:T(8,128)(2,1)S(1)}, bf16[2,8,16,256]{3,2,1,0:T(8,128)(2,1)S(1)}, u32[]{:S(2)}, u32[]{:S(2)}) collective-permute-start(bf16[2,8,16,256]{3,2,1,0:T(8,128)(2,1)S(1)} %get-tuple-element.11), channel_id=1, source_target_pairs={{0,1},{1,0},{2,3},{3,2},{4,5},{5,4},{6,7},{7,6},{8,9},{9,8},{10,11... | collective-permute-start | bytes 393224 | tf_op jit(solution)/shard_map/ppermute | solution.py:55
  32.6 7.8 %collective-permute-start.7 = (bf16[2,8,16,256]{3,2,1,0:T(8,128)(2,1)S(1)}, bf16[2,8,16,256]{3,2,1,0:T(8,128)(2,1)S(1)}, u32[]{:S(2)}, u32[]{:S(2)}) collective-permute-start(bf16[2,8,16,256]{3,2,1,0:T(8,128)(2,1)S(1)} %get-tuple-element.21), channel_id=1, source_target_pairs={{0,24},{8,0},{16,8},{24,16},{1,25},{9,1},{17,9},{25,17},{2,26},{10... | collective-permute-start | bytes 393224 | tf_op jit(solution)/shard_map/ppermute | solution.py:55
  35.4 8.7 %collective-permute-start.6 = (bf16[2,8,16,256]{3,2,1,0:T(8,128)(2,1)S(1)}, bf16[2,8,16,256]{3,2,1,0:T(8,128)(2,1)S(1)}, u32[]{:S(2)}, u32[]{:S(2)}) collective-permute-start(bf16[2,8,16,256]{3,2,1,0:T(8,128)(2,1)S(1)} %get-tuple-element.21), channel_id=1, source_target_pairs={{0,16},{8,24},{16,0},{24,8},{1,17},{9,25},{17,1},{25,9},{2,18},{10... | collective-permute-start | bytes 393224 | tf_op jit(solution)/shard_map/ppermute | solution.py:55
  36.2 7.9 %collective-permute-start.5 = (bf16[2,8,16,256]{3,2,1,0:T(8,128)(2,1)S(1)}, bf16[2,8,16,256]{3,2,1,0:T(8,128)(2,1)S(1)}, u32[]{:S(2)}, u32[]{:S(2)}) collective-permute-start(bf16[2,8,16,256]{3,2,1,0:T(8,128)(2,1)S(1)} %get-tuple-element.21), channel_id=1, source_target_pairs={{0,8},{8,16},{16,24},{24,0},{1,9},{9,17},{17,25},{25,1},{2,10},{10... | collective-permute-start | bytes 393224 | tf_op jit(solution)/shard_map/ppermute | solution.py:55
  37.1 7.1 %collective-permute-start.10 = (bf16[2,8,16,256]{3,2,1,0:T(8,128)(2,1)S(1)}, bf16[2,8,16,256]{3,2,1,0:T(8,128)(2,1)S(1)}, u32[]{:S(2)}, u32[]{:S(2)}) collective-permute-start(bf16[2,8,16,256]{3,2,1,0:T(8,128)(2,1)S(1)} %get-tuple-element.22), channel_id=1, source_target_pairs={{0,6},{2,0},{4,2},{6,4},{1,7},{3,1},{5,3},{7,5},{8,14},{10,8},{12,... | collective-permute-start | bytes 393224 | tf_op jit(solution)/shard_map/ppermute | solution.py:55
  37.6 7.2 %collective-permute-start.9 = (bf16[2,8,16,256]{3,2,1,0:T(8,128)(2,1)S(1)}, bf16[2,8,16,256]{3,2,1,0:T(8,128)(2,1)S(1)}, u32[]{:S(2)}, u32[]{:S(2)}) collective-permute-start(bf16[2,8,16,256]{3,2,1,0:T(8,128)(2,1)S(1)} %get-tuple-element.22), channel_id=1, source_target_pairs={{0,4},{2,6},{4,0},{6,2},{1,5},{3,7},{5,1},{7,3},{8,12},{10,14},{12... | collective-permute-start | bytes 393224 | tf_op jit(solution)/shard_map/ppermute | solution.py:55
  40.4 5.1 %collective-permute-start.8 = (bf16[2,8,16,256]{3,2,1,0:T(8,128)(2,1)S(1)}, bf16[2,8,16,256]{3,2,1,0:T(8,128)(2,1)S(1)}, u32[]{:S(2)}, u32[]{:S(2)}) collective-permute-start(bf16[2,8,16,256]{3,2,1,0:T(8,128)(2,1)S(1)} %get-tuple-element.22), channel_id=1, source_target_pairs={{0,2},{2,4},{4,6},{6,0},{1,3},{3,5},{5,7},{7,1},{8,10},{10,12},{12... | collective-permute-start | bytes 393224 | tf_op jit(solution)/shard_map/ppermute | solution.py:55
  44.2 27.3 %copy-start.4 = (bf16[2,256,256]{2,1,0:T(8,128)(2,1)S(1)}, bf16[2,256,256]{2,1,0:T(8,128)(2,1)}, u32[]{:S(2)}) copy-start(bf16[2,256,256]{2,1,0:T(8,128)(2,1)} %constant.197.clone.high_ref) | copy-start | bytes 786436
  44.2 27.3 %copy-start.5 = (bf16[2,256,256]{2,1,0:T(8,128)(2,1)S(1)}, bf16[2,256,256]{2,1,0:T(8,128)(2,1)}, u32[]{:S(2)}) copy-start(bf16[2,256,256]{2,1,0:T(8,128)(2,1)} %constant.198.clone.low_ref) | copy-start | bytes 786436
  46.4 22.2 %collective-permute-start.13 = (bf16[4,2,8,16,256]{4,3,2,1,0:T(8,128)(2,1)S(1)}, bf16[4,2,8,16,256]{4,3,2,1,0:T(8,128)(2,1)}, u32[]{:S(2)}, u32[]{:S(2)}) collective-permute-start(bf16[4,2,8,16,256]{4,3,2,1,0:T(8,128)(2,1)S(1)} %pad_maximum_fusion.3), channel_id=1, source_target_pairs={{0,6},{2,0},{4,2},{6,4},{1,7},{3,1},{5,3},{7,5},{8,14},{10,8},{12,... | collective-permute-start | bytes 1572872 | tf_op jit(solution)/shard_map/ppermute | solution.py:55
  50.6 37.0 %collective-permute-start.12 = (bf16[4,2,8,16,256]{4,3,2,1,0:T(8,128)(2,1)S(1)}, bf16[4,2,8,16,256]{4,3,2,1,0:T(8,128)(2,1)}, u32[]{:S(2)}, u32[]{:S(2)}) collective-permute-start(bf16[4,2,8,16,256]{4,3,2,1,0:T(8,128)(2,1)S(1)} %pad_maximum_fusion.3), channel_id=1, source_target_pairs={{0,4},{2,6},{4,0},{6,2},{1,5},{3,7},{5,1},{7,3},{8,12},{10,14},{12... | collective-permute-start | bytes 1572872 | tf_op jit(solution)/shard_map/ppermute | solution.py:55
  50.7 36.9 %collective-permute-start.11 = (bf16[4,2,8,16,256]{4,3,2,1,0:T(8,128)(2,1)S(1)}, bf16[4,2,8,16,256]{4,3,2,1,0:T(8,128)(2,1)}, u32[]{:S(2)}, u32[]{:S(2)}) collective-permute-start(bf16[4,2,8,16,256]{4,3,2,1,0:T(8,128)(2,1)S(1)} %pad_maximum_fusion.3), channel_id=1, source_target_pairs={{0,2},{2,4},{4,6},{6,0},{1,3},{3,5},{5,7},{7,1},{8,10},{10,12},{12... | collective-permute-start | bytes 1572872 | tf_op jit(solution)/shard_map/ppermute | solution.py:55
  52.7 37.2 %collective-permute-start.15 = (bf16[4,2,8,16,256]{4,3,2,1,0:T(8,128)(2,1)}, bf16[4,2,8,16,256]{4,3,2,1,0:T(8,128)(2,1)}, u32[]{:S(2)}, u32[]{:S(2)}) collective-permute-start(bf16[4,2,8,16,256]{4,3,2,1,0:T(8,128)(2,1)} %pad_maximum_fusion.4), channel_id=1, source_target_pairs={{0,16},{8,24},{16,0},{24,8},{1,17},{9,25},{17,1},{25,9},{2,18},{10... | collective-permute-start | bytes 1572872 | tf_op jit(solution)/shard_map/ppermute | solution.py:55
  54.8 35.1 %collective-permute-start.14 = (bf16[4,2,8,16,256]{4,3,2,1,0:T(8,128)(2,1)}, bf16[4,2,8,16,256]{4,3,2,1,0:T(8,128)(2,1)}, u32[]{:S(2)}, u32[]{:S(2)}) collective-permute-start(bf16[4,2,8,16,256]{4,3,2,1,0:T(8,128)(2,1)} %pad_maximum_fusion.4), channel_id=1, source_target_pairs={{0,8},{8,16},{16,24},{24,0},{1,9},{9,17},{17,25},{25,1},{2,10},{10... | collective-permute-start | bytes 1572872 | tf_op jit(solution)/shard_map/ppermute | solution.py:55
  57.0 46.3 %all-to-all-start = ((f32[32,8,1024]{2,1,0:T(8,128)}), f32[32,8,1024]{2,1,0:T(8,128)S(1)}, u32[]{:S(2)}, u32[]{:S(2)}) async-start(f32[32,8,1024]{2,1,0:T(8,128)} %bitcast.23), calls=%async_computation | async-start | bytes 2097152 | tf_op jit(solution)/shard_map/all_to_all | solution.py:436
  68.7 21.2 %collective-permute-start.16 = (bf16[4,2,8,16,256]{4,3,2,1,0:T(8,128)(2,1)}, bf16[4,2,8,16,256]{4,3,2,1,0:T(8,128)(2,1)S(1)}, u32[]{:S(2)}, u32[]{:S(2)}) collective-permute-start(bf16[4,2,8,16,256]{4,3,2,1,0:T(8,128)(2,1)} %pad_maximum_fusion.4), channel_id=1, source_target_pairs={{0,24},{8,0},{16,8},{24,16},{1,25},{9,1},{17,9},{25,17},{2,26},{10... | collective-permute-start | bytes 1572872 | tf_op jit(solution)/shard_map/ppermute | solution.py:55
  104.5 38.2 %copy-start.1 = (s32[64]{0:T(128)S(1)}, s32[64]{0:T(128)}, u32[]{:S(2)}) copy-start(s32[64]{0:T(128)} %partner_ref.1) | copy-start | bytes 772
  119.7 22.9 %all-to-all-start.2 = ((f32[16,2,16,128]{3,2,1,0:T(8,128)}), f32[16,2,16,128]{3,2,1,0:T(8,128)S(1)}, u32[]{:S(2)}, u32[]{:S(2)}) async-start(f32[16,2,16,128]{3,2,1,0:T(8,128)} %broadcast_in_dim.16), calls=%async_computation.2 | async-start | bytes 524288 | tf_op jit(solution)/shard_map/all_to_all | solution.py:65
  (4 other events, 35.4 us)

commit v11 on v10

--- a/solution.py
+++ b/solution.py
@@ -16,7 +16,7 @@
 NG = 8192
 PLANE = NX * NY
 HALF = NZ // 2 + 1
-LINE_BLOCKS = 4
+LINE_BLOCKS = 8
 LINE_STEPS = 32 // LINE_BLOCKS
 LINE_ROWS = 48
 NORM = 1.0 / math.sqrt(NG)
@@ -442,11 +442,17 @@
 
     parts = lax.all_to_all(blocks, ("x", "y"), split_axis=0, concat_axis=0, tiled=True)
     mine = jnp.sum(parts.reshape(16, 2, 16, 128), axis=0)
-    everyone = copies_to_all(mine, ("zl", "co", "zh")).reshape(8, 2, 2, 16, 128)
-    everyone = everyone[:, 0] + everyone[:, 1]
-    mine = lax.dynamic_index_in_dim(everyone, ka_place, keepdims=False)
-    everyone = everyone.reshape(8, 2, 8, 256).transpose(0, 2, 1, 3).reshape(64, 512)
-    select = (partner[None, :] == owned[:, None]).astype(F32)
+    mine = mine + turned(mine, "zh", 1)
+    close = spread(mine, "zl")
+    everyone = jnp.stack([close, turned(close, "co", 1)]).reshape(2, 4, 2, 8, 256)
+    everyone = everyone.transpose(0, 1, 3, 2, 4).reshape(64, 512)
+    slot = jnp.arange(64, dtype=jnp.int32)
+    level = (lax.axis_index("zl") - slot // 8) & 3
+    core = (lax.axis_index("co") + slot // 32) & 1
+    holds = (level * 2 + core) * 8 + slot % 8
+    number = jnp.arange(64, dtype=jnp.int32)
+    source = jnp.sum(jnp.where(partner[None, :] == owned[:, None], number[None, :], 0), axis=1)
+    select = (source[:, None] == holds[None, :]).astype(F32)
     mirror = jnp.dot(select, everyone, precision=EXACT)
     mirror = mirror.reshape(8, 2, 2, 128).transpose(1, 0, 2, 3).reshape(32, 128)
     lane = jnp.arange(128, dtype=jnp.int32)

time: 157 us -> 155 us (0.987)
  blocking collectives: 25.7 us -> 12.3 us
  starting transfers between devices: 54.5 us -> 63.9 us
  waiting for transfers between devices: 31 us -> 33.1 us
    all_to_all x1 -> x0, blocking collectives: 13.8 us -> none  [on_device(): lax.all_to_all(blocks, ('x', 'y'), split_axis=0, concat_axis=0, tiled=True)]
    ppermute x17 -> x22, starting transfers between devices: 32.3 us -> 45.3 us  [turned(): lax.ppermute(value, axis, [(i, (i + step) % size) for i in range(size)])]
    ppermute x17 -> x22, waiting for transfers between devices: 18.7 us -> 26.3 us  [turned(): lax.ppermute(value, axis, [(i, (i + step) % size) for i in range(size)])]
    all_to_all x1, waiting for transfers between devices: 12.2 us -> 6.78 us  [on_device(): lax.all_to_all(blocks, ('x', 'y'), split_axis=0, concat_axis=0, tiled=True)]
    all_to_all x1, starting transfers between devices: 10.6 us -> 7 us  [on_device(): lax.all_to_all(blocks, ('x', 'y'), split_axis=0, concat_axis=0, tiled=True)]
  transfers between devices with their start and end apart: 19 -> 24, of which waited for: 9 -> 12; matrix products, arithmetic and copies ran while one was open for 3% -> 3% of each run, Pallas kernels for 18% -> 18%
where the time goes in v11:
time: 155 us; the launch traced here: 154 us
  starting transfers between devices  63.9 us (41%)
  Pallas kernels  33.5 us (22%)
  waiting for transfers between devices  33.1 us (21%)
  blocking collectives  12.3 us (8%)
  other arithmetic  5.86 us (4%)
  local copies, waits for them, and re-layouts  4.05 us (3%)
    ppermute x22, starting transfers between devices, turned(): lax.ppermute(value, axis, [(i, (i + step) % size) for i in range(size)])  45.3 us
    ppermute x22, waiting for transfers between devices, turned(): lax.ppermute(value, axis, [(i, (i + step) % size) for i in range(size)])  26.3 us
    pallas_call x1, Pallas kernels, screened_transform(): pl.pallas_call(screened_kernel, grid=(LINE_STEPS + HALF,), in_specs=[pl.B...  13.3 us
    all_to_all x1, blocking collectives, copies_to_all(): return lax.all_to_all(copies, axes, split_axis=0, concat_axis=0, tiled=True)  12.3 us
    pallas_call x1, Pallas kernels, response(): pl.pallas_call(response_kernel, grid_spec=pltpu.PrefetchScalarGridSpec(nu...  11.8 us
    all_to_all x1, starting transfers between devices, on_device(): lax.all_to_all(planes, GA, split_axis=0, concat_axis=0, tiled=True)  11.6 us
    all_to_all x1, starting transfers between devices, on_device(): lax.all_to_all(blocks, ('x', 'y'), split_axis=0, concat_axis=0, tiled=True)  7 us
    all_to_all x1, waiting for transfers between devices, on_device(): lax.all_to_all(blocks, ('x', 'y'), split_axis=0, concat_axis=0, tiled=True)  6.78 us
  transfers between devices with their start and end apart: 24, of which 12 were waited for; matrix products, arithmetic and copies ran while one was open for 3% of the time, Pallas kernels for 18%

profile of v11, /device:TPU:8, one launch (start us, length us, event | category | flops | bytes accessed | tf_op | source)
XLA Modules:
  0.0 154.0 jit_solution(4894191536453654383)
XLA Ops:
  1.6 4.7 %collective-permute-start.2 = (bf16[8,32,256]{2,1,0:T(8,128)(2,1)S(1)}, bf16[8,32,256]{2,1,0:T(8,128)(2,1)S(1)}, u32[]{:S(2)}, u32[]{:S(2)}) collective-permute-start(bf16[8,32,256]{2,1,0:T(8,128)(2,1)S(1)} %bitcast.83), channel_id=1, source_target_pairs={{0,192},{64,0},{128,64},{192,128},{1,193},{65,1},{129,65},{193,129... | collective-permute-start | bytes 393224 | tf_op jit(solution)/shard_map/ppermute | solution.py:55
  7.0 3.2 %collective-permute-done.2 = bf16[8,32,256]{2,1,0:T(8,128)(2,1)S(1)} collective-permute-done((bf16[8,32,256]{2,1,0:T(8,128)(2,1)S(1)}, bf16[8,32,256]{2,1,0:T(8,128)(2,1)S(1)}, u32[]{:S(2)}, u32[]{:S(2)}) %collective-permute-start.2) | collective-permute-done | bytes 131104 | tf_op jit(solution)/shard_map/ppermute | solution.py:55
  10.2 7.3 %collective-permute-done.1 = bf16[8,32,256]{2,1,0:T(8,128)(2,1)S(1)} collective-permute-done((bf16[8,32,256]{2,1,0:T(8,128)(2,1)S(1)}, bf16[8,32,256]{2,1,0:T(8,128)(2,1)S(1)}, u32[]{:S(2)}, u32[]{:S(2)}) %collective-permute-start.1) | collective-permute-done | bytes 131104 | tf_op jit(solution)/shard_map/ppermute | solution.py:55
  20.3 2.9 %partner_choice.1 = (bf16[2,8,16,256]{3,2,1,0:T(8,128)(2,1)S(1)}, bf16[8,16,256]{2,1,0:T(8,128)(2,1)S(1)}) custom-call(s32[64]{0:T(128)S(1)} %copy-done, s32[2]{0:T(128)S(1)} %pad_add_fusion.place_ref, bf16[256,256]{1,0:T(8,128)(2,1)S(1)} %fusion.5.flip_ref, bf16[32,32,256]{2,1,0:T(8,128)(2,1)S(1)} %bitcast.77, ...), custom_call_target="tpu_custom_call" | custom-call | tf_op jit(solution)/shard_map/partner_choice/pallas_call | solution.py:189
  23.1 5.5 %collective-permute-start.4 = (bf16[2,8,16,256]{3,2,1,0:T(8,128)(2,1)S(1)}, bf16[2,8,16,256]{3,2,1,0:T(8,128)(2,1)S(1)}, u32[]{:S(2)}, u32[]{:S(2)}) collective-permute-start(bf16[2,8,16,256]{3,2,1,0:T(8,128)(2,1)S(1)} %get-tuple-element.11), channel_id=1, source_target_pairs={{0,1},{1,0},{2,3},{3,2},{4,5},{5,4},{6,7},{7,6},{8,9},{9,8},{10,11... | collective-permute-start | bytes 393224 | tf_op jit(solution)/shard_map/ppermute | solution.py:55
  28.6 4.1 %collective-permute-done.4 = bf16[2,8,16,256]{3,2,1,0:T(8,128)(2,1)S(1)} collective-permute-done((bf16[2,8,16,256]{3,2,1,0:T(8,128)(2,1)S(1)}, bf16[2,8,16,256]{3,2,1,0:T(8,128)(2,1)S(1)}, u32[]{:S(2)}, u32[]{:S(2)}) %collective-permute-start.4) | collective-permute-done | bytes 131104 | tf_op jit(solution)/shard_map/ppermute | solution.py:55
  32.7 2.8 %collective-permute-start.7 = (bf16[2,8,16,256]{3,2,1,0:T(8,128)(2,1)S(1)}, bf16[2,8,16,256]{3,2,1,0:T(8,128)(2,1)S(1)}, u32[]{:S(2)}, u32[]{:S(2)}) collective-permute-start(bf16[2,8,16,256]{3,2,1,0:T(8,128)(2,1)S(1)} %get-tuple-element.23), channel_id=1, source_target_pairs={{0,24},{8,0},{16,8},{24,16},{1,25},{9,1},{17,9},{25,17},{2,26},{10... | collective-permute-start | bytes 393224 | tf_op jit(solution)/shard_map/ppermute | solution.py:55
  37.7 2.6 %collective-permute-start.9 = (bf16[2,8,16,256]{3,2,1,0:T(8,128)(2,1)S(1)}, bf16[2,8,16,256]{3,2,1,0:T(8,128)(2,1)S(1)}, u32[]{:S(2)}, u32[]{:S(2)}) collective-permute-start(bf16[2,8,16,256]{3,2,1,0:T(8,128)(2,1)S(1)} %get-tuple-element.24), channel_id=1, source_target_pairs={{0,4},{2,6},{4,0},{6,2},{1,5},{3,7},{5,1},{7,3},{8,12},{10,14},{12... | collective-permute-start | bytes 393224 | tf_op jit(solution)/shard_map/ppermute | solution.py:55
  46.6 2.9 %collective-permute-start.13 = (bf16[4,2,8,16,256]{4,3,2,1,0:T(8,128)(2,1)S(1)}, bf16[4,2,8,16,256]{4,3,2,1,0:T(8,128)(2,1)}, u32[]{:S(2)}, u32[]{:S(2)}) collective-permute-start(bf16[4,2,8,16,256]{4,3,2,1,0:T(8,128)(2,1)S(1)} %pad_maximum_fusion.3), channel_id=1, source_target_pairs={{0,6},{2,0},{4,2},{6,4},{1,7},{3,1},{5,3},{7,5},{8,14},{10,8},{12,... | collective-permute-start | bytes 1572872 | tf_op jit(solution)/shard_map/ppermute | solution.py:55
  52.8 2.1 %collective-permute-start.15 = (bf16[4,2,8,16,256]{4,3,2,1,0:T(8,128)(2,1)}, bf16[4,2,8,16,256]{4,3,2,1,0:T(8,128)(2,1)}, u32[]{:S(2)}, u32[]{:S(2)}) collective-permute-start(bf16[4,2,8,16,256]{4,3,2,1,0:T(8,128)(2,1)} %pad_maximum_fusion.4), channel_id=1, source_target_pairs={{0,16},{8,24},{16,0},{24,8},{1,17},{9,25},{17,1},{25,9},{2,18},{10... | collective-permute-start | bytes 1572872 | tf_op jit(solution)/shard_map/ppermute | solution.py:55
  54.9 2.3 %collective-permute-start.14 = (bf16[4,2,8,16,256]{4,3,2,1,0:T(8,128)(2,1)}, bf16[4,2,8,16,256]{4,3,2,1,0:T(8,128)(2,1)}, u32[]{:S(2)}, u32[]{:S(2)}) collective-permute-start(bf16[4,2,8,16,256]{4,3,2,1,0:T(8,128)(2,1)} %pad_maximum_fusion.4), channel_id=1, source_target_pairs={{0,8},{8,16},{16,24},{24,0},{1,9},{9,17},{17,25},{25,1},{2,10},{10... | collective-permute-start | bytes 1572872 | tf_op jit(solution)/shard_map/ppermute | solution.py:55
  57.1 11.6 %all-to-all-start = ((f32[32,8,1024]{2,1,0:T(8,128)}), f32[32,8,1024]{2,1,0:T(8,128)S(1)}, u32[]{:S(2)}, u32[]{:S(2)}) async-start(f32[32,8,1024]{2,1,0:T(8,128)} %bitcast.23), calls=%async_computation | async-start | bytes 2097152 | tf_op jit(solution)/shard_map/all_to_all | solution.py:436
  68.8 2.8 %collective-permute-start.16 = (bf16[4,2,8,16,256]{4,3,2,1,0:T(8,128)(2,1)}, bf16[4,2,8,16,256]{4,3,2,1,0:T(8,128)(2,1)S(1)}, u32[]{:S(2)}, u32[]{:S(2)}) collective-permute-start(bf16[4,2,8,16,256]{4,3,2,1,0:T(8,128)(2,1)} %pad_maximum_fusion.4), channel_id=1, source_target_pairs={{0,24},{8,0},{16,8},{24,16},{1,25},{9,1},{17,9},{25,17},{2,26},{10... | collective-permute-start | bytes 1572872 | tf_op jit(solution)/shard_map/ppermute | solution.py:55
  71.6 2.2 %copy-done.3 = bf16[256,8192]{1,0:T(8,128)(2,1)S(1)} copy-done((bf16[256,8192]{1,0:T(8,128)(2,1)S(1)}, bf16[256,8192]{1,0:T(8,128)(2,1)}, u32[]{:S(2)}) %copy-start.3) | copy-done | bytes 4194328
  73.8 13.3 %screened_transform.1 = (bf16[17,512,256]{2,1,0:T(8,128)(2,1)S(1)}, f32[8,128]{1,0:T(8,128)}) custom-call(s32[32,1,256]{2,1,0:T(1,128)S(1)} %bitcast.80, bf16[96,32]{1,0:T(8,128)(2,1)S(1)} %copy-done.8, bf16[2,256,256]{2,1,0:T(8,128)(2,1)S(1)} %copy-done.4, bf16[2,256,256]{2,1,0:T(8,128)(2,1)S(1)} %copy-done.5, bf16[256,8192]{1,0:T(8,128)(2,1)S(1)} %copy-done.3), custom_call_target="tpu_custom_call" | custom-call | flops 13690208256 | bytes 9437184 | tf_op jit(solution)/shard_map/screened_transform/pallas_call | solution.py:132
  91.5 11.8 %valence_response.1.r_ref = f32[1024,256]{1,0:T(8,128)S(1)} custom-call(s32[1]{0:T(128)} %bitcast.25.place_ref, bf16[32,8,16,256]{3,2,1,0:T(8,128)(2,1)S(1)} %bitcast.68, bf16[32,8,16,256]{3,2,1,0:T(8,128)(2,1)S(1)} %bitcast.72, bf16[32,8,16,256]{3,2,1,0:T(8,128)(2,1)S(1)} %bitcast.69, bf16[32,8,16,256]{3,2,1,0:T(8,128)(2,1)S(1)} %bitcast.73, ...), custom_call_target="tpu_custom_call" | custom-call | flops 36507222016 | bytes 9437184 | tf_op jit(solution)/shard_map/valence_response/pallas_call | solution.py:293
  105.9 7.0 %all-to-all-start.1 = ((f32[32,16,128]{2,1,0:T(8,128)}), f32[32,16,128]{2,1,0:T(8,128)S(1)}, u32[]{:S(2)}, u32[]{:S(2)}) async-start(f32[32,16,128]{2,1,0:T(8,128)} %kernel_blocks.1), calls=%async_computation.1 | async-start | bytes 524288 | tf_op jit(solution)/shard_map/all_to_all | solution.py:443
  113.1 6.8 %all-to-all-done.1 = f32[32,16,128]{2,1,0:T(8,128)S(1)} async-done(((f32[32,16,128]{2,1,0:T(8,128)}), f32[32,16,128]{2,1,0:T(8,128)S(1)}, u32[]{:S(2)}, u32[]{:S(2)}) %all-to-all-start.1) | async-done | bytes 262176 | tf_op jit(solution)/shard_map/all_to_all | solution.py:443
  119.9 5.5 %collective-permute-start.17 = (f32[2,16,128]{2,1,0:T(8,128)S(1)}, f32[2,16,128]{2,1,0:T(8,128)S(1)}, u32[]{:S(2)}, u32[]{:S(2)}) collective-permute-start(f32[2,16,128]{2,1,0:T(8,128)S(1)} %reduce_sum.18), channel_id=1, source_target_pairs={{0,1},{1,0},{2,3},{3,2},{4,5},{5,4},{6,7},{7,6},{8,9},{9,8},{10,11... | collective-permute-start | bytes 49160 | tf_op jit(solution)/shard_map/ppermute | solution.py:55
  125.4 2.4 %collective-permute-done.17 = f32[2,16,128]{2,1,0:T(8,128)S(1)} collective-permute-done((f32[2,16,128]{2,1,0:T(8,128)S(1)}, f32[2,16,128]{2,1,0:T(8,128)S(1)}, u32[]{:S(2)}, u32[]{:S(2)}) %collective-permute-start.17) | collective-permute-done | bytes 16416 | tf_op jit(solution)/shard_map/ppermute | solution.py:55
  127.8 2.6 %collective-permute-start.20 = (f32[2,16,128]{2,1,0:T(8,128)S(1)}, f32[2,16,128]{2,1,0:T(8,128)S(1)}, u32[]{:S(2)}, u32[]{:S(2)}) collective-permute-start(f32[2,16,128]{2,1,0:T(8,128)S(1)} %get-tuple-element.21), channel_id=1, source_target_pairs={{0,192},{64,0},{128,64},{192,128},{1,193},{65,1},{129,65},{193,129... | collective-permute-start | bytes 49160 | tf_op jit(solution)/shard_map/ppermute | solution.py:55
  130.4 3.0 %collective-permute-start.19 = (f32[2,16,128]{2,1,0:T(8,128)S(1)}, f32[2,16,128]{2,1,0:T(8,128)S(1)}, u32[]{:S(2)}, u32[]{:S(2)}) collective-permute-start(f32[2,16,128]{2,1,0:T(8,128)S(1)} %get-tuple-element.21), channel_id=1, source_target_pairs={{0,128},{64,192},{128,0},{192,64},{1,129},{65,193},{129,1},{193,65... | collective-permute-start | bytes 49160 | tf_op jit(solution)/shard_map/ppermute | solution.py:55
  135.3 3.6 %collective-permute-done.18 = f32[2,16,128]{2,1,0:T(8,128)S(1)} collective-permute-done((f32[2,16,128]{2,1,0:T(8,128)S(1)}, f32[2,16,128]{2,1,0:T(8,128)S(1)}, u32[]{:S(2)}, u32[]{:S(2)}) %collective-permute-start.18) | collective-permute-done | bytes 16416 | tf_op jit(solution)/shard_map/ppermute | solution.py:55
  140.8 12.3 %all_to_all.21.full_ref = bf16[16,2,32,128]{3,2,1,0:T(8,128)(2,1)S(1)} all-to-all(bf16[16,2,32,128]{3,2,1,0:T(8,128)(2,1)S(1)} %broadcast_in_dim.50), channel_id=1, replica_groups=mesh['zl'=4,'co'=2,'x'=4,'y'=4,'zh'=2] {'x','y'}, dimensions={0} | all-to-all | bytes 524288 | tf_op jit(solution)/shard_map/all_to_all | solution.py:65
  (84 shorter events, 27.9 us)
Async XLA Ops:
  1.6 8.6 %collective-permute-start.2 = (bf16[8,32,256]{2,1,0:T(8,128)(2,1)S(1)}, bf16[8,32,256]{2,1,0:T(8,128)(2,1)S(1)}, u32[]{:S(2)}, u32[]{:S(2)}) collective-permute-start(bf16[8,32,256]{2,1,0:T(8,128)(2,1)S(1)} %bitcast.83), channel_id=1, source_target_pairs={{0,192},{64,0},{128,64},{192,128},{1,193},{65,1},{129,65},{193,129... | collective-permute-start | bytes 393224 | tf_op jit(solution)/shard_map/ppermute | solution.py:55
  6.3 11.2 %collective-permute-start.1 = (bf16[8,32,256]{2,1,0:T(8,128)(2,1)S(1)}, bf16[8,32,256]{2,1,0:T(8,128)(2,1)S(1)}, u32[]{:S(2)}, u32[]{:S(2)}) collective-permute-start(bf16[8,32,256]{2,1,0:T(8,128)(2,1)S(1)} %bitcast.84), channel_id=1, source_target_pairs={{0,128},{64,192},{128,0},{192,64},{1,129},{65,193},{129,1},{193,65... | collective-permute-start | bytes 393224 | tf_op jit(solution)/shard_map/ppermute | solution.py:55
  6.3 11.2 %collective-permute-start = (bf16[8,32,256]{2,1,0:T(8,128)(2,1)S(1)}, bf16[8,32,256]{2,1,0:T(8,128)(2,1)S(1)}, u32[]{:S(2)}, u32[]{:S(2)}) collective-permute-start(bf16[8,32,256]{2,1,0:T(8,128)(2,1)S(1)} %bitcast.85), channel_id=1, source_target_pairs={{0,64},{64,128},{128,192},{192,0},{1,65},{65,129},{129,193},{193,1... | collective-permute-start | bytes 393224 | tf_op jit(solution)/shard_map/ppermute | solution.py:55
  17.6 2.0 %collective-permute-start.3 = (bf16[32,32,256]{2,1,0:T(8,128)(2,1)S(1)}, bf16[32,32,256]{2,1,0:T(8,128)(2,1)S(1)}, u32[]{:S(2)}, u32[]{:S(2)}) collective-permute-start(bf16[32,32,256]{2,1,0:T(8,128)(2,1)S(1)} %bitcast.76), channel_id=1, source_target_pairs={{0,32},{32,0},{1,33},{33,1},{2,34},{34,2},{3,35},{35,3},{4,36},{36... | collective-permute-start | bytes 1572872 | tf_op jit(solution)/shard_map/ppermute | solution.py:55
  23.1 9.6 %collective-permute-start.4 = (bf16[2,8,16,256]{3,2,1,0:T(8,128)(2,1)S(1)}, bf16[2,8,16,256]{3,2,1,0:T(8,128)(2,1)S(1)}, u32[]{:S(2)}, u32[]{:S(2)}) collective-permute-start(bf16[2,8,16,256]{3,2,1,0:T(8,128)(2,1)S(1)} %get-tuple-element.11), channel_id=1, source_target_pairs={{0,1},{1,0},{2,3},{3,2},{4,5},{5,4},{6,7},{7,6},{8,9},{9,8},{10,11... | collective-permute-start | bytes 393224 | tf_op jit(solution)/shard_map/ppermute | solution.py:55
  32.7 7.8 %collective-permute-start.7 = (bf16[2,8,16,256]{3,2,1,0:T(8,128)(2,1)S(1)}, bf16[2,8,16,256]{3,2,1,0:T(8,128)(2,1)S(1)}, u32[]{:S(2)}, u32[]{:S(2)}) collective-permute-start(bf16[2,8,16,256]{3,2,1,0:T(8,128)(2,1)S(1)} %get-tuple-element.23), channel_id=1, source_target_pairs={{0,24},{8,0},{16,8},{24,16},{1,25},{9,1},{17,9},{25,17},{2,26},{10... | collective-permute-start | bytes 393224 | tf_op jit(solution)/shard_map/ppermute | solution.py:55
  35.6 8.7 %collective-permute-start.6 = (bf16[2,8,16,256]{3,2,1,0:T(8,128)(2,1)S(1)}, bf16[2,8,16,256]{3,2,1,0:T(8,128)(2,1)S(1)}, u32[]{:S(2)}, u32[]{:S(2)}) collective-permute-start(bf16[2,8,16,256]{3,2,1,0:T(8,128)(2,1)S(1)} %get-tuple-element.23), channel_id=1, source_target_pairs={{0,16},{8,24},{16,0},{24,8},{1,17},{9,25},{17,1},{25,9},{2,18},{10... | collective-permute-start | bytes 393224 | tf_op jit(solution)/shard_map/ppermute | solution.py:55
  36.4 7.9 %collective-permute-start.5 = (bf16[2,8,16,256]{3,2,1,0:T(8,128)(2,1)S(1)}, bf16[2,8,16,256]{3,2,1,0:T(8,128)(2,1)S(1)}, u32[]{:S(2)}, u32[]{:S(2)}) collective-permute-start(bf16[2,8,16,256]{3,2,1,0:T(8,128)(2,1)S(1)} %get-tuple-element.23), channel_id=1, source_target_pairs={{0,8},{8,16},{16,24},{24,0},{1,9},{9,17},{17,25},{25,1},{2,10},{10... | collective-permute-start | bytes 393224 | tf_op jit(solution)/shard_map/ppermute | solution.py:55
  37.3 7.1 %collective-permute-start.10 = (bf16[2,8,16,256]{3,2,1,0:T(8,128)(2,1)S(1)}, bf16[2,8,16,256]{3,2,1,0:T(8,128)(2,1)S(1)}, u32[]{:S(2)}, u32[]{:S(2)}) collective-permute-start(bf16[2,8,16,256]{3,2,1,0:T(8,128)(2,1)S(1)} %get-tuple-element.24), channel_id=1, source_target_pairs={{0,6},{2,0},{4,2},{6,4},{1,7},{3,1},{5,3},{7,5},{8,14},{10,8},{12,... | collective-permute-start | bytes 393224 | tf_op jit(solution)/shard_map/ppermute | solution.py:55
  37.7 7.1 %collective-permute-start.9 = (bf16[2,8,16,256]{3,2,1,0:T(8,128)(2,1)S(1)}, bf16[2,8,16,256]{3,2,1,0:T(8,128)(2,1)S(1)}, u32[]{:S(2)}, u32[]{:S(2)}) collective-permute-start(bf16[2,8,16,256]{3,2,1,0:T(8,128)(2,1)S(1)} %get-tuple-element.24), channel_id=1, source_target_pairs={{0,4},{2,6},{4,0},{6,2},{1,5},{3,7},{5,1},{7,3},{8,12},{10,14},{12... | collective-permute-start | bytes 393224 | tf_op jit(solution)/shard_map/ppermute | solution.py:55
  40.5 5.2 %collective-permute-start.8 = (bf16[2,8,16,256]{3,2,1,0:T(8,128)(2,1)S(1)}, bf16[2,8,16,256]{3,2,1,0:T(8,128)(2,1)S(1)}, u32[]{:S(2)}, u32[]{:S(2)}) collective-permute-start(bf16[2,8,16,256]{3,2,1,0:T(8,128)(2,1)S(1)} %get-tuple-element.24), channel_id=1, source_target_pairs={{0,2},{2,4},{4,6},{6,0},{1,3},{3,5},{5,7},{7,1},{8,10},{10,12},{12... | collective-permute-start | bytes 393224 | tf_op jit(solution)/shard_map/ppermute | solution.py:55
  46.6 22.2 %collective-permute-start.13 = (bf16[4,2,8,16,256]{4,3,2,1,0:T(8,128)(2,1)S(1)}, bf16[4,2,8,16,256]{4,3,2,1,0:T(8,128)(2,1)}, u32[]{:S(2)}, u32[]{:S(2)}) collective-permute-start(bf16[4,2,8,16,256]{4,3,2,1,0:T(8,128)(2,1)S(1)} %pad_maximum_fusion.3), channel_id=1, source_target_pairs={{0,6},{2,0},{4,2},{6,4},{1,7},{3,1},{5,3},{7,5},{8,14},{10,8},{12,... | collective-permute-start | bytes 1572872 | tf_op jit(solution)/shard_map/ppermute | solution.py:55
  50.7 36.4 %collective-permute-start.12 = (bf16[4,2,8,16,256]{4,3,2,1,0:T(8,128)(2,1)S(1)}, bf16[4,2,8,16,256]{4,3,2,1,0:T(8,128)(2,1)}, u32[]{:S(2)}, u32[]{:S(2)}) collective-permute-start(bf16[4,2,8,16,256]{4,3,2,1,0:T(8,128)(2,1)S(1)} %pad_maximum_fusion.3), channel_id=1, source_target_pairs={{0,4},{2,6},{4,0},{6,2},{1,5},{3,7},{5,1},{7,3},{8,12},{10,14},{12... | collective-permute-start | bytes 1572872 | tf_op jit(solution)/shard_map/ppermute | solution.py:55
  50.8 36.3 %collective-permute-start.11 = (bf16[4,2,8,16,256]{4,3,2,1,0:T(8,128)(2,1)S(1)}, bf16[4,2,8,16,256]{4,3,2,1,0:T(8,128)(2,1)}, u32[]{:S(2)}, u32[]{:S(2)}) collective-permute-start(bf16[4,2,8,16,256]{4,3,2,1,0:T(8,128)(2,1)S(1)} %pad_maximum_fusion.3), channel_id=1, source_target_pairs={{0,2},{2,4},{4,6},{6,0},{1,3},{3,5},{5,7},{7,1},{8,10},{10,12},{12... | collective-permute-start | bytes 1572872 | tf_op jit(solution)/shard_map/ppermute | solution.py:55
  52.8 37.1 %collective-permute-start.15 = (bf16[4,2,8,16,256]{4,3,2,1,0:T(8,128)(2,1)}, bf16[4,2,8,16,256]{4,3,2,1,0:T(8,128)(2,1)}, u32[]{:S(2)}, u32[]{:S(2)}) collective-permute-start(bf16[4,2,8,16,256]{4,3,2,1,0:T(8,128)(2,1)} %pad_maximum_fusion.4), channel_id=1, source_target_pairs={{0,16},{8,24},{16,0},{24,8},{1,17},{9,25},{17,1},{25,9},{2,18},{10... | collective-permute-start | bytes 1572872 | tf_op jit(solution)/shard_map/ppermute | solution.py:55
  54.9 35.1 %collective-permute-start.14 = (bf16[4,2,8,16,256]{4,3,2,1,0:T(8,128)(2,1)}, bf16[4,2,8,16,256]{4,3,2,1,0:T(8,128)(2,1)}, u32[]{:S(2)}, u32[]{:S(2)}) collective-permute-start(bf16[4,2,8,16,256]{4,3,2,1,0:T(8,128)(2,1)} %pad_maximum_fusion.4), channel_id=1, source_target_pairs={{0,8},{8,16},{16,24},{24,0},{1,9},{9,17},{17,25},{25,1},{2,10},{10... | collective-permute-start | bytes 1572872 | tf_op jit(solution)/shard_map/ppermute | solution.py:55
  57.1 46.3 %all-to-all-start = ((f32[32,8,1024]{2,1,0:T(8,128)}), f32[32,8,1024]{2,1,0:T(8,128)S(1)}, u32[]{:S(2)}, u32[]{:S(2)}) async-start(f32[32,8,1024]{2,1,0:T(8,128)} %bitcast.23), calls=%async_computation | async-start | bytes 2097152 | tf_op jit(solution)/shard_map/all_to_all | solution.py:436
  68.8 21.1 %collective-permute-start.16 = (bf16[4,2,8,16,256]{4,3,2,1,0:T(8,128)(2,1)}, bf16[4,2,8,16,256]{4,3,2,1,0:T(8,128)(2,1)S(1)}, u32[]{:S(2)}, u32[]{:S(2)}) collective-permute-start(bf16[4,2,8,16,256]{4,3,2,1,0:T(8,128)(2,1)} %pad_maximum_fusion.4), channel_id=1, source_target_pairs={{0,24},{8,0},{16,8},{24,16},{1,25},{9,1},{17,9},{25,17},{2,26},{10... | collective-permute-start | bytes 1572872 | tf_op jit(solution)/shard_map/ppermute | solution.py:55
  105.9 14.0 %all-to-all-start.1 = ((f32[32,16,128]{2,1,0:T(8,128)}), f32[32,16,128]{2,1,0:T(8,128)S(1)}, u32[]{:S(2)}, u32[]{:S(2)}) async-start(f32[32,16,128]{2,1,0:T(8,128)} %kernel_blocks.1), calls=%async_computation.1 | async-start | bytes 524288 | tf_op jit(solution)/shard_map/all_to_all | solution.py:443
  119.9 7.8 %collective-permute-start.17 = (f32[2,16,128]{2,1,0:T(8,128)S(1)}, f32[2,16,128]{2,1,0:T(8,128)S(1)}, u32[]{:S(2)}, u32[]{:S(2)}) collective-permute-start(f32[2,16,128]{2,1,0:T(8,128)S(1)} %reduce_sum.18), channel_id=1, source_target_pairs={{0,1},{1,0},{2,3},{3,2},{4,5},{5,4},{6,7},{7,6},{8,9},{9,8},{10,11... | collective-permute-start | bytes 49160 | tf_op jit(solution)/shard_map/ppermute | solution.py:55
  127.8 7.5 %collective-permute-start.20 = (f32[2,16,128]{2,1,0:T(8,128)S(1)}, f32[2,16,128]{2,1,0:T(8,128)S(1)}, u32[]{:S(2)}, u32[]{:S(2)}) collective-permute-start(f32[2,16,128]{2,1,0:T(8,128)S(1)} %get-tuple-element.21), channel_id=1, source_target_pairs={{0,192},{64,0},{128,64},{192,128},{1,193},{65,1},{129,65},{193,129... | collective-permute-start | bytes 49160 | tf_op jit(solution)/shard_map/ppermute | solution.py:55
  130.4 5.0 %collective-permute-start.19 = (f32[2,16,128]{2,1,0:T(8,128)S(1)}, f32[2,16,128]{2,1,0:T(8,128)S(1)}, u32[]{:S(2)}, u32[]{:S(2)}) collective-permute-start(f32[2,16,128]{2,1,0:T(8,128)S(1)} %get-tuple-element.21), channel_id=1, source_target_pairs={{0,128},{64,192},{128,0},{192,64},{1,129},{65,193},{129,1},{193,65... | collective-permute-start | bytes 49160 | tf_op jit(solution)/shard_map/ppermute | solution.py:55
  133.4 5.5 %collective-permute-start.18 = (f32[2,16,128]{2,1,0:T(8,128)S(1)}, f32[2,16,128]{2,1,0:T(8,128)S(1)}, u32[]{:S(2)}, u32[]{:S(2)}) collective-permute-start(f32[2,16,128]{2,1,0:T(8,128)S(1)} %get-tuple-element.21), channel_id=1, source_target_pairs={{0,64},{64,128},{128,192},{192,0},{1,65},{65,129},{129,193},{193,1... | collective-permute-start | bytes 49160 | tf_op jit(solution)/shard_map/ppermute | solution.py:55
  138.9 1.3 collective-permute-start.21
  (9 other events, 181.3 us)

commit v12 on v11

--- a/solution.py
+++ b/solution.py
@@ -168,7 +168,6 @@
 def choose_kernel(partner_ref, place_ref, flip_ref, near_ref, far_ref, val_ref, cond_ref):
     level, core = place_ref[0], place_ref[1]
     for m in range(8):
-        val_ref[0, m] = dot(near_ref[m, :16], flip_ref[...]).astype(BF)
         wanted = partner_ref[(level * 2 + core) * 8 + m]
         back = (level - wanted // 16) & 3
         at = back * 8 + (wanted & 7)
@@ -176,11 +175,14 @@
 
         def take(ref, m=m, at=at):
             row = ref[at]
-            val_ref[1, m] = dot(row[:16], flip_ref[...]).astype(BF)
+            val_ref[1, m] = row[:16]
             cond_ref[m] = row[16:]
 
         pl.when(near)(functools.partial(take, near_ref))
         pl.when(jnp.logical_not(near))(functools.partial(take, far_ref))
+    for part, rows in ((0, near_ref[:8, :16]), (1, val_ref[1])):
+        turned_rows = dot(rows.reshape(128, 256), flip_ref[...]).astype(BF)
+        val_ref[part] = turned_rows.reshape(8, 16, 256)
 
 
 def choose(partner, near, far, flip):

time: 155 us -> 153 us (0.987)
  Pallas kernels: 33.5 us -> 31.6 us
    pallas_call x1, Pallas kernels: 2.86 us -> 0.94 us  [choose(): pl.pallas_call(choose_kernel, in_specs=[pl.BlockSpec(memory_space=pltpu.S...]
where the time goes in v12:
time: 153 us; the launch traced here: 152 us
  starting transfers between devices  64.1 us (42%)
  waiting for transfers between devices  33 us (22%)
  Pallas kernels  31.6 us (21%)
  blocking collectives  12.3 us (8%)
  other arithmetic  5.86 us (4%)
  local copies, waits for them, and re-layouts  4.05 us (3%)
    ppermute x22, starting transfers between devices, turned(): lax.ppermute(value, axis, [(i, (i + step) % size) for i in range(size)])  45.5 us
    ppermute x22, waiting for transfers between devices, turned(): lax.ppermute(value, axis, [(i, (i + step) % size) for i in range(size)])  26.2 us
    pallas_call x1, Pallas kernels, screened_transform(): pl.pallas_call(screened_kernel, grid=(LINE_STEPS + HALF,), in_specs=[pl.B...  13.3 us
    all_to_all x1, blocking collectives, copies_to_all(): return lax.all_to_all(copies, axes, split_axis=0, concat_axis=0, tiled=True)  12.3 us
    pallas_call x1, Pallas kernels, response(): pl.pallas_call(response_kernel, grid_spec=pltpu.PrefetchScalarGridSpec(nu...  11.8 us
    all_to_all x1, starting transfers between devices, on_device(): lax.all_to_all(planes, GA, split_axis=0, concat_axis=0, tiled=True)  11.6 us
    all_to_all x1, starting transfers between devices, on_device(): lax.all_to_all(blocks, ('x', 'y'), split_axis=0, concat_axis=0, tiled=True)  6.99 us
    all_to_all x1, waiting for transfers between devices, on_device(): lax.all_to_all(blocks, ('x', 'y'), split_axis=0, concat_axis=0, tiled=True)  6.78 us
  transfers between devices with their start and end apart: 24, of which 12 were waited for; matrix products, arithmetic and copies ran while one was open for 3% of the time, Pallas kernels for 18%

profile of v12, /device:TPU:8, one launch (start us, length us, event | category | flops | bytes accessed | tf_op | source)
XLA Modules:
  0.0 152.2 jit_solution(16258089199929264813)
XLA Ops:
  1.6 4.7 %collective-permute-start.2 = (bf16[8,32,256]{2,1,0:T(8,128)(2,1)S(1)}, bf16[8,32,256]{2,1,0:T(8,128)(2,1)S(1)}, u32[]{:S(2)}, u32[]{:S(2)}) collective-permute-start(bf16[8,32,256]{2,1,0:T(8,128)(2,1)S(1)} %bitcast.83), channel_id=1, source_target_pairs={{0,192},{64,0},{128,64},{192,128},{1,193},{65,1},{129,65},{193,129... | collective-permute-start | bytes 393224 | tf_op jit(solution)/shard_map/ppermute | solution.py:55
  7.0 3.2 %collective-permute-done.2 = bf16[8,32,256]{2,1,0:T(8,128)(2,1)S(1)} collective-permute-done((bf16[8,32,256]{2,1,0:T(8,128)(2,1)S(1)}, bf16[8,32,256]{2,1,0:T(8,128)(2,1)S(1)}, u32[]{:S(2)}, u32[]{:S(2)}) %collective-permute-start.2) | collective-permute-done | bytes 131104 | tf_op jit(solution)/shard_map/ppermute | solution.py:55
  10.2 7.3 %collective-permute-done.1 = bf16[8,32,256]{2,1,0:T(8,128)(2,1)S(1)} collective-permute-done((bf16[8,32,256]{2,1,0:T(8,128)(2,1)S(1)}, bf16[8,32,256]{2,1,0:T(8,128)(2,1)S(1)}, u32[]{:S(2)}, u32[]{:S(2)}) %collective-permute-start.1) | collective-permute-done | bytes 131104 | tf_op jit(solution)/shard_map/ppermute | solution.py:55
  21.2 5.5 %collective-permute-start.4 = (bf16[2,8,16,256]{3,2,1,0:T(8,128)(2,1)S(1)}, bf16[2,8,16,256]{3,2,1,0:T(8,128)(2,1)S(1)}, u32[]{:S(2)}, u32[]{:S(2)}) collective-permute-start(bf16[2,8,16,256]{3,2,1,0:T(8,128)(2,1)S(1)} %get-tuple-element.11), channel_id=1, source_target_pairs={{0,1},{1,0},{2,3},{3,2},{4,5},{5,4},{6,7},{7,6},{8,9},{9,8},{10,11... | collective-permute-start | bytes 393224 | tf_op jit(solution)/shard_map/ppermute | solution.py:55
  26.8 4.1 %collective-permute-done.4 = bf16[2,8,16,256]{3,2,1,0:T(8,128)(2,1)S(1)} collective-permute-done((bf16[2,8,16,256]{3,2,1,0:T(8,128)(2,1)S(1)}, bf16[2,8,16,256]{3,2,1,0:T(8,128)(2,1)S(1)}, u32[]{:S(2)}, u32[]{:S(2)}) %collective-permute-start.4) | collective-permute-done | bytes 131104 | tf_op jit(solution)/shard_map/ppermute | solution.py:55
  30.9 2.8 %collective-permute-start.7 = (bf16[2,8,16,256]{3,2,1,0:T(8,128)(2,1)S(1)}, bf16[2,8,16,256]{3,2,1,0:T(8,128)(2,1)S(1)}, u32[]{:S(2)}, u32[]{:S(2)}) collective-permute-start(bf16[2,8,16,256]{3,2,1,0:T(8,128)(2,1)S(1)} %get-tuple-element.23), channel_id=1, source_target_pairs={{0,24},{8,0},{16,8},{24,16},{1,25},{9,1},{17,9},{25,17},{2,26},{10... | collective-permute-start | bytes 393224 | tf_op jit(solution)/shard_map/ppermute | solution.py:55
  35.9 2.6 %collective-permute-start.9 = (bf16[2,8,16,256]{3,2,1,0:T(8,128)(2,1)S(1)}, bf16[2,8,16,256]{3,2,1,0:T(8,128)(2,1)S(1)}, u32[]{:S(2)}, u32[]{:S(2)}) collective-permute-start(bf16[2,8,16,256]{3,2,1,0:T(8,128)(2,1)S(1)} %get-tuple-element.24), channel_id=1, source_target_pairs={{0,4},{2,6},{4,0},{6,2},{1,5},{3,7},{5,1},{7,3},{8,12},{10,14},{12... | collective-permute-start | bytes 393224 | tf_op jit(solution)/shard_map/ppermute | solution.py:55
  40.4 2.0 %cond_planes.1 = f32[256,1024]{1,0:T(8,128)} custom-call(bf16[256,512]{1,0:T(8,128)(2,1)S(1)} %copy-done.6, bf16[256,512]{1,0:T(8,128)(2,1)S(1)} %copy-done.7, bf16[8,16,256]{2,1,0:T(8,128)(2,1)S(1)} %slice.14.home_ref, bf16[8,16,256]{2,1,0:T(8,128)(2,1)S(1)} %get-tuple-element.12.away_ref), custom_call_target="tpu_custom_call" | custom-call | flops 1610612736 | bytes 2097152 | tf_op jit(solution)/shard_map/cond_planes/pallas_call | solution.py:224
  44.7 2.9 %collective-permute-start.13 = (bf16[4,2,8,16,256]{4,3,2,1,0:T(8,128)(2,1)S(1)}, bf16[4,2,8,16,256]{4,3,2,1,0:T(8,128)(2,1)}, u32[]{:S(2)}, u32[]{:S(2)}) collective-permute-start(bf16[4,2,8,16,256]{4,3,2,1,0:T(8,128)(2,1)S(1)} %pad_maximum_fusion.3), channel_id=1, source_target_pairs={{0,6},{2,0},{4,2},{6,4},{1,7},{3,1},{5,3},{7,5},{8,14},{10,8},{12,... | collective-permute-start | bytes 1572872 | tf_op jit(solution)/shard_map/ppermute | solution.py:55
  51.0 2.0 %collective-permute-start.15 = (bf16[4,2,8,16,256]{4,3,2,1,0:T(8,128)(2,1)}, bf16[4,2,8,16,256]{4,3,2,1,0:T(8,128)(2,1)}, u32[]{:S(2)}, u32[]{:S(2)}) collective-permute-start(bf16[4,2,8,16,256]{4,3,2,1,0:T(8,128)(2,1)} %pad_maximum_fusion.4), channel_id=1, source_target_pairs={{0,16},{8,24},{16,0},{24,8},{1,17},{9,25},{17,1},{25,9},{2,18},{10... | collective-permute-start | bytes 1572872 | tf_op jit(solution)/shard_map/ppermute | solution.py:55
  53.0 2.3 %collective-permute-start.14 = (bf16[4,2,8,16,256]{4,3,2,1,0:T(8,128)(2,1)}, bf16[4,2,8,16,256]{4,3,2,1,0:T(8,128)(2,1)}, u32[]{:S(2)}, u32[]{:S(2)}) collective-permute-start(bf16[4,2,8,16,256]{4,3,2,1,0:T(8,128)(2,1)} %pad_maximum_fusion.4), channel_id=1, source_target_pairs={{0,8},{8,16},{16,24},{24,0},{1,9},{9,17},{17,25},{25,1},{2,10},{10... | collective-permute-start | bytes 1572872 | tf_op jit(solution)/shard_map/ppermute | solution.py:55
  55.3 11.6 %all-to-all-start = ((f32[32,8,1024]{2,1,0:T(8,128)}), f32[32,8,1024]{2,1,0:T(8,128)S(1)}, u32[]{:S(2)}, u32[]{:S(2)}) async-start(f32[32,8,1024]{2,1,0:T(8,128)} %bitcast.23), calls=%async_computation | async-start | bytes 2097152 | tf_op jit(solution)/shard_map/all_to_all | solution.py:438
  66.9 2.8 %collective-permute-start.16 = (bf16[4,2,8,16,256]{4,3,2,1,0:T(8,128)(2,1)}, bf16[4,2,8,16,256]{4,3,2,1,0:T(8,128)(2,1)S(1)}, u32[]{:S(2)}, u32[]{:S(2)}) collective-permute-start(bf16[4,2,8,16,256]{4,3,2,1,0:T(8,128)(2,1)} %pad_maximum_fusion.4), channel_id=1, source_target_pairs={{0,24},{8,0},{16,8},{24,16},{1,25},{9,1},{17,9},{25,17},{2,26},{10... | collective-permute-start | bytes 1572872 | tf_op jit(solution)/shard_map/ppermute | solution.py:55
  69.7 2.2 %copy-done.3 = bf16[256,8192]{1,0:T(8,128)(2,1)S(1)} copy-done((bf16[256,8192]{1,0:T(8,128)(2,1)S(1)}, bf16[256,8192]{1,0:T(8,128)(2,1)}, u32[]{:S(2)}) %copy-start.3) | copy-done | bytes 4194328
  71.9 13.3 %screened_transform.1 = (bf16[17,512,256]{2,1,0:T(8,128)(2,1)S(1)}, f32[8,128]{1,0:T(8,128)}) custom-call(s32[32,1,256]{2,1,0:T(1,128)S(1)} %bitcast.80, bf16[96,32]{1,0:T(8,128)(2,1)S(1)} %copy-done.8, bf16[2,256,256]{2,1,0:T(8,128)(2,1)S(1)} %copy-done.4, bf16[2,256,256]{2,1,0:T(8,128)(2,1)S(1)} %copy-done.5, bf16[256,8192]{1,0:T(8,128)(2,1)S(1)} %copy-done.3), custom_call_target="tpu_custom_call" | custom-call | flops 13690208256 | bytes 9437184 | tf_op jit(solution)/shard_map/screened_transform/pallas_call | solution.py:132
  89.7 11.8 %valence_response.1.r_ref = f32[1024,256]{1,0:T(8,128)S(1)} custom-call(s32[1]{0:T(128)} %bitcast.25.place_ref, bf16[32,8,16,256]{3,2,1,0:T(8,128)(2,1)S(1)} %bitcast.68, bf16[32,8,16,256]{3,2,1,0:T(8,128)(2,1)S(1)} %bitcast.72, bf16[32,8,16,256]{3,2,1,0:T(8,128)(2,1)S(1)} %bitcast.69, bf16[32,8,16,256]{3,2,1,0:T(8,128)(2,1)S(1)} %bitcast.73, ...), custom_call_target="tpu_custom_call" | custom-call | flops 36507222016 | bytes 9437184 | tf_op jit(solution)/shard_map/valence_response/pallas_call | solution.py:295
  104.1 7.0 %all-to-all-start.1 = ((f32[32,16,128]{2,1,0:T(8,128)}), f32[32,16,128]{2,1,0:T(8,128)S(1)}, u32[]{:S(2)}, u32[]{:S(2)}) async-start(f32[32,16,128]{2,1,0:T(8,128)} %kernel_blocks.1), calls=%async_computation.1 | async-start | bytes 524288 | tf_op jit(solution)/shard_map/all_to_all | solution.py:445
  111.3 6.8 %all-to-all-done.1 = f32[32,16,128]{2,1,0:T(8,128)S(1)} async-done(((f32[32,16,128]{2,1,0:T(8,128)}), f32[32,16,128]{2,1,0:T(8,128)S(1)}, u32[]{:S(2)}, u32[]{:S(2)}) %all-to-all-start.1) | async-done | bytes 262176 | tf_op jit(solution)/shard_map/all_to_all | solution.py:445
  118.1 5.5 %collective-permute-start.17 = (f32[2,16,128]{2,1,0:T(8,128)S(1)}, f32[2,16,128]{2,1,0:T(8,128)S(1)}, u32[]{:S(2)}, u32[]{:S(2)}) collective-permute-start(f32[2,16,128]{2,1,0:T(8,128)S(1)} %reduce_sum.18), channel_id=1, source_target_pairs={{0,1},{1,0},{2,3},{3,2},{4,5},{5,4},{6,7},{7,6},{8,9},{9,8},{10,11... | collective-permute-start | bytes 49160 | tf_op jit(solution)/shard_map/ppermute | solution.py:55
  123.6 2.3 %collective-permute-done.17 = f32[2,16,128]{2,1,0:T(8,128)S(1)} collective-permute-done((f32[2,16,128]{2,1,0:T(8,128)S(1)}, f32[2,16,128]{2,1,0:T(8,128)S(1)}, u32[]{:S(2)}, u32[]{:S(2)}) %collective-permute-start.17) | collective-permute-done | bytes 16416 | tf_op jit(solution)/shard_map/ppermute | solution.py:55
  125.8 3.0 %collective-permute-start.20 = (f32[2,16,128]{2,1,0:T(8,128)S(1)}, f32[2,16,128]{2,1,0:T(8,128)S(1)}, u32[]{:S(2)}, u32[]{:S(2)}) collective-permute-start(f32[2,16,128]{2,1,0:T(8,128)S(1)} %get-tuple-element.21), channel_id=1, source_target_pairs={{0,192},{64,0},{128,64},{192,128},{1,193},{65,1},{129,65},{193,129... | collective-permute-start | bytes 49160 | tf_op jit(solution)/shard_map/ppermute | solution.py:55
  128.8 2.8 %collective-permute-start.19 = (f32[2,16,128]{2,1,0:T(8,128)S(1)}, f32[2,16,128]{2,1,0:T(8,128)S(1)}, u32[]{:S(2)}, u32[]{:S(2)}) collective-permute-start(f32[2,16,128]{2,1,0:T(8,128)S(1)} %get-tuple-element.21), channel_id=1, source_target_pairs={{0,128},{64,192},{128,0},{192,64},{1,129},{65,193},{129,1},{193,65... | collective-permute-start | bytes 49160 | tf_op jit(solution)/shard_map/ppermute | solution.py:55
  133.5 3.6 %collective-permute-done.18 = f32[2,16,128]{2,1,0:T(8,128)S(1)} collective-permute-done((f32[2,16,128]{2,1,0:T(8,128)S(1)}, f32[2,16,128]{2,1,0:T(8,128)S(1)}, u32[]{:S(2)}, u32[]{:S(2)}) %collective-permute-start.18) | collective-permute-done | bytes 16416 | tf_op jit(solution)/shard_map/ppermute | solution.py:55
  139.0 12.3 %all_to_all.21.full_ref = bf16[16,2,32,128]{3,2,1,0:T(8,128)(2,1)S(1)} all-to-all(bf16[16,2,32,128]{3,2,1,0:T(8,128)(2,1)S(1)} %broadcast_in_dim.50), channel_id=1, replica_groups=mesh['zl'=4,'co'=2,'x'=4,'y'=4,'zh'=2] {'x','y'}, dimensions={0} | all-to-all | bytes 524288 | tf_op jit(solution)/shard_map/all_to_all | solution.py:65
  (84 shorter events, 26.8 us)
Async XLA Ops:
  1.6 8.6 %collective-permute-start.2 = (bf16[8,32,256]{2,1,0:T(8,128)(2,1)S(1)}, bf16[8,32,256]{2,1,0:T(8,128)(2,1)S(1)}, u32[]{:S(2)}, u32[]{:S(2)}) collective-permute-start(bf16[8,32,256]{2,1,0:T(8,128)(2,1)S(1)} %bitcast.83), channel_id=1, source_target_pairs={{0,192},{64,0},{128,64},{192,128},{1,193},{65,1},{129,65},{193,129... | collective-permute-start | bytes 393224 | tf_op jit(solution)/shard_map/ppermute | solution.py:55
  6.3 11.2 %collective-permute-start.1 = (bf16[8,32,256]{2,1,0:T(8,128)(2,1)S(1)}, bf16[8,32,256]{2,1,0:T(8,128)(2,1)S(1)}, u32[]{:S(2)}, u32[]{:S(2)}) collective-permute-start(bf16[8,32,256]{2,1,0:T(8,128)(2,1)S(1)} %bitcast.84), channel_id=1, source_target_pairs={{0,128},{64,192},{128,0},{192,64},{1,129},{65,193},{129,1},{193,65... | collective-permute-start | bytes 393224 | tf_op jit(solution)/shard_map/ppermute | solution.py:55
  6.3 11.2 %collective-permute-start = (bf16[8,32,256]{2,1,0:T(8,128)(2,1)S(1)}, bf16[8,32,256]{2,1,0:T(8,128)(2,1)S(1)}, u32[]{:S(2)}, u32[]{:S(2)}) collective-permute-start(bf16[8,32,256]{2,1,0:T(8,128)(2,1)S(1)} %bitcast.85), channel_id=1, source_target_pairs={{0,64},{64,128},{128,192},{192,0},{1,65},{65,129},{129,193},{193,1... | collective-permute-start | bytes 393224 | tf_op jit(solution)/shard_map/ppermute | solution.py:55
  17.6 2.0 %collective-permute-start.3 = (bf16[32,32,256]{2,1,0:T(8,128)(2,1)S(1)}, bf16[32,32,256]{2,1,0:T(8,128)(2,1)S(1)}, u32[]{:S(2)}, u32[]{:S(2)}) collective-permute-start(bf16[32,32,256]{2,1,0:T(8,128)(2,1)S(1)} %bitcast.76), channel_id=1, source_target_pairs={{0,32},{32,0},{1,33},{33,1},{2,34},{34,2},{3,35},{35,3},{4,36},{36... | collective-permute-start | bytes 1572872 | tf_op jit(solution)/shard_map/ppermute | solution.py:55
  21.2 9.6 %collective-permute-start.4 = (bf16[2,8,16,256]{3,2,1,0:T(8,128)(2,1)S(1)}, bf16[2,8,16,256]{3,2,1,0:T(8,128)(2,1)S(1)}, u32[]{:S(2)}, u32[]{:S(2)}) collective-permute-start(bf16[2,8,16,256]{3,2,1,0:T(8,128)(2,1)S(1)} %get-tuple-element.11), channel_id=1, source_target_pairs={{0,1},{1,0},{2,3},{3,2},{4,5},{5,4},{6,7},{7,6},{8,9},{9,8},{10,11... | collective-permute-start | bytes 393224 | tf_op jit(solution)/shard_map/ppermute | solution.py:55
  30.9 7.8 %collective-permute-start.7 = (bf16[2,8,16,256]{3,2,1,0:T(8,128)(2,1)S(1)}, bf16[2,8,16,256]{3,2,1,0:T(8,128)(2,1)S(1)}, u32[]{:S(2)}, u32[]{:S(2)}) collective-permute-start(bf16[2,8,16,256]{3,2,1,0:T(8,128)(2,1)S(1)} %get-tuple-element.23), channel_id=1, source_target_pairs={{0,24},{8,0},{16,8},{24,16},{1,25},{9,1},{17,9},{25,17},{2,26},{10... | collective-permute-start | bytes 393224 | tf_op jit(solution)/shard_map/ppermute | solution.py:55
  33.7 8.7 %collective-permute-start.6 = (bf16[2,8,16,256]{3,2,1,0:T(8,128)(2,1)S(1)}, bf16[2,8,16,256]{3,2,1,0:T(8,128)(2,1)S(1)}, u32[]{:S(2)}, u32[]{:S(2)}) collective-permute-start(bf16[2,8,16,256]{3,2,1,0:T(8,128)(2,1)S(1)} %get-tuple-element.23), channel_id=1, source_target_pairs={{0,16},{8,24},{16,0},{24,8},{1,17},{9,25},{17,1},{25,9},{2,18},{10... | collective-permute-start | bytes 393224 | tf_op jit(solution)/shard_map/ppermute | solution.py:55
  34.5 7.9 %collective-permute-start.5 = (bf16[2,8,16,256]{3,2,1,0:T(8,128)(2,1)S(1)}, bf16[2,8,16,256]{3,2,1,0:T(8,128)(2,1)S(1)}, u32[]{:S(2)}, u32[]{:S(2)}) collective-permute-start(bf16[2,8,16,256]{3,2,1,0:T(8,128)(2,1)S(1)} %get-tuple-element.23), channel_id=1, source_target_pairs={{0,8},{8,16},{16,24},{24,0},{1,9},{9,17},{17,25},{25,1},{2,10},{10... | collective-permute-start | bytes 393224 | tf_op jit(solution)/shard_map/ppermute | solution.py:55
  35.4 7.1 %collective-permute-start.10 = (bf16[2,8,16,256]{3,2,1,0:T(8,128)(2,1)S(1)}, bf16[2,8,16,256]{3,2,1,0:T(8,128)(2,1)S(1)}, u32[]{:S(2)}, u32[]{:S(2)}) collective-permute-start(bf16[2,8,16,256]{3,2,1,0:T(8,128)(2,1)S(1)} %get-tuple-element.24), channel_id=1, source_target_pairs={{0,6},{2,0},{4,2},{6,4},{1,7},{3,1},{5,3},{7,5},{8,14},{10,8},{12,... | collective-permute-start | bytes 393224 | tf_op jit(solution)/shard_map/ppermute | solution.py:55
  35.9 7.1 %collective-permute-start.9 = (bf16[2,8,16,256]{3,2,1,0:T(8,128)(2,1)S(1)}, bf16[2,8,16,256]{3,2,1,0:T(8,128)(2,1)S(1)}, u32[]{:S(2)}, u32[]{:S(2)}) collective-permute-start(bf16[2,8,16,256]{3,2,1,0:T(8,128)(2,1)S(1)} %get-tuple-element.24), channel_id=1, source_target_pairs={{0,4},{2,6},{4,0},{6,2},{1,5},{3,7},{5,1},{7,3},{8,12},{10,14},{12... | collective-permute-start | bytes 393224 | tf_op jit(solution)/shard_map/ppermute | solution.py:55
  38.7 5.2 %collective-permute-start.8 = (bf16[2,8,16,256]{3,2,1,0:T(8,128)(2,1)S(1)}, bf16[2,8,16,256]{3,2,1,0:T(8,128)(2,1)S(1)}, u32[]{:S(2)}, u32[]{:S(2)}) collective-permute-start(bf16[2,8,16,256]{3,2,1,0:T(8,128)(2,1)S(1)} %get-tuple-element.24), channel_id=1, source_target_pairs={{0,2},{2,4},{4,6},{6,0},{1,3},{3,5},{5,7},{7,1},{8,10},{10,12},{12... | collective-permute-start | bytes 393224 | tf_op jit(solution)/shard_map/ppermute | solution.py:55
  44.7 22.2 %collective-permute-start.13 = (bf16[4,2,8,16,256]{4,3,2,1,0:T(8,128)(2,1)S(1)}, bf16[4,2,8,16,256]{4,3,2,1,0:T(8,128)(2,1)}, u32[]{:S(2)}, u32[]{:S(2)}) collective-permute-start(bf16[4,2,8,16,256]{4,3,2,1,0:T(8,128)(2,1)S(1)} %pad_maximum_fusion.3), channel_id=1, source_target_pairs={{0,6},{2,0},{4,2},{6,4},{1,7},{3,1},{5,3},{7,5},{8,14},{10,8},{12,... | collective-permute-start | bytes 1572872 | tf_op jit(solution)/shard_map/ppermute | solution.py:55
  48.8 36.4 %collective-permute-start.12 = (bf16[4,2,8,16,256]{4,3,2,1,0:T(8,128)(2,1)S(1)}, bf16[4,2,8,16,256]{4,3,2,1,0:T(8,128)(2,1)}, u32[]{:S(2)}, u32[]{:S(2)}) collective-permute-start(bf16[4,2,8,16,256]{4,3,2,1,0:T(8,128)(2,1)S(1)} %pad_maximum_fusion.3), channel_id=1, source_target_pairs={{0,4},{2,6},{4,0},{6,2},{1,5},{3,7},{5,1},{7,3},{8,12},{10,14},{12... | collective-permute-start | bytes 1572872 | tf_op jit(solution)/shard_map/ppermute | solution.py:55
  49.0 36.3 %collective-permute-start.11 = (bf16[4,2,8,16,256]{4,3,2,1,0:T(8,128)(2,1)S(1)}, bf16[4,2,8,16,256]{4,3,2,1,0:T(8,128)(2,1)}, u32[]{:S(2)}, u32[]{:S(2)}) collective-permute-start(bf16[4,2,8,16,256]{4,3,2,1,0:T(8,128)(2,1)S(1)} %pad_maximum_fusion.3), channel_id=1, source_target_pairs={{0,2},{2,4},{4,6},{6,0},{1,3},{3,5},{5,7},{7,1},{8,10},{10,12},{12... | collective-permute-start | bytes 1572872 | tf_op jit(solution)/shard_map/ppermute | solution.py:55
  51.0 37.1 %collective-permute-start.15 = (bf16[4,2,8,16,256]{4,3,2,1,0:T(8,128)(2,1)}, bf16[4,2,8,16,256]{4,3,2,1,0:T(8,128)(2,1)}, u32[]{:S(2)}, u32[]{:S(2)}) collective-permute-start(bf16[4,2,8,16,256]{4,3,2,1,0:T(8,128)(2,1)} %pad_maximum_fusion.4), channel_id=1, source_target_pairs={{0,16},{8,24},{16,0},{24,8},{1,17},{9,25},{17,1},{25,9},{2,18},{10... | collective-permute-start | bytes 1572872 | tf_op jit(solution)/shard_map/ppermute | solution.py:55
  53.0 35.0 %collective-permute-start.14 = (bf16[4,2,8,16,256]{4,3,2,1,0:T(8,128)(2,1)}, bf16[4,2,8,16,256]{4,3,2,1,0:T(8,128)(2,1)}, u32[]{:S(2)}, u32[]{:S(2)}) collective-permute-start(bf16[4,2,8,16,256]{4,3,2,1,0:T(8,128)(2,1)} %pad_maximum_fusion.4), channel_id=1, source_target_pairs={{0,8},{8,16},{16,24},{24,0},{1,9},{9,17},{17,25},{25,1},{2,10},{10... | collective-permute-start | bytes 1572872 | tf_op jit(solution)/shard_map/ppermute | solution.py:55
  55.3 46.2 %all-to-all-start = ((f32[32,8,1024]{2,1,0:T(8,128)}), f32[32,8,1024]{2,1,0:T(8,128)S(1)}, u32[]{:S(2)}, u32[]{:S(2)}) async-start(f32[32,8,1024]{2,1,0:T(8,128)} %bitcast.23), calls=%async_computation | async-start | bytes 2097152 | tf_op jit(solution)/shard_map/all_to_all | solution.py:438
  66.9 21.1 %collective-permute-start.16 = (bf16[4,2,8,16,256]{4,3,2,1,0:T(8,128)(2,1)}, bf16[4,2,8,16,256]{4,3,2,1,0:T(8,128)(2,1)S(1)}, u32[]{:S(2)}, u32[]{:S(2)}) collective-permute-start(bf16[4,2,8,16,256]{4,3,2,1,0:T(8,128)(2,1)} %pad_maximum_fusion.4), channel_id=1, source_target_pairs={{0,24},{8,0},{16,8},{24,16},{1,25},{9,1},{17,9},{25,17},{2,26},{10... | collective-permute-start | bytes 1572872 | tf_op jit(solution)/shard_map/ppermute | solution.py:55
  104.1 14.0 %all-to-all-start.1 = ((f32[32,16,128]{2,1,0:T(8,128)}), f32[32,16,128]{2,1,0:T(8,128)S(1)}, u32[]{:S(2)}, u32[]{:S(2)}) async-start(f32[32,16,128]{2,1,0:T(8,128)} %kernel_blocks.1), calls=%async_computation.1 | async-start | bytes 524288 | tf_op jit(solution)/shard_map/all_to_all | solution.py:445
  118.1 7.8 %collective-permute-start.17 = (f32[2,16,128]{2,1,0:T(8,128)S(1)}, f32[2,16,128]{2,1,0:T(8,128)S(1)}, u32[]{:S(2)}, u32[]{:S(2)}) collective-permute-start(f32[2,16,128]{2,1,0:T(8,128)S(1)} %reduce_sum.18), channel_id=1, source_target_pairs={{0,1},{1,0},{2,3},{3,2},{4,5},{5,4},{6,7},{7,6},{8,9},{9,8},{10,11... | collective-permute-start | bytes 49160 | tf_op jit(solution)/shard_map/ppermute | solution.py:55
  125.8 7.7 %collective-permute-start.20 = (f32[2,16,128]{2,1,0:T(8,128)S(1)}, f32[2,16,128]{2,1,0:T(8,128)S(1)}, u32[]{:S(2)}, u32[]{:S(2)}) collective-permute-start(f32[2,16,128]{2,1,0:T(8,128)S(1)} %get-tuple-element.21), channel_id=1, source_target_pairs={{0,192},{64,0},{128,64},{192,128},{1,193},{65,1},{129,65},{193,129... | collective-permute-start | bytes 49160 | tf_op jit(solution)/shard_map/ppermute | solution.py:55
  128.8 4.7 %collective-permute-start.19 = (f32[2,16,128]{2,1,0:T(8,128)S(1)}, f32[2,16,128]{2,1,0:T(8,128)S(1)}, u32[]{:S(2)}, u32[]{:S(2)}) collective-permute-start(f32[2,16,128]{2,1,0:T(8,128)S(1)} %get-tuple-element.21), channel_id=1, source_target_pairs={{0,128},{64,192},{128,0},{192,64},{1,129},{65,193},{129,1},{193,65... | collective-permute-start | bytes 49160 | tf_op jit(solution)/shard_map/ppermute | solution.py:55
  131.6 5.5 %collective-permute-start.18 = (f32[2,16,128]{2,1,0:T(8,128)S(1)}, f32[2,16,128]{2,1,0:T(8,128)S(1)}, u32[]{:S(2)}, u32[]{:S(2)}) collective-permute-start(f32[2,16,128]{2,1,0:T(8,128)S(1)} %get-tuple-element.21), channel_id=1, source_target_pairs={{0,64},{64,128},{128,192},{192,0},{1,65},{65,129},{129,193},{193,1... | collective-permute-start | bytes 49160 | tf_op jit(solution)/shard_map/ppermute | solution.py:55
  137.1 1.3 collective-permute-start.21
  (9 other events, 177.5 us)

commit v13 on v12

--- a/solution.py
+++ b/solution.py
@@ -423,6 +423,8 @@
     negative = (NX - index // NY) % NX * NY + (NY - index % NY) % NY
     negative = jnp.where(place > NZ // 2, negative, index)
     flip = (index[:, None] == negative[None, :]).astype(BF)
+    tables = line_tables(gmap, place)
+    near, tables = lax.optimization_barrier((near, tables))
     far = turned(near, "co", 1)
 
     vals, away_cond = choose(partner, near, far, flip)
@@ -439,7 +441,7 @@
     home = jnp.stack(homes).reshape(32, 8, 16, 256)
     away = jnp.stack(aways).reshape(32, 8, 16, 256)
     rows = response(place, home, away, wide)
-    cond = cond_spectrum(*line_tables(gmap, place), columns)
+    cond = cond_spectrum(*tables, columns)
     blocks = kernel_blocks(cond, rows)
 
     parts = lax.all_to_all(blocks, ("x", "y"), split_axis=0, concat_axis=0, tiled=True)

time: 153 us -> 152 us (level)
  waiting for transfers between devices: 33 us -> 31.1 us
    ppermute x22, waiting for transfers between devices: 26.2 us -> 24.3 us  [turned(): lax.ppermute(value, axis, [(i, (i + step) % size) for i in range(size)])]
  transfers between devices with their start and end apart: 24 -> 24, of which waited for: 12 -> 12; matrix products, arithmetic and copies ran while one was open for 3% -> 4% of each run, Pallas kernels for 18% -> 18%
where the time goes in v13:
time: 152 us; the launch traced here: 151 us
  starting transfers between devices  64.1 us (42%)
  Pallas kernels  31.6 us (21%)
  waiting for transfers between devices  31.1 us (20%)
  blocking collectives  12.3 us (8%)
  other arithmetic  6.55 us (4%)
  local copies, waits for them, and re-layouts  4.05 us (3%)
    ppermute x22, starting transfers between devices, turned(): lax.ppermute(value, axis, [(i, (i + step) % size) for i in range(size)])  45.5 us
    ppermute x22, waiting for transfers between devices, turned(): lax.ppermute(value, axis, [(i, (i + step) % size) for i in range(size)])  24.3 us
    pallas_call x1, Pallas kernels, screened_transform(): pl.pallas_call(screened_kernel, grid=(LINE_STEPS + HALF,), in_specs=[pl.B...  13.3 us
    all_to_all x1, blocking collectives, copies_to_all(): return lax.all_to_all(copies, axes, split_axis=0, concat_axis=0, tiled=True)  12.3 us
    pallas_call x1, Pallas kernels, response(): pl.pallas_call(response_kernel, grid_spec=pltpu.PrefetchScalarGridSpec(nu...  11.8 us
    all_to_all x1, starting transfers between devices, on_device(): lax.all_to_all(planes, GA, split_axis=0, concat_axis=0, tiled=True)  11.6 us
    all_to_all x1, starting transfers between devices, on_device(): lax.all_to_all(blocks, ('x', 'y'), split_axis=0, concat_axis=0, tiled=True)  6.99 us
    all_to_all x1, waiting for transfers between devices, on_device(): lax.all_to_all(blocks, ('x', 'y'), split_axis=0, concat_axis=0, tiled=True)  6.78 us
  transfers between devices with their start and end apart: 24, of which 12 were waited for; matrix products, arithmetic and copies ran while one was open for 4% of the time, Pallas kernels for 18%

profile of v13, /device:TPU:8, one launch (start us, length us, event | category | flops | bytes accessed | tf_op | source)
XLA Modules:
  0.0 150.9 jit_solution(5626905824563258977)
XLA Ops:
  1.6 4.7 %collective-permute-start.2 = (bf16[8,32,256]{2,1,0:T(8,128)(2,1)S(1)}, bf16[8,32,256]{2,1,0:T(8,128)(2,1)S(1)}, u32[]{:S(2)}, u32[]{:S(2)}) collective-permute-start(bf16[8,32,256]{2,1,0:T(8,128)(2,1)S(1)} %bitcast.83), channel_id=1, source_target_pairs={{0,192},{64,0},{128,64},{192,128},{1,193},{65,1},{129,65},{193,129... | collective-permute-start | bytes 393224 | tf_op jit(solution)/shard_map/ppermute | solution.py:55
  10.2 7.3 %collective-permute-done.1 = bf16[8,32,256]{2,1,0:T(8,128)(2,1)S(1)} collective-permute-done((bf16[8,32,256]{2,1,0:T(8,128)(2,1)S(1)}, bf16[8,32,256]{2,1,0:T(8,128)(2,1)S(1)}, u32[]{:S(2)}, u32[]{:S(2)}) %collective-permute-start.1) | collective-permute-done | bytes 131104 | tf_op jit(solution)/shard_map/ppermute | solution.py:55
  21.2 5.5 %collective-permute-start.4 = (bf16[2,8,16,256]{3,2,1,0:T(8,128)(2,1)S(1)}, bf16[2,8,16,256]{3,2,1,0:T(8,128)(2,1)S(1)}, u32[]{:S(2)}, u32[]{:S(2)}) collective-permute-start(bf16[2,8,16,256]{3,2,1,0:T(8,128)(2,1)S(1)} %get-tuple-element.17), channel_id=1, source_target_pairs={{0,1},{1,0},{2,3},{3,2},{4,5},{5,4},{6,7},{7,6},{8,9},{9,8},{10,11... | collective-permute-start | bytes 393224 | tf_op jit(solution)/shard_map/ppermute | solution.py:55
  26.8 4.1 %collective-permute-done.4 = bf16[2,8,16,256]{3,2,1,0:T(8,128)(2,1)S(1)} collective-permute-done((bf16[2,8,16,256]{3,2,1,0:T(8,128)(2,1)S(1)}, bf16[2,8,16,256]{3,2,1,0:T(8,128)(2,1)S(1)}, u32[]{:S(2)}, u32[]{:S(2)}) %collective-permute-start.4) | collective-permute-done | bytes 131104 | tf_op jit(solution)/shard_map/ppermute | solution.py:55
  30.9 2.8 %collective-permute-start.7 = (bf16[2,8,16,256]{3,2,1,0:T(8,128)(2,1)S(1)}, bf16[2,8,16,256]{3,2,1,0:T(8,128)(2,1)S(1)}, u32[]{:S(2)}, u32[]{:S(2)}) collective-permute-start(bf16[2,8,16,256]{3,2,1,0:T(8,128)(2,1)S(1)} %get-tuple-element.29), channel_id=1, source_target_pairs={{0,24},{8,0},{16,8},{24,16},{1,25},{9,1},{17,9},{25,17},{2,26},{10... | collective-permute-start | bytes 393224 | tf_op jit(solution)/shard_map/ppermute | solution.py:55
  35.9 2.6 %collective-permute-start.9 = (bf16[2,8,16,256]{3,2,1,0:T(8,128)(2,1)S(1)}, bf16[2,8,16,256]{3,2,1,0:T(8,128)(2,1)S(1)}, u32[]{:S(2)}, u32[]{:S(2)}) collective-permute-start(bf16[2,8,16,256]{3,2,1,0:T(8,128)(2,1)S(1)} %get-tuple-element.30), channel_id=1, source_target_pairs={{0,4},{2,6},{4,0},{6,2},{1,5},{3,7},{5,1},{7,3},{8,12},{10,14},{12... | collective-permute-start | bytes 393224 | tf_op jit(solution)/shard_map/ppermute | solution.py:55
  40.4 2.0 %cond_planes.1 = f32[256,1024]{1,0:T(8,128)} custom-call(bf16[256,512]{1,0:T(8,128)(2,1)S(1)} %copy-done.6, bf16[256,512]{1,0:T(8,128)(2,1)S(1)} %copy-done.7, bf16[8,16,256]{2,1,0:T(8,128)(2,1)S(1)} %slice.14.home_ref, bf16[8,16,256]{2,1,0:T(8,128)(2,1)S(1)} %get-tuple-element.18.away_ref), custom_call_target="tpu_custom_call" | custom-call | flops 1610612736 | bytes 2097152 | tf_op jit(solution)/shard_map/cond_planes/pallas_call | solution.py:224
  44.7 2.9 %collective-permute-start.13 = (bf16[4,2,8,16,256]{4,3,2,1,0:T(8,128)(2,1)S(1)}, bf16[4,2,8,16,256]{4,3,2,1,0:T(8,128)(2,1)}, u32[]{:S(2)}, u32[]{:S(2)}) collective-permute-start(bf16[4,2,8,16,256]{4,3,2,1,0:T(8,128)(2,1)S(1)} %pad_maximum_fusion.3), channel_id=1, source_target_pairs={{0,6},{2,0},{4,2},{6,4},{1,7},{3,1},{5,3},{7,5},{8,14},{10,8},{12,... | collective-permute-start | bytes 1572872 | tf_op jit(solution)/shard_map/ppermute | solution.py:55
  47.6 2.0 %collective-permute-start.11 = (bf16[4,2,8,16,256]{4,3,2,1,0:T(8,128)(2,1)S(1)}, bf16[4,2,8,16,256]{4,3,2,1,0:T(8,128)(2,1)}, u32[]{:S(2)}, u32[]{:S(2)}) collective-permute-start(bf16[4,2,8,16,256]{4,3,2,1,0:T(8,128)(2,1)S(1)} %pad_maximum_fusion.3), channel_id=1, source_target_pairs={{0,2},{2,4},{4,6},{6,0},{1,3},{3,5},{5,7},{7,1},{8,10},{10,12},{12... | collective-permute-start | bytes 1572872 | tf_op jit(solution)/shard_map/ppermute | solution.py:55
  49.7 2.1 %collective-permute-start.15 = (bf16[4,2,8,16,256]{4,3,2,1,0:T(8,128)(2,1)}, bf16[4,2,8,16,256]{4,3,2,1,0:T(8,128)(2,1)}, u32[]{:S(2)}, u32[]{:S(2)}) collective-permute-start(bf16[4,2,8,16,256]{4,3,2,1,0:T(8,128)(2,1)} %pad_maximum_fusion.4), channel_id=1, source_target_pairs={{0,16},{8,24},{16,0},{24,8},{1,17},{9,25},{17,1},{25,9},{2,18},{10... | collective-permute-start | bytes 1572872 | tf_op jit(solution)/shard_map/ppermute | solution.py:55
  51.7 2.3 %collective-permute-start.14 = (bf16[4,2,8,16,256]{4,3,2,1,0:T(8,128)(2,1)}, bf16[4,2,8,16,256]{4,3,2,1,0:T(8,128)(2,1)}, u32[]{:S(2)}, u32[]{:S(2)}) collective-permute-start(bf16[4,2,8,16,256]{4,3,2,1,0:T(8,128)(2,1)} %pad_maximum_fusion.4), channel_id=1, source_target_pairs={{0,8},{8,16},{16,24},{24,0},{1,9},{9,17},{17,25},{25,1},{2,10},{10... | collective-permute-start | bytes 1572872 | tf_op jit(solution)/shard_map/ppermute | solution.py:55
  54.0 11.6 %all-to-all-start = ((f32[32,8,1024]{2,1,0:T(8,128)}), f32[32,8,1024]{2,1,0:T(8,128)S(1)}, u32[]{:S(2)}, u32[]{:S(2)}) async-start(f32[32,8,1024]{2,1,0:T(8,128)} %bitcast.23), calls=%async_computation | async-start | bytes 2097152 | tf_op jit(solution)/shard_map/all_to_all | solution.py:440
  65.6 2.8 %collective-permute-start.16 = (bf16[4,2,8,16,256]{4,3,2,1,0:T(8,128)(2,1)}, bf16[4,2,8,16,256]{4,3,2,1,0:T(8,128)(2,1)S(1)}, u32[]{:S(2)}, u32[]{:S(2)}) collective-permute-start(bf16[4,2,8,16,256]{4,3,2,1,0:T(8,128)(2,1)} %pad_maximum_fusion.4), channel_id=1, source_target_pairs={{0,24},{8,0},{16,8},{24,16},{1,25},{9,1},{17,9},{25,17},{2,26},{10... | collective-permute-start | bytes 1572872 | tf_op jit(solution)/shard_map/ppermute | solution.py:55
  68.4 2.2 %copy-done.3 = bf16[256,8192]{1,0:T(8,128)(2,1)S(1)} copy-done((bf16[256,8192]{1,0:T(8,128)(2,1)S(1)}, bf16[256,8192]{1,0:T(8,128)(2,1)}, u32[]{:S(2)}) %copy-start.3) | copy-done | bytes 4194328
  70.6 13.3 %screened_transform.1 = (bf16[17,512,256]{2,1,0:T(8,128)(2,1)S(1)}, f32[8,128]{1,0:T(8,128)}) custom-call(s32[32,1,256]{2,1,0:T(1,128)S(1)} %bitcast.80, bf16[96,32]{1,0:T(8,128)(2,1)S(1)} %copy-done.8, bf16[2,256,256]{2,1,0:T(8,128)(2,1)S(1)} %copy-done.4, bf16[2,256,256]{2,1,0:T(8,128)(2,1)S(1)} %copy-done.5, bf16[256,8192]{1,0:T(8,128)(2,1)S(1)} %copy-done.3), custom_call_target="tpu_custom_call" | custom-call | flops 13690208256 | bytes 9437184 | tf_op jit(solution)/shard_map/screened_transform/pallas_call | solution.py:132
  88.4 11.8 %valence_response.1.r_ref = f32[1024,256]{1,0:T(8,128)S(1)} custom-call(s32[1]{0:T(128)} %bitcast.25.place_ref, bf16[32,8,16,256]{3,2,1,0:T(8,128)(2,1)S(1)} %bitcast.68, bf16[32,8,16,256]{3,2,1,0:T(8,128)(2,1)S(1)} %bitcast.72, bf16[32,8,16,256]{3,2,1,0:T(8,128)(2,1)S(1)} %bitcast.69, bf16[32,8,16,256]{3,2,1,0:T(8,128)(2,1)S(1)} %bitcast.73, ...), custom_call_target="tpu_custom_call" | custom-call | flops 36507222016 | bytes 9437184 | tf_op jit(solution)/shard_map/valence_response/pallas_call | solution.py:295
  102.8 7.0 %all-to-all-start.1 = ((f32[32,16,128]{2,1,0:T(8,128)}), f32[32,16,128]{2,1,0:T(8,128)S(1)}, u32[]{:S(2)}, u32[]{:S(2)}) async-start(f32[32,16,128]{2,1,0:T(8,128)} %kernel_blocks.1), calls=%async_computation.1 | async-start | bytes 524288 | tf_op jit(solution)/shard_map/all_to_all | solution.py:447
  110.0 6.8 %all-to-all-done.1 = f32[32,16,128]{2,1,0:T(8,128)S(1)} async-done(((f32[32,16,128]{2,1,0:T(8,128)}), f32[32,16,128]{2,1,0:T(8,128)S(1)}, u32[]{:S(2)}, u32[]{:S(2)}) %all-to-all-start.1) | async-done | bytes 262176 | tf_op jit(solution)/shard_map/all_to_all | solution.py:447
  116.8 5.5 %collective-permute-start.17 = (f32[2,16,128]{2,1,0:T(8,128)S(1)}, f32[2,16,128]{2,1,0:T(8,128)S(1)}, u32[]{:S(2)}, u32[]{:S(2)}) collective-permute-start(f32[2,16,128]{2,1,0:T(8,128)S(1)} %reduce_sum.18), channel_id=1, source_target_pairs={{0,1},{1,0},{2,3},{3,2},{4,5},{5,4},{6,7},{7,6},{8,9},{9,8},{10,11... | collective-permute-start | bytes 49160 | tf_op jit(solution)/shard_map/ppermute | solution.py:55
  122.2 2.3 %collective-permute-done.17 = f32[2,16,128]{2,1,0:T(8,128)S(1)} collective-permute-done((f32[2,16,128]{2,1,0:T(8,128)S(1)}, f32[2,16,128]{2,1,0:T(8,128)S(1)}, u32[]{:S(2)}, u32[]{:S(2)}) %collective-permute-start.17) | collective-permute-done | bytes 16416 | tf_op jit(solution)/shard_map/ppermute | solution.py:55
  124.5 3.0 %collective-permute-start.20 = (f32[2,16,128]{2,1,0:T(8,128)S(1)}, f32[2,16,128]{2,1,0:T(8,128)S(1)}, u32[]{:S(2)}, u32[]{:S(2)}) collective-permute-start(f32[2,16,128]{2,1,0:T(8,128)S(1)} %get-tuple-element.27), channel_id=1, source_target_pairs={{0,192},{64,0},{128,64},{192,128},{1,193},{65,1},{129,65},{193,129... | collective-permute-start | bytes 49160 | tf_op jit(solution)/shard_map/ppermute | solution.py:55
  127.5 2.8 %collective-permute-start.19 = (f32[2,16,128]{2,1,0:T(8,128)S(1)}, f32[2,16,128]{2,1,0:T(8,128)S(1)}, u32[]{:S(2)}, u32[]{:S(2)}) collective-permute-start(f32[2,16,128]{2,1,0:T(8,128)S(1)} %get-tuple-element.27), channel_id=1, source_target_pairs={{0,128},{64,192},{128,0},{192,64},{1,129},{65,193},{129,1},{193,65... | collective-permute-start | bytes 49160 | tf_op jit(solution)/shard_map/ppermute | solution.py:55
  132.2 3.6 %collective-permute-done.18 = f32[2,16,128]{2,1,0:T(8,128)S(1)} collective-permute-done((f32[2,16,128]{2,1,0:T(8,128)S(1)}, f32[2,16,128]{2,1,0:T(8,128)S(1)}, u32[]{:S(2)}, u32[]{:S(2)}) %collective-permute-start.18) | collective-permute-done | bytes 16416 | tf_op jit(solution)/shard_map/ppermute | solution.py:55
  137.7 12.3 %all_to_all.21.full_ref = bf16[16,2,32,128]{3,2,1,0:T(8,128)(2,1)S(1)} all-to-all(bf16[16,2,32,128]{3,2,1,0:T(8,128)(2,1)S(1)} %broadcast_in_dim.50), channel_id=1, replica_groups=mesh['zl'=4,'co'=2,'x'=4,'y'=4,'zh'=2] {'x','y'}, dimensions={0} | all-to-all | bytes 524288 | tf_op jit(solution)/shard_map/all_to_all | solution.py:65
  (84 shorter events, 26.7 us)
Async XLA Ops:
  1.6 8.6 %collective-permute-start.2 = (bf16[8,32,256]{2,1,0:T(8,128)(2,1)S(1)}, bf16[8,32,256]{2,1,0:T(8,128)(2,1)S(1)}, u32[]{:S(2)}, u32[]{:S(2)}) collective-permute-start(bf16[8,32,256]{2,1,0:T(8,128)(2,1)S(1)} %bitcast.83), channel_id=1, source_target_pairs={{0,192},{64,0},{128,64},{192,128},{1,193},{65,1},{129,65},{193,129... | collective-permute-start | bytes 393224 | tf_op jit(solution)/shard_map/ppermute | solution.py:55
  6.3 11.2 %collective-permute-start.1 = (bf16[8,32,256]{2,1,0:T(8,128)(2,1)S(1)}, bf16[8,32,256]{2,1,0:T(8,128)(2,1)S(1)}, u32[]{:S(2)}, u32[]{:S(2)}) collective-permute-start(bf16[8,32,256]{2,1,0:T(8,128)(2,1)S(1)} %bitcast.84), channel_id=1, source_target_pairs={{0,128},{64,192},{128,0},{192,64},{1,129},{65,193},{129,1},{193,65... | collective-permute-start | bytes 393224 | tf_op jit(solution)/shard_map/ppermute | solution.py:55
  6.3 11.2 %collective-permute-start = (bf16[8,32,256]{2,1,0:T(8,128)(2,1)S(1)}, bf16[8,32,256]{2,1,0:T(8,128)(2,1)S(1)}, u32[]{:S(2)}, u32[]{:S(2)}) collective-permute-start(bf16[8,32,256]{2,1,0:T(8,128)(2,1)S(1)} %bitcast.85), channel_id=1, source_target_pairs={{0,64},{64,128},{128,192},{192,0},{1,65},{65,129},{129,193},{193,1... | collective-permute-start | bytes 393224 | tf_op jit(solution)/shard_map/ppermute | solution.py:55
  17.6 2.0 %collective-permute-start.3 = (bf16[32,32,256]{2,1,0:T(8,128)(2,1)S(1)}, bf16[32,32,256]{2,1,0:T(8,128)(2,1)S(1)}, u32[]{:S(2)}, u32[]{:S(2)}) collective-permute-start(bf16[32,32,256]{2,1,0:T(8,128)(2,1)S(1)} %bitcast.76), channel_id=1, source_target_pairs={{0,32},{32,0},{1,33},{33,1},{2,34},{34,2},{3,35},{35,3},{4,36},{36... | collective-permute-start | bytes 1572872 | tf_op jit(solution)/shard_map/ppermute | solution.py:55
  21.2 9.6 %collective-permute-start.4 = (bf16[2,8,16,256]{3,2,1,0:T(8,128)(2,1)S(1)}, bf16[2,8,16,256]{3,2,1,0:T(8,128)(2,1)S(1)}, u32[]{:S(2)}, u32[]{:S(2)}) collective-permute-start(bf16[2,8,16,256]{3,2,1,0:T(8,128)(2,1)S(1)} %get-tuple-element.17), channel_id=1, source_target_pairs={{0,1},{1,0},{2,3},{3,2},{4,5},{5,4},{6,7},{7,6},{8,9},{9,8},{10,11... | collective-permute-start | bytes 393224 | tf_op jit(solution)/shard_map/ppermute | solution.py:55
  30.9 7.8 %collective-permute-start.7 = (bf16[2,8,16,256]{3,2,1,0:T(8,128)(2,1)S(1)}, bf16[2,8,16,256]{3,2,1,0:T(8,128)(2,1)S(1)}, u32[]{:S(2)}, u32[]{:S(2)}) collective-permute-start(bf16[2,8,16,256]{3,2,1,0:T(8,128)(2,1)S(1)} %get-tuple-element.29), channel_id=1, source_target_pairs={{0,24},{8,0},{16,8},{24,16},{1,25},{9,1},{17,9},{25,17},{2,26},{10... | collective-permute-start | bytes 393224 | tf_op jit(solution)/shard_map/ppermute | solution.py:55
  33.7 8.7 %collective-permute-start.6 = (bf16[2,8,16,256]{3,2,1,0:T(8,128)(2,1)S(1)}, bf16[2,8,16,256]{3,2,1,0:T(8,128)(2,1)S(1)}, u32[]{:S(2)}, u32[]{:S(2)}) collective-permute-start(bf16[2,8,16,256]{3,2,1,0:T(8,128)(2,1)S(1)} %get-tuple-element.29), channel_id=1, source_target_pairs={{0,16},{8,24},{16,0},{24,8},{1,17},{9,25},{17,1},{25,9},{2,18},{10... | collective-permute-start | bytes 393224 | tf_op jit(solution)/shard_map/ppermute | solution.py:55
  34.5 7.9 %collective-permute-start.5 = (bf16[2,8,16,256]{3,2,1,0:T(8,128)(2,1)S(1)}, bf16[2,8,16,256]{3,2,1,0:T(8,128)(2,1)S(1)}, u32[]{:S(2)}, u32[]{:S(2)}) collective-permute-start(bf16[2,8,16,256]{3,2,1,0:T(8,128)(2,1)S(1)} %get-tuple-element.29), channel_id=1, source_target_pairs={{0,8},{8,16},{16,24},{24,0},{1,9},{9,17},{17,25},{25,1},{2,10},{10... | collective-permute-start | bytes 393224 | tf_op jit(solution)/shard_map/ppermute | solution.py:55
  35.4 7.1 %collective-permute-start.10 = (bf16[2,8,16,256]{3,2,1,0:T(8,128)(2,1)S(1)}, bf16[2,8,16,256]{3,2,1,0:T(8,128)(2,1)S(1)}, u32[]{:S(2)}, u32[]{:S(2)}) collective-permute-start(bf16[2,8,16,256]{3,2,1,0:T(8,128)(2,1)S(1)} %get-tuple-element.30), channel_id=1, source_target_pairs={{0,6},{2,0},{4,2},{6,4},{1,7},{3,1},{5,3},{7,5},{8,14},{10,8},{12,... | collective-permute-start | bytes 393224 | tf_op jit(solution)/shard_map/ppermute | solution.py:55
  35.9 7.1 %collective-permute-start.9 = (bf16[2,8,16,256]{3,2,1,0:T(8,128)(2,1)S(1)}, bf16[2,8,16,256]{3,2,1,0:T(8,128)(2,1)S(1)}, u32[]{:S(2)}, u32[]{:S(2)}) collective-permute-start(bf16[2,8,16,256]{3,2,1,0:T(8,128)(2,1)S(1)} %get-tuple-element.30), channel_id=1, source_target_pairs={{0,4},{2,6},{4,0},{6,2},{1,5},{3,7},{5,1},{7,3},{8,12},{10,14},{12... | collective-permute-start | bytes 393224 | tf_op jit(solution)/shard_map/ppermute | solution.py:55
  38.7 5.2 %collective-permute-start.8 = (bf16[2,8,16,256]{3,2,1,0:T(8,128)(2,1)S(1)}, bf16[2,8,16,256]{3,2,1,0:T(8,128)(2,1)S(1)}, u32[]{:S(2)}, u32[]{:S(2)}) collective-permute-start(bf16[2,8,16,256]{3,2,1,0:T(8,128)(2,1)S(1)} %get-tuple-element.30), channel_id=1, source_target_pairs={{0,2},{2,4},{4,6},{6,0},{1,3},{3,5},{5,7},{7,1},{8,10},{10,12},{12... | collective-permute-start | bytes 393224 | tf_op jit(solution)/shard_map/ppermute | solution.py:55
  44.7 20.9 %collective-permute-start.13 = (bf16[4,2,8,16,256]{4,3,2,1,0:T(8,128)(2,1)S(1)}, bf16[4,2,8,16,256]{4,3,2,1,0:T(8,128)(2,1)}, u32[]{:S(2)}, u32[]{:S(2)}) collective-permute-start(bf16[4,2,8,16,256]{4,3,2,1,0:T(8,128)(2,1)S(1)} %pad_maximum_fusion.3), channel_id=1, source_target_pairs={{0,6},{2,0},{4,2},{6,4},{1,7},{3,1},{5,3},{7,5},{8,14},{10,8},{12,... | collective-permute-start | bytes 1572872 | tf_op jit(solution)/shard_map/ppermute | solution.py:55
  47.6 36.3 %collective-permute-start.12 = (bf16[4,2,8,16,256]{4,3,2,1,0:T(8,128)(2,1)S(1)}, bf16[4,2,8,16,256]{4,3,2,1,0:T(8,128)(2,1)}, u32[]{:S(2)}, u32[]{:S(2)}) collective-permute-start(bf16[4,2,8,16,256]{4,3,2,1,0:T(8,128)(2,1)S(1)} %pad_maximum_fusion.3), channel_id=1, source_target_pairs={{0,4},{2,6},{4,0},{6,2},{1,5},{3,7},{5,1},{7,3},{8,12},{10,14},{12... | collective-permute-start | bytes 1572872 | tf_op jit(solution)/shard_map/ppermute | solution.py:55
  47.6 36.3 %collective-permute-start.11 = (bf16[4,2,8,16,256]{4,3,2,1,0:T(8,128)(2,1)S(1)}, bf16[4,2,8,16,256]{4,3,2,1,0:T(8,128)(2,1)}, u32[]{:S(2)}, u32[]{:S(2)}) collective-permute-start(bf16[4,2,8,16,256]{4,3,2,1,0:T(8,128)(2,1)S(1)} %pad_maximum_fusion.3), channel_id=1, source_target_pairs={{0,2},{2,4},{4,6},{6,0},{1,3},{3,5},{5,7},{7,1},{8,10},{10,12},{12... | collective-permute-start | bytes 1572872 | tf_op jit(solution)/shard_map/ppermute | solution.py:55
  49.7 37.1 %collective-permute-start.15 = (bf16[4,2,8,16,256]{4,3,2,1,0:T(8,128)(2,1)}, bf16[4,2,8,16,256]{4,3,2,1,0:T(8,128)(2,1)}, u32[]{:S(2)}, u32[]{:S(2)}) collective-permute-start(bf16[4,2,8,16,256]{4,3,2,1,0:T(8,128)(2,1)} %pad_maximum_fusion.4), channel_id=1, source_target_pairs={{0,16},{8,24},{16,0},{24,8},{1,17},{9,25},{17,1},{25,9},{2,18},{10... | collective-permute-start | bytes 1572872 | tf_op jit(solution)/shard_map/ppermute | solution.py:55
  51.7 35.0 %collective-permute-start.14 = (bf16[4,2,8,16,256]{4,3,2,1,0:T(8,128)(2,1)}, bf16[4,2,8,16,256]{4,3,2,1,0:T(8,128)(2,1)}, u32[]{:S(2)}, u32[]{:S(2)}) collective-permute-start(bf16[4,2,8,16,256]{4,3,2,1,0:T(8,128)(2,1)} %pad_maximum_fusion.4), channel_id=1, source_target_pairs={{0,8},{8,16},{16,24},{24,0},{1,9},{9,17},{17,25},{25,1},{2,10},{10... | collective-permute-start | bytes 1572872 | tf_op jit(solution)/shard_map/ppermute | solution.py:55
  54.0 46.2 %all-to-all-start = ((f32[32,8,1024]{2,1,0:T(8,128)}), f32[32,8,1024]{2,1,0:T(8,128)S(1)}, u32[]{:S(2)}, u32[]{:S(2)}) async-start(f32[32,8,1024]{2,1,0:T(8,128)} %bitcast.23), calls=%async_computation | async-start | bytes 2097152 | tf_op jit(solution)/shard_map/all_to_all | solution.py:440
  65.6 21.1 %collective-permute-start.16 = (bf16[4,2,8,16,256]{4,3,2,1,0:T(8,128)(2,1)}, bf16[4,2,8,16,256]{4,3,2,1,0:T(8,128)(2,1)S(1)}, u32[]{:S(2)}, u32[]{:S(2)}) collective-permute-start(bf16[4,2,8,16,256]{4,3,2,1,0:T(8,128)(2,1)} %pad_maximum_fusion.4), channel_id=1, source_target_pairs={{0,24},{8,0},{16,8},{24,16},{1,25},{9,1},{17,9},{25,17},{2,26},{10... | collective-permute-start | bytes 1572872 | tf_op jit(solution)/shard_map/ppermute | solution.py:55
  102.8 14.0 %all-to-all-start.1 = ((f32[32,16,128]{2,1,0:T(8,128)}), f32[32,16,128]{2,1,0:T(8,128)S(1)}, u32[]{:S(2)}, u32[]{:S(2)}) async-start(f32[32,16,128]{2,1,0:T(8,128)} %kernel_blocks.1), calls=%async_computation.1 | async-start | bytes 524288 | tf_op jit(solution)/shard_map/all_to_all | solution.py:447
  116.8 7.8 %collective-permute-start.17 = (f32[2,16,128]{2,1,0:T(8,128)S(1)}, f32[2,16,128]{2,1,0:T(8,128)S(1)}, u32[]{:S(2)}, u32[]{:S(2)}) collective-permute-start(f32[2,16,128]{2,1,0:T(8,128)S(1)} %reduce_sum.18), channel_id=1, source_target_pairs={{0,1},{1,0},{2,3},{3,2},{4,5},{5,4},{6,7},{7,6},{8,9},{9,8},{10,11... | collective-permute-start | bytes 49160 | tf_op jit(solution)/shard_map/ppermute | solution.py:55
  124.5 7.7 %collective-permute-start.20 = (f32[2,16,128]{2,1,0:T(8,128)S(1)}, f32[2,16,128]{2,1,0:T(8,128)S(1)}, u32[]{:S(2)}, u32[]{:S(2)}) collective-permute-start(f32[2,16,128]{2,1,0:T(8,128)S(1)} %get-tuple-element.27), channel_id=1, source_target_pairs={{0,192},{64,0},{128,64},{192,128},{1,193},{65,1},{129,65},{193,129... | collective-permute-start | bytes 49160 | tf_op jit(solution)/shard_map/ppermute | solution.py:55
  127.5 4.7 %collective-permute-start.19 = (f32[2,16,128]{2,1,0:T(8,128)S(1)}, f32[2,16,128]{2,1,0:T(8,128)S(1)}, u32[]{:S(2)}, u32[]{:S(2)}) collective-permute-start(f32[2,16,128]{2,1,0:T(8,128)S(1)} %get-tuple-element.27), channel_id=1, source_target_pairs={{0,128},{64,192},{128,0},{192,64},{1,129},{65,193},{129,1},{193,65... | collective-permute-start | bytes 49160 | tf_op jit(solution)/shard_map/ppermute | solution.py:55
  130.3 5.5 %collective-permute-start.18 = (f32[2,16,128]{2,1,0:T(8,128)S(1)}, f32[2,16,128]{2,1,0:T(8,128)S(1)}, u32[]{:S(2)}, u32[]{:S(2)}) collective-permute-start(f32[2,16,128]{2,1,0:T(8,128)S(1)} %get-tuple-element.27), channel_id=1, source_target_pairs={{0,64},{64,128},{128,192},{192,0},{1,65},{65,129},{129,193},{193,1... | collective-permute-start | bytes 49160 | tf_op jit(solution)/shard_map/ppermute | solution.py:55
  135.8 1.3 collective-permute-start.21
  (9 other events, 194.6 us)
